TPU v7x, 32 devices: a whole 2x2x4 slice. The times are simulated.
32 devices in a mesh: group: 4 (over x, core), ctx: 8 (over z, y).
Axes of the slice: x: 2, y: 2, z: 4, core: 2. Of those that a mesh axis runs over, the one named last changes fastest.
Arguments:
- outer_gate: bfloat16 [4096, 4096], P('group', 'ctx'), may hold values from -6 to 6
- inner_gate: bfloat16 [4096, 4096], P('group', 'ctx'), may hold values from -6 to 6
- signal: bfloat16 [4096, 4096], P('group', 'ctx'), may hold values from -6 to 6
- cotangent: bfloat16 [4096, 4096], P('group', 'ctx'), may hold values from -6 to 6
- out_weight: bfloat16 [4096, 4096], P('group'), may hold values from -0.09375 to 0.09375
- filter_taps: float32 [4096, 4096], P('group', 'ctx'), may hold values from -6 to 6
- skip_gain: float32 [4096], P('group'), may hold values from -4 to 4
Outputs:
- grad_outer: bfloat16 [4096, 4096], P('group', 'ctx')
- grad_inner: bfloat16 [4096, 4096], P('group', 'ctx')
- grad_signal: bfloat16 [4096, 4096], P('group', 'ctx')
- grad_taps: float32 [4096, 4096], P('group', 'ctx')
All inputs are finite; a program needn't handle non-finite values.
Results may differ from a plain program's by a relative error of at most 0.014.
Values may be sent and summed in bfloat16 or wider, within the bound.
No kernel may reach another device: no remote copies, remote signals or barrier semaphores. Data moves between devices by JAX's collectives and lax.ppermute only.
A program may use at most 128 MiB of HBM per device.

v0:
```python
import math

import jax
import jax.numpy as jnp
from jax import lax
from jax.sharding import PartitionSpec as P

HIGHER = lax.Precision.HIGH


def contract(form, left, right):
    return jnp.einsum(form, left, right, precision=HIGHER, preferred_element_type=jnp.float32)


def make_tables(outer_len, inner_len, fft_len):
    two_pi = 2.0 * math.pi
    freq_outer = jnp.arange(outer_len, dtype=jnp.int32)
    pos_outer = jnp.arange(outer_len // 2, dtype=jnp.int32)
    inner_index = jnp.arange(inner_len, dtype=jnp.int32)
    angle_outer = (freq_outer[:, None] * pos_outer[None, :] % outer_len).astype(jnp.float32) * (
        two_pi / outer_len
    )
    angle_inner = (inner_index[:, None] * inner_index[None, :] % inner_len).astype(jnp.float32) * (
        two_pi / inner_len
    )
    angle_twist = (freq_outer[:, None] * inner_index[None, :] % fft_len).astype(jnp.float32) * (
        two_pi / fft_len
    )
    cos_outer = jnp.cos(angle_outer)
    sin_outer = jnp.sin(angle_outer)
    cos_inner = jnp.cos(angle_inner)
    sin_inner = jnp.sin(angle_inner)
    forward_outer = jnp.concatenate([cos_outer.T, -sin_outer.T], axis=1)
    forward_inner = jnp.concatenate(
        [
            jnp.concatenate([cos_inner, -sin_inner], axis=1),
            jnp.concatenate([sin_inner, cos_inner], axis=1),
        ],
        axis=0,
    )
    inverse_inner = jnp.concatenate(
        [
            jnp.concatenate([cos_inner, sin_inner], axis=1),
            jnp.concatenate([-sin_inner, cos_inner], axis=1),
        ],
        axis=0,
    )
    inverse_outer = jnp.concatenate([cos_outer, -sin_outer], axis=0)
    return (
        forward_outer,
        forward_inner,
        inverse_inner,
        inverse_outer,
        jnp.cos(angle_twist),
        jnp.sin(angle_twist),
    )


def forward_dft(rows, tables):
    forward_outer, forward_inner, inverse_inner, inverse_outer, cos_twist, sin_twist = tables
    outer_len = cos_twist.shape[0]
    inner_len = cos_twist.shape[1]
    lanes = rows.shape[0]
    shaped = rows.reshape(lanes, outer_len // 2, inner_len)
    first = contract("cnm,nk->ckm", shaped, forward_outer)
    first_re = first[:, :outer_len]
    first_im = first[:, outer_len:]
    twist_re = first_re * cos_twist + first_im * sin_twist
    twist_im = first_im * cos_twist - first_re * sin_twist
    both = contract("ckm,mj->ckj", jnp.concatenate([twist_re, twist_im], axis=2), forward_inner)
    return (both[:, :, :inner_len], both[:, :, inner_len:])


def inverse_dft(spec, tables):
    forward_outer, forward_inner, inverse_inner, inverse_outer, cos_twist, sin_twist = tables
    outer_len = cos_twist.shape[0]
    inner_len = cos_twist.shape[1]
    spec_re, spec_im = spec
    back = contract("ckj,jm->ckm", jnp.concatenate([spec_re, spec_im], axis=2), inverse_inner)
    back_re = back[:, :, :inner_len]
    back_im = back[:, :, inner_len:]
    turn_re = back_re * cos_twist - back_im * sin_twist
    turn_im = back_im * cos_twist + back_re * sin_twist
    result = contract("ckm,kn->cnm", jnp.concatenate([turn_re, turn_im], axis=1), inverse_outer)
    fft_len = outer_len * inner_len
    return (result / fft_len).reshape(result.shape[0], -1)


def times_plain(left, right):
    return (left[0] * right[0] - left[1] * right[1], left[0] * right[1] + left[1] * right[0])


def times_conj(left, right):
    return (left[0] * right[0] + left[1] * right[1], left[1] * right[0] - left[0] * right[1])


def channel_work(product_rows, grad_rows, taps_rows, scale):
    seq_len = product_rows.shape[1]
    fft_len = 2 * seq_len
    inner_len = 128
    tables = make_tables(fft_len // inner_len, inner_len, fft_len)
    spec_prod = forward_dft(product_rows.astype(jnp.float32), tables)
    spec_grad = forward_dft(grad_rows.astype(jnp.float32), tables)
    spec_taps = forward_dft(taps_rows, tables)
    response = inverse_dft(times_plain(spec_prod, spec_taps), tables).astype(jnp.bfloat16)
    back_signal = inverse_dft(times_conj(spec_grad, spec_taps), tables).astype(jnp.bfloat16)
    grad_taps = scale * inverse_dft(times_conj(spec_grad, spec_prod), tables)
    return (response, back_signal, grad_taps)


def elementwise(left, right):
    return (left.astype(jnp.float32) * right.astype(jnp.float32)).astype(jnp.bfloat16)


def per_device(outer_gate, inner_gate, signal, cotangent, out_weight, filter_taps, skip_gain):
    ch_dev, tok_local = outer_gate.shape
    n_ctx = lax.axis_size("ctx")
    ch_slice = ch_dev // n_ctx
    seq_len = n_ctx * tok_local
    scale = 1.0 / math.sqrt(seq_len)
    upstream = jnp.dot(
        out_weight,
        lax.all_gather(cotangent, "group", axis=0, tiled=True),
        preferred_element_type=jnp.float32,
    ).astype(jnp.bfloat16)
    is_first = (lax.axis_index("ctx") == 0).astype(jnp.float32)
    eff_taps = filter_taps * scale
    eff_taps = eff_taps.at[:, 0].add(is_first * skip_gain)

    def to_channels(array):
        return array.reshape(n_ctx, ch_slice, tok_local)

    def rows_of(array):
        return array.reshape(ch_slice, seq_len)

    def to_positions(array):
        return array.reshape(1, ch_slice, seq_len)

    def merged(array):
        return array.reshape(ch_dev, tok_local)

    taps_rows = rows_of(
        lax.all_to_all(
            to_channels(eff_taps).astype(jnp.bfloat16),
            "ctx",
            split_axis=0,
            concat_axis=2,
            tiled=True,
        ).astype(jnp.float32)
    )
    product = elementwise(inner_gate, signal)
    grad_prod = elementwise(upstream, outer_gate)
    prod_moved, grad_moved = (
        lax.all_to_all(to_channels(product), "ctx", split_axis=0, concat_axis=2, tiled=True),
        lax.all_to_all(to_channels(grad_prod), "ctx", split_axis=0, concat_axis=2, tiled=True),
    )
    response, back_signal, grad_taps = channel_work(
        rows_of(prod_moved), rows_of(grad_moved), taps_rows, scale
    )
    resp_home, back_home = (
        lax.all_to_all(to_positions(response), "ctx", split_axis=2, concat_axis=0, tiled=True),
        lax.all_to_all(to_positions(back_signal), "ctx", split_axis=2, concat_axis=0, tiled=True),
    )
    response_seq = merged(resp_home)
    back_seq = merged(back_home)
    grad_outer = elementwise(upstream, response_seq)
    grad_inner = elementwise(back_seq, signal)
    grad_signal = elementwise(back_seq, inner_gate)
    taps_home = lax.all_to_all(
        to_positions(grad_taps).astype(jnp.bfloat16), "ctx", split_axis=2, concat_axis=0, tiled=True
    ).astype(jnp.float32)
    return (grad_outer, grad_inner, grad_signal, merged(taps_home))


def solution(mesh):
    in_specs = (
        P("group", "ctx"),
        P("group", "ctx"),
        P("group", "ctx"),
        P("group", "ctx"),
        P("group", None),
        P("group", "ctx"),
        P("group"),
    )
    out_specs = (P("group", "ctx"), P("group", "ctx"), P("group", "ctx"), P("group", "ctx"))
    return jax.shard_map(
        per_device, mesh=mesh, in_specs=in_specs, out_specs=out_specs, check_vma=False
    )
```

profile of v0, /device:TPU:0, one launch (start us, length us, event | category | flops | bytes accessed | tf_op | source)
XLA Modules:
  0.0 423.5 jit_solution(7999982414506869150)
XLA Ops:
  15.5 7.3 %all-to-all-start.1 = ((bf16[8,128,512]{2,1,0:T(8,128)(2,1)}), bf16[8,128,512]{2,1,0:T(8,128)(2,1)S(1)}, u32[]{:S(2)}, u32[]{:S(2)}) async-start(bf16[8,128,512]{2,1,0:T(8,128)(2,1)} %bitcast.8), calls=%async_computation.1 | async-start | bytes 2097152 | tf_op jit(solution)/shard_map/all_to_all | solution.py:143
  22.8 24.0 %all-gather.2.cloned.1.call-done = bf16[4096,512]{1,0:T(8,128)(2,1)} async-done(((bf16[1024,512]{1,0:T(8,128)(2,1)}), bf16[4096,512]{1,0:T(8,128)(2,1)}) %all-gather.2.cloned.1.call-update) | async-done | bytes 4194320 | tf_op jit(solution)/shard_map/all_gather | solution.py:123
  46.8 10.7 %fusion.25 = (bf16[1024,512]{1,0:T(8,128)(2,1)}, bf16[1024,512]{1,0:T(8,128)(2,1)}) fusion(bf16[1024,512]{1,0:T(8,128)(2,1)} %param.9, bf16[1024,4096]{1,0:T(8,128)(2,1)} %param.13, bf16[4096,512]{1,0:T(8,128)(2,1)} %all-gather.2.cloned.1.call-done), kind=kOutput, calls=%fused_computation.57 | convolution fusion | flops 4297588736 | bytes 15728640 | tf_op jit(solution)/shard_map/dot_general | solution.py:121
  57.4 5.8 %all-to-all-start.3 = ((bf16[8,128,512]{2,1,0:T(8,128)(2,1)}), bf16[8,128,512]{2,1,0:T(8,128)(2,1)S(1)}, u32[]{:S(2)}, u32[]{:S(2)}) async-start(bf16[8,128,512]{2,1,0:T(8,128)(2,1)} %bitcast.17), calls=%async_computation.3 | async-start | bytes 2097152 | tf_op jit(solution)/shard_map/all_to_all | solution.py:155
  65.4 5.7 %convolution_bitcast_fusion.1 = f32[128,128,128]{2,1,0:T(8,128)} fusion(bf16[128,32,128]{2,1,0:T(8,128)(2,1)S(1)} %reshape_reshape.3, f32[32,64]{1,0:T(8,128)S(1)} %get-tuple-element.45, f32[32,64]{1,0:T(8,128)S(1)} %get-tuple-element.46), kind=kOutput, calls=%fused_computation.49 | convolution fusion | flops 402657280 | bytes 9453568 | tf_op jit(solution)/shard_map/cnm,nk->ckm/dot_general | solution.py:12
  71.0 18.3 %all-to-all-done.3 = bf16[8,128,512]{2,1,0:T(8,128)(2,1)S(1)} async-done(((bf16[8,128,512]{2,1,0:T(8,128)(2,1)}), bf16[8,128,512]{2,1,0:T(8,128)(2,1)S(1)}, u32[]{:S(2)}, u32[]{:S(2)}) %all-to-all-start.3) | async-done | bytes 1048608 | tf_op jit(solution)/shard_map/all_to_all | solution.py:155
  94.0 5.9 %multiply_add_fusion.4 = (f32[128,64,128]{2,1,0:T(8,128)}, f32[128,64,128]{2,1,0:T(8,128)}, f32[128,64,128]{2,1,0:T(8,128)S(1)}, f32[128,64,128]{2,1,0:T(8,128)}) fusion(f32[128,128,128]{2,1,0:T(8,128)S(1)} %convolution_bitcast_fusion, f32[64,128]{1,0:T(8,128)S(1)} %get-tuple-element.47, f32[64,128]{1,0:T(8,128)S(1)} %get-tuple-element.48, ...), kind=kLoop, calls=%fused_computation.39 | loop fusion | flops 12582912 | bytes 33619968 | tf_op jit(solution)/shard_map/add | solution.py:68
  99.8 4.4 %pad_maximum_fusion.3 = f32[128,64,256]{2,1,0:T(8,128)S(1)} fusion(f32[128,64,128]{2,1,0:T(8,128)} %get-tuple-element.27, f32[128,64,128]{2,1,0:T(8,128)} %get-tuple-element.26), kind=kLoop, calls=%fused_computation.7 | loop fusion | flops 2097152 | bytes 16777216 | tf_op jit(solution)/shard_map/concatenate | solution.py:70
  107.5 7.9 %fusion.18 = f32[128,64,256]{2,0,1:T(8,128)S(1)} fusion(f32[128,64,256]{2,1,0:T(8,128)S(1)} %pad_maximum_fusion.3, f32[128,128]{1,0:T(8,128)S(1)} %get-tuple-element.50, f32[128,128]{1,0:T(8,128)S(1)} %get-tuple-element.49, f32[128,128]{1,0:T(8,128)S(1)} %fusion.68), kind=kOutput, calls=%fused_computation.24 | convolution fusion | flops 3221422080 | bytes 16973824 | tf_op jit(solution)/shard_map/ckm,mj->ckj/dot_general | solution.py:12
  115.3 8.3 %fusion.20 = f32[128,64,256]{2,0,1:T(8,128)S(1)} fusion(f32[128,64,256]{2,1,0:T(8,128)S(1)} %pad_maximum_fusion.1, f32[128,128]{1,0:T(8,128)S(1)} %get-tuple-element.50, f32[128,128]{1,0:T(8,128)S(1)} %get-tuple-element.49, f32[128,128]{1,0:T(8,128)S(1)} %fusion.68), kind=kOutput, calls=%fused_computation.26 | convolution fusion | flops 3221422080 | bytes 16973824 | tf_op jit(solution)/shard_map/ckm,mj->ckj/dot_general | solution.py:12
  123.7 3.7 multiply_add_fusion.3
  131.2 7.8 %fusion.14 = f32[128,64,256]{2,1,0:T(8,128)S(1)} fusion(f32[128,64,256]{2,0,1:T(8,128)S(1)} %pad_maximum_fusion.4, f32[128,128]{1,0:T(8,128)S(1)} %get-tuple-element.50, f32[128,128]{1,0:T(8,128)S(1)} %fusion.68, f32[128,128]{1,0:T(8,128)S(1)} %get-tuple-element.49), kind=kOutput, calls=%fused_computation.20 | convolution fusion | flops 3221422080 | bytes 16973824 | tf_op jit(solution)/shard_map/ckj,jm->ckm/dot_general | solution.py:12
  140.3 3.3 fusion.38
  147.5 22.4 %reduce.8 = bf16[4096,128]{1,0:T(8,128)(2,1)S(1)} reduce(bf16[4096,1,128]{2,1,0:T(2,128)(2,1)S(1)} %bitcast.83, bf16[]{:T(256)} %broadcast.161), dimensions={1}, to_apply=%bitcast.69.reduce_sub_computation | reduce | bytes 2097154
  170.1 29.4 %all_to_all.72 = bf16[8,2,32768]{2,1,0:T(2,128)(2,1)S(1)} all-to-all(bf16[8,2,32768]{2,1,0:T(2,128)(2,1)S(1)} %reshape.172), channel_id=1, replica_groups=mesh['group'=4,'ctx'=8] {'ctx'}, dimensions={0} | all-to-all | bytes 2097152 | tf_op jit(solution)/shard_map/all_to_all | solution.py:162
  205.7 3.5 fusion.26
  209.2 28.9 %all_to_all.73 = bf16[8,128,512]{2,1,0:T(8,128)(2,1)S(1)} all-to-all(bf16[8,128,512]{2,1,0:T(8,128)(2,1)S(1)} %bitcast.89), channel_id=1, replica_groups=mesh['group'=4,'ctx'=8] {'ctx'}, dimensions={0} | all-to-all | bytes 2097152 | tf_op jit(solution)/shard_map/all_to_all | solution.py:154
  243.5 4.2 pad_maximum_fusion
  247.8 14.7 %fusion.22 = f32[128,64,256]{2,0,1:T(8,128)} fusion(f32[128,64,256]{2,1,0:T(8,128)} %pad_maximum_fusion, f32[128,128]{1,0:T(8,128)S(1)} %get-tuple-element.50, f32[128,128]{1,0:T(8,128)S(1)} %get-tuple-element.49, f32[128,128]{1,0:T(8,128)S(1)} %fusion.68), kind=kOutput, calls=%fused_computation.28 | convolution fusion | flops 3221422080 | bytes 16973824 | tf_op jit(solution)/shard_map/ckm,mj->ckj/dot_general | solution.py:12
  262.4 11.0 %multiply_add_fusion.1 = (f32[128,64,128]{2,0,1:T(8,128)}, f32[128,64,128]{2,0,1:T(8,128)}, f32[128,64,128]{2,0,1:T(8,128)S(1)}, f32[128,64,128]{2,0,1:T(8,128)}) fusion(f32[128,64,256]{2,0,1:T(8,128)S(1)} %bitcast.81, f32[128,64,256]{2,0,1:T(8,128)} %fusion.22, f32[128,64,256]{2,0,1:T(8,128)} %copy-done.1), kind=kLoop, calls=%fused_computation.33 | loop fusion | flops 12582912 | bytes 41943040 | tf_op jit(solution)/shard_map/add | solution.py:94
  273.4 4.2 pad_maximum_fusion.5
  277.6 7.8 %fusion.12 = f32[128,64,256]{2,1,0:T(8,128)S(1)} fusion(f32[128,64,256]{2,0,1:T(8,128)S(1)} %pad_maximum_fusion.5, f32[128,128]{1,0:T(8,128)S(1)} %get-tuple-element.50, f32[128,128]{1,0:T(8,128)S(1)} %fusion.68, f32[128,128]{1,0:T(8,128)S(1)} %get-tuple-element.49), kind=kOutput, calls=%fused_computation.18 | convolution fusion | flops 3221422080 | bytes 16973824 | tf_op jit(solution)/shard_map/ckj,jm->ckm/dot_general | solution.py:12
  288.4 9.3 %fusion.16 = f32[128,64,256]{2,1,0:T(8,128)} fusion(f32[128,64,256]{2,0,1:T(8,128)S(1)} %pad_maximum_fusion.2, f32[128,128]{1,0:T(8,128)S(1)} %get-tuple-element.50, f32[128,128]{1,0:T(8,128)S(1)} %fusion.68, f32[128,128]{1,0:T(8,128)S(1)} %get-tuple-element.49), kind=kOutput, calls=%fused_computation.22 | convolution fusion | flops 3221422080 | bytes 16973824 | tf_op jit(solution)/shard_map/ckj,jm->ckm/dot_general | solution.py:12
  297.8 6.5 %multiply_subtract_fusion = (f32[128,64,128]{2,1,0:T(8,128)S(1)}, f32[128,64,128]{2,1,0:T(8,128)S(1)}, f32[128,64,128]{2,1,0:T(8,128)}, f32[128,64,128]{2,1,0:T(8,128)}) fusion(f32[128,64,256]{2,1,0:T(8,128)S(1)} %fusion.12, f32[64,128]{1,0:T(8,128)S(1)} %get-tuple-element.47, f32[64,128]{1,0:T(8,128)S(1)} %get-tuple-element.48, f32[128,64,256]{2,1,0:T(8,128)} %fusion.16), kind=kLoop, calls=%fused_computation.31 | loop fusion | flops 12582912 | bytes 33619968 | tf_op jit(solution)/shard_map/sub | solution.py:82
  310.7 22.4 %reduce.10 = bf16[4096,128]{1,0:T(8,128)(2,1)S(1)} reduce(bf16[4096,1,128]{2,1,0:T(2,128)(2,1)S(1)} %bitcast.86, bf16[]{:T(256)} %broadcast.161), dimensions={1}, to_apply=%bitcast.71.reduce_sub_computation | reduce | bytes 2097154
  334.2 3.8 all-to-all-start.5
  338.0 6.2 %fusion.35 = bf16[128,32,128]{2,1,0:T(8,128)(2,1)S(1)} fusion(f32[128,64,128]{2,1,0:T(8,128)} %get-tuple-element.39, f32[128,64,128]{2,1,0:T(8,128)} %get-tuple-element.40, f32[64,32]{0,1:T(8,128)S(1)} %get-tuple-element.51, f32[64,32]{0,1:T(8,128)S(1)} %get-tuple-element.52), kind=kOutput, calls=%fused_computation.66 | convolution fusion | flops 405803008 | bytes 9453568 | tf_op jit(solution)/shard_map/ckm,kn->cnm/dot_general | solution.py:12
  345.5 5.0 %copy.50 = bf16[1,128,4096]{1,0,2:T(2,128)(2,1)S(1)} copy(bf16[1,128,4096]{2,1,0:T(8,128)(2,1)} %convert_element_type.230) | data formatting | bytes 2097152 | tf_op jit(solution)/shard_map/convert_element_type | solution.py:105
  350.5 23.3 %reduce.9 = bf16[4096,128]{1,0:T(8,128)(2,1)} reduce(bf16[4096,1,128]{2,1,0:T(2,128)(2,1)S(1)} %bitcast.84, bf16[]{:T(256)} %broadcast.161), dimensions={1}, to_apply=%bitcast.67.reduce_sub_computation | reduce | bytes 2097154
  376.0 6.0 %all-to-all-start.2 = ((bf16[8,2,32768]{2,1,0:T(2,128)(2,1)}), bf16[8,2,32768]{2,1,0:T(2,128)(2,1)}, u32[]{:S(2)}, u32[]{:S(2)}) async-start(bf16[8,2,32768]{2,1,0:T(2,128)(2,1)} %reshape.170), calls=%async_computation.2 | async-start | bytes 2097152 | tf_op jit(solution)/shard_map/all_to_all | solution.py:161
  389.2 17.9 %all-to-all-done.2 = bf16[8,2,32768]{2,1,0:T(2,128)(2,1)} async-done(((bf16[8,2,32768]{2,1,0:T(2,128)(2,1)}), bf16[8,2,32768]{2,1,0:T(2,128)(2,1)}, u32[]{:S(2)}, u32[]{:S(2)}) %all-to-all-start.2) | async-done | bytes 1048608 | tf_op jit(solution)/shard_map/all_to_all | solution.py:161
  407.0 4.3 %reshape.171 = bf16[4096,1,128]{2,1,0:T(2,128)(2,1)S(1)} reshape(bf16[8,2,32768]{2,1,0:T(2,128)(2,1)} %all-to-all-done.2) | data formatting | bytes 2097152
  (67 shorter events, 64.9 us)
Async XLA Ops:
  7.2 4.3 %copy-start.5 = (f32[1024]{0:T(1024)S(1)}, f32[1024]{0:T(1024)}, u32[]{:S(2)}) copy-start(f32[1024]{0:T(1024)} %param.15) | copy-start | bytes 12292
  7.2 39.6 %all-gather.2.cloned.1.call-start = ((), (), s32[]{:S(2)}) async-start(), calls=%async_computation.6 | async-start | bytes 5242880 | tf_op jit(solution)/shard_map/all_gather | solution.py:123
  15.5 42.0 %all-to-all-start.1 = ((bf16[8,128,512]{2,1,0:T(8,128)(2,1)}), bf16[8,128,512]{2,1,0:T(8,128)(2,1)S(1)}, u32[]{:S(2)}, u32[]{:S(2)}) async-start(bf16[8,128,512]{2,1,0:T(8,128)(2,1)} %bitcast.8), calls=%async_computation.1 | async-start | bytes 2097152 | tf_op jit(solution)/shard_map/all_to_all | solution.py:143
  57.4 31.9 %all-to-all-start.3 = ((bf16[8,128,512]{2,1,0:T(8,128)(2,1)}), bf16[8,128,512]{2,1,0:T(8,128)(2,1)S(1)}, u32[]{:S(2)}, u32[]{:S(2)}) async-start(bf16[8,128,512]{2,1,0:T(8,128)(2,1)} %bitcast.17), calls=%async_computation.3 | async-start | bytes 2097152 | tf_op jit(solution)/shard_map/all_to_all | solution.py:155
  90.6 3.4 copy-start.2
  115.3 8.3 %copy-start = (f32[128,64,256]{2,0,1:T(8,128)}, f32[128,64,256]{2,0,1:T(8,128)S(1)}, u32[]{:S(2)}) copy-start(f32[128,64,256]{2,0,1:T(8,128)S(1)} %fusion.18) | copy-start | bytes 25165828
  123.7 4.5 %copy-start.1 = (f32[128,64,256]{2,0,1:T(8,128)}, f32[128,64,256]{2,0,1:T(8,128)S(1)}, u32[]{:S(2)}) copy-start(f32[128,64,256]{2,0,1:T(8,128)S(1)} %fusion.20) | copy-start | bytes 25165828
  200.5 5.2 %copy-start.3 = (bf16[1024,512]{1,0:T(8,128)(2,1)S(1)}, bf16[1024,512]{1,0:T(8,128)(2,1)}, u32[]{:S(2)}) copy-start(bf16[1024,512]{1,0:T(8,128)(2,1)} %param.10) | copy-start | bytes 3145732
  243.5 18.9 %slice-start = ((s8[8388608]{0:T(1024)(128)(4,1)}), s8[4194304]{0:T(1024)(128)(4,1)S(1)}, s32[]{:S(2)}) async-start(s8[8388608]{0:T(1024)(128)(4,1)} %bitcast.80), calls=%async_computation.7 | async-start | bytes 8388608
  247.8 14.7 %slice-start.1 = ((s8[8388608]{0:T(1024)(128)(4,1)}), s8[4194304]{0:T(1024)(128)(4,1)S(1)}, s32[]{:S(2)}) async-start(s8[8388608]{0:T(1024)(128)(4,1)} %bitcast.80), calls=%async_computation.8 | async-start | bytes 8388608
  334.2 41.8 %all-to-all-start.5 = ((bf16[8,2,32768]{2,1,0:T(2,128)(2,1)}), bf16[8,2,32768]{2,1,0:T(2,128)(2,1)S(1)}, u32[]{:S(2)}, u32[]{:S(2)}) async-start(bf16[8,2,32768]{2,1,0:T(2,128)(2,1)} %reshape.174), calls=%async_computation.5 | async-start | bytes 2097152 | tf_op jit(solution)/shard_map/all_to_all | solution.py:169
  376.0 31.0 %all-to-all-start.2 = ((bf16[8,2,32768]{2,1,0:T(2,128)(2,1)}), bf16[8,2,32768]{2,1,0:T(2,128)(2,1)}, u32[]{:S(2)}, u32[]{:S(2)}) async-start(bf16[8,2,32768]{2,1,0:T(2,128)(2,1)} %reshape.170), calls=%async_computation.2 | async-start | bytes 2097152 | tf_op jit(solution)/shard_map/all_to_all | solution.py:161
  411.5 3.4 copy-start.4
Sparse Core Ops, SparseCore 0:
  9.6 37.1 all-gather.1
where the time goes:
time: 428 us; the launch traced here: 423 us
  other arithmetic  136 us (32%)
  matrix products  89.8 us (21%)
  waiting for transfers between devices  60.8 us (14%)
  blocking collectives  58.2 us (14%)
  local copies, waits for them, and re-layouts  40.4 us (9%)
  starting transfers between devices  22.9 us (5%)
  between operations  14.9 us (3%)
    dot_general x12, matrix products, contract(): jnp.einsum(form, left, right, precision=HIGHER, preferred_element_type=jn...  79.1 us
    unnamed x4, other arithmetic  68 us
    all_to_all x1, blocking collectives, per_device(): lax.all_to_all(to_positions(back_signal), 'ctx', split_axis=2, concat_axi...  29.4 us
    all_to_all x1, blocking collectives, per_device(): lax.all_to_all(to_channels(product), 'ctx', split_axis=0, concat_axis=2,...  28.9 us
    all_gather x1, waiting for transfers between devices, per_device(): lax.all_gather(cotangent, 'group', axis=0, tiled=True)  24 us
    all_to_all x1, waiting for transfers between devices, per_device(): lax.all_to_all(to_channels(grad_prod), 'ctx', split_axis=0, concat_axis=2...  18.3 us
    all_to_all x1, waiting for transfers between devices, per_device(): lax.all_to_all(to_positions(response), 'ctx', split_axis=2, concat_axis=0...  17.9 us
    unnamed x24, local copies, waits for them, and re-layouts  15 us
  transfers between devices with their start and end apart: 5, of which 3 were waited for; matrix products, arithmetic and copies ran while one was open for 17% of the time, Pallas kernels for 0%

commit v1 on v0

v1 whole, which is shorter than its diff:
```python
import functools
import math

import jax
import jax.numpy as jnp
import ml_dtypes
import numpy as np
from jax import lax
from jax.experimental import pallas as pl
from jax.experimental.pallas import tpu as pltpu
from jax.sharding import PartitionSpec as P

SLABS = 32
GROUP = 8
STEP = 2 * GROUP
F32 = jnp.float32
BF16 = jnp.bfloat16


def make_tables(inner):
    slab = np.arange(SLABS)
    freq = np.arange(SLABS) + 0.5
    angle = 2.0 * np.pi / (2 * SLABS) * np.outer(freq, slab)
    eye = np.eye(GROUP)
    first = np.concatenate([np.kron(np.cos(angle), eye), np.kron(-np.sin(angle), eye)], axis=0)
    last = first.T
    within = np.arange(inner)
    turn = np.repeat(2.0 * np.pi / (2 * SLABS * inner) * np.outer(freq, within), GROUP, axis=0)
    circle = 2.0 * np.pi / inner * (np.outer(within, within) % inner)
    cos, sin = np.cos(circle), np.sin(circle)
    forward = np.block([[cos, -sin], [sin, cos]])
    narrow = ml_dtypes.bfloat16
    return (
        first.astype(narrow),
        last.astype(narrow),
        np.cos(turn).astype(np.float32),
        np.sin(turn).astype(np.float32),
        forward.astype(narrow),
        forward.T.astype(narrow),
    )


def gather_slabs(block, inner):
    sources, _, local = block.shape
    wide = block.astype(F32)
    halves = []
    for half in range(2):
        pieces = [
            wide[src, half * GROUP : (half + 1) * GROUP, at : at + inner]
            for src in range(sources)
            for at in range(0, local, inner)
        ]
        halves.append(jnp.concatenate(pieces, axis=0))
    return jnp.concatenate(halves, axis=1).astype(BF16)


def forward_dft(rows, first, cos, sin, forward, inner):
    stage = jnp.dot(first, rows, preferred_element_type=F32)
    half_rows = SLABS * GROUP
    turned = []
    for half in range(2):
        lanes = slice(half * inner, (half + 1) * inner)
        real, imag = stage[:half_rows, lanes], stage[half_rows:, lanes]
        turned.append(
            jnp.concatenate([real * cos + imag * sin, imag * cos - real * sin], axis=1).astype(BF16)
        )
    spec = jnp.dot(jnp.concatenate(turned, axis=0), forward, preferred_element_type=F32)
    return (spec[:, :inner], spec[:, inner:])


def inverse_dft(spec, last, cos, sin, backward, inner):
    both = jnp.concatenate(spec, axis=1).astype(BF16)
    stage = jnp.dot(both, backward, preferred_element_type=F32)
    half_rows = SLABS * GROUP
    turned = []
    for half in range(2):
        rows = slice(half * half_rows, (half + 1) * half_rows)
        real, imag = stage[rows, :inner], stage[rows, inner:]
        turned.append(
            jnp.concatenate([real * cos - imag * sin, imag * cos + real * sin], axis=0).astype(BF16)
        )
    return jnp.dot(last, jnp.concatenate(turned, axis=1), preferred_element_type=F32)


def scatter_slabs(rows, scale, out, lead, inner):
    sources, local = out.shape[0], out.shape[-1]
    per = local // inner
    scaled = rows * scale
    for src in range(sources):
        for part in range(per):
            at = (src * per + part) * GROUP
            tile = jnp.concatenate(
                [scaled[at : at + GROUP, :inner], scaled[at : at + GROUP, inner:]], axis=0
            ).astype(BF16)
            lanes = slice(part * inner, (part + 1) * inner)
            if lead is None:
                out[src, :, lanes] = tile
            else:
                out[src, lead, :, lanes] = tile


def times_plain(left, right):
    return (left[0] * right[0] - left[1] * right[1], left[0] * right[1] + left[1] * right[0])


def times_conj(left, right):
    return (left[0] * right[0] + left[1] * right[1], left[1] * right[0] - left[0] * right[1])


def response_kernel(inner, pair, first, last, cos, sin, forward, backward, out):
    tables = (first[...], cos[...], sin[...], forward[...], inner)
    prod = forward_dft(gather_slabs(pair[:, 0], inner), *tables)
    taps = forward_dft(gather_slabs(pair[:, 1], inner), *tables)
    rows = inverse_dft(times_plain(prod, taps), last[...], cos[...], sin[...], backward[...], inner)
    scatter_slabs(rows, 1.0 / (SLABS * inner), out, None, inner)


def backward_kernel(inner, scale, pair, grad, first, last, cos, sin, forward, backward, out):
    tables = (first[...], cos[...], sin[...], forward[...], inner)
    back_tables = (last[...], cos[...], sin[...], backward[...], inner)
    grad_spec = forward_dft(gather_slabs(grad[...], inner), *tables)
    taps = forward_dft(gather_slabs(pair[:, 1], inner), *tables)
    rows = inverse_dft(times_conj(grad_spec, taps), *back_tables)
    scatter_slabs(rows, 1.0 / (SLABS * inner), out, 0, inner)
    prod = forward_dft(gather_slabs(pair[:, 0], inner), *tables)
    rows = inverse_dft(times_conj(grad_spec, prod), *back_tables)
    scatter_slabs(rows, scale / (SLABS * inner), out, 1, inner)


def conv_call(kernel, operands, lead, inner, transforms):
    sources, channels, local = operands[0].shape[0], operands[0].shape[-2], operands[0].shape[-1]
    tables = make_tables(inner)

    def moved(shape):
        middle = shape[1:-2]
        return pl.BlockSpec(
            (sources,) + middle + (STEP, local), lambda i: (0,) * (1 + len(middle)) + (i, 0)
        )

    def whole(table):
        return pl.BlockSpec(table.shape, lambda i: (0, 0))

    out_shape = (sources,) + lead + (channels, local)
    rows = channels * SLABS
    flops = transforms * rows * (2 * (2 * inner) ** 2 + 4 * SLABS * GROUP * inner)
    return pl.pallas_call(
        kernel,
        grid=(channels // STEP,),
        in_specs=[moved(op.shape) for op in operands] + [whole(t) for t in tables],
        out_specs=moved(out_shape),
        out_shape=jax.ShapeDtypeStruct(out_shape, BF16),
        compiler_params=pltpu.CompilerParams(vmem_limit_bytes=40 * 1024 * 1024),
        cost_estimate=pl.CostEstimate(
            flops=flops, bytes_accessed=2 * rows * inner * 4, transcendentals=0
        ),
    )(*operands, *[jnp.asarray(t) for t in tables])


def elementwise(left, right):
    return (left.astype(F32) * right.astype(F32)).astype(BF16)


def per_device(outer_gate, inner_gate, signal, cotangent, out_weight, filter_taps, skip_gain):
    ch_dev, tok_local = outer_gate.shape
    n_ctx = lax.axis_size("ctx")
    ch_slice = ch_dev // n_ctx
    seq_len = n_ctx * tok_local
    inner = seq_len // SLABS
    scale = 1.0 / math.sqrt(seq_len)

    def swap(array):
        return lax.all_to_all(array, "ctx", split_axis=0, concat_axis=0, tiled=True)

    def split(array):
        return array.reshape(n_ctx, ch_slice, tok_local)

    gathered = lax.all_gather(cotangent, "group", axis=0, tiled=True)
    product = elementwise(inner_gate, signal)
    at_zero = (lax.axis_index("ctx") == 0) & (
        lax.broadcasted_iota(jnp.int32, (ch_dev, tok_local), 1) == 0
    )
    eff_taps = (filter_taps * scale + jnp.where(at_zero, skip_gain[:, None], 0.0)).astype(BF16)
    pair = swap(jnp.stack([split(product), split(eff_taps)], axis=1))
    upstream = jnp.dot(out_weight, gathered, preferred_element_type=F32).astype(BF16)
    grad_prod = elementwise(upstream, outer_gate)
    grad = swap(split(grad_prod))
    response = conv_call(functools.partial(response_kernel, inner), (pair,), (), inner, 3)
    resp_home = swap(response)
    backs = conv_call(functools.partial(backward_kernel, inner, scale), (pair, grad), (2,), inner, 5)
    backs_home = swap(backs)
    back_home = backs_home[:, 0].reshape(ch_dev, tok_local)
    grad_outer = elementwise(upstream, resp_home.reshape(ch_dev, tok_local))
    grad_inner = elementwise(back_home, signal)
    grad_signal = elementwise(back_home, inner_gate)
    grad_taps = backs_home[:, 1].reshape(ch_dev, tok_local).astype(F32)
    return (grad_outer, grad_inner, grad_signal, grad_taps)


def solution(mesh):
    in_specs = (
        P("group", "ctx"),
        P("group", "ctx"),
        P("group", "ctx"),
        P("group", "ctx"),
        P("group", None),
        P("group", "ctx"),
        P("group"),
    )
    out_specs = (P("group", "ctx"), P("group", "ctx"), P("group", "ctx"), P("group", "ctx"))
    return jax.shard_map(
        per_device, mesh=mesh, in_specs=in_specs, out_specs=out_specs, check_vma=False
    )
```

time: 428 us -> 217 us (0.51); the launches traced: 423 us -> 217 us
  other arithmetic: 136 us -> 5.9 us
  blocking collectives: 58.2 us -> 164 us
  matrix products: 89.8 us -> 10.7 us
  waiting for transfers between devices: 60.8 us -> 0.68 us
  local copies, waits for them, and re-layouts: 40.4 us -> 0.65 us
  starting transfers between devices: 22.9 us -> 0.04 us
  Pallas kernels: 0 us -> 20.6 us
    all_to_all x2 -> x4, blocking collectives: 58.2 us -> 164 us  [swap(): return lax.all_to_all(array, 'ctx', split_axis=0, concat_axis=0, tiled=True)]
    dot_general x13 -> x1, matrix products: 89.8 us -> 10.7 us  [per_device(): jnp.dot(out_weight, gathered, preferred_element_type=F32).astype(BF16)]
    unnamed x4 -> x0, other arithmetic: 68 us -> none
    all_to_all x4 -> x0, waiting for transfers between devices: 36.2 us -> none  [the longest x1 18.3 us: per_device(): lax.all_to_all(to_channels(grad_prod), 'ctx', split_axis=0, concat_axis=2...]
    all_gather x1, waiting for transfers between devices: 24 us -> 0.01 us  [per_device(): gathered = lax.all_gather(cotangent, 'group', axis=0, tiled=True)]
    all_to_all x4 -> x0, starting transfers between devices: 22.9 us -> none  [the longest x1 7.28 us: per_device(): lax.all_to_all(to_channels(eff_taps).astype(jnp.bfloat16), 'ctx', split_a...]
    concatenate x6 -> x0, other arithmetic: 22.1 us -> none  [the longest x3 11.8 us: forward_dft(): jnp.concatenate([twist_re, twist_im], axis=2)]
    add x4 -> x0, other arithmetic: 21.8 us -> none  [the longest x2 14.7 us: times_conj(): left[0] * right[0] + left[1] * right[1]]
  transfers between devices with their start and end apart: 5 -> 1, of which waited for: 3 -> 0; matrix products, arithmetic and copies ran while one was open for 17% -> 1% of each run, Pallas kernels for 0% -> 4%
where the time goes in v1:
time: 217 us
  blocking collectives  164 us (76%)
  Pallas kernels  20.6 us (9%)
  between operations  14.2 us (7%)
  matrix products  10.7 us (5%)
  other arithmetic  5.9 us (3%)
    all_to_all x4, blocking collectives, swap(): return lax.all_to_all(array, 'ctx', split_axis=0, concat_axis=0, tiled=True)  164 us
    pallas_call x2, Pallas kernels, conv_call(): pl.pallas_call(kernel, grid=(channels // STEP,), in_specs=[moved(op.shape...  20.6 us
    dot_general x1, matrix products, per_device(): jnp.dot(out_weight, gathered, preferred_element_type=F32).astype(BF16)  10.7 us
  transfers between devices with their start and end apart: 1, of which 0 were waited for; matrix products, arithmetic and copies ran while one was open for 1% of the time, Pallas kernels for 4%

profile of v1, /device:TPU:0, one launch (start us, length us, event | category | flops | bytes accessed | tf_op | source)
XLA Modules:
  0.0 217.1 jit_solution(17433559653107537275)
XLA Ops:
  7.2 0.0 copy-start.9
  7.2 0.0 copy-start.8
  7.2 0.0 all-gather.2.cloned.1.call-start
  7.2 0.7 all-gather.2.cloned.1.call-update
  7.9 1.8 fusion.2
  9.8 0.0 copy-done.9
  9.8 0.0 copy-done.8
  9.8 0.3 add_convert_fusion
  10.1 0.2 pad_maximum_fusion
  10.3 0.0 copy-start
  10.3 0.0 copy-start.1
  10.3 0.0 copy-start.2
  10.3 0.0 copy-start.3
  10.3 0.0 copy-start.4
  10.4 0.0 copy-start.5
  10.4 55.5 %all_to_all.20.pair = bf16[8,2,128,512]{3,2,1,0:T(8,128)(2,1)S(1)} all-to-all(bf16[8,2,128,512]{3,2,1,0:T(8,128)(2,1)S(1)} %pad_maximum_fusion), channel_id=1, replica_groups=mesh['group'=4,'ctx'=8] {'ctx'}, dimensions={0} | all-to-all | bytes 4194304 | tf_op jit(solution)/shard_map/all_to_all | solution.py:172
  65.8 0.0 copy-done
  65.8 0.0 copy-done.1
  65.8 0.0 copy-done.2
  65.8 0.0 copy-done.3
  65.9 8.2 %shard_map.210 = bf16[8,128,512]{2,1,0:T(8,128)(2,1)S(1)} custom-call(bf16[8,2,128,512]{3,2,1,0:T(8,128)(2,1)S(1)} %all_to_all.20.pair, bf16[512,256]{1,0:T(8,128)(2,1)S(1)} %copy-done.1, bf16[256,512]{1,0:T(8,128)(2,1)S(1)} %copy-done, f32[256,128]{1,0:T(8,128)S(1)} %copy-done.5, f32[256,128]{1,0:T(8,128)S(1)} %copy-done.4, bf16[256,256]{1,0:T(8,128)(2,1)S(1)} %copy-done.3, ...), custom_call_target="tpu_custom_call" | custom-call | flops 3221225472 | bytes 4194304 | tf_op jit(solution)/shard_map/pallas_call | solution.py:146
  74.1 29.0 %all_to_all.21 = bf16[8,128,512]{2,1,0:T(8,128)(2,1)} all-to-all(bf16[8,128,512]{2,1,0:T(8,128)(2,1)S(1)} %shard_map.210), channel_id=1, replica_groups=mesh['group'=4,'ctx'=8] {'ctx'}, dimensions={0} | all-to-all | bytes 2097152 | tf_op jit(solution)/shard_map/all_to_all | solution.py:172
  103.1 10.7 %fusion.1 = (bf16[1024,512]{1,0:T(8,128)(2,1)S(1)}, bf16[1024,512]{1,0:T(8,128)(2,1)}) fusion(bf16[1024,512]{1,0:T(8,128)(2,1)} %param.19, bf16[8,128,512]{2,1,0:T(8,128)(2,1)} %all_to_all.21, bf16[1024,4096]{1,0:T(8,128)(2,1)} %param.23, bf16[4096,512]{1,0:T(8,128)(2,1)} %all-gather.2.cloned.1.call-done), kind=kOutput, calls=%fused_computation.6 | convolution fusion | flops 4299161600 | bytes 16777216 | tf_op jit(solution)/shard_map/dot_general | solution.py:184
  113.8 28.7 %all_to_all.22.grad = bf16[8,128,512]{2,1,0:T(8,128)(2,1)S(1)} all-to-all(bf16[8,128,512]{2,1,0:T(8,128)(2,1)S(1)} %bitcast.17), channel_id=1, replica_groups=mesh['group'=4,'ctx'=8] {'ctx'}, dimensions={0} | all-to-all | bytes 2097152 | tf_op jit(solution)/shard_map/all_to_all | solution.py:172
  142.4 12.4 %shard_map.211 = bf16[8,2,128,512]{3,2,1,0:T(8,128)(2,1)S(1)} custom-call(bf16[8,2,128,512]{3,2,1,0:T(8,128)(2,1)S(1)} %all_to_all.20.pair, bf16[8,128,512]{2,1,0:T(8,128)(2,1)S(1)} %all_to_all.22.grad, bf16[512,256]{1,0:T(8,128)(2,1)S(1)} %copy-done.1, bf16[256,512]{1,0:T(8,128)(2,1)S(1)} %copy-done, f32[256,128]{1,0:T(8,128)S(1)} %copy-done.5, ...), custom_call_target="tpu_custom_call" | custom-call | flops 5368709120 | bytes 4194304 | tf_op jit(solution)/shard_map/pallas_call | solution.py:146
  154.8 51.2 %all_to_all.23 = bf16[8,2,128,512]{3,2,1,0:T(8,128)(2,1)S(1)} all-to-all(bf16[8,2,128,512]{3,2,1,0:T(8,128)(2,1)S(1)} %shard_map.211), channel_id=1, replica_groups=mesh['group'=4,'ctx'=8] {'ctx'}, dimensions={0} | all-to-all | bytes 4194304 | tf_op jit(solution)/shard_map/all_to_all | solution.py:172
  206.0 0.2 fusion.6
  206.2 0.0 copy-start.6
  206.2 0.0 copy-start.7
  206.2 1.7 bitcast_convert_fusion
  207.9 0.4 copy-done.7
  208.3 1.9 fusion.4
  (5 shorter events, 0.0 us)
Async XLA Ops:
  7.2 2.6 %copy-start.9 = (f32[1024]{0:T(1024)S(1)}, f32[1024]{0:T(1024)}, u32[]{:S(2)}) copy-start(f32[1024]{0:T(1024)} %param.25) | copy-start | bytes 12292
  7.2 2.6 %copy-start.8 = (f32[1024,512]{1,0:T(8,128)S(1)}, f32[1024,512]{1,0:T(8,128)}, u32[]{:S(2)}) copy-start(f32[1024,512]{1,0:T(8,128)} %param.24) | copy-start | bytes 6291460
  7.2 95.9 %all-gather.2.cloned.1.call-start = ((), (), s32[]{:S(2)}) async-start(), calls=%async_computation.4 | async-start | bytes 5242880 | tf_op jit(solution)/shard_map/all_gather | solution.py:177
  10.3 55.5 %copy-start = (bf16[256,512]{1,0:T(8,128)(2,1)S(1)}, bf16[256,512]{1,0:T(8,128)(2,1)}, u32[]{:S(2)}) copy-start(bf16[256,512]{1,0:T(8,128)(2,1)} %constant.24.clone.last) | copy-start | bytes 786436
  10.3 55.5 %copy-start.1 = (bf16[512,256]{1,0:T(8,128)(2,1)S(1)}, bf16[512,256]{1,0:T(8,128)(2,1)}, u32[]{:S(2)}) copy-start(bf16[512,256]{1,0:T(8,128)(2,1)} %constant.9.clone.first) | copy-start | bytes 786436
  10.3 55.5 %copy-start.2 = (bf16[256,256]{1,0:T(8,128)(2,1)S(1)}, bf16[256,256]{1,0:T(8,128)(2,1)}, u32[]{:S(2)}) copy-start(bf16[256,256]{1,0:T(8,128)(2,1)} %constant.28.clone.backward) | copy-start | bytes 393220
  10.3 55.5 %copy-start.3 = (bf16[256,256]{1,0:T(8,128)(2,1)S(1)}, bf16[256,256]{1,0:T(8,128)(2,1)}, u32[]{:S(2)}) copy-start(bf16[256,256]{1,0:T(8,128)(2,1)} %constant.27.clone.forward) | copy-start | bytes 393220
  10.3 55.5 %copy-start.4 = (f32[256,128]{1,0:T(8,128)S(1)}, f32[256,128]{1,0:T(8,128)}, u32[]{:S(2)}) copy-start(f32[256,128]{1,0:T(8,128)} %constant.26.clone.sin) | copy-start | bytes 393220
  10.4 55.5 %copy-start.5 = (f32[256,128]{1,0:T(8,128)S(1)}, f32[256,128]{1,0:T(8,128)}, u32[]{:S(2)}) copy-start(f32[256,128]{1,0:T(8,128)} %constant.25.clone.cos) | copy-start | bytes 393220
  206.2 1.7 copy-start.6
  206.2 2.1 copy-start.7
Sparse Core Ops, SparseCore 0:
  9.6 37.1 all-gather.1

commit v2 on v1

--- a/solution.py
+++ b/solution.py
@@ -183,10 +183,13 @@
     pair = swap(jnp.stack([split(product), split(eff_taps)], axis=1))
     upstream = jnp.dot(out_weight, gathered, preferred_element_type=F32).astype(BF16)
     grad_prod = elementwise(upstream, outer_gate)
+    pair, grad_prod = lax.optimization_barrier((pair, grad_prod))
     grad = swap(split(grad_prod))
     response = conv_call(functools.partial(response_kernel, inner), (pair,), (), inner, 3)
+    grad, response = lax.optimization_barrier((grad, response))
+    backs = conv_call(functools.partial(backward_kernel, inner, scale), (pair, grad), (2,), inner, 5)
     resp_home = swap(response)
-    backs = conv_call(functools.partial(backward_kernel, inner, scale), (pair, grad), (2,), inner, 5)
+    resp_home, backs = lax.optimization_barrier((resp_home, backs))
     backs_home = swap(backs)
     back_home = backs_home[:, 0].reshape(ch_dev, tok_local)
     grad_outer = elementwise(upstream, resp_home.reshape(ch_dev, tok_local))

time: 217 us -> 191 us (0.88)
  blocking collectives: 164 us -> 0 us
  waiting for transfers between devices: 0.68 us -> 106 us
  starting transfers between devices: 0.04 us -> 18.9 us
  local copies, waits for them, and re-layouts: 0.65 us -> 10.4 us
  other arithmetic: 5.9 us -> 9.83 us
    all_to_all x4 -> x0, blocking collectives: 164 us -> none  [swap(): return lax.all_to_all(array, 'ctx', split_axis=0, concat_axis=0, tiled=True)]
    all_to_all x0 -> x4, waiting for transfers between devices: none -> 77.4 us  [swap(): return lax.all_to_all(array, 'ctx', split_axis=0, concat_axis=0, tiled=True)]
    all_gather x1, waiting for transfers between devices: 0.01 us -> 27.4 us  [per_device(): gathered = lax.all_gather(cotangent, 'group', axis=0, tiled=True)]
    all_to_all x0 -> x4, starting transfers between devices: none -> 18.9 us  [swap(): return lax.all_to_all(array, 'ctx', split_axis=0, concat_axis=0, tiled=True)]
    unnamed x20 -> x36, local copies, waits for them, and re-layouts: 0.47 us -> 10.2 us
    convert_element_type x2 -> x3, other arithmetic: 3.72 us -> 6.34 us  [elementwise(): return (left.astype(F32) * right.astype(F32)).astype(BF16)]
  transfers between devices with their start and end apart: 1 -> 5, of which waited for: 0 -> 5; matrix products, arithmetic and copies ran while one was open for 1% -> 9% of each run, Pallas kernels for 4% -> 11%
where the time goes in v2:
time: 191 us; the launch traced here: 190 us
  waiting for transfers between devices  106 us (55%)
  Pallas kernels  20.6 us (11%)
  starting transfers between devices  18.9 us (10%)
  between operations  14.2 us (7%)
  local copies, waits for them, and re-layouts  10.4 us (5%)
  matrix products  10.4 us (5%)
  other arithmetic  9.83 us (5%)
    all_to_all x4, waiting for transfers between devices, swap(): return lax.all_to_all(array, 'ctx', split_axis=0, concat_axis=0, tiled=True)  77.4 us
    all_gather x1, waiting for transfers between devices, per_device(): gathered = lax.all_gather(cotangent, 'group', axis=0, tiled=True)  27.4 us
    pallas_call x2, Pallas kernels, conv_call(): pl.pallas_call(kernel, grid=(channels // STEP,), in_specs=[moved(op.shape...  20.6 us
    all_to_all x4, starting transfers between devices, swap(): return lax.all_to_all(array, 'ctx', split_axis=0, concat_axis=0, tiled=True)  18.9 us
    dot_general x1, matrix products, per_device(): jnp.dot(out_weight, gathered, preferred_element_type=F32).astype(BF16)  10.4 us
    unnamed x36, local copies, waits for them, and re-layouts  10.2 us
    convert_element_type x3, other arithmetic, elementwise(): return (left.astype(F32) * right.astype(F32)).astype(BF16)  6.34 us
  transfers between devices with their start and end apart: 5, of which 5 were waited for; matrix products, arithmetic and copies ran while one was open for 9% of the time, Pallas kernels for 11%

profile of v2, /device:TPU:0, one launch (start us, length us, event | category | flops | bytes accessed | tf_op | source)
XLA Modules:
  0.0 189.9 jit_solution(12315586441926447900)
XLA Ops:
  7.2 0.7 all-gather.2.cloned.1.call-update
  7.9 2.0 %fusion.2 = bf16[1024,512]{1,0:T(8,128)(2,1)S(1)} fusion(bf16[1024,512]{1,0:T(8,128)(2,1)} %param.21, bf16[1024,512]{1,0:T(8,128)(2,1)} %param.20), kind=kLoop, calls=%fused_computation.7 | loop fusion | flops 2097152 | bytes 3145728 | tf_op jit(solution)/shard_map/convert_element_type | solution.py:160
  9.9 0.2 copy-done.14
  10.1 0.3 add_convert_fusion
  10.4 1.5 pad_maximum_fusion
  11.9 7.4 %all-to-all-start = ((bf16[8,2,128,512]{3,2,1,0:T(8,128)(2,1)}), bf16[8,2,128,512]{3,2,1,0:T(8,128)(2,1)S(1)}, u32[]{:S(2)}, u32[]{:S(2)}) async-start(bf16[8,2,128,512]{3,2,1,0:T(8,128)(2,1)} %pad_maximum_fusion), calls=%async_computation | async-start | bytes 4194304 | tf_op jit(solution)/shard_map/all_to_all | solution.py:172
  19.4 27.4 %all-gather.2.cloned.1.call-done = bf16[4096,512]{1,0:T(8,128)(2,1)} async-done(((bf16[1024,512]{1,0:T(8,128)(2,1)}), bf16[4096,512]{1,0:T(8,128)(2,1)}) %all-gather.2.cloned.1.call-update) | async-done | bytes 4194320 | tf_op jit(solution)/shard_map/all_gather | solution.py:177
  46.8 10.4 %fusion = (bf16[1024,512]{1,0:T(8,128)(2,1)}, bf16[1024,512]{1,0:T(8,128)(2,1)}) fusion(bf16[1024,512]{1,0:T(8,128)(2,1)S(1)} %copy-done.17, bf16[1024,4096]{1,0:T(8,128)(2,1)} %param.23, bf16[4096,512]{1,0:T(8,128)(2,1)} %all-gather.2.cloned.1.call-done), kind=kOutput, calls=%fused_computation.5 | convolution fusion | flops 4297588736 | bytes 15728640 | tf_op jit(solution)/shard_map/dot_general | solution.py:184
  57.2 10.4 %all-to-all-done.pair = bf16[8,2,128,512]{3,2,1,0:T(8,128)(2,1)S(1)} async-done(((bf16[8,2,128,512]{3,2,1,0:T(8,128)(2,1)}), bf16[8,2,128,512]{3,2,1,0:T(8,128)(2,1)S(1)}, u32[]{:S(2)}, u32[]{:S(2)}) %all-to-all-start) | async-done | bytes 2097184 | tf_op jit(solution)/shard_map/all_to_all | solution.py:172
  67.6 3.6 %all-to-all-start.1 = ((bf16[8,128,512]{2,1,0:T(8,128)(2,1)}), bf16[8,128,512]{2,1,0:T(8,128)(2,1)S(1)}, u32[]{:S(2)}, u32[]{:S(2)}) async-start(bf16[8,128,512]{2,1,0:T(8,128)(2,1)} %bitcast.17), calls=%async_computation.1 | async-start | bytes 2097152 | tf_op jit(solution)/shard_map/all_to_all | solution.py:172
  71.3 0.9 copy-done.3
  72.2 0.9 copy-done.6
  73.1 0.9 copy-done.8
  74.0 0.9 copy-done.10
  74.9 8.2 %shard_map.210 = bf16[8,128,512]{2,1,0:T(8,128)(2,1)S(1)} custom-call(bf16[8,2,128,512]{3,2,1,0:T(8,128)(2,1)S(1)} %all-to-all-done.pair, bf16[512,256]{1,0:T(8,128)(2,1)S(1)} %copy-done.3, bf16[256,512]{1,0:T(8,128)(2,1)S(1)} %copy-done.2, f32[256,128]{1,0:T(8,128)S(1)} %copy-done.10, f32[256,128]{1,0:T(8,128)S(1)} %copy-done.8, ...), custom_call_target="tpu_custom_call" | custom-call | flops 3221225472 | bytes 4194304 | tf_op jit(solution)/shard_map/pallas_call | solution.py:146
  83.2 1.0 copy-done.1
  84.1 13.1 %all-to-all-done.1.grad = bf16[8,128,512]{2,1,0:T(8,128)(2,1)S(1)} async-done(((bf16[8,128,512]{2,1,0:T(8,128)(2,1)}), bf16[8,128,512]{2,1,0:T(8,128)(2,1)S(1)}, u32[]{:S(2)}, u32[]{:S(2)}) %all-to-all-start.1) | async-done | bytes 1048608 | tf_op jit(solution)/shard_map/all_to_all | solution.py:172
  97.2 4.2 %all-to-all-start.2 = ((bf16[8,128,512]{2,1,0:T(8,128)(2,1)}), bf16[8,128,512]{2,1,0:T(8,128)(2,1)}, u32[]{:S(2)}, u32[]{:S(2)}) async-start(bf16[8,128,512]{2,1,0:T(8,128)(2,1)} %copy-done.1), calls=%async_computation.2 | async-start | bytes 2097152 | tf_op jit(solution)/shard_map/all_to_all | solution.py:172
  101.5 0.9 copy-done.4
  102.4 0.9 copy-done.7
  103.3 0.9 copy-done.9
  104.2 0.9 copy-done.11
  105.1 12.4 %shard_map.211 = bf16[8,2,128,512]{3,2,1,0:T(8,128)(2,1)S(1)} custom-call(bf16[8,2,128,512]{3,2,1,0:T(8,128)(2,1)S(1)} %all-to-all-done.pair, bf16[8,128,512]{2,1,0:T(8,128)(2,1)S(1)} %all-to-all-done.1.grad, bf16[512,256]{1,0:T(8,128)(2,1)S(1)} %copy-done.4, bf16[256,512]{1,0:T(8,128)(2,1)S(1)} %copy-done.2, f32[256,128]{1,0:T(8,128)S(1)} %copy-done.11, ...), custom_call_target="tpu_custom_call" | custom-call | flops 5368709120 | bytes 4194304 | tf_op jit(solution)/shard_map/pallas_call | solution.py:146
  117.5 1.3 copy-done
  118.8 8.2 %all-to-all-done.2 = bf16[8,128,512]{2,1,0:T(8,128)(2,1)} async-done(((bf16[8,128,512]{2,1,0:T(8,128)(2,1)}), bf16[8,128,512]{2,1,0:T(8,128)(2,1)}, u32[]{:S(2)}, u32[]{:S(2)}) %all-to-all-start.2) | async-done | bytes 1048608 | tf_op jit(solution)/shard_map/all_to_all | solution.py:172
  127.1 3.6 %all-to-all-start.3 = ((bf16[8,2,128,512]{3,2,1,0:T(8,128)(2,1)}), bf16[8,2,128,512]{3,2,1,0:T(8,128)(2,1)S(1)}, u32[]{:S(2)}, u32[]{:S(2)}) async-start(bf16[8,2,128,512]{3,2,1,0:T(8,128)(2,1)} %copy-done), calls=%async_computation.3 | async-start | bytes 4194304 | tf_op jit(solution)/shard_map/all_to_all | solution.py:172
  130.7 2.5 %fusion.1 = bf16[1024,512]{1,0:T(8,128)(2,1)} fusion(bf16[1024,512]{1,0:T(8,128)(2,1)S(1)} %copy-done.15, bf16[8,128,512]{2,1,0:T(8,128)(2,1)} %all-to-all-done.2), kind=kLoop, calls=%fused_computation.6 | loop fusion | flops 2097152 | bytes 3145728 | tf_op jit(solution)/shard_map/convert_element_type | solution.py:160
  133.2 45.7 %all-to-all-done.3 = bf16[8,2,128,512]{3,2,1,0:T(8,128)(2,1)S(1)} async-done(((bf16[8,2,128,512]{3,2,1,0:T(8,128)(2,1)}), bf16[8,2,128,512]{3,2,1,0:T(8,128)(2,1)S(1)}, u32[]{:S(2)}, u32[]{:S(2)}) %all-to-all-start.3) | async-done | bytes 2097184 | tf_op jit(solution)/shard_map/all_to_all | solution.py:172
  178.9 0.2 fusion.6
  179.1 1.7 bitcast_convert_fusion
  180.8 0.4 copy-done.13
  181.2 1.9 fusion.4
  (26 shorter events, 0.1 us)
Async XLA Ops:
  7.2 2.8 %copy-start.16 = (f32[1024]{0:T(1024)S(1)}, f32[1024]{0:T(1024)}, u32[]{:S(2)}) copy-start(f32[1024]{0:T(1024)} %param.25) | copy-start | bytes 12292
  7.2 39.6 %all-gather.2.cloned.1.call-start = ((), (), s32[]{:S(2)}) async-start(), calls=%async_computation.4 | async-start | bytes 5242880 | tf_op jit(solution)/shard_map/all_gather | solution.py:177
  7.9 2.2 %copy-start.14 = (f32[1024,512]{1,0:T(8,128)S(1)}, f32[1024,512]{1,0:T(8,128)}, u32[]{:S(2)}) copy-start(f32[1024,512]{1,0:T(8,128)} %param.24) | copy-start | bytes 6291460
  11.9 34.8 %copy-start.17 = (bf16[1024,512]{1,0:T(8,128)(2,1)S(1)}, bf16[1024,512]{1,0:T(8,128)(2,1)}, u32[]{:S(2)}) copy-start(bf16[1024,512]{1,0:T(8,128)(2,1)} %param.19) | copy-start | bytes 3145732
  11.9 55.7 %all-to-all-start = ((bf16[8,2,128,512]{3,2,1,0:T(8,128)(2,1)}), bf16[8,2,128,512]{3,2,1,0:T(8,128)(2,1)S(1)}, u32[]{:S(2)}, u32[]{:S(2)}) async-start(bf16[8,2,128,512]{3,2,1,0:T(8,128)(2,1)} %pad_maximum_fusion), calls=%async_computation | async-start | bytes 4194304 | tf_op jit(solution)/shard_map/all_to_all | solution.py:172
  57.2 14.1 %copy-start.2 = (bf16[256,512]{1,0:T(8,128)(2,1)S(1)}, bf16[256,512]{1,0:T(8,128)(2,1)}, u32[]{:S(2)}) copy-start(bf16[256,512]{1,0:T(8,128)(2,1)} %constant.24.clone.last) | copy-start | bytes 786436
  57.2 14.1 %copy-start.5 = (bf16[256,256]{1,0:T(8,128)(2,1)S(1)}, bf16[256,256]{1,0:T(8,128)(2,1)}, u32[]{:S(2)}) copy-start(bf16[256,256]{1,0:T(8,128)(2,1)} %constant.28.clone.backward) | copy-start | bytes 393220
  67.6 29.6 %all-to-all-start.1 = ((bf16[8,128,512]{2,1,0:T(8,128)(2,1)}), bf16[8,128,512]{2,1,0:T(8,128)(2,1)S(1)}, u32[]{:S(2)}, u32[]{:S(2)}) async-start(bf16[8,128,512]{2,1,0:T(8,128)(2,1)} %bitcast.17), calls=%async_computation.1 | async-start | bytes 2097152 | tf_op jit(solution)/shard_map/all_to_all | solution.py:172
  71.3 1.0 copy-start.3
  72.2 0.9 copy-start.6
  73.1 0.9 copy-start.8
  74.0 0.9 copy-start.10
  83.2 1.0 copy-start.1
  97.2 29.9 %all-to-all-start.2 = ((bf16[8,128,512]{2,1,0:T(8,128)(2,1)}), bf16[8,128,512]{2,1,0:T(8,128)(2,1)}, u32[]{:S(2)}, u32[]{:S(2)}) async-start(bf16[8,128,512]{2,1,0:T(8,128)(2,1)} %copy-done.1), calls=%async_computation.2 | async-start | bytes 2097152 | tf_op jit(solution)/shard_map/all_to_all | solution.py:172
  101.4 1.0 copy-start.4
  102.4 0.9 copy-start.7
  103.3 0.9 copy-start.9
  104.2 0.9 copy-start.11
  117.5 1.3 copy-start
  118.8 11.8 %copy-start.15 = (bf16[1024,512]{1,0:T(8,128)(2,1)S(1)}, bf16[1024,512]{1,0:T(8,128)(2,1)}, u32[]{:S(2)}) copy-start(bf16[1024,512]{1,0:T(8,128)(2,1)} %get-tuple-element.21) | copy-start | bytes 3145732
  127.1 51.8 %all-to-all-start.3 = ((bf16[8,2,128,512]{3,2,1,0:T(8,128)(2,1)}), bf16[8,2,128,512]{3,2,1,0:T(8,128)(2,1)S(1)}, u32[]{:S(2)}, u32[]{:S(2)}) async-start(bf16[8,2,128,512]{3,2,1,0:T(8,128)(2,1)} %copy-done), calls=%async_computation.3 | async-start | bytes 4194304 | tf_op jit(solution)/shard_map/all_to_all | solution.py:172
  179.1 1.7 copy-start.12
  179.1 2.1 %copy-start.13 = (bf16[1024,512]{1,0:T(8,128)(2,1)S(1)}, bf16[1024,512]{1,0:T(8,128)(2,1)}, u32[]{:S(2)}) copy-start(bf16[1024,512]{1,0:T(8,128)(2,1)} %param.20) | copy-start | bytes 3145732
Sparse Core Ops, SparseCore 0:
  9.6 37.1 all-gather.1

commit v3 on v1

v3 whole, which is shorter than its diff:
```python
import functools
import math

import jax
import jax.numpy as jnp
import ml_dtypes
import numpy as np
from jax import lax
from jax.experimental import pallas as pl
from jax.experimental.pallas import tpu as pltpu
from jax.sharding import PartitionSpec as P

SLABS = 32
GROUP = 8
STEP = 2 * GROUP
F32 = jnp.float32
BF16 = jnp.bfloat16


def make_tables(inner, chunks):
    slab = np.arange(SLABS)
    freq = np.arange(SLABS) + 0.5
    angle = 2.0 * np.pi / (2 * SLABS) * np.outer(freq, slab)
    eye = np.eye(GROUP)
    first = np.concatenate([np.kron(np.cos(angle), eye), np.kron(-np.sin(angle), eye)], axis=0)
    blocks = first.reshape(first.shape[0], chunks, -1)
    order = np.arange(chunks)
    first = np.stack([blocks[:, order ^ p].reshape(first.shape) for p in range(chunks)])
    last = first.transpose(0, 2, 1)
    within = np.arange(inner)
    turn = np.repeat(2.0 * np.pi / (2 * SLABS * inner) * np.outer(freq, within), GROUP, axis=0)
    circle = 2.0 * np.pi / inner * (np.outer(within, within) % inner)
    cos, sin = np.cos(circle), np.sin(circle)
    forward = np.block([[cos, -sin], [sin, cos]])
    narrow = ml_dtypes.bfloat16
    return (
        first.astype(narrow),
        last.astype(narrow),
        np.cos(turn).astype(np.float32),
        np.sin(turn).astype(np.float32),
        forward.astype(narrow),
        forward.T.astype(narrow),
    )


def gather_slabs(blocks, inner):
    local = blocks[0].shape[1]
    wide = [block.astype(F32) for block in blocks]
    halves = []
    for half in range(2):
        rows = slice(half * GROUP, (half + 1) * GROUP)
        pieces = [block[rows, at : at + inner] for block in wide for at in range(0, local, inner)]
        halves.append(jnp.concatenate(pieces, axis=0))
    return jnp.concatenate(halves, axis=1).astype(BF16)


def forward_dft(rows, first, cos, sin, forward, inner):
    stage = jnp.dot(first, rows, preferred_element_type=F32)
    half_rows = SLABS * GROUP
    turned = []
    for half in range(2):
        lanes = slice(half * inner, (half + 1) * inner)
        real, imag = stage[:half_rows, lanes], stage[half_rows:, lanes]
        turned.append(
            jnp.concatenate([real * cos + imag * sin, imag * cos - real * sin], axis=1).astype(BF16)
        )
    spec = jnp.dot(jnp.concatenate(turned, axis=0), forward, preferred_element_type=F32)
    return (spec[:, :inner], spec[:, inner:])


def inverse_dft(spec, last, cos, sin, backward, inner):
    both = jnp.concatenate(spec, axis=1).astype(BF16)
    stage = jnp.dot(both, backward, preferred_element_type=F32)
    half_rows = SLABS * GROUP
    turned = []
    for half in range(2):
        rows = slice(half * half_rows, (half + 1) * half_rows)
        real, imag = stage[rows, :inner], stage[rows, inner:]
        turned.append(
            jnp.concatenate([real * cos - imag * sin, imag * cos + real * sin], axis=0).astype(BF16)
        )
    return jnp.dot(last, jnp.concatenate(turned, axis=1), preferred_element_type=F32)


def scatter_slabs(rows, scale, outs, lead, inner):
    local = outs[0].shape[-1]
    per = local // inner
    scaled = rows * scale
    for src, out in enumerate(outs):
        for part in range(per):
            at = (src * per + part) * GROUP
            tile = jnp.concatenate(
                [scaled[at : at + GROUP, :inner], scaled[at : at + GROUP, inner:]], axis=0
            ).astype(BF16)
            lanes = slice(part * inner, (part + 1) * inner)
            if lead is None:
                out[:, lanes] = tile
            else:
                out[lead, :, lanes] = tile


def times_plain(left, right):
    return (left[0] * right[0] - left[1] * right[1], left[0] * right[1] + left[1] * right[0])


def times_conj(left, right):
    return (left[0] * right[0] + left[1] * right[1], left[1] * right[0] - left[0] * right[1])


def response_kernel(chunks, inner, me, *refs):
    pair, refs = refs[:chunks], refs[chunks:]
    (first, last, cos, sin, forward, backward), outs = refs[:6], refs[6:]
    tables = (first[...], cos[...], sin[...], forward[...], inner)
    prod = forward_dft(gather_slabs([ref[0] for ref in pair], inner), *tables)
    taps = forward_dft(gather_slabs([ref[1] for ref in pair], inner), *tables)
    rows = inverse_dft(times_plain(prod, taps), last[...], cos[...], sin[...], backward[...], inner)
    scatter_slabs(rows, 1.0 / (SLABS * inner), outs, None, inner)


def backward_kernel(chunks, inner, scale, me, *refs):
    pair, grad, refs = refs[:chunks], refs[chunks : 2 * chunks], refs[2 * chunks :]
    (first, last, cos, sin, forward, backward), outs = refs[:6], refs[6:]
    tables = (first[...], cos[...], sin[...], forward[...], inner)
    back_tables = (last[...], cos[...], sin[...], backward[...], inner)
    grad_spec = forward_dft(gather_slabs([ref[...] for ref in grad], inner), *tables)
    taps = forward_dft(gather_slabs([ref[1] for ref in pair], inner), *tables)
    rows = inverse_dft(times_conj(grad_spec, taps), *back_tables)
    scatter_slabs(rows, 1.0 / (SLABS * inner), outs, 0, inner)
    prod = forward_dft(gather_slabs([ref[0] for ref in pair], inner), *tables)
    rows = inverse_dft(times_conj(grad_spec, prod), *back_tables)
    scatter_slabs(rows, scale / (SLABS * inner), outs, 1, inner)


def conv_call(kernel, me, operands, tables, lead, inner, transforms):
    chunks, shape = len(operands[0]), operands[0][0].shape
    channels, local = shape[-2:]
    def rows_of(shape):
        middle = shape[:-2]
        return pl.BlockSpec(
            middle + (STEP, local), lambda i, me: (0,) * len(middle) + (i, 0)
        )

    def whole(table):
        return pl.BlockSpec(table.shape, lambda i, me: (0, 0))

    out_shape = lead + (channels, local)
    rows = channels * SLABS
    flops = transforms * rows * (2 * (2 * inner) ** 2 + 4 * SLABS * GROUP * inner)
    flat = [chunk for operand in operands for chunk in operand]
    return pl.pallas_call(
        kernel,
        grid_spec=pltpu.PrefetchScalarGridSpec(
            num_scalar_prefetch=1,
            grid=(channels // STEP,),
            in_specs=[rows_of(chunk.shape) for chunk in flat] + [whole(t) for t in tables],
            out_specs=[rows_of(out_shape)] * chunks,
        ),
        out_shape=[jax.ShapeDtypeStruct(out_shape, BF16)] * chunks,
        compiler_params=pltpu.CompilerParams(vmem_limit_bytes=40 * 1024 * 1024),
        cost_estimate=pl.CostEstimate(
            flops=flops, bytes_accessed=2 * rows * inner * 4, transcendentals=0
        ),
    )(me, *flat, *tables)


def elementwise(left, right):
    return (left.astype(F32) * right.astype(F32)).astype(BF16)


def prepare_kernel(chunks, scale, me, inner_gate, signal, taps, gain, *outs):
    at_zero = (me[0] == 0) & (lax.broadcasted_iota(jnp.int32, taps.shape[1:], 1) == 0)
    for d, out in enumerate(outs):
        at = me[0] ^ d
        out[0] = elementwise(inner_gate[at], signal[at])
        out[1] = (taps[at] * scale + jnp.where(at_zero, gain[at], 0.0)).astype(BF16)


def project_kernel(chunks, me, weight, gathered, gate, upstream, *outs):
    step = pl.program_id(0)
    rows = weight.shape[0] // 2
    total = jnp.dot(weight[...], gathered[...], preferred_element_type=F32).astype(BF16)
    upstream[...] = total.reshape(upstream.shape)
    low = elementwise(total[:rows], gate[0])
    high = elementwise(total[rows:], gate[1])
    swapped = (me[0] & 1) == 1
    for pair in range(chunks // 2):

        @pl.when(step == pair)
        def _():
            outs[2 * pair][...] = jnp.where(swapped, high, low)
            outs[2 * pair + 1][...] = jnp.where(swapped, low, high)


def outer_kernel(chunks, me, upstream, *refs):
    chunk, out = refs[:chunks], refs[chunks]
    for d in range(chunks):
        at = me[0] ^ d
        out[at] = elementwise(upstream[at], chunk[d][...])


def finish_kernel(chunks, me, inner_gate, signal, *refs):
    chunk, (grad_inner, grad_signal, grad_taps) = refs[:chunks], refs[chunks:]
    for d in range(chunks):
        at = me[0] ^ d
        back = chunk[d][0]
        grad_inner[at] = elementwise(back, signal[at])
        grad_signal[at] = elementwise(back, inner_gate[at])
        grad_taps[at] = chunk[d][1].astype(F32)


def rowwise_call(kernel, me, wholes, pieces, out_shapes, rows):
    def spec(shape):
        lead = shape[:-2]
        return pl.BlockSpec(
            lead + (rows, shape[-1]), lambda i, me: (0,) * len(lead) + (i, 0)
        )

    channels = wholes[0].shape[1]
    size = sum(math.prod(x.shape) * x.dtype.itemsize for x in (*wholes, *pieces, *out_shapes))
    return pl.pallas_call(
        kernel,
        grid_spec=pltpu.PrefetchScalarGridSpec(
            num_scalar_prefetch=1,
            grid=(channels // rows,),
            in_specs=[spec(x.shape) for x in (*wholes, *pieces)],
            out_specs=[spec(x.shape) for x in out_shapes],
        ),
        out_shape=out_shapes,
        compiler_params=pltpu.CompilerParams(vmem_limit_bytes=32 * 1024 * 1024),
        cost_estimate=pl.CostEstimate(flops=size, bytes_accessed=size, transcendentals=0),
    )(me, *wholes, *pieces)


def project_call(me, weight, gathered, gate):
    chunks, channels, local = gate.shape
    depth = weight.shape[1]

    def pair(i, me):
        return (me[0] >> 1) ^ i

    rows = 2 * channels
    return pl.pallas_call(
        functools.partial(project_kernel, chunks),
        grid_spec=pltpu.PrefetchScalarGridSpec(
            num_scalar_prefetch=1,
            grid=(chunks // 2,),
            in_specs=[
                pl.BlockSpec((rows, depth), lambda i, me: (pair(i, me), 0)),
                pl.BlockSpec((depth, local), lambda i, me: (0, 0)),
                pl.BlockSpec((2, channels, local), lambda i, me: (pair(i, me), 0, 0)),
            ],
            out_specs=[pl.BlockSpec((2, channels, local), lambda i, me: (pair(i, me), 0, 0))]
            + [pl.BlockSpec((channels, local), lambda i, me: (0, 0))] * chunks,
        ),
        out_shape=[jax.ShapeDtypeStruct(gate.shape, BF16)]
        + [jax.ShapeDtypeStruct((channels, local), BF16)] * chunks,
        compiler_params=pltpu.CompilerParams(vmem_limit_bytes=40 * 1024 * 1024),
        cost_estimate=pl.CostEstimate(
            flops=2 * weight.size * local, bytes_accessed=2 * weight.size, transcendentals=0
        ),
    )(me, weight, gathered, gate)


def exchange(parts):
    count = len(parts)
    if count > 8:
        order = lax.axis_index("ctx") ^ jnp.arange(count)
        sent = jnp.take(jnp.stack(parts), order, axis=0)
        came = lax.all_to_all(sent, "ctx", split_axis=0, concat_axis=0, tiled=True)
        return list(jnp.take(came, order, axis=0))
    came = [None] * count
    came[0] = parts[0]
    for d in reversed(range(1, count)):
        came[d] = lax.ppermute(parts[d], "ctx", [(p, p ^ d) for p in range(count)])
    return came


def after(parts, other):
    held, _ = lax.optimization_barrier((parts[0], other))
    return [held] + list(parts[1:])


def per_device(outer_gate, inner_gate, signal, cotangent, out_weight, filter_taps, skip_gain):
    ch_dev, tok_local = outer_gate.shape
    n_ctx = lax.axis_size("ctx")
    ch_slice = ch_dev // n_ctx
    seq_len = n_ctx * tok_local
    inner = seq_len // SLABS
    scale = 1.0 / math.sqrt(seq_len)
    me = lax.axis_index("ctx").reshape(1)

    def split(array):
        return array.reshape(n_ctx, ch_slice, -1)

    def flat(array):
        return array.reshape(ch_dev, tok_local)

    def shapes(lead, dtype, count):
        return [jax.ShapeDtypeStruct(lead + (ch_slice, tok_local), dtype)] * count

    tables = [jnp.asarray(table) for table in make_tables(inner, n_ctx)]
    tables = [table if table.ndim == 2 else table[me[0]] for table in tables]
    gathered = lax.all_gather(cotangent, "group", axis=0, tiled=True)
    pair = exchange(
        rowwise_call(
            functools.partial(prepare_kernel, n_ctx, scale),
            me,
            (split(inner_gate), split(signal), split(filter_taps), split(skip_gain)),
            (),
            shapes((2,), BF16, n_ctx),
            32,
        )
    )
    upstream, *grad = project_call(me, out_weight, gathered, split(outer_gate))
    grad_came = exchange(grad)
    response = conv_call(
        functools.partial(response_kernel, n_ctx, inner), me, (after(pair, grad[0]),), tables, (), inner, 3
    )
    resp_came = exchange(response)
    backs = conv_call(
        functools.partial(backward_kernel, n_ctx, inner, scale),
        me,
        (pair, after(grad_came, response[0])),
        tables,
        (2,),
        inner,
        5,
    )
    backs_came = exchange(backs)
    (grad_outer,) = rowwise_call(
        functools.partial(outer_kernel, n_ctx),
        me,
        (upstream,),
        after(resp_came, backs[0]),
        shapes((n_ctx,), BF16, 1),
        32,
    )
    grad_inner, grad_signal, grad_taps = rowwise_call(
        functools.partial(finish_kernel, n_ctx),
        me,
        (split(inner_gate), split(signal)),
        backs_came,
        shapes((n_ctx,), BF16, 2) + shapes((n_ctx,), F32, 1),
        32,
    )
    return (flat(grad_outer), flat(grad_inner), flat(grad_signal), flat(grad_taps))


def solution(mesh):
    in_specs = (
        P("group", "ctx"),
        P("group", "ctx"),
        P("group", "ctx"),
        P("group", "ctx"),
        P("group", None),
        P("group", "ctx"),
        P("group"),
    )
    out_specs = (P("group", "ctx"), P("group", "ctx"), P("group", "ctx"), P("group", "ctx"))
    return jax.shard_map(
        per_device, mesh=mesh, in_specs=in_specs, out_specs=out_specs, check_vma=False
    )
```

time: 217 us -> 179 us (0.82)
  the two profiles are of different devices: /device:TPU:0 before, /device:TPU:18 now
where the time goes in v3:
time: 179 us; the launch traced here: 178 us
  waiting for transfers between devices  77.5 us (43%)
  starting transfers between devices  41.3 us (23%)
  Pallas kernels  37.4 us (21%)
  between operations  14.2 us (8%)
  local copies, waits for them, and re-layouts  7.88 us (4%)
    ppermute x28, waiting for transfers between devices, exchange(): came[d] = lax.ppermute(parts[d], 'ctx', [(p, p ^ d) for p in range(count)])  65.5 us
    ppermute x28, starting transfers between devices, exchange(): came[d] = lax.ppermute(parts[d], 'ctx', [(p, p ^ d) for p in range(count)])  41.3 us
    pallas_call x2, Pallas kernels, conv_call(): pl.pallas_call(kernel, grid_spec=pltpu.PrefetchScalarGridSpec(num_scalar_...  23.1 us
    all_gather x1, waiting for transfers between devices, per_device(): gathered = lax.all_gather(cotangent, 'group', axis=0, tiled=True)  11.3 us
    pallas_call x1, Pallas kernels, project_call(): pl.pallas_call(functools.partial(project_kernel, chunks), grid_spec=pltpu...  7.35 us
    pallas_call x3, Pallas kernels, rowwise_call(): pl.pallas_call(kernel, grid_spec=pltpu.PrefetchScalarGridSpec(num_scalar_...  6.93 us
    unnamed x24, local copies, waits for them, and re-layouts  5.03 us
  transfers between devices with their start and end apart: 29, of which 12 were waited for; matrix products, arithmetic and copies ran while one was open for 2% of the time, Pallas kernels for 19%

profile of v3, /device:TPU:18, one launch (start us, length us, event | category | flops | bytes accessed | tf_op | source)
XLA Modules:
  0.0 178.2 jit_solution(286218825847762127)
XLA Ops:
  8.8 1.2 copy-done.1
  10.1 1.6 copy-done.3
  11.7 2.1 %shard_map.157 = (bf16[2,128,512]{2,1,0:T(8,128)(2,1)S(1)}, bf16[2,128,512]{2,1,0:T(8,128)(2,1)}, bf16[2,128,512]{2,1,0:T(8,128)(2,1)}, bf16[2,128,512]{2,1,0:T(...) custom-call(s32[1]{0:T(128)} %bitcast.me, ...), custom_call_target="tpu_custom_call" | custom-call | flops 6295552 | bytes 6295552 | tf_op jit(solution)/shard_map/pallas_call | solution.py:220
  13.8 1.6 collective-permute-start
  15.4 1.6 collective-permute-start.1
  17.7 3.5 %collective-permute-start.4 = (bf16[2,128,512]{2,1,0:T(8,128)(2,1)}, bf16[2,128,512]{2,1,0:T(8,128)(2,1)}, u32[]{:S(2)}, u32[]{:S(2)}) collective-permute-start(bf16[2,128,512]{2,1,0:T(8,128)(2,1)} %get-tuple-element.51), channel_id=1, source_target_pairs={{0,5},{1,4},{2,7},{3,6},{4,1},{5,0},{6,3},{7,2},{8,13},{9,12},{10,... | collective-permute-start | bytes 786440 | tf_op jit(solution)/shard_map/ppermute | solution.py:274
  22.8 9.9 %collective-permute-done.1.refs_2_ = bf16[2,128,512]{2,1,0:T(8,128)(2,1)S(1)} collective-permute-done((bf16[2,128,512]{2,1,0:T(8,128)(2,1)}, bf16[2,128,512]{2,1,0:T(8,128)(2,1)S(1)}, u32[]{:S(2)}, u32[]{:S(2)}) %collective-permute-start.1) | collective-permute-done | bytes 262176 | tf_op jit(solution)/shard_map/ppermute | solution.py:274
  32.9 11.3 %all-gather.2.cloned.1.call-done.gathered = bf16[4096,512]{1,0:T(8,128)(2,1)} async-done(((bf16[1024,512]{1,0:T(8,128)(2,1)}), bf16[4096,512]{1,0:T(8,128)(2,1)}) %all-gather.2.cloned.1.call-update) | async-done | bytes 4194320 | tf_op jit(solution)/shard_map/all_gather | solution.py:303
  44.2 2.2 %copy-done.4 = bf16[4096,512]{1,0:T(8,128)(2,1)S(1)} copy-done((bf16[4096,512]{1,0:T(8,128)(2,1)S(1)}, bf16[4096,512]{1,0:T(8,128)(2,1)}, u32[]{:S(2)}) %copy-start.4) | copy-done | bytes 4194328
  46.4 7.3 %shard_map.156 = (bf16[8,128,512]{2,1,0:T(8,128)(2,1)S(1)}, bf16[128,512]{1,0:T(8,128)(2,1)S(1)}, bf16[128,512]{1,0:T(8,128)(2,1)S(1)}, bf16[128,512]{1,0:T(8,12...) custom-call(s32[1]{0:T(128)} %bitcast.me, ...), custom_call_target="tpu_custom_call" | custom-call | flops 4294967296 | bytes 8388608 | tf_op jit(solution)/shard_map/pallas_call | solution.py:242
  53.8 1.5 collective-permute-start.7
  55.3 1.5 collective-permute-start.8
  59.4 2.3 %collective-permute-done.5.refs_6_ = bf16[2,128,512]{2,1,0:T(8,128)(2,1)} collective-permute-done((bf16[2,128,512]{2,1,0:T(8,128)(2,1)}, bf16[2,128,512]{2,1,0:T(8,128)(2,1)}, u32[]{:S(2)}, u32[]{:S(2)}) %collective-permute-start.5) | collective-permute-done | bytes 262176 | tf_op jit(solution)/shard_map/ppermute | solution.py:274
  61.6 13.6 %collective-permute-done.6.refs_7_ = bf16[2,128,512]{2,1,0:T(8,128)(2,1)} collective-permute-done((bf16[2,128,512]{2,1,0:T(8,128)(2,1)}, bf16[2,128,512]{2,1,0:T(8,128)(2,1)}, u32[]{:S(2)}, u32[]{:S(2)}) %collective-permute-start.6) | collective-permute-done | bytes 262176 | tf_op jit(solution)/shard_map/ppermute | solution.py:274
  76.5 9.3 %shard_map.158 = (bf16[128,512]{1,0:T(8,128)(2,1)S(1)}, bf16[128,512]{1,0:T(8,128)(2,1)S(1)}, bf16[128,512]{1,0:T(8,128)(2,1)S(1)}, bf16[128,512]{1,0:T(8,128)(2...) custom-call(s32[1]{0:T(128)} %bitcast.me, ...), custom_call_target="tpu_custom_call" | custom-call | flops 3221225472 | bytes 4194304 | tf_op jit(solution)/shard_map/pallas_call | solution.py:150
  85.8 2.4 %collective-permute-start.14 = (bf16[128,512]{1,0:T(8,128)(2,1)S(1)}, bf16[128,512]{1,0:T(8,128)(2,1)S(1)}, u32[]{:S(2)}, u32[]{:S(2)}) collective-permute-start(bf16[128,512]{1,0:T(8,128)(2,1)S(1)} %get-tuple-element.65), channel_id=1, source_target_pairs={{0,1},{1,0},{2,3},{3,2},{4,5},{5,4},{6,7},{7,6},{8,9},{9,8},{10,11... | collective-permute-start | bytes 393224 | tf_op jit(solution)/shard_map/ppermute | solution.py:274
  88.2 2.4 %collective-permute-start.15 = (bf16[128,512]{1,0:T(8,128)(2,1)S(1)}, bf16[128,512]{1,0:T(8,128)(2,1)S(1)}, u32[]{:S(2)}, u32[]{:S(2)}) collective-permute-start(bf16[128,512]{1,0:T(8,128)(2,1)S(1)} %get-tuple-element.66), channel_id=1, source_target_pairs={{0,2},{1,3},{2,0},{3,1},{4,6},{5,7},{6,4},{7,5},{8,10},{9,11},{10,... | collective-permute-start | bytes 393224 | tf_op jit(solution)/shard_map/ppermute | solution.py:274
  91.6 4.2 %collective-permute-start.17 = (bf16[128,512]{1,0:T(8,128)(2,1)S(1)}, bf16[128,512]{1,0:T(8,128)(2,1)S(1)}, u32[]{:S(2)}, u32[]{:S(2)}) collective-permute-start(bf16[128,512]{1,0:T(8,128)(2,1)S(1)} %get-tuple-element.68), channel_id=1, source_target_pairs={{0,4},{1,5},{2,6},{3,7},{4,0},{5,1},{6,2},{7,3},{8,12},{9,13},{10,... | collective-permute-start | bytes 393224 | tf_op jit(solution)/shard_map/ppermute | solution.py:274
  95.9 13.7 %shard_map.159 = (bf16[2,128,512]{2,1,0:T(8,128)(2,1)S(1)}, bf16[2,128,512]{2,1,0:T(8,128)(2,1)S(1)}, bf16[2,128,512]{2,1,0:T(8,128)(2,1)S(1)}, bf16[2,128,512]{...) custom-call(s32[1]{0:T(128)} %bitcast.me, ...), custom_call_target="tpu_custom_call" | custom-call | flops 5368709120 | bytes 4194304 | tf_op jit(solution)/shard_map/pallas_call | solution.py:150
  110.3 1.5 collective-permute-start.18
  111.8 2.9 %collective-permute-start.19 = (bf16[128,512]{1,0:T(8,128)(2,1)S(1)}, bf16[128,512]{1,0:T(8,128)(2,1)S(1)}, u32[]{:S(2)}, u32[]{:S(2)}) collective-permute-start(bf16[128,512]{1,0:T(8,128)(2,1)S(1)} %get-tuple-element.70), channel_id=1, source_target_pairs={{0,6},{1,7},{2,4},{3,5},{4,2},{5,3},{6,0},{7,1},{8,14},{9,15},{10,... | collective-permute-start | bytes 393224 | tf_op jit(solution)/shard_map/ppermute | solution.py:274
  114.7 7.2 %collective-permute-done.18.refs_5_ = bf16[128,512]{1,0:T(8,128)(2,1)S(1)} collective-permute-done((bf16[128,512]{1,0:T(8,128)(2,1)S(1)}, bf16[128,512]{1,0:T(8,128)(2,1)S(1)}, u32[]{:S(2)}, u32[]{:S(2)}) %collective-permute-start.18) | collective-permute-done | bytes 131104 | tf_op jit(solution)/shard_map/ppermute | solution.py:274
  121.9 9.8 %collective-permute-start.23 = (bf16[2,128,512]{2,1,0:T(8,128)(2,1)S(1)}, bf16[2,128,512]{2,1,0:T(8,128)(2,1)S(1)}, u32[]{:S(2)}, u32[]{:S(2)}) collective-permute-start(bf16[2,128,512]{2,1,0:T(8,128)(2,1)S(1)} %get-tuple-element.74), channel_id=1, source_target_pairs={{0,3},{1,2},{2,1},{3,0},{4,7},{5,6},{6,5},{7,4},{8,11},{9,10},{10,... | collective-permute-start | bytes 786440 | tf_op jit(solution)/shard_map/ppermute | solution.py:274
  131.7 5.7 %collective-permute-done.19.refs_6_ = bf16[128,512]{1,0:T(8,128)(2,1)S(1)} collective-permute-done((bf16[128,512]{1,0:T(8,128)(2,1)S(1)}, bf16[128,512]{1,0:T(8,128)(2,1)S(1)}, u32[]{:S(2)}, u32[]{:S(2)}) %collective-permute-start.19) | collective-permute-done | bytes 131104 | tf_op jit(solution)/shard_map/ppermute | solution.py:274
  137.4 2.2 %collective-permute-done.20.refs_7_ = bf16[128,512]{1,0:T(8,128)(2,1)S(1)} collective-permute-done((bf16[128,512]{1,0:T(8,128)(2,1)S(1)}, bf16[128,512]{1,0:T(8,128)(2,1)S(1)}, u32[]{:S(2)}, u32[]{:S(2)}) %collective-permute-start.20) | collective-permute-done | bytes 131104 | tf_op jit(solution)/shard_map/ppermute | solution.py:274
  139.7 3.5 %collective-permute-start.27 = (bf16[2,128,512]{2,1,0:T(8,128)(2,1)S(1)}, bf16[2,128,512]{2,1,0:T(8,128)(2,1)S(1)}, u32[]{:S(2)}, u32[]{:S(2)}) collective-permute-start(bf16[2,128,512]{2,1,0:T(8,128)(2,1)S(1)} %get-tuple-element.78), channel_id=1, source_target_pairs={{0,7},{1,6},{2,5},{3,4},{4,3},{5,2},{6,1},{7,0},{8,15},{9,14},{10,... | collective-permute-start | bytes 786440 | tf_op jit(solution)/shard_map/ppermute | solution.py:274
  143.2 1.7 shard_map.160
  145.0 10.4 %collective-permute-done.24.refs_4_ = bf16[2,128,512]{2,1,0:T(8,128)(2,1)S(1)} collective-permute-done((bf16[2,128,512]{2,1,0:T(8,128)(2,1)S(1)}, bf16[2,128,512]{2,1,0:T(8,128)(2,1)S(1)}, u32[]{:S(2)}, u32[]{:S(2)}) %collective-permute-start.24) | collective-permute-done | bytes 262176 | tf_op jit(solution)/shard_map/ppermute | solution.py:274
  155.4 5.3 %collective-permute-done.25.refs_5_ = bf16[2,128,512]{2,1,0:T(8,128)(2,1)S(1)} collective-permute-done((bf16[2,128,512]{2,1,0:T(8,128)(2,1)S(1)}, bf16[2,128,512]{2,1,0:T(8,128)(2,1)S(1)}, u32[]{:S(2)}, u32[]{:S(2)}) %collective-permute-start.25) | collective-permute-done | bytes 262176 | tf_op jit(solution)/shard_map/ppermute | solution.py:274
  160.7 4.3 %collective-permute-done.26.refs_6_ = bf16[2,128,512]{2,1,0:T(8,128)(2,1)S(1)} collective-permute-done((bf16[2,128,512]{2,1,0:T(8,128)(2,1)S(1)}, bf16[2,128,512]{2,1,0:T(8,128)(2,1)S(1)}, u32[]{:S(2)}, u32[]{:S(2)}) %collective-permute-start.26) | collective-permute-done | bytes 262176 | tf_op jit(solution)/shard_map/ppermute | solution.py:274
  165.0 3.4 %collective-permute-done.27.refs_7_ = bf16[2,128,512]{2,1,0:T(8,128)(2,1)S(1)} collective-permute-done((bf16[2,128,512]{2,1,0:T(8,128)(2,1)S(1)}, bf16[2,128,512]{2,1,0:T(8,128)(2,1)S(1)}, u32[]{:S(2)}, u32[]{:S(2)}) %collective-permute-start.27) | collective-permute-done | bytes 262176 | tf_op jit(solution)/shard_map/ppermute | solution.py:274
  168.4 3.0 %shard_map.161 = (bf16[8,128,512]{2,1,0:T(8,128)(2,1)}, bf16[8,128,512]{2,1,0:T(8,128)(2,1)}, f32[8,128,512]{2,1,0:T(8,128)}) custom-call(s32[1]{0:T(128)} %bitcast.me, bf16[8,128,512]{2,1,0:T(8,128)(2,1)S(1)} %bitcast.15, bf16[8,128,512]{2,1,0:T(8,128)(2,1)S(1)} %bitcast.17, bf16[2,128,512]{2,1,0:T(8,128)(2,1)S(1)} %get-tuple-element.63.refs_0_, ...), custom_call_target="tpu_custom_call" | custom-call | flops 8388608 | bytes 8388608 | tf_op jit(solution)/shard_map/pallas_call | solution.py:220
  (60 shorter events, 9.7 us)
Async XLA Ops:
  7.2 37.0 %all-gather.2.cloned.1.call-start = ((), (), s32[]{:S(2)}) async-start(), calls=%async_computation | async-start | bytes 5242880 | tf_op jit(solution)/shard_map/all_gather | solution.py:303
  11.7 32.6 %copy-start.5 = (bf16[1024,512]{1,0:T(8,128)(2,1)S(1)}, bf16[1024,512]{1,0:T(8,128)(2,1)}, u32[]{:S(2)}) copy-start(bf16[1024,512]{1,0:T(8,128)(2,1)} %param.13) | copy-start | bytes 3145732
  13.8 8.6 %collective-permute-start = (bf16[2,128,512]{2,1,0:T(8,128)(2,1)}, bf16[2,128,512]{2,1,0:T(8,128)(2,1)S(1)}, u32[]{:S(2)}, u32[]{:S(2)}) collective-permute-start(bf16[2,128,512]{2,1,0:T(8,128)(2,1)} %get-tuple-element.47), channel_id=1, source_target_pairs={{0,1},{1,0},{2,3},{3,2},{4,5},{5,4},{6,7},{7,6},{8,9},{9,8},{10,11... | collective-permute-start | bytes 786440 | tf_op jit(solution)/shard_map/ppermute | solution.py:274
  15.4 17.4 %collective-permute-start.1 = (bf16[2,128,512]{2,1,0:T(8,128)(2,1)}, bf16[2,128,512]{2,1,0:T(8,128)(2,1)S(1)}, u32[]{:S(2)}, u32[]{:S(2)}) collective-permute-start(bf16[2,128,512]{2,1,0:T(8,128)(2,1)} %get-tuple-element.48), channel_id=1, source_target_pairs={{0,2},{1,3},{2,0},{3,1},{4,6},{5,7},{6,4},{7,5},{8,10},{9,11},{10,... | collective-permute-start | bytes 786440 | tf_op jit(solution)/shard_map/ppermute | solution.py:274
  17.0 36.8 %collective-permute-start.2 = (bf16[2,128,512]{2,1,0:T(8,128)(2,1)}, bf16[2,128,512]{2,1,0:T(8,128)(2,1)S(1)}, u32[]{:S(2)}, u32[]{:S(2)}) collective-permute-start(bf16[2,128,512]{2,1,0:T(8,128)(2,1)} %get-tuple-element.49), channel_id=1, source_target_pairs={{0,3},{1,2},{2,1},{3,0},{4,7},{5,6},{6,5},{7,4},{8,11},{9,10},{10,... | collective-permute-start | bytes 786440 | tf_op jit(solution)/shard_map/ppermute | solution.py:274
  17.4 38.0 %collective-permute-start.3 = (bf16[2,128,512]{2,1,0:T(8,128)(2,1)}, bf16[2,128,512]{2,1,0:T(8,128)(2,1)S(1)}, u32[]{:S(2)}, u32[]{:S(2)}) collective-permute-start(bf16[2,128,512]{2,1,0:T(8,128)(2,1)} %get-tuple-element.50), channel_id=1, source_target_pairs={{0,4},{1,5},{2,6},{3,7},{4,0},{5,1},{6,2},{7,3},{8,12},{9,13},{10,... | collective-permute-start | bytes 786440 | tf_op jit(solution)/shard_map/ppermute | solution.py:274
  17.7 41.1 %collective-permute-start.4 = (bf16[2,128,512]{2,1,0:T(8,128)(2,1)}, bf16[2,128,512]{2,1,0:T(8,128)(2,1)}, u32[]{:S(2)}, u32[]{:S(2)}) collective-permute-start(bf16[2,128,512]{2,1,0:T(8,128)(2,1)} %get-tuple-element.51), channel_id=1, source_target_pairs={{0,5},{1,4},{2,7},{3,6},{4,1},{5,0},{6,3},{7,2},{8,13},{9,12},{10,... | collective-permute-start | bytes 786440 | tf_op jit(solution)/shard_map/ppermute | solution.py:274
  22.4 39.2 %collective-permute-start.5 = (bf16[2,128,512]{2,1,0:T(8,128)(2,1)}, bf16[2,128,512]{2,1,0:T(8,128)(2,1)}, u32[]{:S(2)}, u32[]{:S(2)}) collective-permute-start(bf16[2,128,512]{2,1,0:T(8,128)(2,1)} %copy-done.7), channel_id=1, source_target_pairs={{0,6},{1,7},{2,4},{3,5},{4,2},{5,3},{6,0},{7,1},{8,14},{9,15},{10,... | collective-permute-start | bytes 786440 | tf_op jit(solution)/shard_map/ppermute | solution.py:274
  32.8 42.5 %collective-permute-start.6 = (bf16[2,128,512]{2,1,0:T(8,128)(2,1)}, bf16[2,128,512]{2,1,0:T(8,128)(2,1)}, u32[]{:S(2)}, u32[]{:S(2)}) collective-permute-start(bf16[2,128,512]{2,1,0:T(8,128)(2,1)} %copy-done.6), channel_id=1, source_target_pairs={{0,7},{1,6},{2,5},{3,4},{4,3},{5,2},{6,1},{7,0},{8,15},{9,14},{10,... | collective-permute-start | bytes 786440 | tf_op jit(solution)/shard_map/ppermute | solution.py:274
  46.4 30.1 %copy-start.11 = (f32[256,128]{1,0:T(8,128)S(1)}, f32[256,128]{1,0:T(8,128)}, u32[]{:S(2)}) copy-start(f32[256,128]{1,0:T(8,128)} %constant.22.clone.refs_10_.refs_18_) | copy-start | bytes 393220
  53.8 21.5 %collective-permute-start.7 = (bf16[128,512]{1,0:T(8,128)(2,1)S(1)}, bf16[128,512]{1,0:T(8,128)(2,1)S(1)}, u32[]{:S(2)}, u32[]{:S(2)}) collective-permute-start(bf16[128,512]{1,0:T(8,128)(2,1)S(1)} %get-tuple-element.56), channel_id=1, source_target_pairs={{0,1},{1,0},{2,3},{3,2},{4,5},{5,4},{6,7},{7,6},{8,9},{9,8},{10,11... | collective-permute-start | bytes 393224 | tf_op jit(solution)/shard_map/ppermute | solution.py:274
  55.3 20.0 %collective-permute-start.8 = (bf16[128,512]{1,0:T(8,128)(2,1)S(1)}, bf16[128,512]{1,0:T(8,128)(2,1)S(1)}, u32[]{:S(2)}, u32[]{:S(2)}) collective-permute-start(bf16[128,512]{1,0:T(8,128)(2,1)S(1)} %get-tuple-element.57), channel_id=1, source_target_pairs={{0,2},{1,3},{2,0},{3,1},{4,6},{5,7},{6,4},{7,5},{8,10},{9,11},{10,... | collective-permute-start | bytes 393224 | tf_op jit(solution)/shard_map/ppermute | solution.py:274
  58.8 27.1 %collective-permute-start.9 = (bf16[128,512]{1,0:T(8,128)(2,1)S(1)}, bf16[128,512]{1,0:T(8,128)(2,1)S(1)}, u32[]{:S(2)}, u32[]{:S(2)}) collective-permute-start(bf16[128,512]{1,0:T(8,128)(2,1)S(1)} %get-tuple-element.58), channel_id=1, source_target_pairs={{0,3},{1,2},{2,1},{3,0},{4,7},{5,6},{6,5},{7,4},{8,11},{9,10},{10,... | collective-permute-start | bytes 393224 | tf_op jit(solution)/shard_map/ppermute | solution.py:274
  61.6 26.6 %collective-permute-start.10 = (bf16[128,512]{1,0:T(8,128)(2,1)S(1)}, bf16[128,512]{1,0:T(8,128)(2,1)S(1)}, u32[]{:S(2)}, u32[]{:S(2)}) collective-permute-start(bf16[128,512]{1,0:T(8,128)(2,1)S(1)} %get-tuple-element.59), channel_id=1, source_target_pairs={{0,4},{1,5},{2,6},{3,7},{4,0},{5,1},{6,2},{7,3},{8,12},{9,13},{10,... | collective-permute-start | bytes 393224 | tf_op jit(solution)/shard_map/ppermute | solution.py:274
  75.3 15.3 %collective-permute-start.11 = (bf16[128,512]{1,0:T(8,128)(2,1)S(1)}, bf16[128,512]{1,0:T(8,128)(2,1)S(1)}, u32[]{:S(2)}, u32[]{:S(2)}) collective-permute-start(bf16[128,512]{1,0:T(8,128)(2,1)S(1)} %get-tuple-element.60), channel_id=1, source_target_pairs={{0,5},{1,4},{2,7},{3,6},{4,1},{5,0},{6,3},{7,2},{8,13},{9,12},{10,... | collective-permute-start | bytes 393224 | tf_op jit(solution)/shard_map/ppermute | solution.py:274
  75.3 16.3 %collective-permute-start.12 = (bf16[128,512]{1,0:T(8,128)(2,1)S(1)}, bf16[128,512]{1,0:T(8,128)(2,1)S(1)}, u32[]{:S(2)}, u32[]{:S(2)}) collective-permute-start(bf16[128,512]{1,0:T(8,128)(2,1)S(1)} %get-tuple-element.61), channel_id=1, source_target_pairs={{0,6},{1,7},{2,4},{3,5},{4,2},{5,3},{6,0},{7,1},{8,14},{9,15},{10,... | collective-permute-start | bytes 393224 | tf_op jit(solution)/shard_map/ppermute | solution.py:274
  75.3 20.6 %collective-permute-start.13 = (bf16[128,512]{1,0:T(8,128)(2,1)S(1)}, bf16[128,512]{1,0:T(8,128)(2,1)S(1)}, u32[]{:S(2)}, u32[]{:S(2)}) collective-permute-start(bf16[128,512]{1,0:T(8,128)(2,1)S(1)} %get-tuple-element.62), channel_id=1, source_target_pairs={{0,7},{1,6},{2,5},{3,4},{4,3},{5,2},{6,1},{7,0},{8,15},{9,14},{10,... | collective-permute-start | bytes 393224 | tf_op jit(solution)/shard_map/ppermute | solution.py:274
  85.8 23.9 %collective-permute-start.14 = (bf16[128,512]{1,0:T(8,128)(2,1)S(1)}, bf16[128,512]{1,0:T(8,128)(2,1)S(1)}, u32[]{:S(2)}, u32[]{:S(2)}) collective-permute-start(bf16[128,512]{1,0:T(8,128)(2,1)S(1)} %get-tuple-element.65), channel_id=1, source_target_pairs={{0,1},{1,0},{2,3},{3,2},{4,5},{5,4},{6,7},{7,6},{8,9},{9,8},{10,11... | collective-permute-start | bytes 393224 | tf_op jit(solution)/shard_map/ppermute | solution.py:274
  88.2 22.1 %collective-permute-start.15 = (bf16[128,512]{1,0:T(8,128)(2,1)S(1)}, bf16[128,512]{1,0:T(8,128)(2,1)S(1)}, u32[]{:S(2)}, u32[]{:S(2)}) collective-permute-start(bf16[128,512]{1,0:T(8,128)(2,1)S(1)} %get-tuple-element.66), channel_id=1, source_target_pairs={{0,2},{1,3},{2,0},{3,1},{4,6},{5,7},{6,4},{7,5},{8,10},{9,11},{10,... | collective-permute-start | bytes 393224 | tf_op jit(solution)/shard_map/ppermute | solution.py:274
  90.6 21.2 %collective-permute-start.16 = (bf16[128,512]{1,0:T(8,128)(2,1)S(1)}, bf16[128,512]{1,0:T(8,128)(2,1)S(1)}, u32[]{:S(2)}, u32[]{:S(2)}) collective-permute-start(bf16[128,512]{1,0:T(8,128)(2,1)S(1)} %get-tuple-element.67), channel_id=1, source_target_pairs={{0,3},{1,2},{2,1},{3,0},{4,7},{5,6},{6,5},{7,4},{8,11},{9,10},{10,... | collective-permute-start | bytes 393224 | tf_op jit(solution)/shard_map/ppermute | solution.py:274
  91.6 23.1 %collective-permute-start.17 = (bf16[128,512]{1,0:T(8,128)(2,1)S(1)}, bf16[128,512]{1,0:T(8,128)(2,1)S(1)}, u32[]{:S(2)}, u32[]{:S(2)}) collective-permute-start(bf16[128,512]{1,0:T(8,128)(2,1)S(1)} %get-tuple-element.68), channel_id=1, source_target_pairs={{0,4},{1,5},{2,6},{3,7},{4,0},{5,1},{6,2},{7,3},{8,12},{9,13},{10,... | collective-permute-start | bytes 393224 | tf_op jit(solution)/shard_map/ppermute | solution.py:274
  109.6 58.7 %copy-start.2 = (bf16[1024,512]{1,0:T(8,128)(2,1)S(1)}, bf16[1024,512]{1,0:T(8,128)(2,1)}, u32[]{:S(2)}) copy-start(bf16[1024,512]{1,0:T(8,128)(2,1)} %param.15) | copy-start | bytes 3145732
  109.6 30.1 %collective-permute-start.21 = (bf16[2,128,512]{2,1,0:T(8,128)(2,1)S(1)}, bf16[2,128,512]{2,1,0:T(8,128)(2,1)S(1)}, u32[]{:S(2)}, u32[]{:S(2)}) collective-permute-start(bf16[2,128,512]{2,1,0:T(8,128)(2,1)S(1)} %get-tuple-element.72), channel_id=1, source_target_pairs={{0,1},{1,0},{2,3},{3,2},{4,5},{5,4},{6,7},{7,6},{8,9},{9,8},{10,11... | collective-permute-start | bytes 786440 | tf_op jit(solution)/shard_map/ppermute | solution.py:274
  109.8 29.9 %collective-permute-start.22 = (bf16[2,128,512]{2,1,0:T(8,128)(2,1)S(1)}, bf16[2,128,512]{2,1,0:T(8,128)(2,1)S(1)}, u32[]{:S(2)}, u32[]{:S(2)}) collective-permute-start(bf16[2,128,512]{2,1,0:T(8,128)(2,1)S(1)} %get-tuple-element.73), channel_id=1, source_target_pairs={{0,2},{1,3},{2,0},{3,1},{4,6},{5,7},{6,4},{7,5},{8,10},{9,11},{10,... | collective-permute-start | bytes 786440 | tf_op jit(solution)/shard_map/ppermute | solution.py:274
  110.3 11.5 %collective-permute-start.18 = (bf16[128,512]{1,0:T(8,128)(2,1)S(1)}, bf16[128,512]{1,0:T(8,128)(2,1)S(1)}, u32[]{:S(2)}, u32[]{:S(2)}) collective-permute-start(bf16[128,512]{1,0:T(8,128)(2,1)S(1)} %get-tuple-element.69), channel_id=1, source_target_pairs={{0,5},{1,4},{2,7},{3,6},{4,1},{5,0},{6,3},{7,2},{8,13},{9,12},{10,... | collective-permute-start | bytes 393224 | tf_op jit(solution)/shard_map/ppermute | solution.py:274
  111.8 25.6 %collective-permute-start.19 = (bf16[128,512]{1,0:T(8,128)(2,1)S(1)}, bf16[128,512]{1,0:T(8,128)(2,1)S(1)}, u32[]{:S(2)}, u32[]{:S(2)}) collective-permute-start(bf16[128,512]{1,0:T(8,128)(2,1)S(1)} %get-tuple-element.70), channel_id=1, source_target_pairs={{0,6},{1,7},{2,4},{3,5},{4,2},{5,3},{6,0},{7,1},{8,14},{9,15},{10,... | collective-permute-start | bytes 393224 | tf_op jit(solution)/shard_map/ppermute | solution.py:274
  114.7 24.9 %collective-permute-start.20 = (bf16[128,512]{1,0:T(8,128)(2,1)S(1)}, bf16[128,512]{1,0:T(8,128)(2,1)S(1)}, u32[]{:S(2)}, u32[]{:S(2)}) collective-permute-start(bf16[128,512]{1,0:T(8,128)(2,1)S(1)} %get-tuple-element.71), channel_id=1, source_target_pairs={{0,7},{1,6},{2,5},{3,4},{4,3},{5,2},{6,1},{7,0},{8,15},{9,14},{10,... | collective-permute-start | bytes 393224 | tf_op jit(solution)/shard_map/ppermute | solution.py:274
  121.9 23.1 %collective-permute-start.23 = (bf16[2,128,512]{2,1,0:T(8,128)(2,1)S(1)}, bf16[2,128,512]{2,1,0:T(8,128)(2,1)S(1)}, u32[]{:S(2)}, u32[]{:S(2)}) collective-permute-start(bf16[2,128,512]{2,1,0:T(8,128)(2,1)S(1)} %get-tuple-element.74), channel_id=1, source_target_pairs={{0,3},{1,2},{2,1},{3,0},{4,7},{5,6},{6,5},{7,4},{8,11},{9,10},{10,... | collective-permute-start | bytes 786440 | tf_op jit(solution)/shard_map/ppermute | solution.py:274
  137.4 18.0 %collective-permute-start.24 = (bf16[2,128,512]{2,1,0:T(8,128)(2,1)S(1)}, bf16[2,128,512]{2,1,0:T(8,128)(2,1)S(1)}, u32[]{:S(2)}, u32[]{:S(2)}) collective-permute-start(bf16[2,128,512]{2,1,0:T(8,128)(2,1)S(1)} %get-tuple-element.75), channel_id=1, source_target_pairs={{0,4},{1,5},{2,6},{3,7},{4,0},{5,1},{6,2},{7,3},{8,12},{9,13},{10,... | collective-permute-start | bytes 786440 | tf_op jit(solution)/shard_map/ppermute | solution.py:274
  139.6 21.1 %collective-permute-start.25 = (bf16[2,128,512]{2,1,0:T(8,128)(2,1)S(1)}, bf16[2,128,512]{2,1,0:T(8,128)(2,1)S(1)}, u32[]{:S(2)}, u32[]{:S(2)}) collective-permute-start(bf16[2,128,512]{2,1,0:T(8,128)(2,1)S(1)} %get-tuple-element.76), channel_id=1, source_target_pairs={{0,5},{1,4},{2,7},{3,6},{4,1},{5,0},{6,3},{7,2},{8,13},{9,12},{10,... | collective-permute-start | bytes 786440 | tf_op jit(solution)/shard_map/ppermute | solution.py:274
  139.7 25.3 %collective-permute-start.26 = (bf16[2,128,512]{2,1,0:T(8,128)(2,1)S(1)}, bf16[2,128,512]{2,1,0:T(8,128)(2,1)S(1)}, u32[]{:S(2)}, u32[]{:S(2)}) collective-permute-start(bf16[2,128,512]{2,1,0:T(8,128)(2,1)S(1)} %get-tuple-element.77), channel_id=1, source_target_pairs={{0,6},{1,7},{2,4},{3,5},{4,2},{5,3},{6,0},{7,1},{8,14},{9,15},{10,... | collective-permute-start | bytes 786440 | tf_op jit(solution)/shard_map/ppermute | solution.py:274
  139.7 28.6 %collective-permute-start.27 = (bf16[2,128,512]{2,1,0:T(8,128)(2,1)S(1)}, bf16[2,128,512]{2,1,0:T(8,128)(2,1)S(1)}, u32[]{:S(2)}, u32[]{:S(2)}) collective-permute-start(bf16[2,128,512]{2,1,0:T(8,128)(2,1)S(1)} %get-tuple-element.78), channel_id=1, source_target_pairs={{0,7},{1,6},{2,5},{3,4},{4,3},{5,2},{6,1},{7,0},{8,15},{9,14},{10,... | collective-permute-start | bytes 786440 | tf_op jit(solution)/shard_map/ppermute | solution.py:274
  (9 other events, 104.0 us)
Sparse Core Ops, SparseCore 0:
  9.6 34.6 all-gather.1

commit v4 on v3

--- a/solution.py
+++ b/solution.py
@@ -17,6 +17,12 @@
 BF16 = jnp.bfloat16
 
 
+def partners(count):
+    half = count // 2
+    far_near = [d for low in reversed(range(half)) for d in (half + low, low)]
+    return [0] + [d for d in far_near if d]
+
+
 def make_tables(inner, chunks):
     slab = np.arange(SLABS)
     freq = np.arange(SLABS) + 0.5
@@ -24,7 +30,7 @@
     eye = np.eye(GROUP)
     first = np.concatenate([np.kron(np.cos(angle), eye), np.kron(-np.sin(angle), eye)], axis=0)
     blocks = first.reshape(first.shape[0], chunks, -1)
-    order = np.arange(chunks)
+    order = np.array(partners(chunks))
     first = np.stack([blocks[:, order ^ p].reshape(first.shape) for p in range(chunks)])
     last = first.transpose(0, 2, 1)
     within = np.arange(inner)
@@ -169,46 +175,52 @@
 
 def prepare_kernel(chunks, scale, me, inner_gate, signal, taps, gain, *outs):
     at_zero = (me[0] == 0) & (lax.broadcasted_iota(jnp.int32, taps.shape[1:], 1) == 0)
-    for d, out in enumerate(outs):
+    for d, out in zip(partners(chunks), outs):
         at = me[0] ^ d
         out[0] = elementwise(inner_gate[at], signal[at])
         out[1] = (taps[at] * scale + jnp.where(at_zero, gain[at], 0.0)).astype(BF16)
 
 
-def project_kernel(chunks, me, weight, gathered, gate, upstream, *outs):
+def project_kernel(chunks, members, me, *refs):
+    weights, blocks = refs[:members], refs[members : 2 * members]
+    gate, upstream, *outs = refs[2 * members :]
     step = pl.program_id(0)
-    rows = weight.shape[0] // 2
-    total = jnp.dot(weight[...], gathered[...], preferred_element_type=F32).astype(BF16)
+    rows = weights[0].shape[0] // 2
+    total = jnp.dot(weights[0][...], blocks[0][...], preferred_element_type=F32)
+    for weight, block in zip(weights[1:], blocks[1:]):
+        total += jnp.dot(weight[...], block[...], preferred_element_type=F32)
+    total = total.astype(BF16)
     upstream[...] = total.reshape(upstream.shape)
     low = elementwise(total[:rows], gate[0])
     high = elementwise(total[rows:], gate[1])
     swapped = (me[0] & 1) == 1
+    place = partners(chunks).index
     for pair in range(chunks // 2):
 
         @pl.when(step == pair)
         def _():
-            outs[2 * pair][...] = jnp.where(swapped, high, low)
-            outs[2 * pair + 1][...] = jnp.where(swapped, low, high)
+            outs[place(2 * pair)][...] = jnp.where(swapped, high, low)
+            outs[place(2 * pair + 1)][...] = jnp.where(swapped, low, high)
 
 
 def outer_kernel(chunks, me, upstream, *refs):
     chunk, out = refs[:chunks], refs[chunks]
-    for d in range(chunks):
+    for d, piece in zip(partners(chunks), chunk):
         at = me[0] ^ d
-        out[at] = elementwise(upstream[at], chunk[d][...])
+        out[at] = elementwise(upstream[at], piece[...])
 
 
 def finish_kernel(chunks, me, inner_gate, signal, *refs):
     chunk, (grad_inner, grad_signal, grad_taps) = refs[:chunks], refs[chunks:]
-    for d in range(chunks):
+    for d, piece in zip(partners(chunks), chunk):
         at = me[0] ^ d
-        back = chunk[d][0]
+        back = piece[0]
         grad_inner[at] = elementwise(back, signal[at])
         grad_signal[at] = elementwise(back, inner_gate[at])
-        grad_taps[at] = chunk[d][1].astype(F32)
-
-
-def rowwise_call(kernel, me, wholes, pieces, out_shapes, rows):
+        grad_taps[at] = piece[1].astype(F32)
+
+
+def rowwise_call(kernel, me, wholes, pieces, out_shapes, rows, limit=32):
     def spec(shape):
         lead = shape[:-2]
         return pl.BlockSpec(
@@ -226,29 +238,30 @@
             out_specs=[spec(x.shape) for x in out_shapes],
         ),
         out_shape=out_shapes,
-        compiler_params=pltpu.CompilerParams(vmem_limit_bytes=32 * 1024 * 1024),
+        compiler_params=pltpu.CompilerParams(vmem_limit_bytes=limit * 1024 * 1024),
         cost_estimate=pl.CostEstimate(flops=size, bytes_accessed=size, transcendentals=0),
     )(me, *wholes, *pieces)
 
 
-def project_call(me, weight, gathered, gate):
+def project_call(me, weight, blocks, gate):
     chunks, channels, local = gate.shape
-    depth = weight.shape[1]
+    members, depth = len(blocks), blocks[0].shape[0]
 
     def pair(i, me):
         return (me[0] >> 1) ^ i
 
     rows = 2 * channels
     return pl.pallas_call(
-        functools.partial(project_kernel, chunks),
+        functools.partial(project_kernel, chunks, members),
         grid_spec=pltpu.PrefetchScalarGridSpec(
             num_scalar_prefetch=1,
             grid=(chunks // 2,),
             in_specs=[
-                pl.BlockSpec((rows, depth), lambda i, me: (pair(i, me), 0)),
-                pl.BlockSpec((depth, local), lambda i, me: (0, 0)),
-                pl.BlockSpec((2, channels, local), lambda i, me: (pair(i, me), 0, 0)),
-            ],
+                pl.BlockSpec((rows, depth), lambda i, me, j=j: (pair(i, me), me[1] ^ j))
+                for j in range(members)
+            ]
+            + [pl.BlockSpec((depth, local), lambda i, me: (0, 0))] * members
+            + [pl.BlockSpec((2, channels, local), lambda i, me: (pair(i, me), 0, 0))],
             out_specs=[pl.BlockSpec((2, channels, local), lambda i, me: (pair(i, me), 0, 0))]
             + [pl.BlockSpec((channels, local), lambda i, me: (0, 0))] * chunks,
         ),
@@ -258,21 +271,33 @@
         cost_estimate=pl.CostEstimate(
             flops=2 * weight.size * local, bytes_accessed=2 * weight.size, transcendentals=0
         ),
-    )(me, weight, gathered, gate)
+    )(me, *[weight] * members, *blocks, gate)
+
+
+def gather_group(block):
+    count = lax.axis_size("group")
+    held, bit = {0: block}, count // 2
+    while bit:
+        for j in list(held):
+            pairs = [(g, g ^ bit) for g in range(count)]
+            held[j ^ bit] = lax.ppermute(held[j], "group", pairs)
+        bit //= 2
+    return [held[j] for j in range(count)]
 
 
 def exchange(parts):
     count = len(parts)
+    order = partners(count)
     if count > 8:
-        order = lax.axis_index("ctx") ^ jnp.arange(count)
-        sent = jnp.take(jnp.stack(parts), order, axis=0)
+        blocks = lax.axis_index("ctx") ^ jnp.arange(count)
+        where = np.argsort(order)
+        sent = jnp.take(jnp.take(jnp.stack(parts), where, axis=0), blocks, axis=0)
         came = lax.all_to_all(sent, "ctx", split_axis=0, concat_axis=0, tiled=True)
-        return list(jnp.take(came, order, axis=0))
-    came = [None] * count
-    came[0] = parts[0]
-    for d in reversed(range(1, count)):
-        came[d] = lax.ppermute(parts[d], "ctx", [(p, p ^ d) for p in range(count)])
-    return came
+        return list(jnp.take(jnp.take(came, blocks, axis=0), np.array(order), axis=0))
+    return [parts[0]] + [
+        lax.ppermute(part, "ctx", [(p, p ^ d) for p in range(count)])
+        for d, part in zip(order[1:], parts[1:])
+    ]
 
 
 def after(parts, other):
@@ -287,7 +312,7 @@
     seq_len = n_ctx * tok_local
     inner = seq_len // SLABS
     scale = 1.0 / math.sqrt(seq_len)
-    me = lax.axis_index("ctx").reshape(1)
+    me = jnp.stack([lax.axis_index("ctx"), lax.axis_index("group")])
 
     def split(array):
         return array.reshape(n_ctx, ch_slice, -1)
@@ -300,7 +325,7 @@
 
     tables = [jnp.asarray(table) for table in make_tables(inner, n_ctx)]
     tables = [table if table.ndim == 2 else table[me[0]] for table in tables]
-    gathered = lax.all_gather(cotangent, "group", axis=0, tiled=True)
+    gathered = gather_group(cotangent)
     pair = exchange(
         rowwise_call(
             functools.partial(prepare_kernel, n_ctx, scale),
@@ -309,13 +334,15 @@
             (),
             shapes((2,), BF16, n_ctx),
             32,
+            limit=60,
         )
     )
     upstream, *grad = project_call(me, out_weight, gathered, split(outer_gate))
-    grad_came = exchange(grad)
     response = conv_call(
         functools.partial(response_kernel, n_ctx, inner), me, (after(pair, grad[0]),), tables, (), inner, 3
     )
+    grad[-2:], _ = lax.optimization_barrier((grad[-2:], response[0]))
+    grad_came = exchange(grad)
     resp_came = exchange(response)
     backs = conv_call(
         functools.partial(backward_kernel, n_ctx, inner, scale),

time: 179 us -> 190 us (1.061)
  the two profiles are of different devices: /device:TPU:18 before, /device:TPU:0 now
where the time goes in v4:
time: 190 us; the launch traced here: 189 us
  waiting for transfers between devices  86.9 us (46%)
  starting transfers between devices  53.8 us (28%)
  Pallas kernels  43.5 us (23%)
  local copies, waits for them, and re-layouts  3.7 us (2%)
    ppermute x28, waiting for transfers between devices, exchange(): lax.ppermute(part, 'ctx', [(p, p ^ d) for p in range(count)])  63.5 us
    ppermute x28, starting transfers between devices, exchange(): lax.ppermute(part, 'ctx', [(p, p ^ d) for p in range(count)])  50.8 us
    pallas_call x2, Pallas kernels, conv_call(): pl.pallas_call(kernel, grid_spec=pltpu.PrefetchScalarGridSpec(num_scalar_...  24 us
    ppermute x3, waiting for transfers between devices, gather_group(): held[j ^ bit] = lax.ppermute(held[j], 'group', pairs)  23.4 us
    pallas_call x3, Pallas kernels, rowwise_call(): pl.pallas_call(kernel, grid_spec=pltpu.PrefetchScalarGridSpec(num_scalar_...  11 us
    pallas_call x1, Pallas kernels, project_call(): pl.pallas_call(functools.partial(project_kernel, chunks, members), grid_s...  8.49 us
  transfers between devices with their start and end apart: 31, of which 10 were waited for; matrix products, arithmetic and copies ran while one was open for 2% of the time, Pallas kernels for 21%

profile of v4, /device:TPU:0, one launch (start us, length us, event | category | flops | bytes accessed | tf_op | source)
XLA Modules:
  0.0 189.4 jit_solution(1785955211432462831)
XLA Ops:
  0.6 3.0 %collective-permute-start.1 = (bf16[1024,512]{1,0:T(8,128)(2,1)}, bf16[1024,512]{1,0:T(8,128)(2,1)S(1)}, u32[]{:S(2)}, u32[]{:S(2)}) collective-permute-start(bf16[1024,512]{1,0:T(8,128)(2,1)} %refs_4_.1), channel_id=1, source_target_pairs={{0,16},{8,24},{16,0},{24,8},{1,17},{9,25},{17,1},{25,9},{2,18},{10... | collective-permute-start | bytes 3145736 | tf_op jit(solution)/shard_map/ppermute | solution.py:283
  3.6 23.4 %collective-permute-done.1.refs_6_ = bf16[1024,512]{1,0:T(8,128)(2,1)S(1)} collective-permute-done((bf16[1024,512]{1,0:T(8,128)(2,1)}, bf16[1024,512]{1,0:T(8,128)(2,1)S(1)}, u32[]{:S(2)}, u32[]{:S(2)}) %collective-permute-start.1) | collective-permute-done | bytes 1048608 | tf_op jit(solution)/shard_map/ppermute | solution.py:283
  27.0 1.7 copy.17.gain
  29.3 5.1 %shard_map.157 = (bf16[2,128,512]{2,1,0:T(8,128)(2,1)}, bf16[2,128,512]{2,1,0:T(8,128)(2,1)}, bf16[2,128,512]{2,1,0:T(8,128)(2,1)}, bf16[2,128,512]{2,1,0:T(8,12...) custom-call(s32[2]{0:T(128)} %pad_add_fusion.me, ...), custom_call_target="tpu_custom_call" | custom-call | flops 6295552 | bytes 6295552 | tf_op jit(solution)/shard_map/pallas_call | solution.py:232
  34.4 4.9 %collective-permute-start.3 = (bf16[2,128,512]{2,1,0:T(8,128)(2,1)}, bf16[2,128,512]{2,1,0:T(8,128)(2,1)S(1)}, u32[]{:S(2)}, u32[]{:S(2)}) collective-permute-start(bf16[2,128,512]{2,1,0:T(8,128)(2,1)} %get-tuple-element.49), channel_id=1, source_target_pairs={{0,7},{1,6},{2,5},{3,4},{4,3},{5,2},{6,1},{7,0},{8,15},{9,14},{10,... | collective-permute-start | bytes 786440 | tf_op jit(solution)/shard_map/ppermute | solution.py:298
  42.1 4.7 %collective-permute-done.3.refs_1_ = bf16[2,128,512]{2,1,0:T(8,128)(2,1)S(1)} collective-permute-done((bf16[2,128,512]{2,1,0:T(8,128)(2,1)}, bf16[2,128,512]{2,1,0:T(8,128)(2,1)S(1)}, u32[]{:S(2)}, u32[]{:S(2)}) %collective-permute-start.3) | collective-permute-done | bytes 262176 | tf_op jit(solution)/shard_map/ppermute | solution.py:298
  46.7 8.6 %collective-permute-start.6 = (bf16[2,128,512]{2,1,0:T(8,128)(2,1)}, bf16[2,128,512]{2,1,0:T(8,128)(2,1)S(1)}, u32[]{:S(2)}, u32[]{:S(2)}) collective-permute-start(bf16[2,128,512]{2,1,0:T(8,128)(2,1)} %get-tuple-element.52), channel_id=1, source_target_pairs={{0,2},{1,3},{2,0},{3,1},{4,6},{5,7},{6,4},{7,5},{8,10},{9,11},{10,... | collective-permute-start | bytes 786440 | tf_op jit(solution)/shard_map/ppermute | solution.py:298
  55.4 1.8 collective-permute-start.7
  57.9 1.9 collective-permute-start.9
  59.8 8.5 %shard_map.156 = (bf16[8,128,512]{2,1,0:T(8,128)(2,1)S(1)}, bf16[128,512]{1,0:T(8,128)(2,1)S(1)}, bf16[128,512]{1,0:T(8,128)(2,1)S(1)}, bf16[128,512]{1,0:T(8,12...) custom-call(s32[2]{0:T(128)S(1)} %copy-done.4, ...), custom_call_target="tpu_custom_call" | custom-call | flops 4294967296 | bytes 8388608 | tf_op jit(solution)/shard_map/pallas_call | solution.py:254
  68.3 3.3 %collective-permute-start.10 = (bf16[128,512]{1,0:T(8,128)(2,1)S(1)}, bf16[128,512]{1,0:T(8,128)(2,1)S(1)}, u32[]{:S(2)}, u32[]{:S(2)}) collective-permute-start(bf16[128,512]{1,0:T(8,128)(2,1)S(1)} %get-tuple-element.58), channel_id=1, source_target_pairs={{0,7},{1,6},{2,5},{3,4},{4,3},{5,2},{6,1},{7,0},{8,15},{9,14},{10,... | collective-permute-start | bytes 393224 | tf_op jit(solution)/shard_map/ppermute | solution.py:298
  71.9 12.9 %collective-permute-done.7.refs_5_ = bf16[2,128,512]{2,1,0:T(8,128)(2,1)S(1)} collective-permute-done((bf16[2,128,512]{2,1,0:T(8,128)(2,1)}, bf16[2,128,512]{2,1,0:T(8,128)(2,1)S(1)}, u32[]{:S(2)}, u32[]{:S(2)}) %collective-permute-start.7) | collective-permute-done | bytes 262176 | tf_op jit(solution)/shard_map/ppermute | solution.py:298
  84.8 2.4 %collective-permute-start.12 = (bf16[128,512]{1,0:T(8,128)(2,1)S(1)}, bf16[128,512]{1,0:T(8,128)(2,1)S(1)}, u32[]{:S(2)}, u32[]{:S(2)}) collective-permute-start(bf16[128,512]{1,0:T(8,128)(2,1)S(1)} %get-tuple-element.60), channel_id=1, source_target_pairs={{0,6},{1,7},{2,4},{3,5},{4,2},{5,3},{6,0},{7,1},{8,14},{9,15},{10,... | collective-permute-start | bytes 393224 | tf_op jit(solution)/shard_map/ppermute | solution.py:298
  87.2 6.0 %collective-permute-done.9.refs_7_ = bf16[2,128,512]{2,1,0:T(8,128)(2,1)S(1)} collective-permute-done((bf16[2,128,512]{2,1,0:T(8,128)(2,1)}, bf16[2,128,512]{2,1,0:T(8,128)(2,1)S(1)}, u32[]{:S(2)}, u32[]{:S(2)}) %collective-permute-start.9) | collective-permute-done | bytes 262176 | tf_op jit(solution)/shard_map/ppermute | solution.py:298
  93.2 9.8 %shard_map.158 = (bf16[128,512]{1,0:T(8,128)(2,1)S(1)}, bf16[128,512]{1,0:T(8,128)(2,1)S(1)}, bf16[128,512]{1,0:T(8,128)(2,1)S(1)}, bf16[128,512]{1,0:T(8,128)(2...) custom-call(s32[2]{0:T(128)S(1)} %copy-done.4, ...), custom_call_target="tpu_custom_call" | custom-call | flops 3221225472 | bytes 4194304 | tf_op jit(solution)/shard_map/pallas_call | solution.py:156
  104.1 3.4 %collective-permute-start.16 = (bf16[128,512]{1,0:T(8,128)(2,1)S(1)}, bf16[128,512]{1,0:T(8,128)(2,1)S(1)}, u32[]{:S(2)}, u32[]{:S(2)}) collective-permute-start(bf16[128,512]{1,0:T(8,128)(2,1)S(1)} %get-tuple-element.66), channel_id=1, source_target_pairs={{0,4},{1,5},{2,6},{3,7},{4,0},{5,1},{6,2},{7,3},{8,12},{9,13},{10,... | collective-permute-start | bytes 393224 | tf_op jit(solution)/shard_map/ppermute | solution.py:298
  107.5 2.1 %collective-permute-start.17 = (bf16[128,512]{1,0:T(8,128)(2,1)S(1)}, bf16[128,512]{1,0:T(8,128)(2,1)S(1)}, u32[]{:S(2)}, u32[]{:S(2)}) collective-permute-start(bf16[128,512]{1,0:T(8,128)(2,1)S(1)} %get-tuple-element.69), channel_id=1, source_target_pairs={{0,7},{1,6},{2,5},{3,4},{4,3},{5,2},{6,1},{7,0},{8,15},{9,14},{10,... | collective-permute-start | bytes 393224 | tf_op jit(solution)/shard_map/ppermute | solution.py:298
  109.5 2.0 %collective-permute-start.19 = (bf16[128,512]{1,0:T(8,128)(2,1)S(1)}, bf16[128,512]{1,0:T(8,128)(2,1)S(1)}, u32[]{:S(2)}, u32[]{:S(2)}) collective-permute-start(bf16[128,512]{1,0:T(8,128)(2,1)S(1)} %get-tuple-element.71), channel_id=1, source_target_pairs={{0,6},{1,7},{2,4},{3,5},{4,2},{5,3},{6,0},{7,1},{8,14},{9,15},{10,... | collective-permute-start | bytes 393224 | tf_op jit(solution)/shard_map/ppermute | solution.py:298
  111.6 1.8 collective-permute-start.20
  113.3 5.5 %collective-permute-done.16.refs_15_ = bf16[128,512]{1,0:T(8,128)(2,1)S(1)} collective-permute-done((bf16[128,512]{1,0:T(8,128)(2,1)S(1)}, bf16[128,512]{1,0:T(8,128)(2,1)S(1)}, u32[]{:S(2)}, u32[]{:S(2)}) %collective-permute-start.16) | collective-permute-done | bytes 131104 | tf_op jit(solution)/shard_map/ppermute | solution.py:298
  118.8 14.2 %shard_map.159 = (bf16[2,128,512]{2,1,0:T(8,128)(2,1)S(1)}, bf16[2,128,512]{2,1,0:T(8,128)(2,1)S(1)}, bf16[2,128,512]{2,1,0:T(8,128)(2,1)S(1)}, bf16[2,128,512]{...) custom-call(s32[2]{0:T(128)S(1)} %copy-done.4, ...), custom_call_target="tpu_custom_call" | custom-call | flops 5368709120 | bytes 4194304 | tf_op jit(solution)/shard_map/pallas_call | solution.py:156
  134.4 3.4 %collective-permute-start.21 = (bf16[128,512]{1,0:T(8,128)(2,1)S(1)}, bf16[128,512]{1,0:T(8,128)(2,1)S(1)}, u32[]{:S(2)}, u32[]{:S(2)}) collective-permute-start(bf16[128,512]{1,0:T(8,128)(2,1)S(1)} %get-tuple-element.73), channel_id=1, source_target_pairs={{0,5},{1,4},{2,7},{3,6},{4,1},{5,0},{6,3},{7,2},{8,13},{9,12},{10,... | collective-permute-start | bytes 393224 | tf_op jit(solution)/shard_map/ppermute | solution.py:298
  137.8 2.1 %collective-permute-start.22 = (bf16[128,512]{1,0:T(8,128)(2,1)S(1)}, bf16[128,512]{1,0:T(8,128)(2,1)S(1)}, u32[]{:S(2)}, u32[]{:S(2)}) collective-permute-start(bf16[128,512]{1,0:T(8,128)(2,1)S(1)} %get-tuple-element.74), channel_id=1, source_target_pairs={{0,1},{1,0},{2,3},{3,2},{4,5},{5,4},{6,7},{7,6},{8,9},{9,8},{10,11... | collective-permute-start | bytes 393224 | tf_op jit(solution)/shard_map/ppermute | solution.py:298
  139.9 16.4 %collective-permute-done.21.refs_5_ = bf16[128,512]{1,0:T(8,128)(2,1)S(1)} collective-permute-done((bf16[128,512]{1,0:T(8,128)(2,1)S(1)}, bf16[128,512]{1,0:T(8,128)(2,1)S(1)}, u32[]{:S(2)}, u32[]{:S(2)}) %collective-permute-start.21) | collective-permute-done | bytes 131104 | tf_op jit(solution)/shard_map/ppermute | solution.py:298
  156.2 1.9 %collective-permute-start.26 = (bf16[2,128,512]{2,1,0:T(8,128)(2,1)S(1)}, bf16[2,128,512]{2,1,0:T(8,128)(2,1)S(1)}, u32[]{:S(2)}, u32[]{:S(2)}) collective-permute-start(bf16[2,128,512]{2,1,0:T(8,128)(2,1)S(1)} %get-tuple-element.78), channel_id=1, source_target_pairs={{0,6},{1,7},{2,4},{3,5},{4,2},{5,3},{6,0},{7,1},{8,14},{9,15},{10,... | collective-permute-start | bytes 786440 | tf_op jit(solution)/shard_map/ppermute | solution.py:298
  158.2 2.8 %collective-permute-start.27 = (bf16[2,128,512]{2,1,0:T(8,128)(2,1)S(1)}, bf16[2,128,512]{2,1,0:T(8,128)(2,1)S(1)}, u32[]{:S(2)}, u32[]{:S(2)}) collective-permute-start(bf16[2,128,512]{2,1,0:T(8,128)(2,1)S(1)} %get-tuple-element.79), channel_id=1, source_target_pairs={{0,2},{1,3},{2,0},{3,1},{4,6},{5,7},{6,4},{7,5},{8,10},{9,11},{10,... | collective-permute-start | bytes 786440 | tf_op jit(solution)/shard_map/ppermute | solution.py:298
  161.0 5.6 %collective-permute-done.23.refs_7_ = bf16[128,512]{1,0:T(8,128)(2,1)S(1)} collective-permute-done((bf16[128,512]{1,0:T(8,128)(2,1)S(1)}, bf16[128,512]{1,0:T(8,128)(2,1)S(1)}, u32[]{:S(2)}, u32[]{:S(2)}) %collective-permute-start.23) | collective-permute-done | bytes 131104 | tf_op jit(solution)/shard_map/ppermute | solution.py:298
  167.5 3.4 %collective-permute-start.30 = (bf16[2,128,512]{2,1,0:T(8,128)(2,1)S(1)}, bf16[2,128,512]{2,1,0:T(8,128)(2,1)S(1)}, u32[]{:S(2)}, u32[]{:S(2)}) collective-permute-start(bf16[2,128,512]{2,1,0:T(8,128)(2,1)S(1)} %get-tuple-element.82), channel_id=1, source_target_pairs={{0,4},{1,5},{2,6},{3,7},{4,0},{5,1},{6,2},{7,3},{8,12},{9,13},{10,... | collective-permute-start | bytes 786440 | tf_op jit(solution)/shard_map/ppermute | solution.py:298
  170.9 2.3 %shard_map.160 = bf16[8,128,512]{2,1,0:T(8,128)(2,1)} custom-call(s32[2]{0:T(128)S(1)} %copy-done.4, bf16[8,128,512]{2,1,0:T(8,128)(2,1)S(1)} %get-tuple-element.45.upstream, bf16[128,512]{1,0:T(8,128)(2,1)S(1)} %get-tuple-element.68.refs_0_, bf16[128,512]{1,0:T(8,128)(2,1)S(1)} %collective-permute-done.17.refs_1_, ...), custom_call_target="tpu_custom_call" | custom-call | flops 3145728 | bytes 3145728 | tf_op jit(solution)/shard_map/pallas_call | solution.py:232
  173.2 9.8 %collective-permute-done.28.refs_5_ = bf16[2,128,512]{2,1,0:T(8,128)(2,1)S(1)} collective-permute-done((bf16[2,128,512]{2,1,0:T(8,128)(2,1)S(1)}, bf16[2,128,512]{2,1,0:T(8,128)(2,1)S(1)}, u32[]{:S(2)}, u32[]{:S(2)}) %collective-permute-start.28) | collective-permute-done | bytes 262176 | tf_op jit(solution)/shard_map/ppermute | solution.py:298
  183.0 2.7 %collective-permute-done.30.refs_7_ = bf16[2,128,512]{2,1,0:T(8,128)(2,1)S(1)} collective-permute-done((bf16[2,128,512]{2,1,0:T(8,128)(2,1)S(1)}, bf16[2,128,512]{2,1,0:T(8,128)(2,1)S(1)}, u32[]{:S(2)}, u32[]{:S(2)}) %collective-permute-start.30) | collective-permute-done | bytes 262176 | tf_op jit(solution)/shard_map/ppermute | solution.py:298
  185.8 3.6 %shard_map.161 = (bf16[8,128,512]{2,1,0:T(8,128)(2,1)}, bf16[8,128,512]{2,1,0:T(8,128)(2,1)}, f32[8,128,512]{2,1,0:T(8,128)}) custom-call(s32[2]{0:T(128)S(1)} %copy-done.4, bf16[8,128,512]{2,1,0:T(8,128)(2,1)S(1)} %bitcast.16, bf16[8,128,512]{2,1,0:T(8,128)(2,1)S(1)} %bitcast.18, bf16[2,128,512]{2,1,0:T(8,128)(2,1)S(1)} %get-tuple-element.67.refs_0_, ...), custom_call_target="tpu_custom_call" | custom-call | flops 8388608 | bytes 8388608 | tf_op jit(solution)/shard_map/pallas_call | solution.py:232
  (60 shorter events, 7.7 us)
Async XLA Ops:
  0.6 26.4 %collective-permute-start.1 = (bf16[1024,512]{1,0:T(8,128)(2,1)}, bf16[1024,512]{1,0:T(8,128)(2,1)S(1)}, u32[]{:S(2)}, u32[]{:S(2)}) collective-permute-start(bf16[1024,512]{1,0:T(8,128)(2,1)} %refs_4_.1), channel_id=1, source_target_pairs={{0,16},{8,24},{16,0},{24,8},{1,17},{9,25},{17,1},{25,9},{2,18},{10... | collective-permute-start | bytes 3145736 | tf_op jit(solution)/shard_map/ppermute | solution.py:283
  3.6 53.6 %collective-permute-start = (bf16[1024,512]{1,0:T(8,128)(2,1)}, bf16[1024,512]{1,0:T(8,128)(2,1)}, u32[]{:S(2)}, u32[]{:S(2)}) collective-permute-start(bf16[1024,512]{1,0:T(8,128)(2,1)} %refs_4_.1), channel_id=1, source_target_pairs={{0,8},{8,0},{16,24},{24,16},{1,9},{9,1},{17,25},{25,17},{2,10},{10... | collective-permute-start | bytes 3145736 | tf_op jit(solution)/shard_map/ppermute | solution.py:283
  27.0 30.9 %collective-permute-start.2 = (bf16[1024,512]{1,0:T(8,128)(2,1)S(1)}, bf16[1024,512]{1,0:T(8,128)(2,1)}, u32[]{:S(2)}, u32[]{:S(2)}) collective-permute-start(bf16[1024,512]{1,0:T(8,128)(2,1)S(1)} %collective-permute-done.1.refs_6_), channel_id=1, source_target_pairs={{0,8},{8,0},{16,24},{24,16},{1,9},{9,1},{17,25},{25,17},{2,10},{10... | collective-permute-start | bytes 3145736 | tf_op jit(solution)/shard_map/ppermute | solution.py:283
  34.4 12.3 %collective-permute-start.3 = (bf16[2,128,512]{2,1,0:T(8,128)(2,1)}, bf16[2,128,512]{2,1,0:T(8,128)(2,1)S(1)}, u32[]{:S(2)}, u32[]{:S(2)}) collective-permute-start(bf16[2,128,512]{2,1,0:T(8,128)(2,1)} %get-tuple-element.49), channel_id=1, source_target_pairs={{0,7},{1,6},{2,5},{3,4},{4,3},{5,2},{6,1},{7,0},{8,15},{9,14},{10,... | collective-permute-start | bytes 786440 | tf_op jit(solution)/shard_map/ppermute | solution.py:298
  39.3 16.1 %collective-permute-start.4 = (bf16[2,128,512]{2,1,0:T(8,128)(2,1)}, bf16[2,128,512]{2,1,0:T(8,128)(2,1)}, u32[]{:S(2)}, u32[]{:S(2)}) collective-permute-start(bf16[2,128,512]{2,1,0:T(8,128)(2,1)} %get-tuple-element.50), channel_id=1, source_target_pairs={{0,3},{1,2},{2,1},{3,0},{4,7},{5,6},{6,5},{7,4},{8,11},{9,10},{10,... | collective-permute-start | bytes 786440 | tf_op jit(solution)/shard_map/ppermute | solution.py:298
  39.3 29.0 %collective-permute-start.5 = (bf16[2,128,512]{2,1,0:T(8,128)(2,1)}, bf16[2,128,512]{2,1,0:T(8,128)(2,1)}, u32[]{:S(2)}, u32[]{:S(2)}) collective-permute-start(bf16[2,128,512]{2,1,0:T(8,128)(2,1)} %get-tuple-element.51), channel_id=1, source_target_pairs={{0,6},{1,7},{2,4},{3,5},{4,2},{5,3},{6,0},{7,1},{8,14},{9,15},{10,... | collective-permute-start | bytes 786440 | tf_op jit(solution)/shard_map/ppermute | solution.py:298
  46.7 24.9 %collective-permute-start.6 = (bf16[2,128,512]{2,1,0:T(8,128)(2,1)}, bf16[2,128,512]{2,1,0:T(8,128)(2,1)S(1)}, u32[]{:S(2)}, u32[]{:S(2)}) collective-permute-start(bf16[2,128,512]{2,1,0:T(8,128)(2,1)} %get-tuple-element.52), channel_id=1, source_target_pairs={{0,2},{1,3},{2,0},{3,1},{4,6},{5,7},{6,4},{7,5},{8,10},{9,11},{10,... | collective-permute-start | bytes 786440 | tf_op jit(solution)/shard_map/ppermute | solution.py:298
  55.4 29.4 %collective-permute-start.7 = (bf16[2,128,512]{2,1,0:T(8,128)(2,1)}, bf16[2,128,512]{2,1,0:T(8,128)(2,1)S(1)}, u32[]{:S(2)}, u32[]{:S(2)}) collective-permute-start(bf16[2,128,512]{2,1,0:T(8,128)(2,1)} %get-tuple-element.53), channel_id=1, source_target_pairs={{0,5},{1,4},{2,7},{3,6},{4,1},{5,0},{6,3},{7,2},{8,13},{9,12},{10,... | collective-permute-start | bytes 786440 | tf_op jit(solution)/shard_map/ppermute | solution.py:298
  57.2 30.0 %collective-permute-start.8 = (bf16[2,128,512]{2,1,0:T(8,128)(2,1)}, bf16[2,128,512]{2,1,0:T(8,128)(2,1)S(1)}, u32[]{:S(2)}, u32[]{:S(2)}) collective-permute-start(bf16[2,128,512]{2,1,0:T(8,128)(2,1)} %get-tuple-element.54), channel_id=1, source_target_pairs={{0,1},{1,0},{2,3},{3,2},{4,5},{5,4},{6,7},{7,6},{8,9},{9,8},{10,11... | collective-permute-start | bytes 786440 | tf_op jit(solution)/shard_map/ppermute | solution.py:298
  57.9 35.3 %collective-permute-start.9 = (bf16[2,128,512]{2,1,0:T(8,128)(2,1)}, bf16[2,128,512]{2,1,0:T(8,128)(2,1)S(1)}, u32[]{:S(2)}, u32[]{:S(2)}) collective-permute-start(bf16[2,128,512]{2,1,0:T(8,128)(2,1)} %get-tuple-element.55), channel_id=1, source_target_pairs={{0,4},{1,5},{2,6},{3,7},{4,0},{5,1},{6,2},{7,3},{8,12},{9,13},{10,... | collective-permute-start | bytes 786440 | tf_op jit(solution)/shard_map/ppermute | solution.py:298
  68.3 34.7 %collective-permute-start.10 = (bf16[128,512]{1,0:T(8,128)(2,1)S(1)}, bf16[128,512]{1,0:T(8,128)(2,1)S(1)}, u32[]{:S(2)}, u32[]{:S(2)}) collective-permute-start(bf16[128,512]{1,0:T(8,128)(2,1)S(1)} %get-tuple-element.58), channel_id=1, source_target_pairs={{0,7},{1,6},{2,5},{3,4},{4,3},{5,2},{6,1},{7,0},{8,15},{9,14},{10,... | collective-permute-start | bytes 393224 | tf_op jit(solution)/shard_map/ppermute | solution.py:298
  71.7 32.4 %collective-permute-start.11 = (bf16[128,512]{1,0:T(8,128)(2,1)S(1)}, bf16[128,512]{1,0:T(8,128)(2,1)S(1)}, u32[]{:S(2)}, u32[]{:S(2)}) collective-permute-start(bf16[128,512]{1,0:T(8,128)(2,1)S(1)} %get-tuple-element.59), channel_id=1, source_target_pairs={{0,3},{1,2},{2,1},{3,0},{4,7},{5,6},{6,5},{7,4},{8,11},{9,10},{10,... | collective-permute-start | bytes 393224 | tf_op jit(solution)/shard_map/ppermute | solution.py:298
  84.8 22.7 %collective-permute-start.12 = (bf16[128,512]{1,0:T(8,128)(2,1)S(1)}, bf16[128,512]{1,0:T(8,128)(2,1)S(1)}, u32[]{:S(2)}, u32[]{:S(2)}) collective-permute-start(bf16[128,512]{1,0:T(8,128)(2,1)S(1)} %get-tuple-element.60), channel_id=1, source_target_pairs={{0,6},{1,7},{2,4},{3,5},{4,2},{5,3},{6,0},{7,1},{8,14},{9,15},{10,... | collective-permute-start | bytes 393224 | tf_op jit(solution)/shard_map/ppermute | solution.py:298
  87.2 22.4 %collective-permute-start.13 = (bf16[128,512]{1,0:T(8,128)(2,1)S(1)}, bf16[128,512]{1,0:T(8,128)(2,1)S(1)}, u32[]{:S(2)}, u32[]{:S(2)}) collective-permute-start(bf16[128,512]{1,0:T(8,128)(2,1)S(1)} %get-tuple-element.61), channel_id=1, source_target_pairs={{0,2},{1,3},{2,0},{3,1},{4,6},{5,7},{6,4},{7,5},{8,10},{9,11},{10,... | collective-permute-start | bytes 393224 | tf_op jit(solution)/shard_map/ppermute | solution.py:298
  93.2 16.4 %collective-permute-start.14 = (bf16[128,512]{1,0:T(8,128)(2,1)S(1)}, bf16[128,512]{1,0:T(8,128)(2,1)S(1)}, u32[]{:S(2)}, u32[]{:S(2)}) collective-permute-start(bf16[128,512]{1,0:T(8,128)(2,1)S(1)} %get-tuple-element.62), channel_id=1, source_target_pairs={{0,5},{1,4},{2,7},{3,6},{4,1},{5,0},{6,3},{7,2},{8,13},{9,12},{10,... | collective-permute-start | bytes 393224 | tf_op jit(solution)/shard_map/ppermute | solution.py:298
  103.0 8.5 %collective-permute-start.15 = (bf16[128,512]{1,0:T(8,128)(2,1)S(1)}, bf16[128,512]{1,0:T(8,128)(2,1)S(1)}, u32[]{:S(2)}, u32[]{:S(2)}) collective-permute-start(bf16[128,512]{1,0:T(8,128)(2,1)S(1)} %get-tuple-element.65), channel_id=1, source_target_pairs={{0,1},{1,0},{2,3},{3,2},{4,5},{5,4},{6,7},{7,6},{8,9},{9,8},{10,11... | collective-permute-start | bytes 393224 | tf_op jit(solution)/shard_map/ppermute | solution.py:298
  104.1 14.7 %collective-permute-start.16 = (bf16[128,512]{1,0:T(8,128)(2,1)S(1)}, bf16[128,512]{1,0:T(8,128)(2,1)S(1)}, u32[]{:S(2)}, u32[]{:S(2)}) collective-permute-start(bf16[128,512]{1,0:T(8,128)(2,1)S(1)} %get-tuple-element.66), channel_id=1, source_target_pairs={{0,4},{1,5},{2,6},{3,7},{4,0},{5,1},{6,2},{7,3},{8,12},{9,13},{10,... | collective-permute-start | bytes 393224 | tf_op jit(solution)/shard_map/ppermute | solution.py:298
  107.5 26.9 %collective-permute-start.17 = (bf16[128,512]{1,0:T(8,128)(2,1)S(1)}, bf16[128,512]{1,0:T(8,128)(2,1)S(1)}, u32[]{:S(2)}, u32[]{:S(2)}) collective-permute-start(bf16[128,512]{1,0:T(8,128)(2,1)S(1)} %get-tuple-element.69), channel_id=1, source_target_pairs={{0,7},{1,6},{2,5},{3,4},{4,3},{5,2},{6,1},{7,0},{8,15},{9,14},{10,... | collective-permute-start | bytes 393224 | tf_op jit(solution)/shard_map/ppermute | solution.py:298
  109.5 24.8 %collective-permute-start.18 = (bf16[128,512]{1,0:T(8,128)(2,1)S(1)}, bf16[128,512]{1,0:T(8,128)(2,1)S(1)}, u32[]{:S(2)}, u32[]{:S(2)}) collective-permute-start(bf16[128,512]{1,0:T(8,128)(2,1)S(1)} %get-tuple-element.70), channel_id=1, source_target_pairs={{0,3},{1,2},{2,1},{3,0},{4,7},{5,6},{6,5},{7,4},{8,11},{9,10},{10,... | collective-permute-start | bytes 393224 | tf_op jit(solution)/shard_map/ppermute | solution.py:298
  109.5 28.2 %collective-permute-start.19 = (bf16[128,512]{1,0:T(8,128)(2,1)S(1)}, bf16[128,512]{1,0:T(8,128)(2,1)S(1)}, u32[]{:S(2)}, u32[]{:S(2)}) collective-permute-start(bf16[128,512]{1,0:T(8,128)(2,1)S(1)} %get-tuple-element.71), channel_id=1, source_target_pairs={{0,6},{1,7},{2,4},{3,5},{4,2},{5,3},{6,0},{7,1},{8,14},{9,15},{10,... | collective-permute-start | bytes 393224 | tf_op jit(solution)/shard_map/ppermute | solution.py:298
  111.6 28.3 %collective-permute-start.20 = (bf16[128,512]{1,0:T(8,128)(2,1)S(1)}, bf16[128,512]{1,0:T(8,128)(2,1)S(1)}, u32[]{:S(2)}, u32[]{:S(2)}) collective-permute-start(bf16[128,512]{1,0:T(8,128)(2,1)S(1)} %get-tuple-element.72), channel_id=1, source_target_pairs={{0,2},{1,3},{2,0},{3,1},{4,6},{5,7},{6,4},{7,5},{8,10},{9,11},{10,... | collective-permute-start | bytes 393224 | tf_op jit(solution)/shard_map/ppermute | solution.py:298
  133.0 52.7 %copy-start = (bf16[1024,512]{1,0:T(8,128)(2,1)S(1)}, bf16[1024,512]{1,0:T(8,128)(2,1)}, u32[]{:S(2)}) copy-start(bf16[1024,512]{1,0:T(8,128)(2,1)} %param.14) | copy-start | bytes 3145732
  133.1 33.5 %collective-permute-start.24 = (bf16[2,128,512]{2,1,0:T(8,128)(2,1)S(1)}, bf16[2,128,512]{2,1,0:T(8,128)(2,1)S(1)}, u32[]{:S(2)}, u32[]{:S(2)}) collective-permute-start(bf16[2,128,512]{2,1,0:T(8,128)(2,1)S(1)} %get-tuple-element.76), channel_id=1, source_target_pairs={{0,7},{1,6},{2,5},{3,4},{4,3},{5,2},{6,1},{7,0},{8,15},{9,14},{10,... | collective-permute-start | bytes 786440 | tf_op jit(solution)/shard_map/ppermute | solution.py:298
  134.4 33.1 %collective-permute-start.25 = (bf16[2,128,512]{2,1,0:T(8,128)(2,1)S(1)}, bf16[2,128,512]{2,1,0:T(8,128)(2,1)S(1)}, u32[]{:S(2)}, u32[]{:S(2)}) collective-permute-start(bf16[2,128,512]{2,1,0:T(8,128)(2,1)S(1)} %get-tuple-element.77), channel_id=1, source_target_pairs={{0,3},{1,2},{2,1},{3,0},{4,7},{5,6},{6,5},{7,4},{8,11},{9,10},{10,... | collective-permute-start | bytes 786440 | tf_op jit(solution)/shard_map/ppermute | solution.py:298
  134.4 21.9 %collective-permute-start.21 = (bf16[128,512]{1,0:T(8,128)(2,1)S(1)}, bf16[128,512]{1,0:T(8,128)(2,1)S(1)}, u32[]{:S(2)}, u32[]{:S(2)}) collective-permute-start(bf16[128,512]{1,0:T(8,128)(2,1)S(1)} %get-tuple-element.73), channel_id=1, source_target_pairs={{0,5},{1,4},{2,7},{3,6},{4,1},{5,0},{6,3},{7,2},{8,13},{9,12},{10,... | collective-permute-start | bytes 393224 | tf_op jit(solution)/shard_map/ppermute | solution.py:298
  137.8 20.4 %collective-permute-start.22 = (bf16[128,512]{1,0:T(8,128)(2,1)S(1)}, bf16[128,512]{1,0:T(8,128)(2,1)S(1)}, u32[]{:S(2)}, u32[]{:S(2)}) collective-permute-start(bf16[128,512]{1,0:T(8,128)(2,1)S(1)} %get-tuple-element.74), channel_id=1, source_target_pairs={{0,1},{1,0},{2,3},{3,2},{4,5},{5,4},{6,7},{7,6},{8,9},{9,8},{10,11... | collective-permute-start | bytes 393224 | tf_op jit(solution)/shard_map/ppermute | solution.py:298
  139.9 26.7 %collective-permute-start.23 = (bf16[128,512]{1,0:T(8,128)(2,1)S(1)}, bf16[128,512]{1,0:T(8,128)(2,1)S(1)}, u32[]{:S(2)}, u32[]{:S(2)}) collective-permute-start(bf16[128,512]{1,0:T(8,128)(2,1)S(1)} %get-tuple-element.75), channel_id=1, source_target_pairs={{0,4},{1,5},{2,6},{3,7},{4,0},{5,1},{6,2},{7,3},{8,12},{9,13},{10,... | collective-permute-start | bytes 393224 | tf_op jit(solution)/shard_map/ppermute | solution.py:298
  156.2 17.0 %collective-permute-start.26 = (bf16[2,128,512]{2,1,0:T(8,128)(2,1)S(1)}, bf16[2,128,512]{2,1,0:T(8,128)(2,1)S(1)}, u32[]{:S(2)}, u32[]{:S(2)}) collective-permute-start(bf16[2,128,512]{2,1,0:T(8,128)(2,1)S(1)} %get-tuple-element.78), channel_id=1, source_target_pairs={{0,6},{1,7},{2,4},{3,5},{4,2},{5,3},{6,0},{7,1},{8,14},{9,15},{10,... | collective-permute-start | bytes 786440 | tf_op jit(solution)/shard_map/ppermute | solution.py:298
  158.2 15.1 %collective-permute-start.27 = (bf16[2,128,512]{2,1,0:T(8,128)(2,1)S(1)}, bf16[2,128,512]{2,1,0:T(8,128)(2,1)S(1)}, u32[]{:S(2)}, u32[]{:S(2)}) collective-permute-start(bf16[2,128,512]{2,1,0:T(8,128)(2,1)S(1)} %get-tuple-element.79), channel_id=1, source_target_pairs={{0,2},{1,3},{2,0},{3,1},{4,6},{5,7},{6,4},{7,5},{8,10},{9,11},{10,... | collective-permute-start | bytes 786440 | tf_op jit(solution)/shard_map/ppermute | solution.py:298
  166.5 16.5 %collective-permute-start.28 = (bf16[2,128,512]{2,1,0:T(8,128)(2,1)S(1)}, bf16[2,128,512]{2,1,0:T(8,128)(2,1)S(1)}, u32[]{:S(2)}, u32[]{:S(2)}) collective-permute-start(bf16[2,128,512]{2,1,0:T(8,128)(2,1)S(1)} %get-tuple-element.80), channel_id=1, source_target_pairs={{0,5},{1,4},{2,7},{3,6},{4,1},{5,0},{6,3},{7,2},{8,13},{9,12},{10,... | collective-permute-start | bytes 786440 | tf_op jit(solution)/shard_map/ppermute | solution.py:298
  166.6 16.5 %collective-permute-start.29 = (bf16[2,128,512]{2,1,0:T(8,128)(2,1)S(1)}, bf16[2,128,512]{2,1,0:T(8,128)(2,1)S(1)}, u32[]{:S(2)}, u32[]{:S(2)}) collective-permute-start(bf16[2,128,512]{2,1,0:T(8,128)(2,1)S(1)} %get-tuple-element.81), channel_id=1, source_target_pairs={{0,1},{1,0},{2,3},{3,2},{4,5},{5,4},{6,7},{7,6},{8,9},{9,8},{10,11... | collective-permute-start | bytes 786440 | tf_op jit(solution)/shard_map/ppermute | solution.py:298
  167.5 18.2 %collective-permute-start.30 = (bf16[2,128,512]{2,1,0:T(8,128)(2,1)S(1)}, bf16[2,128,512]{2,1,0:T(8,128)(2,1)S(1)}, u32[]{:S(2)}, u32[]{:S(2)}) collective-permute-start(bf16[2,128,512]{2,1,0:T(8,128)(2,1)S(1)} %get-tuple-element.82), channel_id=1, source_target_pairs={{0,4},{1,5},{2,6},{3,7},{4,0},{5,1},{6,2},{7,3},{8,12},{9,13},{10,... | collective-permute-start | bytes 786440 | tf_op jit(solution)/shard_map/ppermute | solution.py:298
  (9 other events, 311.1 us)

commit v5 on v4

--- a/solution.py
+++ b/solution.py
@@ -274,12 +274,20 @@
     )(me, *[weight] * members, *blocks, gate)
 
 
-def gather_group(block):
+def gather_start(block):
     count = lax.axis_size("group")
-    held, bit = {0: block}, count // 2
+    return lax.ppermute(block, "group", [(g, g ^ (count // 2)) for g in range(count)])
+
+
+def gather_rest(block, far, other):
+    count = lax.axis_size("group")
+    bit = count // 2
+    (block, far), _ = lax.optimization_barrier(((block, far), other))
+    held = {0: block, bit: far}
+    bit //= 2
     while bit:
+        pairs = [(g, g ^ bit) for g in range(count)]
         for j in list(held):
-            pairs = [(g, g ^ bit) for g in range(count)]
             held[j ^ bit] = lax.ppermute(held[j], "group", pairs)
         bit //= 2
     return [held[j] for j in range(count)]
@@ -325,7 +333,7 @@
 
     tables = [jnp.asarray(table) for table in make_tables(inner, n_ctx)]
     tables = [table if table.ndim == 2 else table[me[0]] for table in tables]
-    gathered = gather_group(cotangent)
+    far = gather_start(cotangent)
     pair = exchange(
         rowwise_call(
             functools.partial(prepare_kernel, n_ctx, scale),
@@ -337,6 +345,7 @@
             limit=60,
         )
     )
+    gathered = gather_rest(cotangent, far, pair[2])
     upstream, *grad = project_call(me, out_weight, gathered, split(outer_gate))
     response = conv_call(
         functools.partial(response_kernel, n_ctx, inner), me, (after(pair, grad[0]),), tables, (), inner, 3

time: 190 us -> 178 us (0.937)
  waiting for transfers between devices: 86.9 us -> 68.4 us
  starting transfers between devices: 53.8 us -> 60.8 us
    ppermute x3, waiting for transfers between devices: 23.4 us -> 6.97 us  [the longest x1 6.96 us: gather_start(): lax.ppermute(block, 'group', [(g, g ^ count // 2) for g in range(count)])]
    ppermute x28, starting transfers between devices: 50.8 us -> 57.3 us  [exchange(): lax.ppermute(part, 'ctx', [(p, p ^ d) for p in range(count)])]
    ppermute x28, waiting for transfers between devices: 63.5 us -> 61.5 us  [exchange(): lax.ppermute(part, 'ctx', [(p, p ^ d) for p in range(count)])]
  transfers between devices with their start and end apart: 31 -> 31, of which waited for: 10 -> 11; matrix products, arithmetic and copies ran while one was open for 2% -> 2% of each run, Pallas kernels for 21% -> 22%
where the time goes in v5:
time: 178 us
  waiting for transfers between devices  68.4 us (38%)
  starting transfers between devices  60.8 us (34%)
  Pallas kernels  43.6 us (24%)
  local copies, waits for them, and re-layouts  3.7 us (2%)
    ppermute x28, waiting for transfers between devices, exchange(): lax.ppermute(part, 'ctx', [(p, p ^ d) for p in range(count)])  61.5 us
    ppermute x28, starting transfers between devices, exchange(): lax.ppermute(part, 'ctx', [(p, p ^ d) for p in range(count)])  57.3 us
    pallas_call x2, Pallas kernels, conv_call(): pl.pallas_call(kernel, grid_spec=pltpu.PrefetchScalarGridSpec(num_scalar_...  24 us
    pallas_call x3, Pallas kernels, rowwise_call(): pl.pallas_call(kernel, grid_spec=pltpu.PrefetchScalarGridSpec(num_scalar_...  11 us
    pallas_call x1, Pallas kernels, project_call(): pl.pallas_call(functools.partial(project_kernel, chunks, members), grid_s...  8.57 us
    ppermute x1, waiting for transfers between devices, gather_start(): lax.ppermute(block, 'group', [(g, g ^ count // 2) for g in range(count)])  6.96 us
  transfers between devices with their start and end apart: 31, of which 11 were waited for; matrix products, arithmetic and copies ran while one was open for 2% of the time, Pallas kernels for 22%

profile of v5, /device:TPU:0, one launch (start us, length us, event | category | flops | bytes accessed | tf_op | source)
XLA Modules:
  0.0 178.0 jit_solution(18422708500330182691)
XLA Ops:
  0.6 3.0 %collective-permute-start = (bf16[1024,512]{1,0:T(8,128)(2,1)}, bf16[1024,512]{1,0:T(8,128)(2,1)S(1)}, u32[]{:S(2)}, u32[]{:S(2)}) collective-permute-start(bf16[1024,512]{1,0:T(8,128)(2,1)} %refs_4_), channel_id=1, source_target_pairs={{0,16},{8,24},{16,0},{24,8},{1,17},{9,25},{17,1},{25,9},{2,18},{10... | collective-permute-start | bytes 3145736 | tf_op jit(solution)/shard_map/ppermute | solution.py:279
  3.6 1.7 copy.17.gain
  6.0 5.1 %shard_map.156 = (bf16[2,128,512]{2,1,0:T(8,128)(2,1)}, bf16[2,128,512]{2,1,0:T(8,128)(2,1)}, bf16[2,128,512]{2,1,0:T(8,128)(2,1)}, bf16[2,128,512]{2,1,0:T(8,12...) custom-call(s32[2]{0:T(128)} %pad_add_fusion.me, ...), custom_call_target="tpu_custom_call" | custom-call | flops 6295552 | bytes 6295552 | tf_op jit(solution)/shard_map/pallas_call | solution.py:232
  11.1 2.6 %collective-permute-start.1 = (bf16[2,128,512]{2,1,0:T(8,128)(2,1)}, bf16[2,128,512]{2,1,0:T(8,128)(2,1)S(1)}, u32[]{:S(2)}, u32[]{:S(2)}) collective-permute-start(bf16[2,128,512]{2,1,0:T(8,128)(2,1)} %get-tuple-element.47), channel_id=1, source_target_pairs={{0,3},{1,2},{2,1},{3,0},{4,7},{5,6},{6,5},{7,4},{8,11},{9,10},{10,... | collective-permute-start | bytes 786440 | tf_op jit(solution)/shard_map/ppermute | solution.py:306
  13.7 6.3 %collective-permute-done.1.refs_2_ = bf16[2,128,512]{2,1,0:T(8,128)(2,1)S(1)} collective-permute-done((bf16[2,128,512]{2,1,0:T(8,128)(2,1)}, bf16[2,128,512]{2,1,0:T(8,128)(2,1)S(1)}, u32[]{:S(2)}, u32[]{:S(2)}) %collective-permute-start.1) | collective-permute-done | bytes 262176 | tf_op jit(solution)/shard_map/ppermute | solution.py:306
  20.0 7.0 %collective-permute-done.refs_6_ = bf16[1024,512]{1,0:T(8,128)(2,1)S(1)} collective-permute-done((bf16[1024,512]{1,0:T(8,128)(2,1)}, bf16[1024,512]{1,0:T(8,128)(2,1)S(1)}, u32[]{:S(2)}, u32[]{:S(2)}) %collective-permute-start) | collective-permute-done | bytes 1048608 | tf_op jit(solution)/shard_map/ppermute | solution.py:279
  27.5 4.8 %collective-permute-start.4 = (bf16[2,128,512]{2,1,0:T(8,128)(2,1)}, bf16[2,128,512]{2,1,0:T(8,128)(2,1)}, u32[]{:S(2)}, u32[]{:S(2)}) collective-permute-start(bf16[2,128,512]{2,1,0:T(8,128)(2,1)} %get-tuple-element.54), channel_id=1, source_target_pairs={{0,7},{1,6},{2,5},{3,4},{4,3},{5,2},{6,1},{7,0},{8,15},{9,14},{10,... | collective-permute-start | bytes 786440 | tf_op jit(solution)/shard_map/ppermute | solution.py:306
  34.5 5.5 %collective-permute-done.4.refs_1_ = bf16[2,128,512]{2,1,0:T(8,128)(2,1)} collective-permute-done((bf16[2,128,512]{2,1,0:T(8,128)(2,1)}, bf16[2,128,512]{2,1,0:T(8,128)(2,1)}, u32[]{:S(2)}, u32[]{:S(2)}) %collective-permute-start.4) | collective-permute-done | bytes 262176 | tf_op jit(solution)/shard_map/ppermute | solution.py:306
  40.0 13.0 %collective-permute-start.7 = (bf16[2,128,512]{2,1,0:T(8,128)(2,1)}, bf16[2,128,512]{2,1,0:T(8,128)(2,1)S(1)}, u32[]{:S(2)}, u32[]{:S(2)}) collective-permute-start(bf16[2,128,512]{2,1,0:T(8,128)(2,1)} %get-tuple-element.57), channel_id=1, source_target_pairs={{0,5},{1,4},{2,7},{3,6},{4,1},{5,0},{6,3},{7,2},{8,13},{9,12},{10,... | collective-permute-start | bytes 786440 | tf_op jit(solution)/shard_map/ppermute | solution.py:306
  53.6 8.6 %shard_map.157 = (bf16[8,128,512]{2,1,0:T(8,128)(2,1)S(1)}, bf16[128,512]{1,0:T(8,128)(2,1)S(1)}, bf16[128,512]{1,0:T(8,128)(2,1)S(1)}, bf16[128,512]{1,0:T(8,12...) custom-call(s32[2]{0:T(128)S(1)} %copy-done.4, ...), custom_call_target="tpu_custom_call" | custom-call | flops 4294967296 | bytes 8388608 | tf_op jit(solution)/shard_map/pallas_call | solution.py:254
  62.2 2.3 %collective-permute-start.10 = (bf16[128,512]{1,0:T(8,128)(2,1)S(1)}, bf16[128,512]{1,0:T(8,128)(2,1)S(1)}, u32[]{:S(2)}, u32[]{:S(2)}) collective-permute-start(bf16[128,512]{1,0:T(8,128)(2,1)S(1)} %get-tuple-element.62), channel_id=1, source_target_pairs={{0,7},{1,6},{2,5},{3,4},{4,3},{5,2},{6,1},{7,0},{8,15},{9,14},{10,... | collective-permute-start | bytes 393224 | tf_op jit(solution)/shard_map/ppermute | solution.py:306
  64.4 8.8 %collective-permute-start.11 = (bf16[128,512]{1,0:T(8,128)(2,1)S(1)}, bf16[128,512]{1,0:T(8,128)(2,1)S(1)}, u32[]{:S(2)}, u32[]{:S(2)}) collective-permute-start(bf16[128,512]{1,0:T(8,128)(2,1)S(1)} %get-tuple-element.63), channel_id=1, source_target_pairs={{0,3},{1,2},{2,1},{3,0},{4,7},{5,6},{6,5},{7,4},{8,11},{9,10},{10,... | collective-permute-start | bytes 393224 | tf_op jit(solution)/shard_map/ppermute | solution.py:306
  73.2 2.5 %collective-permute-done.7.refs_5_ = bf16[2,128,512]{2,1,0:T(8,128)(2,1)S(1)} collective-permute-done((bf16[2,128,512]{2,1,0:T(8,128)(2,1)}, bf16[2,128,512]{2,1,0:T(8,128)(2,1)S(1)}, u32[]{:S(2)}, u32[]{:S(2)}) %collective-permute-start.7) | collective-permute-done | bytes 262176 | tf_op jit(solution)/shard_map/ppermute | solution.py:306
  75.7 2.5 %collective-permute-start.12 = (bf16[128,512]{1,0:T(8,128)(2,1)S(1)}, bf16[128,512]{1,0:T(8,128)(2,1)S(1)}, u32[]{:S(2)}, u32[]{:S(2)}) collective-permute-start(bf16[128,512]{1,0:T(8,128)(2,1)S(1)} %get-tuple-element.64), channel_id=1, source_target_pairs={{0,6},{1,7},{2,4},{3,5},{4,2},{5,3},{6,0},{7,1},{8,14},{9,15},{10,... | collective-permute-start | bytes 393224 | tf_op jit(solution)/shard_map/ppermute | solution.py:306
  78.2 5.9 %collective-permute-done.9.refs_7_ = bf16[2,128,512]{2,1,0:T(8,128)(2,1)S(1)} collective-permute-done((bf16[2,128,512]{2,1,0:T(8,128)(2,1)}, bf16[2,128,512]{2,1,0:T(8,128)(2,1)S(1)}, u32[]{:S(2)}, u32[]{:S(2)}) %collective-permute-start.9) | collective-permute-done | bytes 262176 | tf_op jit(solution)/shard_map/ppermute | solution.py:306
  84.1 9.8 %shard_map.158 = (bf16[128,512]{1,0:T(8,128)(2,1)S(1)}, bf16[128,512]{1,0:T(8,128)(2,1)S(1)}, bf16[128,512]{1,0:T(8,128)(2,1)S(1)}, bf16[128,512]{1,0:T(8,128)(2...) custom-call(s32[2]{0:T(128)S(1)} %copy-done.4, ...), custom_call_target="tpu_custom_call" | custom-call | flops 3221225472 | bytes 4194304 | tf_op jit(solution)/shard_map/pallas_call | solution.py:156
  95.0 3.3 %collective-permute-start.16 = (bf16[128,512]{1,0:T(8,128)(2,1)S(1)}, bf16[128,512]{1,0:T(8,128)(2,1)S(1)}, u32[]{:S(2)}, u32[]{:S(2)}) collective-permute-start(bf16[128,512]{1,0:T(8,128)(2,1)S(1)} %get-tuple-element.70), channel_id=1, source_target_pairs={{0,4},{1,5},{2,6},{3,7},{4,0},{5,1},{6,2},{7,3},{8,12},{9,13},{10,... | collective-permute-start | bytes 393224 | tf_op jit(solution)/shard_map/ppermute | solution.py:306
  98.3 3.4 %collective-permute-start.17 = (bf16[128,512]{1,0:T(8,128)(2,1)S(1)}, bf16[128,512]{1,0:T(8,128)(2,1)S(1)}, u32[]{:S(2)}, u32[]{:S(2)}) collective-permute-start(bf16[128,512]{1,0:T(8,128)(2,1)S(1)} %get-tuple-element.73), channel_id=1, source_target_pairs={{0,7},{1,6},{2,5},{3,4},{4,3},{5,2},{6,1},{7,0},{8,15},{9,14},{10,... | collective-permute-start | bytes 393224 | tf_op jit(solution)/shard_map/ppermute | solution.py:306
  101.8 2.0 %collective-permute-start.19 = (bf16[128,512]{1,0:T(8,128)(2,1)S(1)}, bf16[128,512]{1,0:T(8,128)(2,1)S(1)}, u32[]{:S(2)}, u32[]{:S(2)}) collective-permute-start(bf16[128,512]{1,0:T(8,128)(2,1)S(1)} %get-tuple-element.75), channel_id=1, source_target_pairs={{0,6},{1,7},{2,4},{3,5},{4,2},{5,3},{6,0},{7,1},{8,14},{9,15},{10,... | collective-permute-start | bytes 393224 | tf_op jit(solution)/shard_map/ppermute | solution.py:306
  105.2 2.4 %collective-permute-done.16.refs_15_ = bf16[128,512]{1,0:T(8,128)(2,1)S(1)} collective-permute-done((bf16[128,512]{1,0:T(8,128)(2,1)S(1)}, bf16[128,512]{1,0:T(8,128)(2,1)S(1)}, u32[]{:S(2)}, u32[]{:S(2)}) %collective-permute-start.16) | collective-permute-done | bytes 131104 | tf_op jit(solution)/shard_map/ppermute | solution.py:306
  107.7 14.2 %shard_map.159 = (bf16[2,128,512]{2,1,0:T(8,128)(2,1)S(1)}, bf16[2,128,512]{2,1,0:T(8,128)(2,1)S(1)}, bf16[2,128,512]{2,1,0:T(8,128)(2,1)S(1)}, bf16[2,128,512]{...) custom-call(s32[2]{0:T(128)S(1)} %copy-done.4, ...), custom_call_target="tpu_custom_call" | custom-call | flops 5368709120 | bytes 4194304 | tf_op jit(solution)/shard_map/pallas_call | solution.py:156
  122.0 2.1 %collective-permute-start.24 = (bf16[2,128,512]{2,1,0:T(8,128)(2,1)S(1)}, bf16[2,128,512]{2,1,0:T(8,128)(2,1)S(1)}, u32[]{:S(2)}, u32[]{:S(2)}) collective-permute-start(bf16[2,128,512]{2,1,0:T(8,128)(2,1)S(1)} %get-tuple-element.80), channel_id=1, source_target_pairs={{0,7},{1,6},{2,5},{3,4},{4,3},{5,2},{6,1},{7,0},{8,15},{9,14},{10,... | collective-permute-start | bytes 786440 | tf_op jit(solution)/shard_map/ppermute | solution.py:306
  124.0 3.9 %collective-permute-start.21 = (bf16[128,512]{1,0:T(8,128)(2,1)S(1)}, bf16[128,512]{1,0:T(8,128)(2,1)S(1)}, u32[]{:S(2)}, u32[]{:S(2)}) collective-permute-start(bf16[128,512]{1,0:T(8,128)(2,1)S(1)} %get-tuple-element.77), channel_id=1, source_target_pairs={{0,5},{1,4},{2,7},{3,6},{4,1},{5,0},{6,3},{7,2},{8,13},{9,12},{10,... | collective-permute-start | bytes 393224 | tf_op jit(solution)/shard_map/ppermute | solution.py:306
  128.9 22.4 %collective-permute-done.21.refs_5_ = bf16[128,512]{1,0:T(8,128)(2,1)S(1)} collective-permute-done((bf16[128,512]{1,0:T(8,128)(2,1)S(1)}, bf16[128,512]{1,0:T(8,128)(2,1)S(1)}, u32[]{:S(2)}, u32[]{:S(2)}) %collective-permute-start.21) | collective-permute-done | bytes 131104 | tf_op jit(solution)/shard_map/ppermute | solution.py:306
  151.3 1.7 collective-permute-done.23.refs_7_
  152.9 2.5 %collective-permute-start.28 = (bf16[2,128,512]{2,1,0:T(8,128)(2,1)S(1)}, bf16[2,128,512]{2,1,0:T(8,128)(2,1)S(1)}, u32[]{:S(2)}, u32[]{:S(2)}) collective-permute-start(bf16[2,128,512]{2,1,0:T(8,128)(2,1)S(1)} %get-tuple-element.84), channel_id=1, source_target_pairs={{0,5},{1,4},{2,7},{3,6},{4,1},{5,0},{6,3},{7,2},{8,13},{9,12},{10,... | collective-permute-start | bytes 786440 | tf_op jit(solution)/shard_map/ppermute | solution.py:306
  155.4 1.7 collective-permute-start.29
  157.3 2.3 %shard_map.160 = bf16[8,128,512]{2,1,0:T(8,128)(2,1)} custom-call(s32[2]{0:T(128)S(1)} %copy-done.4, bf16[8,128,512]{2,1,0:T(8,128)(2,1)S(1)} %get-tuple-element.50.upstream, bf16[128,512]{1,0:T(8,128)(2,1)S(1)} %get-tuple-element.72.refs_0_, bf16[128,512]{1,0:T(8,128)(2,1)S(1)} %collective-permute-done.17.refs_1_, ...), custom_call_target="tpu_custom_call" | custom-call | flops 3145728 | bytes 3145728 | tf_op jit(solution)/shard_map/pallas_call | solution.py:232
  159.6 3.7 %collective-permute-done.27.refs_4_ = bf16[2,128,512]{2,1,0:T(8,128)(2,1)S(1)} collective-permute-done((bf16[2,128,512]{2,1,0:T(8,128)(2,1)S(1)}, bf16[2,128,512]{2,1,0:T(8,128)(2,1)S(1)}, u32[]{:S(2)}, u32[]{:S(2)}) %collective-permute-start.27) | collective-permute-done | bytes 262176 | tf_op jit(solution)/shard_map/ppermute | solution.py:306
  163.3 7.8 %collective-permute-done.28.refs_5_ = bf16[2,128,512]{2,1,0:T(8,128)(2,1)S(1)} collective-permute-done((bf16[2,128,512]{2,1,0:T(8,128)(2,1)S(1)}, bf16[2,128,512]{2,1,0:T(8,128)(2,1)S(1)}, u32[]{:S(2)}, u32[]{:S(2)}) %collective-permute-start.28) | collective-permute-done | bytes 262176 | tf_op jit(solution)/shard_map/ppermute | solution.py:306
  171.2 3.2 %collective-permute-done.30.refs_7_ = bf16[2,128,512]{2,1,0:T(8,128)(2,1)S(1)} collective-permute-done((bf16[2,128,512]{2,1,0:T(8,128)(2,1)S(1)}, bf16[2,128,512]{2,1,0:T(8,128)(2,1)S(1)}, u32[]{:S(2)}, u32[]{:S(2)}) %collective-permute-start.30) | collective-permute-done | bytes 262176 | tf_op jit(solution)/shard_map/ppermute | solution.py:306
  174.4 3.6 %shard_map.161 = (bf16[8,128,512]{2,1,0:T(8,128)(2,1)}, bf16[8,128,512]{2,1,0:T(8,128)(2,1)}, f32[8,128,512]{2,1,0:T(8,128)}) custom-call(s32[2]{0:T(128)S(1)} %copy-done.4, bf16[8,128,512]{2,1,0:T(8,128)(2,1)S(1)} %bitcast.16, bf16[8,128,512]{2,1,0:T(8,128)(2,1)S(1)} %bitcast.18, bf16[2,128,512]{2,1,0:T(8,128)(2,1)S(1)} %get-tuple-element.71.refs_0_, ...), custom_call_target="tpu_custom_call" | custom-call | flops 8388608 | bytes 8388608 | tf_op jit(solution)/shard_map/pallas_call | solution.py:232
  (60 shorter events, 7.8 us)
Async XLA Ops:
  0.6 26.4 %collective-permute-start = (bf16[1024,512]{1,0:T(8,128)(2,1)}, bf16[1024,512]{1,0:T(8,128)(2,1)S(1)}, u32[]{:S(2)}, u32[]{:S(2)}) collective-permute-start(bf16[1024,512]{1,0:T(8,128)(2,1)} %refs_4_), channel_id=1, source_target_pairs={{0,16},{8,24},{16,0},{24,8},{1,17},{9,25},{17,1},{25,9},{2,18},{10... | collective-permute-start | bytes 3145736 | tf_op jit(solution)/shard_map/ppermute | solution.py:279
  11.1 8.9 %collective-permute-start.1 = (bf16[2,128,512]{2,1,0:T(8,128)(2,1)}, bf16[2,128,512]{2,1,0:T(8,128)(2,1)S(1)}, u32[]{:S(2)}, u32[]{:S(2)}) collective-permute-start(bf16[2,128,512]{2,1,0:T(8,128)(2,1)} %get-tuple-element.47), channel_id=1, source_target_pairs={{0,3},{1,2},{2,1},{3,0},{4,7},{5,6},{6,5},{7,4},{8,11},{9,10},{10,... | collective-permute-start | bytes 786440 | tf_op jit(solution)/shard_map/ppermute | solution.py:306
  27.0 25.9 %collective-permute-start.2 = (bf16[1024,512]{1,0:T(8,128)(2,1)S(1)}, bf16[1024,512]{1,0:T(8,128)(2,1)}, u32[]{:S(2)}, u32[]{:S(2)}) collective-permute-start(bf16[1024,512]{1,0:T(8,128)(2,1)S(1)} %copy-done.2), channel_id=1, source_target_pairs={{0,8},{8,0},{16,24},{24,16},{1,9},{9,1},{17,25},{25,17},{2,10},{10... | collective-permute-start | bytes 3145736 | tf_op jit(solution)/shard_map/ppermute | solution.py:291
  27.0 26.4 %collective-permute-start.3 = (bf16[1024,512]{1,0:T(8,128)(2,1)S(1)}, bf16[1024,512]{1,0:T(8,128)(2,1)}, u32[]{:S(2)}, u32[]{:S(2)}) collective-permute-start(bf16[1024,512]{1,0:T(8,128)(2,1)S(1)} %collective-permute-done.refs_6_), channel_id=1, source_target_pairs={{0,8},{8,0},{16,24},{24,16},{1,9},{9,1},{17,25},{25,17},{2,10},{10... | collective-permute-start | bytes 3145736 | tf_op jit(solution)/shard_map/ppermute | solution.py:291
  27.5 12.4 %collective-permute-start.4 = (bf16[2,128,512]{2,1,0:T(8,128)(2,1)}, bf16[2,128,512]{2,1,0:T(8,128)(2,1)}, u32[]{:S(2)}, u32[]{:S(2)}) collective-permute-start(bf16[2,128,512]{2,1,0:T(8,128)(2,1)} %get-tuple-element.54), channel_id=1, source_target_pairs={{0,7},{1,6},{2,5},{3,4},{4,3},{5,2},{6,1},{7,0},{8,15},{9,14},{10,... | collective-permute-start | bytes 786440 | tf_op jit(solution)/shard_map/ppermute | solution.py:306
  32.3 29.8 %collective-permute-start.5 = (bf16[2,128,512]{2,1,0:T(8,128)(2,1)}, bf16[2,128,512]{2,1,0:T(8,128)(2,1)}, u32[]{:S(2)}, u32[]{:S(2)}) collective-permute-start(bf16[2,128,512]{2,1,0:T(8,128)(2,1)} %get-tuple-element.55), channel_id=1, source_target_pairs={{0,6},{1,7},{2,4},{3,5},{4,2},{5,3},{6,0},{7,1},{8,14},{9,15},{10,... | collective-permute-start | bytes 786440 | tf_op jit(solution)/shard_map/ppermute | solution.py:306
  32.5 31.9 %collective-permute-start.6 = (bf16[2,128,512]{2,1,0:T(8,128)(2,1)}, bf16[2,128,512]{2,1,0:T(8,128)(2,1)}, u32[]{:S(2)}, u32[]{:S(2)}) collective-permute-start(bf16[2,128,512]{2,1,0:T(8,128)(2,1)} %get-tuple-element.56), channel_id=1, source_target_pairs={{0,2},{1,3},{2,0},{3,1},{4,6},{5,7},{6,4},{7,5},{8,10},{9,11},{10,... | collective-permute-start | bytes 786440 | tf_op jit(solution)/shard_map/ppermute | solution.py:306
  40.0 35.7 %collective-permute-start.7 = (bf16[2,128,512]{2,1,0:T(8,128)(2,1)}, bf16[2,128,512]{2,1,0:T(8,128)(2,1)S(1)}, u32[]{:S(2)}, u32[]{:S(2)}) collective-permute-start(bf16[2,128,512]{2,1,0:T(8,128)(2,1)} %get-tuple-element.57), channel_id=1, source_target_pairs={{0,5},{1,4},{2,7},{3,6},{4,1},{5,0},{6,3},{7,2},{8,13},{9,12},{10,... | collective-permute-start | bytes 786440 | tf_op jit(solution)/shard_map/ppermute | solution.py:306
  52.9 25.2 %collective-permute-start.8 = (bf16[2,128,512]{2,1,0:T(8,128)(2,1)}, bf16[2,128,512]{2,1,0:T(8,128)(2,1)S(1)}, u32[]{:S(2)}, u32[]{:S(2)}) collective-permute-start(bf16[2,128,512]{2,1,0:T(8,128)(2,1)} %get-tuple-element.58), channel_id=1, source_target_pairs={{0,1},{1,0},{2,3},{3,2},{4,5},{5,4},{6,7},{7,6},{8,9},{9,8},{10,11... | collective-permute-start | bytes 786440 | tf_op jit(solution)/shard_map/ppermute | solution.py:306
  53.5 30.6 %collective-permute-start.9 = (bf16[2,128,512]{2,1,0:T(8,128)(2,1)}, bf16[2,128,512]{2,1,0:T(8,128)(2,1)S(1)}, u32[]{:S(2)}, u32[]{:S(2)}) collective-permute-start(bf16[2,128,512]{2,1,0:T(8,128)(2,1)} %get-tuple-element.59), channel_id=1, source_target_pairs={{0,4},{1,5},{2,6},{3,7},{4,0},{5,1},{6,2},{7,3},{8,12},{9,13},{10,... | collective-permute-start | bytes 786440 | tf_op jit(solution)/shard_map/ppermute | solution.py:306
  62.2 31.7 %collective-permute-start.10 = (bf16[128,512]{1,0:T(8,128)(2,1)S(1)}, bf16[128,512]{1,0:T(8,128)(2,1)S(1)}, u32[]{:S(2)}, u32[]{:S(2)}) collective-permute-start(bf16[128,512]{1,0:T(8,128)(2,1)S(1)} %get-tuple-element.62), channel_id=1, source_target_pairs={{0,7},{1,6},{2,5},{3,4},{4,3},{5,2},{6,1},{7,0},{8,15},{9,14},{10,... | collective-permute-start | bytes 393224 | tf_op jit(solution)/shard_map/ppermute | solution.py:306
  64.4 30.6 %collective-permute-start.11 = (bf16[128,512]{1,0:T(8,128)(2,1)S(1)}, bf16[128,512]{1,0:T(8,128)(2,1)S(1)}, u32[]{:S(2)}, u32[]{:S(2)}) collective-permute-start(bf16[128,512]{1,0:T(8,128)(2,1)S(1)} %get-tuple-element.63), channel_id=1, source_target_pairs={{0,3},{1,2},{2,1},{3,0},{4,7},{5,6},{6,5},{7,4},{8,11},{9,10},{10,... | collective-permute-start | bytes 393224 | tf_op jit(solution)/shard_map/ppermute | solution.py:306
  75.7 22.7 %collective-permute-start.12 = (bf16[128,512]{1,0:T(8,128)(2,1)S(1)}, bf16[128,512]{1,0:T(8,128)(2,1)S(1)}, u32[]{:S(2)}, u32[]{:S(2)}) collective-permute-start(bf16[128,512]{1,0:T(8,128)(2,1)S(1)} %get-tuple-element.64), channel_id=1, source_target_pairs={{0,6},{1,7},{2,4},{3,5},{4,2},{5,3},{6,0},{7,1},{8,14},{9,15},{10,... | collective-permute-start | bytes 393224 | tf_op jit(solution)/shard_map/ppermute | solution.py:306
  78.2 23.6 %collective-permute-start.13 = (bf16[128,512]{1,0:T(8,128)(2,1)S(1)}, bf16[128,512]{1,0:T(8,128)(2,1)S(1)}, u32[]{:S(2)}, u32[]{:S(2)}) collective-permute-start(bf16[128,512]{1,0:T(8,128)(2,1)S(1)} %get-tuple-element.65), channel_id=1, source_target_pairs={{0,2},{1,3},{2,0},{3,1},{4,6},{5,7},{6,4},{7,5},{8,10},{9,11},{10,... | collective-permute-start | bytes 393224 | tf_op jit(solution)/shard_map/ppermute | solution.py:306
  84.0 17.7 %collective-permute-start.14 = (bf16[128,512]{1,0:T(8,128)(2,1)S(1)}, bf16[128,512]{1,0:T(8,128)(2,1)S(1)}, u32[]{:S(2)}, u32[]{:S(2)}) collective-permute-start(bf16[128,512]{1,0:T(8,128)(2,1)S(1)} %get-tuple-element.66), channel_id=1, source_target_pairs={{0,5},{1,4},{2,7},{3,6},{4,1},{5,0},{6,3},{7,2},{8,13},{9,12},{10,... | collective-permute-start | bytes 393224 | tf_op jit(solution)/shard_map/ppermute | solution.py:306
  93.9 9.9 %collective-permute-start.15 = (bf16[128,512]{1,0:T(8,128)(2,1)S(1)}, bf16[128,512]{1,0:T(8,128)(2,1)S(1)}, u32[]{:S(2)}, u32[]{:S(2)}) collective-permute-start(bf16[128,512]{1,0:T(8,128)(2,1)S(1)} %get-tuple-element.69), channel_id=1, source_target_pairs={{0,1},{1,0},{2,3},{3,2},{4,5},{5,4},{6,7},{7,6},{8,9},{9,8},{10,11... | collective-permute-start | bytes 393224 | tf_op jit(solution)/shard_map/ppermute | solution.py:306
  95.0 12.7 %collective-permute-start.16 = (bf16[128,512]{1,0:T(8,128)(2,1)S(1)}, bf16[128,512]{1,0:T(8,128)(2,1)S(1)}, u32[]{:S(2)}, u32[]{:S(2)}) collective-permute-start(bf16[128,512]{1,0:T(8,128)(2,1)S(1)} %get-tuple-element.70), channel_id=1, source_target_pairs={{0,4},{1,5},{2,6},{3,7},{4,0},{5,1},{6,2},{7,3},{8,12},{9,13},{10,... | collective-permute-start | bytes 393224 | tf_op jit(solution)/shard_map/ppermute | solution.py:306
  98.3 25.7 %collective-permute-start.17 = (bf16[128,512]{1,0:T(8,128)(2,1)S(1)}, bf16[128,512]{1,0:T(8,128)(2,1)S(1)}, u32[]{:S(2)}, u32[]{:S(2)}) collective-permute-start(bf16[128,512]{1,0:T(8,128)(2,1)S(1)} %get-tuple-element.73), channel_id=1, source_target_pairs={{0,7},{1,6},{2,5},{3,4},{4,3},{5,2},{6,1},{7,0},{8,15},{9,14},{10,... | collective-permute-start | bytes 393224 | tf_op jit(solution)/shard_map/ppermute | solution.py:306
  101.8 22.3 %collective-permute-start.18 = (bf16[128,512]{1,0:T(8,128)(2,1)S(1)}, bf16[128,512]{1,0:T(8,128)(2,1)S(1)}, u32[]{:S(2)}, u32[]{:S(2)}) collective-permute-start(bf16[128,512]{1,0:T(8,128)(2,1)S(1)} %get-tuple-element.74), channel_id=1, source_target_pairs={{0,3},{1,2},{2,1},{3,0},{4,7},{5,6},{6,5},{7,4},{8,11},{9,10},{10,... | collective-permute-start | bytes 393224 | tf_op jit(solution)/shard_map/ppermute | solution.py:306
  101.8 26.2 %collective-permute-start.19 = (bf16[128,512]{1,0:T(8,128)(2,1)S(1)}, bf16[128,512]{1,0:T(8,128)(2,1)S(1)}, u32[]{:S(2)}, u32[]{:S(2)}) collective-permute-start(bf16[128,512]{1,0:T(8,128)(2,1)S(1)} %get-tuple-element.75), channel_id=1, source_target_pairs={{0,6},{1,7},{2,4},{3,5},{4,2},{5,3},{6,0},{7,1},{8,14},{9,15},{10,... | collective-permute-start | bytes 393224 | tf_op jit(solution)/shard_map/ppermute | solution.py:306
  103.8 25.0 %collective-permute-start.20 = (bf16[128,512]{1,0:T(8,128)(2,1)S(1)}, bf16[128,512]{1,0:T(8,128)(2,1)S(1)}, u32[]{:S(2)}, u32[]{:S(2)}) collective-permute-start(bf16[128,512]{1,0:T(8,128)(2,1)S(1)} %get-tuple-element.76), channel_id=1, source_target_pairs={{0,2},{1,3},{2,0},{3,1},{4,6},{5,7},{6,4},{7,5},{8,10},{9,11},{10,... | collective-permute-start | bytes 393224 | tf_op jit(solution)/shard_map/ppermute | solution.py:306
  121.9 52.5 %copy-start = (bf16[1024,512]{1,0:T(8,128)(2,1)S(1)}, bf16[1024,512]{1,0:T(8,128)(2,1)}, u32[]{:S(2)}) copy-start(bf16[1024,512]{1,0:T(8,128)(2,1)} %param.14) | copy-start | bytes 3145732
  122.0 33.5 %collective-permute-start.24 = (bf16[2,128,512]{2,1,0:T(8,128)(2,1)S(1)}, bf16[2,128,512]{2,1,0:T(8,128)(2,1)S(1)}, u32[]{:S(2)}, u32[]{:S(2)}) collective-permute-start(bf16[2,128,512]{2,1,0:T(8,128)(2,1)S(1)} %get-tuple-element.80), channel_id=1, source_target_pairs={{0,7},{1,6},{2,5},{3,4},{4,3},{5,2},{6,1},{7,0},{8,15},{9,14},{10,... | collective-permute-start | bytes 786440 | tf_op jit(solution)/shard_map/ppermute | solution.py:306
  124.0 33.1 %collective-permute-start.25 = (bf16[2,128,512]{2,1,0:T(8,128)(2,1)S(1)}, bf16[2,128,512]{2,1,0:T(8,128)(2,1)S(1)}, u32[]{:S(2)}, u32[]{:S(2)}) collective-permute-start(bf16[2,128,512]{2,1,0:T(8,128)(2,1)S(1)} %get-tuple-element.81), channel_id=1, source_target_pairs={{0,3},{1,2},{2,1},{3,0},{4,7},{5,6},{6,5},{7,4},{8,11},{9,10},{10,... | collective-permute-start | bytes 786440 | tf_op jit(solution)/shard_map/ppermute | solution.py:306
  124.0 27.2 %collective-permute-start.21 = (bf16[128,512]{1,0:T(8,128)(2,1)S(1)}, bf16[128,512]{1,0:T(8,128)(2,1)S(1)}, u32[]{:S(2)}, u32[]{:S(2)}) collective-permute-start(bf16[128,512]{1,0:T(8,128)(2,1)S(1)} %get-tuple-element.77), channel_id=1, source_target_pairs={{0,5},{1,4},{2,7},{3,6},{4,1},{5,0},{6,3},{7,2},{8,13},{9,12},{10,... | collective-permute-start | bytes 393224 | tf_op jit(solution)/shard_map/ppermute | solution.py:306
  127.9 23.3 %collective-permute-start.22 = (bf16[128,512]{1,0:T(8,128)(2,1)S(1)}, bf16[128,512]{1,0:T(8,128)(2,1)S(1)}, u32[]{:S(2)}, u32[]{:S(2)}) collective-permute-start(bf16[128,512]{1,0:T(8,128)(2,1)S(1)} %get-tuple-element.78), channel_id=1, source_target_pairs={{0,1},{1,0},{2,3},{3,2},{4,5},{5,4},{6,7},{7,6},{8,9},{9,8},{10,11... | collective-permute-start | bytes 393224 | tf_op jit(solution)/shard_map/ppermute | solution.py:306
  128.8 24.2 %collective-permute-start.23 = (bf16[128,512]{1,0:T(8,128)(2,1)S(1)}, bf16[128,512]{1,0:T(8,128)(2,1)S(1)}, u32[]{:S(2)}, u32[]{:S(2)}) collective-permute-start(bf16[128,512]{1,0:T(8,128)(2,1)S(1)} %get-tuple-element.79), channel_id=1, source_target_pairs={{0,4},{1,5},{2,6},{3,7},{4,0},{5,1},{6,2},{7,3},{8,12},{9,13},{10,... | collective-permute-start | bytes 393224 | tf_op jit(solution)/shard_map/ppermute | solution.py:306
  151.3 8.4 %collective-permute-start.26 = (bf16[2,128,512]{2,1,0:T(8,128)(2,1)S(1)}, bf16[2,128,512]{2,1,0:T(8,128)(2,1)S(1)}, u32[]{:S(2)}, u32[]{:S(2)}) collective-permute-start(bf16[2,128,512]{2,1,0:T(8,128)(2,1)S(1)} %get-tuple-element.82), channel_id=1, source_target_pairs={{0,6},{1,7},{2,4},{3,5},{4,2},{5,3},{6,0},{7,1},{8,14},{9,15},{10,... | collective-permute-start | bytes 786440 | tf_op jit(solution)/shard_map/ppermute | solution.py:306
  151.3 12.1 %collective-permute-start.27 = (bf16[2,128,512]{2,1,0:T(8,128)(2,1)S(1)}, bf16[2,128,512]{2,1,0:T(8,128)(2,1)S(1)}, u32[]{:S(2)}, u32[]{:S(2)}) collective-permute-start(bf16[2,128,512]{2,1,0:T(8,128)(2,1)S(1)} %get-tuple-element.83), channel_id=1, source_target_pairs={{0,2},{1,3},{2,0},{3,1},{4,6},{5,7},{6,4},{7,5},{8,10},{9,11},{10,... | collective-permute-start | bytes 786440 | tf_op jit(solution)/shard_map/ppermute | solution.py:306
  152.9 18.2 %collective-permute-start.28 = (bf16[2,128,512]{2,1,0:T(8,128)(2,1)S(1)}, bf16[2,128,512]{2,1,0:T(8,128)(2,1)S(1)}, u32[]{:S(2)}, u32[]{:S(2)}) collective-permute-start(bf16[2,128,512]{2,1,0:T(8,128)(2,1)S(1)} %get-tuple-element.84), channel_id=1, source_target_pairs={{0,5},{1,4},{2,7},{3,6},{4,1},{5,0},{6,3},{7,2},{8,13},{9,12},{10,... | collective-permute-start | bytes 786440 | tf_op jit(solution)/shard_map/ppermute | solution.py:306
  155.4 15.7 %collective-permute-start.29 = (bf16[2,128,512]{2,1,0:T(8,128)(2,1)S(1)}, bf16[2,128,512]{2,1,0:T(8,128)(2,1)S(1)}, u32[]{:S(2)}, u32[]{:S(2)}) collective-permute-start(bf16[2,128,512]{2,1,0:T(8,128)(2,1)S(1)} %get-tuple-element.85), channel_id=1, source_target_pairs={{0,1},{1,0},{2,3},{3,2},{4,5},{5,4},{6,7},{7,6},{8,9},{9,8},{10,11... | collective-permute-start | bytes 786440 | tf_op jit(solution)/shard_map/ppermute | solution.py:306
  157.1 17.3 %collective-permute-start.30 = (bf16[2,128,512]{2,1,0:T(8,128)(2,1)S(1)}, bf16[2,128,512]{2,1,0:T(8,128)(2,1)S(1)}, u32[]{:S(2)}, u32[]{:S(2)}) collective-permute-start(bf16[2,128,512]{2,1,0:T(8,128)(2,1)S(1)} %get-tuple-element.86), channel_id=1, source_target_pairs={{0,4},{1,5},{2,6},{3,7},{4,0},{5,1},{6,2},{7,3},{8,12},{9,13},{10,... | collective-permute-start | bytes 786440 | tf_op jit(solution)/shard_map/ppermute | solution.py:306
  (9 other events, 321.1 us)

commit v6 on v5

--- a/solution.py
+++ b/solution.py
@@ -173,12 +173,57 @@
     return (left.astype(F32) * right.astype(F32)).astype(BF16)
 
 
-def prepare_kernel(chunks, scale, me, inner_gate, signal, taps, gain, *outs):
-    at_zero = (me[0] == 0) & (lax.broadcasted_iota(jnp.int32, taps.shape[1:], 1) == 0)
-    for d, out in zip(partners(chunks), outs):
-        at = me[0] ^ d
-        out[0] = elementwise(inner_gate[at], signal[at])
-        out[1] = (taps[at] * scale + jnp.where(at_zero, gain[at], 0.0)).astype(BF16)
+def prepare_kernel(masks, scale, inner_gate, signal, taps, gain, *refs):
+    count = len(masks)
+    outs, (gates, values, filters, sems) = refs[:count], refs[count:]
+    me = lax.axis_index("ctx")
+    copies = []
+    for k, mask in enumerate(masks):
+        at = me ^ mask
+        pairs = ((inner_gate, gates), (signal, values), (taps, filters))
+        copies.append(
+            [
+                pltpu.make_async_copy(src.at[at], dst.at[k], sems.at[k, n])
+                for n, (src, dst) in enumerate(pairs)
+            ]
+        )
+    for group in copies:
+        for copy in group:
+            copy.start()
+    rows, lanes = gates.shape[1], gain.shape[1]
+    shape = (rows, lanes)
+    diagonal = lax.broadcasted_iota(jnp.int32, shape, 0) == lax.broadcasted_iota(jnp.int32, shape, 1)
+    at_zero = (me == 0) & (lax.broadcasted_iota(jnp.int32, filters.shape[1:], 1) == 0)
+    for k, (mask, group, out) in enumerate(zip(masks, copies, outs)):
+        row = gain[pl.ds(me ^ mask, 1), :]
+        column = jnp.sum(jnp.where(diagonal, row, 0.0), axis=1, keepdims=True)
+        for copy in group:
+            copy.wait()
+        out[0] = elementwise(gates[k], values[k])
+        out[1] = (filters[k] * scale + jnp.where(at_zero, column, 0.0)).astype(BF16)
+
+
+def prepare_call(masks, scale, inner_gate, signal, taps, gain):
+    count, (rows, lanes) = len(masks), taps.shape[1:]
+    out = jax.ShapeDtypeStruct((2, rows, lanes), BF16)
+    anywhere = pl.BlockSpec(memory_space=pl.ANY)
+    inside = pl.BlockSpec(memory_space=pltpu.VMEM)
+    return pl.pallas_call(
+        functools.partial(prepare_kernel, masks, scale),
+        in_specs=[anywhere, anywhere, anywhere, inside],
+        out_specs=[inside] * count,
+        out_shape=[out] * count,
+        scratch_shapes=[
+            pltpu.VMEM((count, rows, lanes), BF16),
+            pltpu.VMEM((count, rows, lanes), BF16),
+            pltpu.VMEM((count, rows, lanes), F32),
+            pltpu.SemaphoreType.DMA((count, 3)),
+        ],
+        compiler_params=pltpu.CompilerParams(vmem_limit_bytes=48 * 1024 * 1024),
+        cost_estimate=pl.CostEstimate(
+            flops=8 * count * rows * lanes, bytes_accessed=12 * count * rows * lanes, transcendentals=0
+        ),
+    )(inner_gate, signal, taps, gain)
 
 
 def project_kernel(chunks, members, me, *refs):
@@ -210,14 +255,50 @@
         out[at] = elementwise(upstream[at], piece[...])
 
 
-def finish_kernel(chunks, me, inner_gate, signal, *refs):
-    chunk, (grad_inner, grad_signal, grad_taps) = refs[:chunks], refs[chunks:]
-    for d, piece in zip(partners(chunks), chunk):
-        at = me[0] ^ d
-        back = piece[0]
-        grad_inner[at] = elementwise(back, signal[at])
-        grad_signal[at] = elementwise(back, inner_gate[at])
-        grad_taps[at] = piece[1].astype(F32)
+def finish_kernel(count, me, *refs):
+    gates, refs = refs[:count], refs[count:]
+    values, refs = refs[:count], refs[count:]
+    chunk, (grad_inner, grad_signal, grad_taps) = refs[:count], refs[-3:]
+    step = pl.program_id(0)
+    for k in range(count):
+
+        @pl.when(step == k)
+        def _(k=k):
+            back = chunk[k][0]
+            grad_inner[0] = elementwise(back, values[k][0])
+            grad_signal[0] = elementwise(back, gates[k][0])
+            grad_taps[0] = chunk[k][1].astype(F32)
+
+
+def finish_call(me, masks, inner_gate, signal, chunks, earlier):
+    count, shape = len(masks), inner_gate.shape
+    block = (1,) + shape[1:]
+
+    def place(i, me):
+        mask = masks[0]
+        for k in range(1, count):
+            mask = jnp.where(i == k, masks[k], mask)
+        return (me[0] ^ mask, 0, 0)
+
+    gates = [pl.BlockSpec(block, lambda i, me, mask=mask: (me[0] ^ mask, 0, 0)) for mask in masks]
+    pieces = [pl.BlockSpec(chunk.shape, lambda i, me: (0, 0, 0)) for chunk in chunks]
+    return pl.pallas_call(
+        functools.partial(finish_kernel, count),
+        grid_spec=pltpu.PrefetchScalarGridSpec(
+            num_scalar_prefetch=1,
+            grid=(count,),
+            in_specs=gates * 2 + pieces + [pl.BlockSpec(memory_space=pl.ANY)] * len(earlier),
+            out_specs=[pl.BlockSpec(block, place)] * 3,
+        ),
+        out_shape=[jax.ShapeDtypeStruct(shape, dtype) for dtype in (BF16, BF16, F32)],
+        input_output_aliases={1 + 3 * count + n: n for n in range(len(earlier))},
+        compiler_params=pltpu.CompilerParams(vmem_limit_bytes=32 * 1024 * 1024),
+        cost_estimate=pl.CostEstimate(
+            flops=2 * count * math.prod(shape[1:]),
+            bytes_accessed=16 * count * math.prod(shape[1:]),
+            transcendentals=0,
+        ),
+    )(me, *[inner_gate] * count, *[signal] * count, *chunks, *earlier)
 
 
 def rowwise_call(kernel, me, wholes, pieces, out_shapes, rows, limit=32):
@@ -333,19 +414,15 @@
 
     tables = [jnp.asarray(table) for table in make_tables(inner, n_ctx)]
     tables = [table if table.ndim == 2 else table[me[0]] for table in tables]
+    masks = partners(n_ctx)
+    first = min(4, n_ctx)
+    sources = (scale, split(inner_gate), split(signal), split(filter_taps), split(skip_gain)[:, :, 0])
+    head = prepare_call(masks[1:first], *sources)
+    cotangent, _ = lax.optimization_barrier((cotangent, head[0]))
     far = gather_start(cotangent)
-    pair = exchange(
-        rowwise_call(
-            functools.partial(prepare_kernel, n_ctx, scale),
-            me,
-            (split(inner_gate), split(signal), split(filter_taps), split(skip_gain)),
-            (),
-            shapes((2,), BF16, n_ctx),
-            32,
-            limit=60,
-        )
-    )
-    gathered = gather_rest(cotangent, far, pair[2])
+    own, *rest = prepare_call([0] + masks[first:], *sources)
+    pair = exchange([own, *head, *rest])
+    gathered = gather_rest(cotangent, far, (pair[1:first], rest[:1]))
     upstream, *grad = project_call(me, out_weight, gathered, split(outer_gate))
     response = conv_call(
         functools.partial(response_kernel, n_ctx, inner), me, (after(pair, grad[0]),), tables, (), inner, 3
@@ -371,14 +448,13 @@
         shapes((n_ctx,), BF16, 1),
         32,
     )
-    grad_inner, grad_signal, grad_taps = rowwise_call(
-        functools.partial(finish_kernel, n_ctx),
-        me,
-        (split(inner_gate), split(signal)),
-        backs_came,
-        shapes((n_ctx,), BF16, 2) + shapes((n_ctx,), F32, 1),
-        32,
-    )
+    outs = []
+    cut = n_ctx - 3
+    for low, high in ((0, cut), (cut, n_ctx)):
+        outs = finish_call(
+            me, masks[low:high], split(inner_gate), split(signal), backs_came[low:high], outs
+        )
+    grad_inner, grad_signal, grad_taps = outs
     return (flat(grad_outer), flat(grad_inner), flat(grad_signal), flat(grad_taps))
 
 

time: 178 us -> 167 us (0.938)
  starting transfers between devices: 60.8 us -> 49.9 us
  waiting for transfers between devices: 68.4 us -> 61 us
  local copies, waits for them, and re-layouts: 3.7 us -> 8.85 us
  Pallas kernels: 43.6 us -> 45.6 us
    ppermute x28, starting transfers between devices: 57.3 us -> 46.4 us  [exchange(): lax.ppermute(part, 'ctx', [(p, p ^ d) for p in range(count)])]
    pallas_call x0 -> x4, Pallas kernels: none -> 10.7 us  [the longest x2 5.6 us: finish_call(): pl.pallas_call(functools.partial(finish_kernel, count), grid_spec=pltpu.P...]
    pallas_call x3 -> x1, Pallas kernels: 11 us -> 2.29 us  [rowwise_call(): pl.pallas_call(kernel, grid_spec=pltpu.PrefetchScalarGridSpec(num_scalar_...]
    unnamed x20 -> x38, local copies, waits for them, and re-layouts: 0.05 us -> 6.9 us
    ppermute x1, waiting for transfers between devices: 6.96 us -> 0.42 us  [gather_start(): lax.ppermute(block, 'group', [(g, g ^ count // 2) for g in range(count)])]
  transfers between devices with their start and end apart: 31 -> 31, of which waited for: 11 -> 10; matrix products, arithmetic and copies ran while one was open for 2% -> 1% of each run, Pallas kernels for 22% -> 25%
where the time goes in v6:
time: 167 us; the launch traced here: 166 us
  waiting for transfers between devices  61 us (37%)
  starting transfers between devices  49.9 us (30%)
  Pallas kernels  45.6 us (27%)
  local copies, waits for them, and re-layouts  8.85 us (5%)
    ppermute x28, waiting for transfers between devices, exchange(): lax.ppermute(part, 'ctx', [(p, p ^ d) for p in range(count)])  60.6 us
    ppermute x28, starting transfers between devices, exchange(): lax.ppermute(part, 'ctx', [(p, p ^ d) for p in range(count)])  46.4 us
    pallas_call x2, Pallas kernels, conv_call(): pl.pallas_call(kernel, grid_spec=pltpu.PrefetchScalarGridSpec(num_scalar_...  24.2 us
    pallas_call x1, Pallas kernels, project_call(): pl.pallas_call(functools.partial(project_kernel, chunks, members), grid_s...  8.49 us
    unnamed x38, local copies, waits for them, and re-layouts  6.9 us
    pallas_call x2, Pallas kernels, finish_call(): pl.pallas_call(functools.partial(finish_kernel, count), grid_spec=pltpu.P...  5.6 us
    pallas_call x2, Pallas kernels, prepare_call(): pl.pallas_call(functools.partial(prepare_kernel, masks, scale), in_specs=...  5.08 us
  transfers between devices with their start and end apart: 31, of which 10 were waited for; matrix products, arithmetic and copies ran while one was open for 1% of the time, Pallas kernels for 25%

profile of v6, /device:TPU:0, one launch (start us, length us, event | category | flops | bytes accessed | tf_op | source)
XLA Modules:
  0.0 166.4 jit_solution(3236728880218890332)
XLA Ops:
  3.1 1.6 copy-done.4
  5.4 1.6 shard_map.156
  7.0 3.0 %collective-permute-start = (bf16[1024,512]{1,0:T(8,128)(2,1)S(1)}, bf16[1024,512]{1,0:T(8,128)(2,1)S(1)}, u32[]{:S(2)}, u32[]{:S(2)}) collective-permute-start(bf16[1024,512]{1,0:T(8,128)(2,1)S(1)} %copy-done.5), channel_id=1, source_target_pairs={{0,16},{8,24},{16,0},{24,8},{1,17},{9,25},{17,1},{25,9},{2,18},{10... | collective-permute-start | bytes 3145736 | tf_op jit(solution)/shard_map/ppermute | solution.py:360
  10.0 2.5 %collective-permute-start.2 = (bf16[2,128,512]{2,1,0:T(8,128)(2,1)S(1)}, bf16[2,128,512]{2,1,0:T(8,128)(2,1)S(1)}, u32[]{:S(2)}, u32[]{:S(2)}) collective-permute-start(bf16[2,128,512]{2,1,0:T(8,128)(2,1)S(1)} %get-tuple-element.53), channel_id=1, source_target_pairs={{0,3},{1,2},{2,1},{3,0},{4,7},{5,6},{6,5},{7,4},{8,11},{9,10},{10,... | collective-permute-start | bytes 786440 | tf_op jit(solution)/shard_map/ppermute | solution.py:387
  12.5 2.5 %collective-permute-start.3 = (bf16[2,128,512]{2,1,0:T(8,128)(2,1)S(1)}, bf16[2,128,512]{2,1,0:T(8,128)(2,1)S(1)}, u32[]{:S(2)}, u32[]{:S(2)}) collective-permute-start(bf16[2,128,512]{2,1,0:T(8,128)(2,1)S(1)} %get-tuple-element.54), channel_id=1, source_target_pairs={{0,6},{1,7},{2,4},{3,5},{4,2},{5,3},{6,0},{7,1},{8,14},{9,15},{10,... | collective-permute-start | bytes 786440 | tf_op jit(solution)/shard_map/ppermute | solution.py:387
  16.3 3.5 %shard_map.157 = (bf16[2,128,512]{2,1,0:T(8,128)(2,1)S(1)}, bf16[2,128,512]{2,1,0:T(8,128)(2,1)}, bf16[2,128,512]{2,1,0:T(8,128)(2,1)}, bf16[2,128,512]{2,1,0:T(8,128)(2,1)}, bf16[2,128,512]{2,1,0:T(8,128)(2,1)S(1)}) custom-call(bf16[8,128,512]{2,1,0:T(8,128)(2,1)S(1)} %bitcast.16, bf16[8,128,512]{2,1,0:T(8,128)(2,1)S(1)} %bitcast.26, ...), custom_call_target="tpu_custom_call" | custom-call | flops 2621440 | bytes 3932160 | tf_op jit(solution)/shard_map/pallas_call | solution.py:211
  20.5 7.4 %collective-permute-done.3.refs_3_ = bf16[2,128,512]{2,1,0:T(8,128)(2,1)S(1)} collective-permute-done((bf16[2,128,512]{2,1,0:T(8,128)(2,1)S(1)}, bf16[2,128,512]{2,1,0:T(8,128)(2,1)S(1)}, u32[]{:S(2)}, u32[]{:S(2)}) %collective-permute-start.3) | collective-permute-done | bytes 262176 | tf_op jit(solution)/shard_map/ppermute | solution.py:387
  28.6 3.4 %collective-permute-done.1.refs_1_ = bf16[2,128,512]{2,1,0:T(8,128)(2,1)S(1)} collective-permute-done((bf16[2,128,512]{2,1,0:T(8,128)(2,1)S(1)}, bf16[2,128,512]{2,1,0:T(8,128)(2,1)S(1)}, u32[]{:S(2)}, u32[]{:S(2)}) %collective-permute-start.1) | collective-permute-done | bytes 262176 | tf_op jit(solution)/shard_map/ppermute | solution.py:387
  33.7 5.8 %collective-permute-start.6 = (bf16[2,128,512]{2,1,0:T(8,128)(2,1)}, bf16[2,128,512]{2,1,0:T(8,128)(2,1)}, u32[]{:S(2)}, u32[]{:S(2)}) collective-permute-start(bf16[2,128,512]{2,1,0:T(8,128)(2,1)} %get-tuple-element.55), channel_id=1, source_target_pairs={{0,2},{1,3},{2,0},{3,1},{4,6},{5,7},{6,4},{7,5},{8,10},{9,11},{10,... | collective-permute-start | bytes 786440 | tf_op jit(solution)/shard_map/ppermute | solution.py:387
  39.4 2.1 %collective-permute-start.7 = (bf16[2,128,512]{2,1,0:T(8,128)(2,1)}, bf16[2,128,512]{2,1,0:T(8,128)(2,1)}, u32[]{:S(2)}, u32[]{:S(2)}) collective-permute-start(bf16[2,128,512]{2,1,0:T(8,128)(2,1)} %get-tuple-element.62), channel_id=1, source_target_pairs={{0,5},{1,4},{2,7},{3,6},{4,1},{5,0},{6,3},{7,2},{8,13},{9,12},{10,... | collective-permute-start | bytes 786440 | tf_op jit(solution)/shard_map/ppermute | solution.py:387
  44.1 1.8 %collective-permute-start.9 = (bf16[2,128,512]{2,1,0:T(8,128)(2,1)}, bf16[2,128,512]{2,1,0:T(8,128)(2,1)S(1)}, u32[]{:S(2)}, u32[]{:S(2)}) collective-permute-start(bf16[2,128,512]{2,1,0:T(8,128)(2,1)} %copy-done.14), channel_id=1, source_target_pairs={{0,4},{1,5},{2,6},{3,7},{4,0},{5,1},{6,2},{7,3},{8,12},{9,13},{10,... | collective-permute-start | bytes 786440 | tf_op jit(solution)/shard_map/ppermute | solution.py:387
  46.0 8.5 %shard_map.158 = (bf16[8,128,512]{2,1,0:T(8,128)(2,1)S(1)}, bf16[128,512]{1,0:T(8,128)(2,1)S(1)}, bf16[128,512]{1,0:T(8,128)(2,1)S(1)}, bf16[128,512]{1,0:T(8,12...) custom-call(s32[2]{0:T(128)S(1)} %pad_add_fusion.me, ...), custom_call_target="tpu_custom_call" | custom-call | flops 4294967296 | bytes 8388608 | tf_op jit(solution)/shard_map/pallas_call | solution.py:335
  54.5 3.7 %collective-permute-start.10 = (bf16[128,512]{1,0:T(8,128)(2,1)S(1)}, bf16[128,512]{1,0:T(8,128)(2,1)S(1)}, u32[]{:S(2)}, u32[]{:S(2)}) collective-permute-start(bf16[128,512]{1,0:T(8,128)(2,1)S(1)} %get-tuple-element.67), channel_id=1, source_target_pairs={{0,7},{1,6},{2,5},{3,4},{4,3},{5,2},{6,1},{7,0},{8,15},{9,14},{10,... | collective-permute-start | bytes 393224 | tf_op jit(solution)/shard_map/ppermute | solution.py:387
  58.2 6.8 %collective-permute-done.7.refs_5_ = bf16[2,128,512]{2,1,0:T(8,128)(2,1)} collective-permute-done((bf16[2,128,512]{2,1,0:T(8,128)(2,1)}, bf16[2,128,512]{2,1,0:T(8,128)(2,1)}, u32[]{:S(2)}, u32[]{:S(2)}) %collective-permute-start.7) | collective-permute-done | bytes 262176 | tf_op jit(solution)/shard_map/ppermute | solution.py:387
  64.9 2.5 %collective-permute-start.12 = (bf16[128,512]{1,0:T(8,128)(2,1)S(1)}, bf16[128,512]{1,0:T(8,128)(2,1)S(1)}, u32[]{:S(2)}, u32[]{:S(2)}) collective-permute-start(bf16[128,512]{1,0:T(8,128)(2,1)S(1)} %get-tuple-element.69), channel_id=1, source_target_pairs={{0,6},{1,7},{2,4},{3,5},{4,2},{5,3},{6,0},{7,1},{8,14},{9,15},{10,... | collective-permute-start | bytes 393224 | tf_op jit(solution)/shard_map/ppermute | solution.py:387
  67.4 5.8 %collective-permute-done.9.refs_7_ = bf16[2,128,512]{2,1,0:T(8,128)(2,1)S(1)} collective-permute-done((bf16[2,128,512]{2,1,0:T(8,128)(2,1)}, bf16[2,128,512]{2,1,0:T(8,128)(2,1)S(1)}, u32[]{:S(2)}, u32[]{:S(2)}) %collective-permute-start.9) | collective-permute-done | bytes 262176 | tf_op jit(solution)/shard_map/ppermute | solution.py:387
  73.2 2.8 %collective-permute-start.14 = (bf16[128,512]{1,0:T(8,128)(2,1)S(1)}, bf16[128,512]{1,0:T(8,128)(2,1)S(1)}, u32[]{:S(2)}, u32[]{:S(2)}) collective-permute-start(bf16[128,512]{1,0:T(8,128)(2,1)S(1)} %get-tuple-element.71), channel_id=1, source_target_pairs={{0,5},{1,4},{2,7},{3,6},{4,1},{5,0},{6,3},{7,2},{8,13},{9,12},{10,... | collective-permute-start | bytes 393224 | tf_op jit(solution)/shard_map/ppermute | solution.py:387
  76.1 9.9 %shard_map.159 = (bf16[128,512]{1,0:T(8,128)(2,1)S(1)}, bf16[128,512]{1,0:T(8,128)(2,1)S(1)}, bf16[128,512]{1,0:T(8,128)(2,1)S(1)}, bf16[128,512]{1,0:T(8,128)(2...) custom-call(s32[2]{0:T(128)S(1)} %pad_add_fusion.me, ...), custom_call_target="tpu_custom_call" | custom-call | flops 3221225472 | bytes 4194304 | tf_op jit(solution)/shard_map/pallas_call | solution.py:156
  86.0 1.9 %collective-permute-start.15 = (bf16[128,512]{1,0:T(8,128)(2,1)S(1)}, bf16[128,512]{1,0:T(8,128)(2,1)S(1)}, u32[]{:S(2)}, u32[]{:S(2)}) collective-permute-start(bf16[128,512]{1,0:T(8,128)(2,1)S(1)} %get-tuple-element.74), channel_id=1, source_target_pairs={{0,1},{1,0},{2,3},{3,2},{4,5},{5,4},{6,7},{7,6},{8,9},{9,8},{10,11... | collective-permute-start | bytes 393224 | tf_op jit(solution)/shard_map/ppermute | solution.py:387
  87.9 2.0 %collective-permute-start.17 = (bf16[128,512]{1,0:T(8,128)(2,1)S(1)}, bf16[128,512]{1,0:T(8,128)(2,1)S(1)}, u32[]{:S(2)}, u32[]{:S(2)}) collective-permute-start(bf16[128,512]{1,0:T(8,128)(2,1)S(1)} %get-tuple-element.78), channel_id=1, source_target_pairs={{0,7},{1,6},{2,5},{3,4},{4,3},{5,2},{6,1},{7,0},{8,15},{9,14},{10,... | collective-permute-start | bytes 393224 | tf_op jit(solution)/shard_map/ppermute | solution.py:387
  89.9 2.4 %collective-permute-start.18 = (bf16[128,512]{1,0:T(8,128)(2,1)S(1)}, bf16[128,512]{1,0:T(8,128)(2,1)S(1)}, u32[]{:S(2)}, u32[]{:S(2)}) collective-permute-start(bf16[128,512]{1,0:T(8,128)(2,1)S(1)} %get-tuple-element.79), channel_id=1, source_target_pairs={{0,3},{1,2},{2,1},{3,0},{4,7},{5,6},{6,5},{7,4},{8,11},{9,10},{10,... | collective-permute-start | bytes 393224 | tf_op jit(solution)/shard_map/ppermute | solution.py:387
  93.8 6.2 %collective-permute-done.16.refs_15_ = bf16[128,512]{1,0:T(8,128)(2,1)S(1)} collective-permute-done((bf16[128,512]{1,0:T(8,128)(2,1)S(1)}, bf16[128,512]{1,0:T(8,128)(2,1)S(1)}, u32[]{:S(2)}, u32[]{:S(2)}) %collective-permute-start.16) | collective-permute-done | bytes 131104 | tf_op jit(solution)/shard_map/ppermute | solution.py:387
  100.0 14.3 %shard_map.160 = (bf16[2,128,512]{2,1,0:T(8,128)(2,1)S(1)}, bf16[2,128,512]{2,1,0:T(8,128)(2,1)S(1)}, bf16[2,128,512]{2,1,0:T(8,128)(2,1)S(1)}, bf16[2,128,512]{...) custom-call(s32[2]{0:T(128)S(1)} %pad_add_fusion.me, ...), custom_call_target="tpu_custom_call" | custom-call | flops 5368709120 | bytes 4194304 | tf_op jit(solution)/shard_map/pallas_call | solution.py:156
  115.0 5.0 %collective-permute-start.21 = (bf16[128,512]{1,0:T(8,128)(2,1)S(1)}, bf16[128,512]{1,0:T(8,128)(2,1)S(1)}, u32[]{:S(2)}, u32[]{:S(2)}) collective-permute-start(bf16[128,512]{1,0:T(8,128)(2,1)S(1)} %get-tuple-element.82), channel_id=1, source_target_pairs={{0,5},{1,4},{2,7},{3,6},{4,1},{5,0},{6,3},{7,2},{8,13},{9,12},{10,... | collective-permute-start | bytes 393224 | tf_op jit(solution)/shard_map/ppermute | solution.py:387
  121.2 20.1 %collective-permute-done.21.refs_5_ = bf16[128,512]{1,0:T(8,128)(2,1)S(1)} collective-permute-done((bf16[128,512]{1,0:T(8,128)(2,1)S(1)}, bf16[128,512]{1,0:T(8,128)(2,1)S(1)}, u32[]{:S(2)}, u32[]{:S(2)}) %collective-permute-start.21) | collective-permute-done | bytes 131104 | tf_op jit(solution)/shard_map/ppermute | solution.py:387
  141.2 2.3 %collective-permute-start.29 = (bf16[2,128,512]{2,1,0:T(8,128)(2,1)S(1)}, bf16[2,128,512]{2,1,0:T(8,128)(2,1)S(1)}, u32[]{:S(2)}, u32[]{:S(2)}) collective-permute-start(bf16[2,128,512]{2,1,0:T(8,128)(2,1)S(1)} %get-tuple-element.90), channel_id=1, source_target_pairs={{0,6},{1,7},{2,4},{3,5},{4,2},{5,3},{6,0},{7,1},{8,14},{9,15},{10,... | collective-permute-start | bytes 786440 | tf_op jit(solution)/shard_map/ppermute | solution.py:387
  145.1 2.3 %collective-permute-start.25 = (bf16[2,128,512]{2,1,0:T(8,128)(2,1)S(1)}, bf16[2,128,512]{2,1,0:T(8,128)(2,1)S(1)}, u32[]{:S(2)}, u32[]{:S(2)}) collective-permute-start(bf16[2,128,512]{2,1,0:T(8,128)(2,1)S(1)} %get-tuple-element.86), channel_id=1, source_target_pairs={{0,1},{1,0},{2,3},{3,2},{4,5},{5,4},{6,7},{7,6},{8,9},{9,8},{10,11... | collective-permute-start | bytes 786440 | tf_op jit(solution)/shard_map/ppermute | solution.py:387
  147.5 2.3 %shard_map.161 = bf16[8,128,512]{2,1,0:T(8,128)(2,1)} custom-call(s32[2]{0:T(128)S(1)} %pad_add_fusion.me, bf16[8,128,512]{2,1,0:T(8,128)(2,1)S(1)} %get-tuple-element.58.upstream, bf16[128,512]{1,0:T(8,128)(2,1)S(1)} %get-tuple-element.77.refs_0_, bf16[128,512]{1,0:T(8,128)(2,1)S(1)} %collective-permute-done.17.refs_1_, ...), custom_call_target="tpu_custom_call" | custom-call | flops 3145728 | bytes 3145728 | tf_op jit(solution)/shard_map/pallas_call | solution.py:313
  150.9 4.7 %collective-permute-done.30.refs_14_ = bf16[2,128,512]{2,1,0:T(8,128)(2,1)S(1)} collective-permute-done((bf16[2,128,512]{2,1,0:T(8,128)(2,1)S(1)}, bf16[2,128,512]{2,1,0:T(8,128)(2,1)S(1)}, u32[]{:S(2)}, u32[]{:S(2)}) %collective-permute-start.30) | collective-permute-done | bytes 262176 | tf_op jit(solution)/shard_map/ppermute | solution.py:387
  155.6 3.3 %shard_map.162 = (bf16[8,128,512]{2,1,0:T(8,128)(2,1)}, bf16[8,128,512]{2,1,0:T(8,128)(2,1)}, f32[8,128,512]{2,1,0:T(8,128)}) custom-call(s32[2]{0:T(128)S(1)} %pad_add_fusion.me, bf16[8,128,512]{2,1,0:T(8,128)(2,1)S(1)} %bitcast.17, bf16[8,128,512]{2,1,0:T(8,128)(2,1)S(1)} %bitcast.18, bf16[8,128,512]{2,1,0:T(8,128)(2,1)S(1)} %bitcast.19, ...), custom_call_target="tpu_custom_call" | custom-call | flops 655360 | bytes 5242880 | tf_op jit(solution)/shard_map/pallas_call | solution.py:285
  158.9 5.2 %collective-permute-done.26.refs_8_ = bf16[2,128,512]{2,1,0:T(8,128)(2,1)S(1)} collective-permute-done((bf16[2,128,512]{2,1,0:T(8,128)(2,1)S(1)}, bf16[2,128,512]{2,1,0:T(8,128)(2,1)S(1)}, u32[]{:S(2)}, u32[]{:S(2)}) %collective-permute-start.26) | collective-permute-done | bytes 262176 | tf_op jit(solution)/shard_map/ppermute | solution.py:387
  164.0 2.3 %shard_map.163 = (bf16[8,128,512]{2,1,0:T(8,128)(2,1)}, bf16[8,128,512]{2,1,0:T(8,128)(2,1)}, f32[8,128,512]{2,1,0:T(8,128)}) custom-call(s32[2]{0:T(128)S(1)} %pad_add_fusion.me, bf16[8,128,512]{2,1,0:T(8,128)(2,1)S(1)} %bitcast.22, bf16[8,128,512]{2,1,0:T(8,128)(2,1)S(1)} %bitcast.23, ...), custom_call_target="tpu_custom_call", output_to_operand_aliasing={{0}: (10, {}), {1}: (11, {}), {2}: (12, {})} | custom-call | flops 393216 | bytes 3145728 | tf_op jit(solution)/shard_map/pallas_call | solution.py:285
  (79 shorter events, 16.2 us)
Async XLA Ops:
  7.0 26.2 %collective-permute-start = (bf16[1024,512]{1,0:T(8,128)(2,1)S(1)}, bf16[1024,512]{1,0:T(8,128)(2,1)S(1)}, u32[]{:S(2)}, u32[]{:S(2)}) collective-permute-start(bf16[1024,512]{1,0:T(8,128)(2,1)S(1)} %copy-done.5), channel_id=1, source_target_pairs={{0,16},{8,24},{16,0},{24,8},{1,17},{9,25},{17,1},{25,9},{2,18},{10... | collective-permute-start | bytes 3145736 | tf_op jit(solution)/shard_map/ppermute | solution.py:360
  10.0 10.5 %collective-permute-start.2 = (bf16[2,128,512]{2,1,0:T(8,128)(2,1)S(1)}, bf16[2,128,512]{2,1,0:T(8,128)(2,1)S(1)}, u32[]{:S(2)}, u32[]{:S(2)}) collective-permute-start(bf16[2,128,512]{2,1,0:T(8,128)(2,1)S(1)} %get-tuple-element.53), channel_id=1, source_target_pairs={{0,3},{1,2},{2,1},{3,0},{4,7},{5,6},{6,5},{7,4},{8,11},{9,10},{10,... | collective-permute-start | bytes 786440 | tf_op jit(solution)/shard_map/ppermute | solution.py:387
  12.5 15.4 %collective-permute-start.3 = (bf16[2,128,512]{2,1,0:T(8,128)(2,1)S(1)}, bf16[2,128,512]{2,1,0:T(8,128)(2,1)S(1)}, u32[]{:S(2)}, u32[]{:S(2)}) collective-permute-start(bf16[2,128,512]{2,1,0:T(8,128)(2,1)S(1)} %get-tuple-element.54), channel_id=1, source_target_pairs={{0,6},{1,7},{2,4},{3,5},{4,2},{5,3},{6,0},{7,1},{8,14},{9,15},{10,... | collective-permute-start | bytes 786440 | tf_op jit(solution)/shard_map/ppermute | solution.py:387
  15.0 17.0 %collective-permute-start.1 = (bf16[2,128,512]{2,1,0:T(8,128)(2,1)S(1)}, bf16[2,128,512]{2,1,0:T(8,128)(2,1)S(1)}, u32[]{:S(2)}, u32[]{:S(2)}) collective-permute-start(bf16[2,128,512]{2,1,0:T(8,128)(2,1)S(1)} %get-tuple-element.51), channel_id=1, source_target_pairs={{0,7},{1,6},{2,5},{3,4},{4,3},{5,2},{6,1},{7,0},{8,15},{9,14},{10,... | collective-permute-start | bytes 786440 | tf_op jit(solution)/shard_map/ppermute | solution.py:387
  33.1 11.0 %collective-permute-start.4 = (bf16[1024,512]{1,0:T(8,128)(2,1)S(1)}, bf16[1024,512]{1,0:T(8,128)(2,1)}, u32[]{:S(2)}, u32[]{:S(2)}) collective-permute-start(bf16[1024,512]{1,0:T(8,128)(2,1)S(1)} %copy-done.5), channel_id=1, source_target_pairs={{0,8},{8,0},{16,24},{24,16},{1,9},{9,1},{17,25},{25,17},{2,10},{10... | collective-permute-start | bytes 3145736 | tf_op jit(solution)/shard_map/ppermute | solution.py:372
  33.1 12.8 %collective-permute-start.5 = (bf16[1024,512]{1,0:T(8,128)(2,1)S(1)}, bf16[1024,512]{1,0:T(8,128)(2,1)}, u32[]{:S(2)}, u32[]{:S(2)}) collective-permute-start(bf16[1024,512]{1,0:T(8,128)(2,1)S(1)} %collective-permute-done.refs_6_), channel_id=1, source_target_pairs={{0,8},{8,0},{16,24},{24,16},{1,9},{9,1},{17,25},{25,17},{2,10},{10... | collective-permute-start | bytes 3145736 | tf_op jit(solution)/shard_map/ppermute | solution.py:372
  33.7 39.6 %collective-permute-start.6 = (bf16[2,128,512]{2,1,0:T(8,128)(2,1)}, bf16[2,128,512]{2,1,0:T(8,128)(2,1)}, u32[]{:S(2)}, u32[]{:S(2)}) collective-permute-start(bf16[2,128,512]{2,1,0:T(8,128)(2,1)} %get-tuple-element.55), channel_id=1, source_target_pairs={{0,2},{1,3},{2,0},{3,1},{4,6},{5,7},{6,4},{7,5},{8,10},{9,11},{10,... | collective-permute-start | bytes 786440 | tf_op jit(solution)/shard_map/ppermute | solution.py:387
  39.4 25.5 %collective-permute-start.7 = (bf16[2,128,512]{2,1,0:T(8,128)(2,1)}, bf16[2,128,512]{2,1,0:T(8,128)(2,1)}, u32[]{:S(2)}, u32[]{:S(2)}) collective-permute-start(bf16[2,128,512]{2,1,0:T(8,128)(2,1)} %get-tuple-element.62), channel_id=1, source_target_pairs={{0,5},{1,4},{2,7},{3,6},{4,1},{5,0},{6,3},{7,2},{8,13},{9,12},{10,... | collective-permute-start | bytes 786440 | tf_op jit(solution)/shard_map/ppermute | solution.py:387
  41.6 23.4 %collective-permute-start.8 = (bf16[2,128,512]{2,1,0:T(8,128)(2,1)}, bf16[2,128,512]{2,1,0:T(8,128)(2,1)}, u32[]{:S(2)}, u32[]{:S(2)}) collective-permute-start(bf16[2,128,512]{2,1,0:T(8,128)(2,1)} %get-tuple-element.63), channel_id=1, source_target_pairs={{0,1},{1,0},{2,3},{3,2},{4,5},{5,4},{6,7},{7,6},{8,9},{9,8},{10,11... | collective-permute-start | bytes 786440 | tf_op jit(solution)/shard_map/ppermute | solution.py:387
  44.1 29.1 %collective-permute-start.9 = (bf16[2,128,512]{2,1,0:T(8,128)(2,1)}, bf16[2,128,512]{2,1,0:T(8,128)(2,1)S(1)}, u32[]{:S(2)}, u32[]{:S(2)}) collective-permute-start(bf16[2,128,512]{2,1,0:T(8,128)(2,1)} %copy-done.14), channel_id=1, source_target_pairs={{0,4},{1,5},{2,6},{3,7},{4,0},{5,1},{6,2},{7,3},{8,12},{9,13},{10,... | collective-permute-start | bytes 786440 | tf_op jit(solution)/shard_map/ppermute | solution.py:387
  54.5 31.5 %collective-permute-start.10 = (bf16[128,512]{1,0:T(8,128)(2,1)S(1)}, bf16[128,512]{1,0:T(8,128)(2,1)S(1)}, u32[]{:S(2)}, u32[]{:S(2)}) collective-permute-start(bf16[128,512]{1,0:T(8,128)(2,1)S(1)} %get-tuple-element.67), channel_id=1, source_target_pairs={{0,7},{1,6},{2,5},{3,4},{4,3},{5,2},{6,1},{7,0},{8,15},{9,14},{10,... | collective-permute-start | bytes 393224 | tf_op jit(solution)/shard_map/ppermute | solution.py:387
  64.9 22.9 %collective-permute-start.11 = (bf16[128,512]{1,0:T(8,128)(2,1)S(1)}, bf16[128,512]{1,0:T(8,128)(2,1)S(1)}, u32[]{:S(2)}, u32[]{:S(2)}) collective-permute-start(bf16[128,512]{1,0:T(8,128)(2,1)S(1)} %get-tuple-element.68), channel_id=1, source_target_pairs={{0,3},{1,2},{2,1},{3,0},{4,7},{5,6},{6,5},{7,4},{8,11},{9,10},{10,... | collective-permute-start | bytes 393224 | tf_op jit(solution)/shard_map/ppermute | solution.py:387
  64.9 22.9 %collective-permute-start.12 = (bf16[128,512]{1,0:T(8,128)(2,1)S(1)}, bf16[128,512]{1,0:T(8,128)(2,1)S(1)}, u32[]{:S(2)}, u32[]{:S(2)}) collective-permute-start(bf16[128,512]{1,0:T(8,128)(2,1)S(1)} %get-tuple-element.69), channel_id=1, source_target_pairs={{0,6},{1,7},{2,4},{3,5},{4,2},{5,3},{6,0},{7,1},{8,14},{9,15},{10,... | collective-permute-start | bytes 393224 | tf_op jit(solution)/shard_map/ppermute | solution.py:387
  73.2 16.6 %collective-permute-start.13 = (bf16[128,512]{1,0:T(8,128)(2,1)S(1)}, bf16[128,512]{1,0:T(8,128)(2,1)S(1)}, u32[]{:S(2)}, u32[]{:S(2)}) collective-permute-start(bf16[128,512]{1,0:T(8,128)(2,1)S(1)} %get-tuple-element.70), channel_id=1, source_target_pairs={{0,2},{1,3},{2,0},{3,1},{4,6},{5,7},{6,4},{7,5},{8,10},{9,11},{10,... | collective-permute-start | bytes 393224 | tf_op jit(solution)/shard_map/ppermute | solution.py:387
  73.2 19.1 %collective-permute-start.14 = (bf16[128,512]{1,0:T(8,128)(2,1)S(1)}, bf16[128,512]{1,0:T(8,128)(2,1)S(1)}, u32[]{:S(2)}, u32[]{:S(2)}) collective-permute-start(bf16[128,512]{1,0:T(8,128)(2,1)S(1)} %get-tuple-element.71), channel_id=1, source_target_pairs={{0,5},{1,4},{2,7},{3,6},{4,1},{5,0},{6,3},{7,2},{8,13},{9,12},{10,... | collective-permute-start | bytes 393224 | tf_op jit(solution)/shard_map/ppermute | solution.py:387
  86.0 7.5 %collective-permute-start.15 = (bf16[128,512]{1,0:T(8,128)(2,1)S(1)}, bf16[128,512]{1,0:T(8,128)(2,1)S(1)}, u32[]{:S(2)}, u32[]{:S(2)}) collective-permute-start(bf16[128,512]{1,0:T(8,128)(2,1)S(1)} %get-tuple-element.74), channel_id=1, source_target_pairs={{0,1},{1,0},{2,3},{3,2},{4,5},{5,4},{6,7},{7,6},{8,9},{9,8},{10,11... | collective-permute-start | bytes 393224 | tf_op jit(solution)/shard_map/ppermute | solution.py:387
  87.9 12.1 %collective-permute-start.16 = (bf16[128,512]{1,0:T(8,128)(2,1)S(1)}, bf16[128,512]{1,0:T(8,128)(2,1)S(1)}, u32[]{:S(2)}, u32[]{:S(2)}) collective-permute-start(bf16[128,512]{1,0:T(8,128)(2,1)S(1)} %get-tuple-element.75), channel_id=1, source_target_pairs={{0,4},{1,5},{2,6},{3,7},{4,0},{5,1},{6,2},{7,3},{8,12},{9,13},{10,... | collective-permute-start | bytes 393224 | tf_op jit(solution)/shard_map/ppermute | solution.py:387
  87.9 27.1 %collective-permute-start.17 = (bf16[128,512]{1,0:T(8,128)(2,1)S(1)}, bf16[128,512]{1,0:T(8,128)(2,1)S(1)}, u32[]{:S(2)}, u32[]{:S(2)}) collective-permute-start(bf16[128,512]{1,0:T(8,128)(2,1)S(1)} %get-tuple-element.78), channel_id=1, source_target_pairs={{0,7},{1,6},{2,5},{3,4},{4,3},{5,2},{6,1},{7,0},{8,15},{9,14},{10,... | collective-permute-start | bytes 393224 | tf_op jit(solution)/shard_map/ppermute | solution.py:387
  89.9 25.1 %collective-permute-start.18 = (bf16[128,512]{1,0:T(8,128)(2,1)S(1)}, bf16[128,512]{1,0:T(8,128)(2,1)S(1)}, u32[]{:S(2)}, u32[]{:S(2)}) collective-permute-start(bf16[128,512]{1,0:T(8,128)(2,1)S(1)} %get-tuple-element.79), channel_id=1, source_target_pairs={{0,3},{1,2},{2,1},{3,0},{4,7},{5,6},{6,5},{7,4},{8,11},{9,10},{10,... | collective-permute-start | bytes 393224 | tf_op jit(solution)/shard_map/ppermute | solution.py:387
  92.3 27.7 %collective-permute-start.19 = (bf16[128,512]{1,0:T(8,128)(2,1)S(1)}, bf16[128,512]{1,0:T(8,128)(2,1)S(1)}, u32[]{:S(2)}, u32[]{:S(2)}) collective-permute-start(bf16[128,512]{1,0:T(8,128)(2,1)S(1)} %get-tuple-element.80), channel_id=1, source_target_pairs={{0,6},{1,7},{2,4},{3,5},{4,2},{5,3},{6,0},{7,1},{8,14},{9,15},{10,... | collective-permute-start | bytes 393224 | tf_op jit(solution)/shard_map/ppermute | solution.py:387
  93.5 27.7 %collective-permute-start.20 = (bf16[128,512]{1,0:T(8,128)(2,1)S(1)}, bf16[128,512]{1,0:T(8,128)(2,1)S(1)}, u32[]{:S(2)}, u32[]{:S(2)}) collective-permute-start(bf16[128,512]{1,0:T(8,128)(2,1)S(1)} %get-tuple-element.81), channel_id=1, source_target_pairs={{0,2},{1,3},{2,0},{3,1},{4,6},{5,7},{6,4},{7,5},{8,10},{9,11},{10,... | collective-permute-start | bytes 393224 | tf_op jit(solution)/shard_map/ppermute | solution.py:387
  114.3 41.3 %copy-start.1 = (bf16[1024,512]{1,0:T(8,128)(2,1)S(1)}, bf16[1024,512]{1,0:T(8,128)(2,1)}, u32[]{:S(2)}) copy-start(bf16[1024,512]{1,0:T(8,128)(2,1)} %param.14) | copy-start | bytes 3145732
  114.3 30.8 %collective-permute-start.27 = (bf16[2,128,512]{2,1,0:T(8,128)(2,1)S(1)}, bf16[2,128,512]{2,1,0:T(8,128)(2,1)S(1)}, u32[]{:S(2)}, u32[]{:S(2)}) collective-permute-start(bf16[2,128,512]{2,1,0:T(8,128)(2,1)S(1)} %get-tuple-element.88), channel_id=1, source_target_pairs={{0,7},{1,6},{2,5},{3,4},{4,3},{5,2},{6,1},{7,0},{8,15},{9,14},{10,... | collective-permute-start | bytes 786440 | tf_op jit(solution)/shard_map/ppermute | solution.py:387
  115.0 32.5 %collective-permute-start.28 = (bf16[2,128,512]{2,1,0:T(8,128)(2,1)S(1)}, bf16[2,128,512]{2,1,0:T(8,128)(2,1)S(1)}, u32[]{:S(2)}, u32[]{:S(2)}) collective-permute-start(bf16[2,128,512]{2,1,0:T(8,128)(2,1)S(1)} %get-tuple-element.89), channel_id=1, source_target_pairs={{0,3},{1,2},{2,1},{3,0},{4,7},{5,6},{6,5},{7,4},{8,11},{9,10},{10,... | collective-permute-start | bytes 786440 | tf_op jit(solution)/shard_map/ppermute | solution.py:387
  115.0 26.3 %collective-permute-start.21 = (bf16[128,512]{1,0:T(8,128)(2,1)S(1)}, bf16[128,512]{1,0:T(8,128)(2,1)S(1)}, u32[]{:S(2)}, u32[]{:S(2)}) collective-permute-start(bf16[128,512]{1,0:T(8,128)(2,1)S(1)} %get-tuple-element.82), channel_id=1, source_target_pairs={{0,5},{1,4},{2,7},{3,6},{4,1},{5,0},{6,3},{7,2},{8,13},{9,12},{10,... | collective-permute-start | bytes 393224 | tf_op jit(solution)/shard_map/ppermute | solution.py:387
  120.0 21.3 %collective-permute-start.22 = (bf16[128,512]{1,0:T(8,128)(2,1)S(1)}, bf16[128,512]{1,0:T(8,128)(2,1)S(1)}, u32[]{:S(2)}, u32[]{:S(2)}) collective-permute-start(bf16[128,512]{1,0:T(8,128)(2,1)S(1)} %get-tuple-element.83), channel_id=1, source_target_pairs={{0,1},{1,0},{2,3},{3,2},{4,5},{5,4},{6,7},{7,6},{8,9},{9,8},{10,11... | collective-permute-start | bytes 393224 | tf_op jit(solution)/shard_map/ppermute | solution.py:387
  121.2 22.4 %collective-permute-start.23 = (bf16[128,512]{1,0:T(8,128)(2,1)S(1)}, bf16[128,512]{1,0:T(8,128)(2,1)S(1)}, u32[]{:S(2)}, u32[]{:S(2)}) collective-permute-start(bf16[128,512]{1,0:T(8,128)(2,1)S(1)} %get-tuple-element.84), channel_id=1, source_target_pairs={{0,4},{1,5},{2,6},{3,7},{4,0},{5,1},{6,2},{7,3},{8,12},{9,13},{10,... | collective-permute-start | bytes 393224 | tf_op jit(solution)/shard_map/ppermute | solution.py:387
  141.2 17.6 %collective-permute-start.24 = (bf16[2,128,512]{2,1,0:T(8,128)(2,1)S(1)}, bf16[2,128,512]{2,1,0:T(8,128)(2,1)S(1)}, u32[]{:S(2)}, u32[]{:S(2)}) collective-permute-start(bf16[2,128,512]{2,1,0:T(8,128)(2,1)S(1)} %get-tuple-element.85), channel_id=1, source_target_pairs={{0,5},{1,4},{2,7},{3,6},{4,1},{5,0},{6,3},{7,2},{8,13},{9,12},{10,... | collective-permute-start | bytes 786440 | tf_op jit(solution)/shard_map/ppermute | solution.py:387
  141.2 9.7 %collective-permute-start.29 = (bf16[2,128,512]{2,1,0:T(8,128)(2,1)S(1)}, bf16[2,128,512]{2,1,0:T(8,128)(2,1)S(1)}, u32[]{:S(2)}, u32[]{:S(2)}) collective-permute-start(bf16[2,128,512]{2,1,0:T(8,128)(2,1)S(1)} %get-tuple-element.90), channel_id=1, source_target_pairs={{0,6},{1,7},{2,4},{3,5},{4,2},{5,3},{6,0},{7,1},{8,14},{9,15},{10,... | collective-permute-start | bytes 786440 | tf_op jit(solution)/shard_map/ppermute | solution.py:387
  143.6 12.0 %collective-permute-start.30 = (bf16[2,128,512]{2,1,0:T(8,128)(2,1)S(1)}, bf16[2,128,512]{2,1,0:T(8,128)(2,1)S(1)}, u32[]{:S(2)}, u32[]{:S(2)}) collective-permute-start(bf16[2,128,512]{2,1,0:T(8,128)(2,1)S(1)} %get-tuple-element.91), channel_id=1, source_target_pairs={{0,2},{1,3},{2,0},{3,1},{4,6},{5,7},{6,4},{7,5},{8,10},{9,11},{10,... | collective-permute-start | bytes 786440 | tf_op jit(solution)/shard_map/ppermute | solution.py:387
  145.1 13.8 %collective-permute-start.25 = (bf16[2,128,512]{2,1,0:T(8,128)(2,1)S(1)}, bf16[2,128,512]{2,1,0:T(8,128)(2,1)S(1)}, u32[]{:S(2)}, u32[]{:S(2)}) collective-permute-start(bf16[2,128,512]{2,1,0:T(8,128)(2,1)S(1)} %get-tuple-element.86), channel_id=1, source_target_pairs={{0,1},{1,0},{2,3},{3,2},{4,5},{5,4},{6,7},{7,6},{8,9},{9,8},{10,11... | collective-permute-start | bytes 786440 | tf_op jit(solution)/shard_map/ppermute | solution.py:387
  147.4 16.6 %collective-permute-start.26 = (bf16[2,128,512]{2,1,0:T(8,128)(2,1)S(1)}, bf16[2,128,512]{2,1,0:T(8,128)(2,1)S(1)}, u32[]{:S(2)}, u32[]{:S(2)}) collective-permute-start(bf16[2,128,512]{2,1,0:T(8,128)(2,1)S(1)} %get-tuple-element.87), channel_id=1, source_target_pairs={{0,4},{1,5},{2,6},{3,7},{4,0},{5,1},{6,2},{7,3},{8,12},{9,13},{10,... | collective-permute-start | bytes 786440 | tf_op jit(solution)/shard_map/ppermute | solution.py:387
  (18 other events, 306.5 us)

commit v7 on v6

--- a/solution.py
+++ b/solution.py
@@ -18,9 +18,7 @@
 
 
 def partners(count):
-    half = count // 2
-    far_near = [d for low in reversed(range(half)) for d in (half + low, low)]
-    return [0] + [d for d in far_near if d]
+    return [0] + list(reversed(range(1, count)))
 
 
 def make_tables(inner, chunks):
@@ -219,7 +217,7 @@
             pltpu.VMEM((count, rows, lanes), F32),
             pltpu.SemaphoreType.DMA((count, 3)),
         ],
-        compiler_params=pltpu.CompilerParams(vmem_limit_bytes=48 * 1024 * 1024),
+        compiler_params=pltpu.CompilerParams(vmem_limit_bytes=62 * 1024 * 1024),
         cost_estimate=pl.CostEstimate(
             flops=8 * count * rows * lanes, bytes_accessed=12 * count * rows * lanes, transcendentals=0
         ),
@@ -363,13 +361,15 @@
 def gather_rest(block, far, other):
     count = lax.axis_size("group")
     bit = count // 2
-    (block, far), _ = lax.optimization_barrier(((block, far), other))
     held = {0: block, bit: far}
     bit //= 2
     while bit:
         pairs = [(g, g ^ bit) for g in range(count)]
         for j in list(held):
-            held[j ^ bit] = lax.ppermute(held[j], "group", pairs)
+            sent = held[j]
+            if j:
+                sent, _ = lax.optimization_barrier((sent, other))
+            held[j ^ bit] = lax.ppermute(sent, "group", pairs)
         bit //= 2
     return [held[j] for j in range(count)]
 

time: 167 us -> 161 us (0.964)
  local copies, waits for them, and re-layouts: 8.85 us -> 3.21 us
  waiting for transfers between devices: 61 us -> 58.5 us
  Pallas kernels: 45.6 us -> 47.3 us
    unnamed x38 -> x18, local copies, waits for them, and re-layouts: 6.9 us -> 1.26 us
    ppermute x28, waiting for transfers between devices: 60.6 us -> 58.5 us  [exchange(): lax.ppermute(part, 'ctx', [(p, p ^ d) for p in range(count)])]
    pallas_call x2, Pallas kernels: 5.08 us -> 6.77 us  [prepare_call(): pl.pallas_call(functools.partial(prepare_kernel, masks, scale), in_specs=...]
    ppermute x28, starting transfers between devices: 46.4 us -> 48.1 us  [exchange(): lax.ppermute(part, 'ctx', [(p, p ^ d) for p in range(count)])]
  transfers between devices with their start and end apart: 31 -> 31, of which waited for: 10 -> 9; matrix products, arithmetic and copies ran while one was open for 1% -> 1% of each run, Pallas kernels for 25% -> 26%
where the time goes in v7:
time: 161 us
  waiting for transfers between devices  58.5 us (36%)
  starting transfers between devices  51.1 us (32%)
  Pallas kernels  47.3 us (29%)
  local copies, waits for them, and re-layouts  3.21 us (2%)
    ppermute x28, waiting for transfers between devices, exchange(): lax.ppermute(part, 'ctx', [(p, p ^ d) for p in range(count)])  58.5 us
    ppermute x28, starting transfers between devices, exchange(): lax.ppermute(part, 'ctx', [(p, p ^ d) for p in range(count)])  48.1 us
    pallas_call x2, Pallas kernels, conv_call(): pl.pallas_call(kernel, grid_spec=pltpu.PrefetchScalarGridSpec(num_scalar_...  24.1 us
    pallas_call x1, Pallas kernels, project_call(): pl.pallas_call(functools.partial(project_kernel, chunks, members), grid_s...  8.49 us
    pallas_call x2, Pallas kernels, prepare_call(): pl.pallas_call(functools.partial(prepare_kernel, masks, scale), in_specs=...  6.77 us
    pallas_call x2, Pallas kernels, finish_call(): pl.pallas_call(functools.partial(finish_kernel, count), grid_spec=pltpu.P...  5.61 us
  transfers between devices with their start and end apart: 31, of which 9 were waited for; matrix products, arithmetic and copies ran while one was open for 1% of the time, Pallas kernels for 26%

profile of v7, /device:TPU:0, one launch (start us, length us, event | category | flops | bytes accessed | tf_op | source)
XLA Modules:
  0.0 160.9 jit_solution(17952931598956182857)
XLA Ops:
  0.6 3.2 %shard_map.156 = (bf16[2,128,512]{2,1,0:T(8,128)(2,1)}, bf16[2,128,512]{2,1,0:T(8,128)(2,1)}, bf16[2,128,512]{2,1,0:T(8,128)(2,1)}) custom-call(bf16[8,128,512]{2,1,0:T(8,128)(2,1)} %bitcast.15, bf16[8,128,512]{2,1,0:T(8,128)(2,1)} %bitcast.25, f32[8,128,512]{2,1,0:T(8,128)} %bitcast.36, f32[8,128]{1,0:T(8,128)} %bitcast.42), custom_call_target="tpu_custom_call" | custom-call | flops 1572864 | bytes 2359296 | tf_op jit(solution)/shard_map/pallas_call | solution.py:209
  3.8 3.0 %collective-permute-start.1 = (bf16[1024,512]{1,0:T(8,128)(2,1)S(1)}, bf16[1024,512]{1,0:T(8,128)(2,1)}, u32[]{:S(2)}, u32[]{:S(2)}) collective-permute-start(bf16[1024,512]{1,0:T(8,128)(2,1)S(1)} %copy-done.2), channel_id=1, source_target_pairs={{0,16},{8,24},{16,0},{24,8},{1,17},{9,25},{17,1},{25,9},{2,18},{10... | collective-permute-start | bytes 3145736 | tf_op jit(solution)/shard_map/ppermute | solution.py:358
  6.8 3.6 %collective-permute-start.3 = (bf16[2,128,512]{2,1,0:T(8,128)(2,1)}, bf16[2,128,512]{2,1,0:T(8,128)(2,1)S(1)}, u32[]{:S(2)}, u32[]{:S(2)}) collective-permute-start(bf16[2,128,512]{2,1,0:T(8,128)(2,1)} %get-tuple-element.52), channel_id=1, source_target_pairs={{0,6},{1,7},{2,4},{3,5},{4,2},{5,3},{6,0},{7,1},{8,14},{9,15},{10,... | collective-permute-start | bytes 786440 | tf_op jit(solution)/shard_map/ppermute | solution.py:387
  10.8 2.4 %collective-permute-start.2 = (bf16[2,128,512]{2,1,0:T(8,128)(2,1)}, bf16[2,128,512]{2,1,0:T(8,128)(2,1)S(1)}, u32[]{:S(2)}, u32[]{:S(2)}) collective-permute-start(bf16[2,128,512]{2,1,0:T(8,128)(2,1)} %get-tuple-element.50), channel_id=1, source_target_pairs={{0,7},{1,6},{2,5},{3,4},{4,3},{5,2},{6,1},{7,0},{8,15},{9,14},{10,... | collective-permute-start | bytes 786440 | tf_op jit(solution)/shard_map/ppermute | solution.py:387
  13.3 3.6 %shard_map.157 = (bf16[2,128,512]{2,1,0:T(8,128)(2,1)}, bf16[2,128,512]{2,1,0:T(8,128)(2,1)}, bf16[2,128,512]{2,1,0:T(8,128)(2,1)}, bf16[2,128,512]{2,1,0:T(8,128)(2,1)}, bf16[2,128,512]{2,1,0:T(8,128)(2,1)}) custom-call(bf16[8,128,512]{2,1,0:T(8,128)(2,1)} %bitcast.16, bf16[8,128,512]{2,1,0:T(8,128)(2,1)} %bitcast.26, f32[8,128,512]{2,1,0:T(8,128)} %bitcast.37, ...), custom_call_target="tpu_custom_call" | custom-call | flops 2621440 | bytes 3932160 | tf_op jit(solution)/shard_map/pallas_call | solution.py:209
  16.9 1.3 collective-permute-done.3.refs_2_
  18.1 22.1 %collective-permute-done.4.refs_3_ = bf16[2,128,512]{2,1,0:T(8,128)(2,1)S(1)} collective-permute-done((bf16[2,128,512]{2,1,0:T(8,128)(2,1)}, bf16[2,128,512]{2,1,0:T(8,128)(2,1)S(1)}, u32[]{:S(2)}, u32[]{:S(2)}) %collective-permute-start.4) | collective-permute-done | bytes 262176 | tf_op jit(solution)/shard_map/ppermute | solution.py:387
  40.3 6.2 %collective-permute-start.6 = (bf16[2,128,512]{2,1,0:T(8,128)(2,1)}, bf16[2,128,512]{2,1,0:T(8,128)(2,1)}, u32[]{:S(2)}, u32[]{:S(2)}) collective-permute-start(bf16[2,128,512]{2,1,0:T(8,128)(2,1)} %get-tuple-element.54), channel_id=1, source_target_pairs={{0,4},{1,5},{2,6},{3,7},{4,0},{5,1},{6,2},{7,3},{8,12},{9,13},{10,... | collective-permute-start | bytes 786440 | tf_op jit(solution)/shard_map/ppermute | solution.py:387
  46.5 2.0 %collective-permute-start.8 = (bf16[2,128,512]{2,1,0:T(8,128)(2,1)}, bf16[2,128,512]{2,1,0:T(8,128)(2,1)}, u32[]{:S(2)}, u32[]{:S(2)}) collective-permute-start(bf16[2,128,512]{2,1,0:T(8,128)(2,1)} %get-tuple-element.61), channel_id=1, source_target_pairs={{0,2},{1,3},{2,0},{3,1},{4,6},{5,7},{6,4},{7,5},{8,10},{9,11},{10,... | collective-permute-start | bytes 786440 | tf_op jit(solution)/shard_map/ppermute | solution.py:387
  50.5 1.6 collective-permute-start.9
  53.3 8.5 %shard_map.158 = (bf16[8,128,512]{2,1,0:T(8,128)(2,1)S(1)}, bf16[128,512]{1,0:T(8,128)(2,1)S(1)}, bf16[128,512]{1,0:T(8,128)(2,1)S(1)}, bf16[128,512]{1,0:T(8,12...) custom-call(s32[2]{0:T(128)S(1)} %pad_add_fusion.me, ...), custom_call_target="tpu_custom_call" | custom-call | flops 4294967296 | bytes 8388608 | tf_op jit(solution)/shard_map/pallas_call | solution.py:333
  61.8 1.4 collective-permute-start.10
  63.2 2.5 %collective-permute-start.11 = (bf16[128,512]{1,0:T(8,128)(2,1)S(1)}, bf16[128,512]{1,0:T(8,128)(2,1)S(1)}, u32[]{:S(2)}, u32[]{:S(2)}) collective-permute-start(bf16[128,512]{1,0:T(8,128)(2,1)S(1)} %get-tuple-element.66), channel_id=1, source_target_pairs={{0,6},{1,7},{2,4},{3,5},{4,2},{5,3},{6,0},{7,1},{8,14},{9,15},{10,... | collective-permute-start | bytes 393224 | tf_op jit(solution)/shard_map/ppermute | solution.py:387
  66.7 2.9 %collective-permute-start.13 = (bf16[128,512]{1,0:T(8,128)(2,1)S(1)}, bf16[128,512]{1,0:T(8,128)(2,1)S(1)}, u32[]{:S(2)}, u32[]{:S(2)}) collective-permute-start(bf16[128,512]{1,0:T(8,128)(2,1)S(1)} %get-tuple-element.68), channel_id=1, source_target_pairs={{0,4},{1,5},{2,6},{3,7},{4,0},{5,1},{6,2},{7,3},{8,12},{9,13},{10,... | collective-permute-start | bytes 393224 | tf_op jit(solution)/shard_map/ppermute | solution.py:387
  69.5 1.5 collective-permute-start.14
  71.1 9.8 %shard_map.159 = (bf16[128,512]{1,0:T(8,128)(2,1)S(1)}, bf16[128,512]{1,0:T(8,128)(2,1)S(1)}, bf16[128,512]{1,0:T(8,128)(2,1)S(1)}, bf16[128,512]{1,0:T(8,128)(2...) custom-call(s32[2]{0:T(128)S(1)} %pad_add_fusion.me, ...), custom_call_target="tpu_custom_call" | custom-call | flops 3221225472 | bytes 4194304 | tf_op jit(solution)/shard_map/pallas_call | solution.py:154
  81.4 1.5 collective-permute-start.16
  83.0 2.6 %collective-permute-done.12.refs_11_ = bf16[128,512]{1,0:T(8,128)(2,1)S(1)} collective-permute-done((bf16[128,512]{1,0:T(8,128)(2,1)S(1)}, bf16[128,512]{1,0:T(8,128)(2,1)S(1)}, u32[]{:S(2)}, u32[]{:S(2)}) %collective-permute-start.12) | collective-permute-done | bytes 131104 | tf_op jit(solution)/shard_map/ppermute | solution.py:387
  85.6 1.5 collective-permute-start.17
  87.4 2.9 %collective-permute-start.18 = (bf16[128,512]{1,0:T(8,128)(2,1)S(1)}, bf16[128,512]{1,0:T(8,128)(2,1)S(1)}, u32[]{:S(2)}, u32[]{:S(2)}) collective-permute-start(bf16[128,512]{1,0:T(8,128)(2,1)S(1)} %get-tuple-element.77), channel_id=1, source_target_pairs={{0,6},{1,7},{2,4},{3,5},{4,2},{5,3},{6,0},{7,1},{8,14},{9,15},{10,... | collective-permute-start | bytes 393224 | tf_op jit(solution)/shard_map/ppermute | solution.py:387
  90.3 2.0 %collective-permute-done.15.refs_14_ = bf16[128,512]{1,0:T(8,128)(2,1)S(1)} collective-permute-done((bf16[128,512]{1,0:T(8,128)(2,1)S(1)}, bf16[128,512]{1,0:T(8,128)(2,1)S(1)}, u32[]{:S(2)}, u32[]{:S(2)}) %collective-permute-start.15) | collective-permute-done | bytes 131104 | tf_op jit(solution)/shard_map/ppermute | solution.py:387
  92.3 1.9 %collective-permute-start.20 = (bf16[128,512]{1,0:T(8,128)(2,1)S(1)}, bf16[128,512]{1,0:T(8,128)(2,1)S(1)}, u32[]{:S(2)}, u32[]{:S(2)}) collective-permute-start(bf16[128,512]{1,0:T(8,128)(2,1)S(1)} %get-tuple-element.79), channel_id=1, source_target_pairs={{0,4},{1,5},{2,6},{3,7},{4,0},{5,1},{6,2},{7,3},{8,12},{9,13},{10,... | collective-permute-start | bytes 393224 | tf_op jit(solution)/shard_map/ppermute | solution.py:387
  94.2 14.2 %shard_map.160 = (bf16[2,128,512]{2,1,0:T(8,128)(2,1)S(1)}, bf16[2,128,512]{2,1,0:T(8,128)(2,1)S(1)}, bf16[2,128,512]{2,1,0:T(8,128)(2,1)S(1)}, bf16[2,128,512]{...) custom-call(s32[2]{0:T(128)S(1)} %pad_add_fusion.me, ...), custom_call_target="tpu_custom_call" | custom-call | flops 5368709120 | bytes 4194304 | tf_op jit(solution)/shard_map/pallas_call | solution.py:154
  109.4 2.9 %collective-permute-start.28 = (bf16[2,128,512]{2,1,0:T(8,128)(2,1)S(1)}, bf16[2,128,512]{2,1,0:T(8,128)(2,1)S(1)}, u32[]{:S(2)}, u32[]{:S(2)}) collective-permute-start(bf16[2,128,512]{2,1,0:T(8,128)(2,1)S(1)} %get-tuple-element.87), channel_id=1, source_target_pairs={{0,6},{1,7},{2,4},{3,5},{4,2},{5,3},{6,0},{7,1},{8,14},{9,15},{10,... | collective-permute-start | bytes 786440 | tf_op jit(solution)/shard_map/ppermute | solution.py:387
  112.3 3.0 %collective-permute-start.22 = (bf16[128,512]{1,0:T(8,128)(2,1)S(1)}, bf16[128,512]{1,0:T(8,128)(2,1)S(1)}, u32[]{:S(2)}, u32[]{:S(2)}) collective-permute-start(bf16[128,512]{1,0:T(8,128)(2,1)S(1)} %get-tuple-element.81), channel_id=1, source_target_pairs={{0,2},{1,3},{2,0},{3,1},{4,6},{5,7},{6,4},{7,5},{8,10},{9,11},{10,... | collective-permute-start | bytes 393224 | tf_op jit(solution)/shard_map/ppermute | solution.py:387
  115.8 10.3 %collective-permute-done.21.refs_5_ = bf16[128,512]{1,0:T(8,128)(2,1)S(1)} collective-permute-done((bf16[128,512]{1,0:T(8,128)(2,1)S(1)}, bf16[128,512]{1,0:T(8,128)(2,1)S(1)}, u32[]{:S(2)}, u32[]{:S(2)}) %collective-permute-start.21) | collective-permute-done | bytes 131104 | tf_op jit(solution)/shard_map/ppermute | solution.py:387
  127.6 4.9 %collective-permute-start.29 = (bf16[2,128,512]{2,1,0:T(8,128)(2,1)S(1)}, bf16[2,128,512]{2,1,0:T(8,128)(2,1)S(1)}, u32[]{:S(2)}, u32[]{:S(2)}) collective-permute-start(bf16[2,128,512]{2,1,0:T(8,128)(2,1)S(1)} %get-tuple-element.88), channel_id=1, source_target_pairs={{0,5},{1,4},{2,7},{3,6},{4,1},{5,0},{6,3},{7,2},{8,13},{9,12},{10,... | collective-permute-start | bytes 786440 | tf_op jit(solution)/shard_map/ppermute | solution.py:387
  134.3 2.3 %shard_map.161 = bf16[8,128,512]{2,1,0:T(8,128)(2,1)} custom-call(s32[2]{0:T(128)S(1)} %pad_add_fusion.me, bf16[8,128,512]{2,1,0:T(8,128)(2,1)S(1)} %get-tuple-element.56.upstream, bf16[128,512]{1,0:T(8,128)(2,1)S(1)} %get-tuple-element.75.refs_0_, bf16[128,512]{1,0:T(8,128)(2,1)S(1)} %collective-permute-done.17.refs_1_, ...), custom_call_target="tpu_custom_call" | custom-call | flops 3145728 | bytes 3145728 | tf_op jit(solution)/shard_map/pallas_call | solution.py:311
  136.6 15.3 %collective-permute-done.29.refs_13_ = bf16[2,128,512]{2,1,0:T(8,128)(2,1)S(1)} collective-permute-done((bf16[2,128,512]{2,1,0:T(8,128)(2,1)S(1)}, bf16[2,128,512]{2,1,0:T(8,128)(2,1)S(1)}, u32[]{:S(2)}, u32[]{:S(2)}) %collective-permute-start.29) | collective-permute-done | bytes 262176 | tf_op jit(solution)/shard_map/ppermute | solution.py:387
  151.9 3.5 %collective-permute-done.30.refs_14_ = bf16[2,128,512]{2,1,0:T(8,128)(2,1)S(1)} collective-permute-done((bf16[2,128,512]{2,1,0:T(8,128)(2,1)S(1)}, bf16[2,128,512]{2,1,0:T(8,128)(2,1)S(1)}, u32[]{:S(2)}, u32[]{:S(2)}) %collective-permute-start.30) | collective-permute-done | bytes 262176 | tf_op jit(solution)/shard_map/ppermute | solution.py:387
  155.3 3.3 %shard_map.162 = (bf16[8,128,512]{2,1,0:T(8,128)(2,1)}, bf16[8,128,512]{2,1,0:T(8,128)(2,1)}, f32[8,128,512]{2,1,0:T(8,128)}) custom-call(s32[2]{0:T(128)S(1)} %pad_add_fusion.me, bf16[8,128,512]{2,1,0:T(8,128)(2,1)S(1)} %bitcast.17, bf16[8,128,512]{2,1,0:T(8,128)(2,1)S(1)} %bitcast.18, bf16[8,128,512]{2,1,0:T(8,128)(2,1)S(1)} %bitcast.19, ...), custom_call_target="tpu_custom_call" | custom-call | flops 655360 | bytes 5242880 | tf_op jit(solution)/shard_map/pallas_call | solution.py:283
  158.6 2.4 %shard_map.163 = (bf16[8,128,512]{2,1,0:T(8,128)(2,1)}, bf16[8,128,512]{2,1,0:T(8,128)(2,1)}, f32[8,128,512]{2,1,0:T(8,128)}) custom-call(s32[2]{0:T(128)S(1)} %pad_add_fusion.me, bf16[8,128,512]{2,1,0:T(8,128)(2,1)S(1)} %bitcast.22, bf16[8,128,512]{2,1,0:T(8,128)(2,1)S(1)} %bitcast.23, ...), custom_call_target="tpu_custom_call", output_to_operand_aliasing={{0}: (10, {}), {1}: (11, {}), {2}: (12, {})} | custom-call | flops 393216 | bytes 3145728 | tf_op jit(solution)/shard_map/pallas_call | solution.py:283
  (59 shorter events, 10.3 us)
Async XLA Ops:
  3.8 36.4 %collective-permute-start.1 = (bf16[1024,512]{1,0:T(8,128)(2,1)S(1)}, bf16[1024,512]{1,0:T(8,128)(2,1)}, u32[]{:S(2)}, u32[]{:S(2)}) collective-permute-start(bf16[1024,512]{1,0:T(8,128)(2,1)S(1)} %copy-done.2), channel_id=1, source_target_pairs={{0,16},{8,24},{16,0},{24,8},{1,17},{9,25},{17,1},{25,9},{2,18},{10... | collective-permute-start | bytes 3145736 | tf_op jit(solution)/shard_map/ppermute | solution.py:358
  6.8 11.3 %collective-permute-start.3 = (bf16[2,128,512]{2,1,0:T(8,128)(2,1)}, bf16[2,128,512]{2,1,0:T(8,128)(2,1)S(1)}, u32[]{:S(2)}, u32[]{:S(2)}) collective-permute-start(bf16[2,128,512]{2,1,0:T(8,128)(2,1)} %get-tuple-element.52), channel_id=1, source_target_pairs={{0,6},{1,7},{2,4},{3,5},{4,2},{5,3},{6,0},{7,1},{8,14},{9,15},{10,... | collective-permute-start | bytes 786440 | tf_op jit(solution)/shard_map/ppermute | solution.py:387
  10.4 29.8 %collective-permute-start.4 = (bf16[2,128,512]{2,1,0:T(8,128)(2,1)}, bf16[2,128,512]{2,1,0:T(8,128)(2,1)S(1)}, u32[]{:S(2)}, u32[]{:S(2)}) collective-permute-start(bf16[2,128,512]{2,1,0:T(8,128)(2,1)} %get-tuple-element.53), channel_id=1, source_target_pairs={{0,5},{1,4},{2,7},{3,6},{4,1},{5,0},{6,3},{7,2},{8,13},{9,12},{10,... | collective-permute-start | bytes 786440 | tf_op jit(solution)/shard_map/ppermute | solution.py:387
  10.8 29.4 %collective-permute-start.2 = (bf16[2,128,512]{2,1,0:T(8,128)(2,1)}, bf16[2,128,512]{2,1,0:T(8,128)(2,1)S(1)}, u32[]{:S(2)}, u32[]{:S(2)}) collective-permute-start(bf16[2,128,512]{2,1,0:T(8,128)(2,1)} %get-tuple-element.50), channel_id=1, source_target_pairs={{0,7},{1,6},{2,5},{3,4},{4,3},{5,2},{6,1},{7,0},{8,15},{9,14},{10,... | collective-permute-start | bytes 786440 | tf_op jit(solution)/shard_map/ppermute | solution.py:387
  13.3 37.2 %collective-permute-start = (bf16[1024,512]{1,0:T(8,128)(2,1)S(1)}, bf16[1024,512]{1,0:T(8,128)(2,1)}, u32[]{:S(2)}, u32[]{:S(2)}) collective-permute-start(bf16[1024,512]{1,0:T(8,128)(2,1)S(1)} %copy-done.2), channel_id=1, source_target_pairs={{0,8},{8,0},{16,24},{24,16},{1,9},{9,1},{17,25},{25,17},{2,10},{10... | collective-permute-start | bytes 3145736 | tf_op jit(solution)/shard_map/ppermute | solution.py:372
  40.3 11.8 %collective-permute-start.5 = (bf16[1024,512]{1,0:T(8,128)(2,1)}, bf16[1024,512]{1,0:T(8,128)(2,1)S(1)}, u32[]{:S(2)}, u32[]{:S(2)}) collective-permute-start(bf16[1024,512]{1,0:T(8,128)(2,1)} %collective-permute-done.1.refs_6_), channel_id=1, source_target_pairs={{0,8},{8,0},{16,24},{24,16},{1,9},{9,1},{17,25},{25,17},{2,10},{10... | collective-permute-start | bytes 3145736 | tf_op jit(solution)/shard_map/ppermute | solution.py:372
  40.3 29.3 %collective-permute-start.6 = (bf16[2,128,512]{2,1,0:T(8,128)(2,1)}, bf16[2,128,512]{2,1,0:T(8,128)(2,1)}, u32[]{:S(2)}, u32[]{:S(2)}) collective-permute-start(bf16[2,128,512]{2,1,0:T(8,128)(2,1)} %get-tuple-element.54), channel_id=1, source_target_pairs={{0,4},{1,5},{2,6},{3,7},{4,0},{5,1},{6,2},{7,3},{8,12},{9,13},{10,... | collective-permute-start | bytes 786440 | tf_op jit(solution)/shard_map/ppermute | solution.py:387
  46.5 16.7 %collective-permute-start.7 = (bf16[2,128,512]{2,1,0:T(8,128)(2,1)}, bf16[2,128,512]{2,1,0:T(8,128)(2,1)}, u32[]{:S(2)}, u32[]{:S(2)}) collective-permute-start(bf16[2,128,512]{2,1,0:T(8,128)(2,1)} %get-tuple-element.60), channel_id=1, source_target_pairs={{0,3},{1,2},{2,1},{3,0},{4,7},{5,6},{6,5},{7,4},{8,11},{9,10},{10,... | collective-permute-start | bytes 786440 | tf_op jit(solution)/shard_map/ppermute | solution.py:387
  46.5 19.2 %collective-permute-start.8 = (bf16[2,128,512]{2,1,0:T(8,128)(2,1)}, bf16[2,128,512]{2,1,0:T(8,128)(2,1)}, u32[]{:S(2)}, u32[]{:S(2)}) collective-permute-start(bf16[2,128,512]{2,1,0:T(8,128)(2,1)} %get-tuple-element.61), channel_id=1, source_target_pairs={{0,2},{1,3},{2,0},{3,1},{4,6},{5,7},{6,4},{7,5},{8,10},{9,11},{10,... | collective-permute-start | bytes 786440 | tf_op jit(solution)/shard_map/ppermute | solution.py:387
  50.5 16.2 %collective-permute-start.9 = (bf16[2,128,512]{2,1,0:T(8,128)(2,1)}, bf16[2,128,512]{2,1,0:T(8,128)(2,1)S(1)}, u32[]{:S(2)}, u32[]{:S(2)}) collective-permute-start(bf16[2,128,512]{2,1,0:T(8,128)(2,1)} %get-tuple-element.62), channel_id=1, source_target_pairs={{0,1},{1,0},{2,3},{3,2},{4,5},{5,4},{6,7},{7,6},{8,9},{9,8},{10,11... | collective-permute-start | bytes 786440 | tf_op jit(solution)/shard_map/ppermute | solution.py:387
  61.8 19.1 %collective-permute-start.10 = (bf16[128,512]{1,0:T(8,128)(2,1)S(1)}, bf16[128,512]{1,0:T(8,128)(2,1)S(1)}, u32[]{:S(2)}, u32[]{:S(2)}) collective-permute-start(bf16[128,512]{1,0:T(8,128)(2,1)S(1)} %get-tuple-element.65), channel_id=1, source_target_pairs={{0,7},{1,6},{2,5},{3,4},{4,3},{5,2},{6,1},{7,0},{8,15},{9,14},{10,... | collective-permute-start | bytes 393224 | tf_op jit(solution)/shard_map/ppermute | solution.py:387
  63.2 18.3 %collective-permute-start.11 = (bf16[128,512]{1,0:T(8,128)(2,1)S(1)}, bf16[128,512]{1,0:T(8,128)(2,1)S(1)}, u32[]{:S(2)}, u32[]{:S(2)}) collective-permute-start(bf16[128,512]{1,0:T(8,128)(2,1)S(1)} %get-tuple-element.66), channel_id=1, source_target_pairs={{0,6},{1,7},{2,4},{3,5},{4,2},{5,3},{6,0},{7,1},{8,14},{9,15},{10,... | collective-permute-start | bytes 393224 | tf_op jit(solution)/shard_map/ppermute | solution.py:387
  65.6 19.9 %collective-permute-start.12 = (bf16[128,512]{1,0:T(8,128)(2,1)S(1)}, bf16[128,512]{1,0:T(8,128)(2,1)S(1)}, u32[]{:S(2)}, u32[]{:S(2)}) collective-permute-start(bf16[128,512]{1,0:T(8,128)(2,1)S(1)} %get-tuple-element.67), channel_id=1, source_target_pairs={{0,5},{1,4},{2,7},{3,6},{4,1},{5,0},{6,3},{7,2},{8,13},{9,12},{10,... | collective-permute-start | bytes 393224 | tf_op jit(solution)/shard_map/ppermute | solution.py:387
  66.7 20.8 %collective-permute-start.13 = (bf16[128,512]{1,0:T(8,128)(2,1)S(1)}, bf16[128,512]{1,0:T(8,128)(2,1)S(1)}, u32[]{:S(2)}, u32[]{:S(2)}) collective-permute-start(bf16[128,512]{1,0:T(8,128)(2,1)S(1)} %get-tuple-element.68), channel_id=1, source_target_pairs={{0,4},{1,5},{2,6},{3,7},{4,0},{5,1},{6,2},{7,3},{8,12},{9,13},{10,... | collective-permute-start | bytes 393224 | tf_op jit(solution)/shard_map/ppermute | solution.py:387
  69.5 20.8 %collective-permute-start.14 = (bf16[128,512]{1,0:T(8,128)(2,1)S(1)}, bf16[128,512]{1,0:T(8,128)(2,1)S(1)}, u32[]{:S(2)}, u32[]{:S(2)}) collective-permute-start(bf16[128,512]{1,0:T(8,128)(2,1)S(1)} %get-tuple-element.69), channel_id=1, source_target_pairs={{0,3},{1,2},{2,1},{3,0},{4,7},{5,6},{6,5},{7,4},{8,11},{9,10},{10,... | collective-permute-start | bytes 393224 | tf_op jit(solution)/shard_map/ppermute | solution.py:387
  80.9 11.4 %collective-permute-start.15 = (bf16[128,512]{1,0:T(8,128)(2,1)S(1)}, bf16[128,512]{1,0:T(8,128)(2,1)S(1)}, u32[]{:S(2)}, u32[]{:S(2)}) collective-permute-start(bf16[128,512]{1,0:T(8,128)(2,1)S(1)} %get-tuple-element.72), channel_id=1, source_target_pairs={{0,2},{1,3},{2,0},{3,1},{4,6},{5,7},{6,4},{7,5},{8,10},{9,11},{10,... | collective-permute-start | bytes 393224 | tf_op jit(solution)/shard_map/ppermute | solution.py:387
  81.4 12.7 %collective-permute-start.16 = (bf16[128,512]{1,0:T(8,128)(2,1)S(1)}, bf16[128,512]{1,0:T(8,128)(2,1)S(1)}, u32[]{:S(2)}, u32[]{:S(2)}) collective-permute-start(bf16[128,512]{1,0:T(8,128)(2,1)S(1)} %get-tuple-element.73), channel_id=1, source_target_pairs={{0,1},{1,0},{2,3},{3,2},{4,5},{5,4},{6,7},{7,6},{8,9},{9,8},{10,11... | collective-permute-start | bytes 393224 | tf_op jit(solution)/shard_map/ppermute | solution.py:387
  85.6 23.9 %collective-permute-start.17 = (bf16[128,512]{1,0:T(8,128)(2,1)S(1)}, bf16[128,512]{1,0:T(8,128)(2,1)S(1)}, u32[]{:S(2)}, u32[]{:S(2)}) collective-permute-start(bf16[128,512]{1,0:T(8,128)(2,1)S(1)} %get-tuple-element.76), channel_id=1, source_target_pairs={{0,7},{1,6},{2,5},{3,4},{4,3},{5,2},{6,1},{7,0},{8,15},{9,14},{10,... | collective-permute-start | bytes 393224 | tf_op jit(solution)/shard_map/ppermute | solution.py:387
  87.4 24.9 %collective-permute-start.18 = (bf16[128,512]{1,0:T(8,128)(2,1)S(1)}, bf16[128,512]{1,0:T(8,128)(2,1)S(1)}, u32[]{:S(2)}, u32[]{:S(2)}) collective-permute-start(bf16[128,512]{1,0:T(8,128)(2,1)S(1)} %get-tuple-element.77), channel_id=1, source_target_pairs={{0,6},{1,7},{2,4},{3,5},{4,2},{5,3},{6,0},{7,1},{8,14},{9,15},{10,... | collective-permute-start | bytes 393224 | tf_op jit(solution)/shard_map/ppermute | solution.py:387
  90.3 22.0 %collective-permute-start.19 = (bf16[128,512]{1,0:T(8,128)(2,1)S(1)}, bf16[128,512]{1,0:T(8,128)(2,1)S(1)}, u32[]{:S(2)}, u32[]{:S(2)}) collective-permute-start(bf16[128,512]{1,0:T(8,128)(2,1)S(1)} %get-tuple-element.78), channel_id=1, source_target_pairs={{0,5},{1,4},{2,7},{3,6},{4,1},{5,0},{6,3},{7,2},{8,13},{9,12},{10,... | collective-permute-start | bytes 393224 | tf_op jit(solution)/shard_map/ppermute | solution.py:387
  92.3 23.0 %collective-permute-start.20 = (bf16[128,512]{1,0:T(8,128)(2,1)S(1)}, bf16[128,512]{1,0:T(8,128)(2,1)S(1)}, u32[]{:S(2)}, u32[]{:S(2)}) collective-permute-start(bf16[128,512]{1,0:T(8,128)(2,1)S(1)} %get-tuple-element.79), channel_id=1, source_target_pairs={{0,4},{1,5},{2,6},{3,7},{4,0},{5,1},{6,2},{7,3},{8,12},{9,13},{10,... | collective-permute-start | bytes 393224 | tf_op jit(solution)/shard_map/ppermute | solution.py:387
  108.5 46.9 %copy-start = (bf16[1024,512]{1,0:T(8,128)(2,1)S(1)}, bf16[1024,512]{1,0:T(8,128)(2,1)}, u32[]{:S(2)}) copy-start(bf16[1024,512]{1,0:T(8,128)(2,1)} %param.14) | copy-start | bytes 3145732
  108.5 24.1 %collective-permute-start.27 = (bf16[2,128,512]{2,1,0:T(8,128)(2,1)S(1)}, bf16[2,128,512]{2,1,0:T(8,128)(2,1)S(1)}, u32[]{:S(2)}, u32[]{:S(2)}) collective-permute-start(bf16[2,128,512]{2,1,0:T(8,128)(2,1)S(1)} %get-tuple-element.86), channel_id=1, source_target_pairs={{0,7},{1,6},{2,5},{3,4},{4,3},{5,2},{6,1},{7,0},{8,15},{9,14},{10,... | collective-permute-start | bytes 786440 | tf_op jit(solution)/shard_map/ppermute | solution.py:387
  109.4 24.3 %collective-permute-start.28 = (bf16[2,128,512]{2,1,0:T(8,128)(2,1)S(1)}, bf16[2,128,512]{2,1,0:T(8,128)(2,1)S(1)}, u32[]{:S(2)}, u32[]{:S(2)}) collective-permute-start(bf16[2,128,512]{2,1,0:T(8,128)(2,1)S(1)} %get-tuple-element.87), channel_id=1, source_target_pairs={{0,6},{1,7},{2,4},{3,5},{4,2},{5,3},{6,0},{7,1},{8,14},{9,15},{10,... | collective-permute-start | bytes 786440 | tf_op jit(solution)/shard_map/ppermute | solution.py:387
  112.3 13.8 %collective-permute-start.21 = (bf16[128,512]{1,0:T(8,128)(2,1)S(1)}, bf16[128,512]{1,0:T(8,128)(2,1)S(1)}, u32[]{:S(2)}, u32[]{:S(2)}) collective-permute-start(bf16[128,512]{1,0:T(8,128)(2,1)S(1)} %get-tuple-element.80), channel_id=1, source_target_pairs={{0,3},{1,2},{2,1},{3,0},{4,7},{5,6},{6,5},{7,4},{8,11},{9,10},{10,... | collective-permute-start | bytes 393224 | tf_op jit(solution)/shard_map/ppermute | solution.py:387
  112.3 15.2 %collective-permute-start.22 = (bf16[128,512]{1,0:T(8,128)(2,1)S(1)}, bf16[128,512]{1,0:T(8,128)(2,1)S(1)}, u32[]{:S(2)}, u32[]{:S(2)}) collective-permute-start(bf16[128,512]{1,0:T(8,128)(2,1)S(1)} %get-tuple-element.81), channel_id=1, source_target_pairs={{0,2},{1,3},{2,0},{3,1},{4,6},{5,7},{6,4},{7,5},{8,10},{9,11},{10,... | collective-permute-start | bytes 393224 | tf_op jit(solution)/shard_map/ppermute | solution.py:387
  115.3 17.2 %collective-permute-start.23 = (bf16[128,512]{1,0:T(8,128)(2,1)S(1)}, bf16[128,512]{1,0:T(8,128)(2,1)S(1)}, u32[]{:S(2)}, u32[]{:S(2)}) collective-permute-start(bf16[128,512]{1,0:T(8,128)(2,1)S(1)} %get-tuple-element.82), channel_id=1, source_target_pairs={{0,1},{1,0},{2,3},{3,2},{4,5},{5,4},{6,7},{7,6},{8,9},{9,8},{10,11... | collective-permute-start | bytes 393224 | tf_op jit(solution)/shard_map/ppermute | solution.py:387
  126.1 32.4 %collective-permute-start.24 = (bf16[2,128,512]{2,1,0:T(8,128)(2,1)S(1)}, bf16[2,128,512]{2,1,0:T(8,128)(2,1)S(1)}, u32[]{:S(2)}, u32[]{:S(2)}) collective-permute-start(bf16[2,128,512]{2,1,0:T(8,128)(2,1)S(1)} %get-tuple-element.83), channel_id=1, source_target_pairs={{0,3},{1,2},{2,1},{3,0},{4,7},{5,6},{6,5},{7,4},{8,11},{9,10},{10,... | collective-permute-start | bytes 786440 | tf_op jit(solution)/shard_map/ppermute | solution.py:387
  127.6 24.3 %collective-permute-start.29 = (bf16[2,128,512]{2,1,0:T(8,128)(2,1)S(1)}, bf16[2,128,512]{2,1,0:T(8,128)(2,1)S(1)}, u32[]{:S(2)}, u32[]{:S(2)}) collective-permute-start(bf16[2,128,512]{2,1,0:T(8,128)(2,1)S(1)} %get-tuple-element.88), channel_id=1, source_target_pairs={{0,5},{1,4},{2,7},{3,6},{4,1},{5,0},{6,3},{7,2},{8,13},{9,12},{10,... | collective-permute-start | bytes 786440 | tf_op jit(solution)/shard_map/ppermute | solution.py:387
  132.5 22.8 %collective-permute-start.30 = (bf16[2,128,512]{2,1,0:T(8,128)(2,1)S(1)}, bf16[2,128,512]{2,1,0:T(8,128)(2,1)S(1)}, u32[]{:S(2)}, u32[]{:S(2)}) collective-permute-start(bf16[2,128,512]{2,1,0:T(8,128)(2,1)S(1)} %get-tuple-element.89), channel_id=1, source_target_pairs={{0,4},{1,5},{2,6},{3,7},{4,0},{5,1},{6,2},{7,3},{8,12},{9,13},{10,... | collective-permute-start | bytes 786440 | tf_op jit(solution)/shard_map/ppermute | solution.py:387
  132.5 26.0 %collective-permute-start.25 = (bf16[2,128,512]{2,1,0:T(8,128)(2,1)S(1)}, bf16[2,128,512]{2,1,0:T(8,128)(2,1)S(1)}, u32[]{:S(2)}, u32[]{:S(2)}) collective-permute-start(bf16[2,128,512]{2,1,0:T(8,128)(2,1)S(1)} %get-tuple-element.84), channel_id=1, source_target_pairs={{0,2},{1,3},{2,0},{3,1},{4,6},{5,7},{6,4},{7,5},{8,10},{9,11},{10,... | collective-permute-start | bytes 786440 | tf_op jit(solution)/shard_map/ppermute | solution.py:387
  133.7 24.9 %collective-permute-start.26 = (bf16[2,128,512]{2,1,0:T(8,128)(2,1)S(1)}, bf16[2,128,512]{2,1,0:T(8,128)(2,1)S(1)}, u32[]{:S(2)}, u32[]{:S(2)}) collective-permute-start(bf16[2,128,512]{2,1,0:T(8,128)(2,1)S(1)} %get-tuple-element.85), channel_id=1, source_target_pairs={{0,1},{1,0},{2,3},{3,2},{4,5},{5,4},{6,7},{7,6},{8,9},{9,8},{10,11... | collective-permute-start | bytes 786440 | tf_op jit(solution)/shard_map/ppermute | solution.py:387
  (8 other events, 140.1 us)

commit v8 on v7

--- a/solution.py
+++ b/solution.py
@@ -415,7 +415,7 @@
     tables = [jnp.asarray(table) for table in make_tables(inner, n_ctx)]
     tables = [table if table.ndim == 2 else table[me[0]] for table in tables]
     masks = partners(n_ctx)
-    first = min(4, n_ctx)
+    first = min(3, n_ctx)
     sources = (scale, split(inner_gate), split(signal), split(filter_taps), split(skip_gain)[:, :, 0])
     head = prepare_call(masks[1:first], *sources)
     cotangent, _ = lax.optimization_barrier((cotangent, head[0]))
@@ -423,6 +423,7 @@
     own, *rest = prepare_call([0] + masks[first:], *sources)
     pair = exchange([own, *head, *rest])
     gathered = gather_rest(cotangent, far, (pair[1:first], rest[:1]))
+    gathered = after(gathered, pair[-3:-1])
     upstream, *grad = project_call(me, out_weight, gathered, split(outer_gate))
     response = conv_call(
         functools.partial(response_kernel, n_ctx, inner), me, (after(pair, grad[0]),), tables, (), inner, 3
@@ -449,10 +450,15 @@
         32,
     )
     outs = []
-    cut = n_ctx - 3
-    for low, high in ((0, cut), (cut, n_ctx)):
+    last = range(3, 5)
+    for part in ([k for k in range(n_ctx) if k not in last], last):
         outs = finish_call(
-            me, masks[low:high], split(inner_gate), split(signal), backs_came[low:high], outs
+            me,
+            [masks[k] for k in part],
+            split(inner_gate),
+            split(signal),
+            [backs_came[k] for k in part],
+            outs,
         )
     grad_inner, grad_signal, grad_taps = outs
     return (flat(grad_outer), flat(grad_inner), flat(grad_signal), flat(grad_taps))

time: 161 us -> 163 us (1.012)
  starting transfers between devices: 51.1 us -> 54.9 us
    ppermute x28, waiting for transfers between devices: 58.5 us -> 50.4 us  [exchange(): lax.ppermute(part, 'ctx', [(p, p ^ d) for p in range(count)])]
    ppermute x1, waiting for transfers between devices: 0.01 us -> 6.75 us  [gather_start(): lax.ppermute(block, 'group', [(g, g ^ count // 2) for g in range(count)])]
    ppermute x28, starting transfers between devices: 48.1 us -> 51.9 us  [exchange(): lax.ppermute(part, 'ctx', [(p, p ^ d) for p in range(count)])]
  transfers between devices with their start and end apart: 31 -> 31, of which waited for: 9 -> 11; matrix products, arithmetic and copies ran while one was open for 1% -> 1% of each run, Pallas kernels for 26% -> 26%
where the time goes in v8:
time: 163 us
  waiting for transfers between devices  57.2 us (35%)
  starting transfers between devices  54.9 us (34%)
  Pallas kernels  46.8 us (29%)
  local copies, waits for them, and re-layouts  3.2 us (2%)
    ppermute x28, starting transfers between devices, exchange(): lax.ppermute(part, 'ctx', [(p, p ^ d) for p in range(count)])  51.9 us
    ppermute x28, waiting for transfers between devices, exchange(): lax.ppermute(part, 'ctx', [(p, p ^ d) for p in range(count)])  50.4 us
    pallas_call x2, Pallas kernels, conv_call(): pl.pallas_call(kernel, grid_spec=pltpu.PrefetchScalarGridSpec(num_scalar_...  24.1 us
    pallas_call x1, Pallas kernels, project_call(): pl.pallas_call(functools.partial(project_kernel, chunks, members), grid_s...  8.49 us
    pallas_call x2, Pallas kernels, prepare_call(): pl.pallas_call(functools.partial(prepare_kernel, masks, scale), in_specs=...  6.75 us
    ppermute x1, waiting for transfers between devices, gather_start(): lax.ppermute(block, 'group', [(g, g ^ count // 2) for g in range(count)])  6.75 us
    pallas_call x2, Pallas kernels, finish_call(): pl.pallas_call(functools.partial(finish_kernel, count), grid_spec=pltpu.P...  5.16 us
  transfers between devices with their start and end apart: 31, of which 11 were waited for; matrix products, arithmetic and copies ran while one was open for 1% of the time, Pallas kernels for 26%

profile of v8, /device:TPU:0, one launch (start us, length us, event | category | flops | bytes accessed | tf_op | source)
XLA Modules:
  0.0 162.9 jit_solution(1186735988477281900)
XLA Ops:
  0.6 2.9 %shard_map.156 = (bf16[2,128,512]{2,1,0:T(8,128)(2,1)}, bf16[2,128,512]{2,1,0:T(8,128)(2,1)}) custom-call(bf16[8,128,512]{2,1,0:T(8,128)(2,1)} %bitcast.15, bf16[8,128,512]{2,1,0:T(8,128)(2,1)} %bitcast.25, f32[8,128,512]{2,1,0:T(8,128)} %bitcast.36, f32[8,128]{1,0:T(8,128)} %bitcast.42), custom_call_target="tpu_custom_call" | custom-call | flops 1048576 | bytes 1572864 | tf_op jit(solution)/shard_map/pallas_call | solution.py:209
  3.5 3.0 %collective-permute-start.3 = (bf16[1024,512]{1,0:T(8,128)(2,1)S(1)}, bf16[1024,512]{1,0:T(8,128)(2,1)}, u32[]{:S(2)}, u32[]{:S(2)}) collective-permute-start(bf16[1024,512]{1,0:T(8,128)(2,1)S(1)} %copy-done.2), channel_id=1, source_target_pairs={{0,16},{8,24},{16,0},{24,8},{1,17},{9,25},{17,1},{25,9},{2,18},{10... | collective-permute-start | bytes 3145736 | tf_op jit(solution)/shard_map/ppermute | solution.py:358
  6.5 3.6 %collective-permute-start.5 = (bf16[2,128,512]{2,1,0:T(8,128)(2,1)}, bf16[2,128,512]{2,1,0:T(8,128)(2,1)S(1)}, u32[]{:S(2)}, u32[]{:S(2)}) collective-permute-start(bf16[2,128,512]{2,1,0:T(8,128)(2,1)} %get-tuple-element.56), channel_id=1, source_target_pairs={{0,6},{1,7},{2,4},{3,5},{4,2},{5,3},{6,0},{7,1},{8,14},{9,15},{10,... | collective-permute-start | bytes 786440 | tf_op jit(solution)/shard_map/ppermute | solution.py:387
  11.3 3.9 %shard_map.157 = (bf16[2,128,512]{2,1,0:T(8,128)(2,1)}, bf16[2,128,512]{2,1,0:T(8,128)(2,1)}, bf16[2,128,512]{2,1,0:T(8,128)(2,1)}, bf16[2,128,512]{2,1,0:T(8,12...) custom-call(bf16[8,128,512]{2,1,0:T(8,128)(2,1)} %bitcast.16, bf16[8,128,512]{2,1,0:T(8,128)(2,1)} %bitcast.26, ...), custom_call_target="tpu_custom_call" | custom-call | flops 3145728 | bytes 4718592 | tf_op jit(solution)/shard_map/pallas_call | solution.py:209
  15.2 2.6 %collective-permute-done.5.refs_2_ = bf16[2,128,512]{2,1,0:T(8,128)(2,1)S(1)} collective-permute-done((bf16[2,128,512]{2,1,0:T(8,128)(2,1)}, bf16[2,128,512]{2,1,0:T(8,128)(2,1)S(1)}, u32[]{:S(2)}, u32[]{:S(2)}) %collective-permute-start.5) | collective-permute-done | bytes 262176 | tf_op jit(solution)/shard_map/ppermute | solution.py:387
  17.8 5.2 %collective-permute-done.4.refs_1_ = bf16[2,128,512]{2,1,0:T(8,128)(2,1)S(1)} collective-permute-done((bf16[2,128,512]{2,1,0:T(8,128)(2,1)}, bf16[2,128,512]{2,1,0:T(8,128)(2,1)S(1)}, u32[]{:S(2)}, u32[]{:S(2)}) %collective-permute-start.4) | collective-permute-done | bytes 262176 | tf_op jit(solution)/shard_map/ppermute | solution.py:387
  23.1 6.7 %collective-permute-done.3.refs_6_ = bf16[1024,512]{1,0:T(8,128)(2,1)} collective-permute-done((bf16[1024,512]{1,0:T(8,128)(2,1)S(1)}, bf16[1024,512]{1,0:T(8,128)(2,1)}, u32[]{:S(2)}, u32[]{:S(2)}) %collective-permute-start.3) | collective-permute-done | bytes 1048608 | tf_op jit(solution)/shard_map/ppermute | solution.py:358
  29.8 5.1 %collective-permute-start.7 = (bf16[2,128,512]{2,1,0:T(8,128)(2,1)}, bf16[2,128,512]{2,1,0:T(8,128)(2,1)S(1)}, u32[]{:S(2)}, u32[]{:S(2)}) collective-permute-start(bf16[2,128,512]{2,1,0:T(8,128)(2,1)} %get-tuple-element.57), channel_id=1, source_target_pairs={{0,5},{1,4},{2,7},{3,6},{4,1},{5,0},{6,3},{7,2},{8,13},{9,12},{10,... | collective-permute-start | bytes 786440 | tf_op jit(solution)/shard_map/ppermute | solution.py:387
  35.1 2.7 %collective-permute-start.1 = (bf16[2,128,512]{2,1,0:T(8,128)(2,1)}, bf16[2,128,512]{2,1,0:T(8,128)(2,1)}, u32[]{:S(2)}, u32[]{:S(2)}) collective-permute-start(bf16[2,128,512]{2,1,0:T(8,128)(2,1)} %get-tuple-element.54), channel_id=1, source_target_pairs={{0,2},{1,3},{2,0},{3,1},{4,6},{5,7},{6,4},{7,5},{8,10},{9,11},{10,... | collective-permute-start | bytes 786440 | tf_op jit(solution)/shard_map/ppermute | solution.py:387
  39.9 8.8 %collective-permute-done.refs_5_ = bf16[2,128,512]{2,1,0:T(8,128)(2,1)} collective-permute-done((bf16[2,128,512]{2,1,0:T(8,128)(2,1)}, bf16[2,128,512]{2,1,0:T(8,128)(2,1)}, u32[]{:S(2)}, u32[]{:S(2)}) %collective-permute-start) | collective-permute-done | bytes 262176 | tf_op jit(solution)/shard_map/ppermute | solution.py:387
  48.7 3.1 %collective-permute-start.8 = (bf16[2,128,512]{2,1,0:T(8,128)(2,1)}, bf16[2,128,512]{2,1,0:T(8,128)(2,1)S(1)}, u32[]{:S(2)}, u32[]{:S(2)}) collective-permute-start(bf16[2,128,512]{2,1,0:T(8,128)(2,1)} %get-tuple-element.63), channel_id=1, source_target_pairs={{0,4},{1,5},{2,6},{3,7},{4,0},{5,1},{6,2},{7,3},{8,12},{9,13},{10,... | collective-permute-start | bytes 786440 | tf_op jit(solution)/shard_map/ppermute | solution.py:387
  51.8 6.2 %collective-permute-done.1.refs_6_ = bf16[2,128,512]{2,1,0:T(8,128)(2,1)} collective-permute-done((bf16[2,128,512]{2,1,0:T(8,128)(2,1)}, bf16[2,128,512]{2,1,0:T(8,128)(2,1)}, u32[]{:S(2)}, u32[]{:S(2)}) %collective-permute-start.1) | collective-permute-done | bytes 262176 | tf_op jit(solution)/shard_map/ppermute | solution.py:387
  59.2 8.5 %shard_map.158 = (bf16[8,128,512]{2,1,0:T(8,128)(2,1)S(1)}, bf16[128,512]{1,0:T(8,128)(2,1)S(1)}, bf16[128,512]{1,0:T(8,128)(2,1)S(1)}, bf16[128,512]{1,0:T(8,12...) custom-call(s32[2]{0:T(128)S(1)} %pad_add_fusion.me, ...), custom_call_target="tpu_custom_call" | custom-call | flops 4294967296 | bytes 8388608 | tf_op jit(solution)/shard_map/pallas_call | solution.py:333
  67.7 2.7 %collective-permute-start.10 = (bf16[128,512]{1,0:T(8,128)(2,1)S(1)}, bf16[128,512]{1,0:T(8,128)(2,1)S(1)}, u32[]{:S(2)}, u32[]{:S(2)}) collective-permute-start(bf16[128,512]{1,0:T(8,128)(2,1)S(1)} %get-tuple-element.67), channel_id=1, source_target_pairs={{0,7},{1,6},{2,5},{3,4},{4,3},{5,2},{6,1},{7,0},{8,15},{9,14},{10,... | collective-permute-start | bytes 393224 | tf_op jit(solution)/shard_map/ppermute | solution.py:387
  70.5 2.6 %collective-permute-start.11 = (bf16[128,512]{1,0:T(8,128)(2,1)S(1)}, bf16[128,512]{1,0:T(8,128)(2,1)S(1)}, u32[]{:S(2)}, u32[]{:S(2)}) collective-permute-start(bf16[128,512]{1,0:T(8,128)(2,1)S(1)} %get-tuple-element.68), channel_id=1, source_target_pairs={{0,6},{1,7},{2,4},{3,5},{4,2},{5,3},{6,0},{7,1},{8,14},{9,15},{10,... | collective-permute-start | bytes 393224 | tf_op jit(solution)/shard_map/ppermute | solution.py:387
  73.1 2.4 %collective-permute-start.13 = (bf16[128,512]{1,0:T(8,128)(2,1)S(1)}, bf16[128,512]{1,0:T(8,128)(2,1)S(1)}, u32[]{:S(2)}, u32[]{:S(2)}) collective-permute-start(bf16[128,512]{1,0:T(8,128)(2,1)S(1)} %get-tuple-element.70), channel_id=1, source_target_pairs={{0,4},{1,5},{2,6},{3,7},{4,0},{5,1},{6,2},{7,3},{8,12},{9,13},{10,... | collective-permute-start | bytes 393224 | tf_op jit(solution)/shard_map/ppermute | solution.py:387
  75.8 9.8 %shard_map.159 = (bf16[128,512]{1,0:T(8,128)(2,1)S(1)}, bf16[128,512]{1,0:T(8,128)(2,1)S(1)}, bf16[128,512]{1,0:T(8,128)(2,1)S(1)}, bf16[128,512]{1,0:T(8,128)(2...) custom-call(s32[2]{0:T(128)S(1)} %pad_add_fusion.me, ...), custom_call_target="tpu_custom_call" | custom-call | flops 3221225472 | bytes 4194304 | tf_op jit(solution)/shard_map/pallas_call | solution.py:154
  85.7 3.2 %collective-permute-start.15 = (bf16[128,512]{1,0:T(8,128)(2,1)S(1)}, bf16[128,512]{1,0:T(8,128)(2,1)S(1)}, u32[]{:S(2)}, u32[]{:S(2)}) collective-permute-start(bf16[128,512]{1,0:T(8,128)(2,1)S(1)} %get-tuple-element.74), channel_id=1, source_target_pairs={{0,2},{1,3},{2,0},{3,1},{4,6},{5,7},{6,4},{7,5},{8,10},{9,11},{10,... | collective-permute-start | bytes 393224 | tf_op jit(solution)/shard_map/ppermute | solution.py:387
  88.9 2.1 %collective-permute-done.12.refs_11_ = bf16[128,512]{1,0:T(8,128)(2,1)S(1)} collective-permute-done((bf16[128,512]{1,0:T(8,128)(2,1)S(1)}, bf16[128,512]{1,0:T(8,128)(2,1)S(1)}, u32[]{:S(2)}, u32[]{:S(2)}) %collective-permute-start.12) | collective-permute-done | bytes 131104 | tf_op jit(solution)/shard_map/ppermute | solution.py:387
  91.0 2.7 %collective-permute-start.17 = (bf16[128,512]{1,0:T(8,128)(2,1)S(1)}, bf16[128,512]{1,0:T(8,128)(2,1)S(1)}, u32[]{:S(2)}, u32[]{:S(2)}) collective-permute-start(bf16[128,512]{1,0:T(8,128)(2,1)S(1)} %get-tuple-element.78), channel_id=1, source_target_pairs={{0,7},{1,6},{2,5},{3,4},{4,3},{5,2},{6,1},{7,0},{8,15},{9,14},{10,... | collective-permute-start | bytes 393224 | tf_op jit(solution)/shard_map/ppermute | solution.py:387
  93.7 7.7 %collective-permute-done.13.refs_12_ = bf16[128,512]{1,0:T(8,128)(2,1)S(1)} collective-permute-done((bf16[128,512]{1,0:T(8,128)(2,1)S(1)}, bf16[128,512]{1,0:T(8,128)(2,1)S(1)}, u32[]{:S(2)}, u32[]{:S(2)}) %collective-permute-start.13) | collective-permute-done | bytes 131104 | tf_op jit(solution)/shard_map/ppermute | solution.py:387
  102.7 14.3 %shard_map.160 = (bf16[2,128,512]{2,1,0:T(8,128)(2,1)S(1)}, bf16[2,128,512]{2,1,0:T(8,128)(2,1)S(1)}, bf16[2,128,512]{2,1,0:T(8,128)(2,1)S(1)}, bf16[2,128,512]{...) custom-call(s32[2]{0:T(128)S(1)} %pad_add_fusion.me, ...), custom_call_target="tpu_custom_call" | custom-call | flops 5368709120 | bytes 4194304 | tf_op jit(solution)/shard_map/pallas_call | solution.py:154
  117.0 6.4 %collective-permute-start.26 = (bf16[2,128,512]{2,1,0:T(8,128)(2,1)S(1)}, bf16[2,128,512]{2,1,0:T(8,128)(2,1)S(1)}, u32[]{:S(2)}, u32[]{:S(2)}) collective-permute-start(bf16[2,128,512]{2,1,0:T(8,128)(2,1)S(1)} %get-tuple-element.87), channel_id=1, source_target_pairs={{0,7},{1,6},{2,5},{3,4},{4,3},{5,2},{6,1},{7,0},{8,15},{9,14},{10,... | collective-permute-start | bytes 786440 | tf_op jit(solution)/shard_map/ppermute | solution.py:387
  125.5 2.6 %collective-permute-start.23 = (bf16[128,512]{1,0:T(8,128)(2,1)S(1)}, bf16[128,512]{1,0:T(8,128)(2,1)S(1)}, u32[]{:S(2)}, u32[]{:S(2)}) collective-permute-start(bf16[128,512]{1,0:T(8,128)(2,1)S(1)} %get-tuple-element.84), channel_id=1, source_target_pairs={{0,1},{1,0},{2,3},{3,2},{4,5},{5,4},{6,7},{7,6},{8,9},{9,8},{10,11... | collective-permute-start | bytes 393224 | tf_op jit(solution)/shard_map/ppermute | solution.py:387
  128.1 9.7 %collective-permute-done.21.refs_5_ = bf16[128,512]{1,0:T(8,128)(2,1)S(1)} collective-permute-done((bf16[128,512]{1,0:T(8,128)(2,1)S(1)}, bf16[128,512]{1,0:T(8,128)(2,1)S(1)}, u32[]{:S(2)}, u32[]{:S(2)}) %collective-permute-start.21) | collective-permute-done | bytes 131104 | tf_op jit(solution)/shard_map/ppermute | solution.py:387
  137.8 3.4 %collective-permute-start.28 = (bf16[2,128,512]{2,1,0:T(8,128)(2,1)S(1)}, bf16[2,128,512]{2,1,0:T(8,128)(2,1)S(1)}, u32[]{:S(2)}, u32[]{:S(2)}) collective-permute-start(bf16[2,128,512]{2,1,0:T(8,128)(2,1)S(1)} %get-tuple-element.89), channel_id=1, source_target_pairs={{0,3},{1,2},{2,1},{3,0},{4,7},{5,6},{6,5},{7,4},{8,11},{9,10},{10,... | collective-permute-start | bytes 786440 | tf_op jit(solution)/shard_map/ppermute | solution.py:387
  143.1 2.0 %collective-permute-start.24 = (bf16[2,128,512]{2,1,0:T(8,128)(2,1)S(1)}, bf16[2,128,512]{2,1,0:T(8,128)(2,1)S(1)}, u32[]{:S(2)}, u32[]{:S(2)}) collective-permute-start(bf16[2,128,512]{2,1,0:T(8,128)(2,1)S(1)} %get-tuple-element.85), channel_id=1, source_target_pairs={{0,5},{1,4},{2,7},{3,6},{4,1},{5,0},{6,3},{7,2},{8,13},{9,12},{10,... | collective-permute-start | bytes 786440 | tf_op jit(solution)/shard_map/ppermute | solution.py:387
  145.1 2.4 %collective-permute-start.25 = (bf16[2,128,512]{2,1,0:T(8,128)(2,1)S(1)}, bf16[2,128,512]{2,1,0:T(8,128)(2,1)S(1)}, u32[]{:S(2)}, u32[]{:S(2)}) collective-permute-start(bf16[2,128,512]{2,1,0:T(8,128)(2,1)S(1)} %get-tuple-element.86), channel_id=1, source_target_pairs={{0,4},{1,5},{2,6},{3,7},{4,0},{5,1},{6,2},{7,3},{8,12},{9,13},{10,... | collective-permute-start | bytes 786440 | tf_op jit(solution)/shard_map/ppermute | solution.py:387
  147.5 2.3 %shard_map.161 = bf16[8,128,512]{2,1,0:T(8,128)(2,1)} custom-call(s32[2]{0:T(128)S(1)} %pad_add_fusion.me, bf16[8,128,512]{2,1,0:T(8,128)(2,1)S(1)} %get-tuple-element.59.upstream, bf16[128,512]{1,0:T(8,128)(2,1)S(1)} %get-tuple-element.77.refs_0_, bf16[128,512]{1,0:T(8,128)(2,1)S(1)} %collective-permute-done.17.refs_1_, ...), custom_call_target="tpu_custom_call" | custom-call | flops 3145728 | bytes 3145728 | tf_op jit(solution)/shard_map/pallas_call | solution.py:311
  149.8 2.5 %collective-permute-done.29.refs_16_ = bf16[2,128,512]{2,1,0:T(8,128)(2,1)S(1)} collective-permute-done((bf16[2,128,512]{2,1,0:T(8,128)(2,1)S(1)}, bf16[2,128,512]{2,1,0:T(8,128)(2,1)S(1)}, u32[]{:S(2)}, u32[]{:S(2)}) %collective-permute-start.29) | collective-permute-done | bytes 262176 | tf_op jit(solution)/shard_map/ppermute | solution.py:387
  152.3 3.5 %shard_map.162 = (bf16[8,128,512]{2,1,0:T(8,128)(2,1)}, bf16[8,128,512]{2,1,0:T(8,128)(2,1)}, f32[8,128,512]{2,1,0:T(8,128)}) custom-call(s32[2]{0:T(128)S(1)} %pad_add_fusion.me, bf16[8,128,512]{2,1,0:T(8,128)(2,1)S(1)} %bitcast.17, bf16[8,128,512]{2,1,0:T(8,128)(2,1)S(1)} %bitcast.18, bf16[8,128,512]{2,1,0:T(8,128)(2,1)S(1)} %bitcast.19, ...), custom_call_target="tpu_custom_call" | custom-call | flops 786432 | bytes 6291456 | tf_op jit(solution)/shard_map/pallas_call | solution.py:283
  157.5 3.8 %collective-permute-done.25.refs_5_ = bf16[2,128,512]{2,1,0:T(8,128)(2,1)S(1)} collective-permute-done((bf16[2,128,512]{2,1,0:T(8,128)(2,1)S(1)}, bf16[2,128,512]{2,1,0:T(8,128)(2,1)S(1)}, u32[]{:S(2)}, u32[]{:S(2)}) %collective-permute-start.25) | collective-permute-done | bytes 262176 | tf_op jit(solution)/shard_map/ppermute | solution.py:387
  (59 shorter events, 13.8 us)
Async XLA Ops:
  3.5 26.3 %collective-permute-start.3 = (bf16[1024,512]{1,0:T(8,128)(2,1)S(1)}, bf16[1024,512]{1,0:T(8,128)(2,1)}, u32[]{:S(2)}, u32[]{:S(2)}) collective-permute-start(bf16[1024,512]{1,0:T(8,128)(2,1)S(1)} %copy-done.2), channel_id=1, source_target_pairs={{0,16},{8,24},{16,0},{24,8},{1,17},{9,25},{17,1},{25,9},{2,18},{10... | collective-permute-start | bytes 3145736 | tf_op jit(solution)/shard_map/ppermute | solution.py:358
  6.5 11.3 %collective-permute-start.5 = (bf16[2,128,512]{2,1,0:T(8,128)(2,1)}, bf16[2,128,512]{2,1,0:T(8,128)(2,1)S(1)}, u32[]{:S(2)}, u32[]{:S(2)}) collective-permute-start(bf16[2,128,512]{2,1,0:T(8,128)(2,1)} %get-tuple-element.56), channel_id=1, source_target_pairs={{0,6},{1,7},{2,4},{3,5},{4,2},{5,3},{6,0},{7,1},{8,14},{9,15},{10,... | collective-permute-start | bytes 786440 | tf_op jit(solution)/shard_map/ppermute | solution.py:387
  10.1 12.9 %collective-permute-start.4 = (bf16[2,128,512]{2,1,0:T(8,128)(2,1)}, bf16[2,128,512]{2,1,0:T(8,128)(2,1)S(1)}, u32[]{:S(2)}, u32[]{:S(2)}) collective-permute-start(bf16[2,128,512]{2,1,0:T(8,128)(2,1)} %get-tuple-element.51), channel_id=1, source_target_pairs={{0,7},{1,6},{2,5},{3,4},{4,3},{5,2},{6,1},{7,0},{8,15},{9,14},{10,... | collective-permute-start | bytes 786440 | tf_op jit(solution)/shard_map/ppermute | solution.py:387
  11.3 46.6 %collective-permute-start.2 = (bf16[1024,512]{1,0:T(8,128)(2,1)S(1)}, bf16[1024,512]{1,0:T(8,128)(2,1)}, u32[]{:S(2)}, u32[]{:S(2)}) collective-permute-start(bf16[1024,512]{1,0:T(8,128)(2,1)S(1)} %copy-done.2), channel_id=1, source_target_pairs={{0,8},{8,0},{16,24},{24,16},{1,9},{9,1},{17,25},{25,17},{2,10},{10... | collective-permute-start | bytes 3145736 | tf_op jit(solution)/shard_map/ppermute | solution.py:372
  29.8 28.2 %collective-permute-start.6 = (bf16[1024,512]{1,0:T(8,128)(2,1)}, bf16[1024,512]{1,0:T(8,128)(2,1)S(1)}, u32[]{:S(2)}, u32[]{:S(2)}) collective-permute-start(bf16[1024,512]{1,0:T(8,128)(2,1)} %collective-permute-done.3.refs_6_), channel_id=1, source_target_pairs={{0,8},{8,0},{16,24},{24,16},{1,9},{9,1},{17,25},{25,17},{2,10},{10... | collective-permute-start | bytes 3145736 | tf_op jit(solution)/shard_map/ppermute | solution.py:372
  29.8 45.6 %collective-permute-start.7 = (bf16[2,128,512]{2,1,0:T(8,128)(2,1)}, bf16[2,128,512]{2,1,0:T(8,128)(2,1)S(1)}, u32[]{:S(2)}, u32[]{:S(2)}) collective-permute-start(bf16[2,128,512]{2,1,0:T(8,128)(2,1)} %get-tuple-element.57), channel_id=1, source_target_pairs={{0,5},{1,4},{2,7},{3,6},{4,1},{5,0},{6,3},{7,2},{8,13},{9,12},{10,... | collective-permute-start | bytes 786440 | tf_op jit(solution)/shard_map/ppermute | solution.py:387
  34.9 13.8 %collective-permute-start = (bf16[2,128,512]{2,1,0:T(8,128)(2,1)}, bf16[2,128,512]{2,1,0:T(8,128)(2,1)}, u32[]{:S(2)}, u32[]{:S(2)}) collective-permute-start(bf16[2,128,512]{2,1,0:T(8,128)(2,1)} %get-tuple-element.53), channel_id=1, source_target_pairs={{0,3},{1,2},{2,1},{3,0},{4,7},{5,6},{6,5},{7,4},{8,11},{9,10},{10,... | collective-permute-start | bytes 786440 | tf_op jit(solution)/shard_map/ppermute | solution.py:387
  35.1 22.8 %collective-permute-start.1 = (bf16[2,128,512]{2,1,0:T(8,128)(2,1)}, bf16[2,128,512]{2,1,0:T(8,128)(2,1)}, u32[]{:S(2)}, u32[]{:S(2)}) collective-permute-start(bf16[2,128,512]{2,1,0:T(8,128)(2,1)} %get-tuple-element.54), channel_id=1, source_target_pairs={{0,2},{1,3},{2,0},{3,1},{4,6},{5,7},{6,4},{7,5},{8,10},{9,11},{10,... | collective-permute-start | bytes 786440 | tf_op jit(solution)/shard_map/ppermute | solution.py:387
  48.7 24.4 %collective-permute-start.8 = (bf16[2,128,512]{2,1,0:T(8,128)(2,1)}, bf16[2,128,512]{2,1,0:T(8,128)(2,1)S(1)}, u32[]{:S(2)}, u32[]{:S(2)}) collective-permute-start(bf16[2,128,512]{2,1,0:T(8,128)(2,1)} %get-tuple-element.63), channel_id=1, source_target_pairs={{0,4},{1,5},{2,6},{3,7},{4,0},{5,1},{6,2},{7,3},{8,12},{9,13},{10,... | collective-permute-start | bytes 786440 | tf_op jit(solution)/shard_map/ppermute | solution.py:387
  58.0 15.1 %collective-permute-start.9 = (bf16[2,128,512]{2,1,0:T(8,128)(2,1)}, bf16[2,128,512]{2,1,0:T(8,128)(2,1)S(1)}, u32[]{:S(2)}, u32[]{:S(2)}) collective-permute-start(bf16[2,128,512]{2,1,0:T(8,128)(2,1)} %get-tuple-element.64), channel_id=1, source_target_pairs={{0,1},{1,0},{2,3},{3,2},{4,5},{5,4},{6,7},{7,6},{8,9},{9,8},{10,11... | collective-permute-start | bytes 786440 | tf_op jit(solution)/shard_map/ppermute | solution.py:387
  67.7 18.0 %collective-permute-start.10 = (bf16[128,512]{1,0:T(8,128)(2,1)S(1)}, bf16[128,512]{1,0:T(8,128)(2,1)S(1)}, u32[]{:S(2)}, u32[]{:S(2)}) collective-permute-start(bf16[128,512]{1,0:T(8,128)(2,1)S(1)} %get-tuple-element.67), channel_id=1, source_target_pairs={{0,7},{1,6},{2,5},{3,4},{4,3},{5,2},{6,1},{7,0},{8,15},{9,14},{10,... | collective-permute-start | bytes 393224 | tf_op jit(solution)/shard_map/ppermute | solution.py:387
  70.5 18.4 %collective-permute-start.11 = (bf16[128,512]{1,0:T(8,128)(2,1)S(1)}, bf16[128,512]{1,0:T(8,128)(2,1)S(1)}, u32[]{:S(2)}, u32[]{:S(2)}) collective-permute-start(bf16[128,512]{1,0:T(8,128)(2,1)S(1)} %get-tuple-element.68), channel_id=1, source_target_pairs={{0,6},{1,7},{2,4},{3,5},{4,2},{5,3},{6,0},{7,1},{8,14},{9,15},{10,... | collective-permute-start | bytes 393224 | tf_op jit(solution)/shard_map/ppermute | solution.py:387
  73.1 17.9 %collective-permute-start.12 = (bf16[128,512]{1,0:T(8,128)(2,1)S(1)}, bf16[128,512]{1,0:T(8,128)(2,1)S(1)}, u32[]{:S(2)}, u32[]{:S(2)}) collective-permute-start(bf16[128,512]{1,0:T(8,128)(2,1)S(1)} %get-tuple-element.69), channel_id=1, source_target_pairs={{0,5},{1,4},{2,7},{3,6},{4,1},{5,0},{6,3},{7,2},{8,13},{9,12},{10,... | collective-permute-start | bytes 393224 | tf_op jit(solution)/shard_map/ppermute | solution.py:387
  73.1 28.3 %collective-permute-start.13 = (bf16[128,512]{1,0:T(8,128)(2,1)S(1)}, bf16[128,512]{1,0:T(8,128)(2,1)S(1)}, u32[]{:S(2)}, u32[]{:S(2)}) collective-permute-start(bf16[128,512]{1,0:T(8,128)(2,1)S(1)} %get-tuple-element.70), channel_id=1, source_target_pairs={{0,4},{1,5},{2,6},{3,7},{4,0},{5,1},{6,2},{7,3},{8,12},{9,13},{10,... | collective-permute-start | bytes 393224 | tf_op jit(solution)/shard_map/ppermute | solution.py:387
  75.5 27.2 %collective-permute-start.14 = (bf16[128,512]{1,0:T(8,128)(2,1)S(1)}, bf16[128,512]{1,0:T(8,128)(2,1)S(1)}, u32[]{:S(2)}, u32[]{:S(2)}) collective-permute-start(bf16[128,512]{1,0:T(8,128)(2,1)S(1)} %get-tuple-element.71), channel_id=1, source_target_pairs={{0,3},{1,2},{2,1},{3,0},{4,7},{5,6},{6,5},{7,4},{8,11},{9,10},{10,... | collective-permute-start | bytes 393224 | tf_op jit(solution)/shard_map/ppermute | solution.py:387
  85.7 16.9 %collective-permute-start.15 = (bf16[128,512]{1,0:T(8,128)(2,1)S(1)}, bf16[128,512]{1,0:T(8,128)(2,1)S(1)}, u32[]{:S(2)}, u32[]{:S(2)}) collective-permute-start(bf16[128,512]{1,0:T(8,128)(2,1)S(1)} %get-tuple-element.74), channel_id=1, source_target_pairs={{0,2},{1,3},{2,0},{3,1},{4,6},{5,7},{6,4},{7,5},{8,10},{9,11},{10,... | collective-permute-start | bytes 393224 | tf_op jit(solution)/shard_map/ppermute | solution.py:387
  88.9 13.8 %collective-permute-start.16 = (bf16[128,512]{1,0:T(8,128)(2,1)S(1)}, bf16[128,512]{1,0:T(8,128)(2,1)S(1)}, u32[]{:S(2)}, u32[]{:S(2)}) collective-permute-start(bf16[128,512]{1,0:T(8,128)(2,1)S(1)} %get-tuple-element.75), channel_id=1, source_target_pairs={{0,1},{1,0},{2,3},{3,2},{4,5},{5,4},{6,7},{7,6},{8,9},{9,8},{10,11... | collective-permute-start | bytes 393224 | tf_op jit(solution)/shard_map/ppermute | solution.py:387
  91.0 32.4 %collective-permute-start.17 = (bf16[128,512]{1,0:T(8,128)(2,1)S(1)}, bf16[128,512]{1,0:T(8,128)(2,1)S(1)}, u32[]{:S(2)}, u32[]{:S(2)}) collective-permute-start(bf16[128,512]{1,0:T(8,128)(2,1)S(1)} %get-tuple-element.78), channel_id=1, source_target_pairs={{0,7},{1,6},{2,5},{3,4},{4,3},{5,2},{6,1},{7,0},{8,15},{9,14},{10,... | collective-permute-start | bytes 393224 | tf_op jit(solution)/shard_map/ppermute | solution.py:387
  101.4 23.2 %collective-permute-start.18 = (bf16[128,512]{1,0:T(8,128)(2,1)S(1)}, bf16[128,512]{1,0:T(8,128)(2,1)S(1)}, u32[]{:S(2)}, u32[]{:S(2)}) collective-permute-start(bf16[128,512]{1,0:T(8,128)(2,1)S(1)} %get-tuple-element.79), channel_id=1, source_target_pairs={{0,6},{1,7},{2,4},{3,5},{4,2},{5,3},{6,0},{7,1},{8,14},{9,15},{10,... | collective-permute-start | bytes 393224 | tf_op jit(solution)/shard_map/ppermute | solution.py:387
  102.6 22.0 %collective-permute-start.19 = (bf16[128,512]{1,0:T(8,128)(2,1)S(1)}, bf16[128,512]{1,0:T(8,128)(2,1)S(1)}, u32[]{:S(2)}, u32[]{:S(2)}) collective-permute-start(bf16[128,512]{1,0:T(8,128)(2,1)S(1)} %get-tuple-element.80), channel_id=1, source_target_pairs={{0,5},{1,4},{2,7},{3,6},{4,1},{5,0},{6,3},{7,2},{8,13},{9,12},{10,... | collective-permute-start | bytes 393224 | tf_op jit(solution)/shard_map/ppermute | solution.py:387
  102.6 22.9 %collective-permute-start.20 = (bf16[128,512]{1,0:T(8,128)(2,1)S(1)}, bf16[128,512]{1,0:T(8,128)(2,1)S(1)}, u32[]{:S(2)}, u32[]{:S(2)}) collective-permute-start(bf16[128,512]{1,0:T(8,128)(2,1)S(1)} %get-tuple-element.81), channel_id=1, source_target_pairs={{0,4},{1,5},{2,6},{3,7},{4,0},{5,1},{6,2},{7,3},{8,12},{9,13},{10,... | collective-permute-start | bytes 393224 | tf_op jit(solution)/shard_map/ppermute | solution.py:387
  117.0 35.3 %copy-start = (bf16[1024,512]{1,0:T(8,128)(2,1)S(1)}, bf16[1024,512]{1,0:T(8,128)(2,1)}, u32[]{:S(2)}) copy-start(bf16[1024,512]{1,0:T(8,128)(2,1)} %param.14) | copy-start | bytes 3145732
  117.0 26.1 %collective-permute-start.26 = (bf16[2,128,512]{2,1,0:T(8,128)(2,1)S(1)}, bf16[2,128,512]{2,1,0:T(8,128)(2,1)S(1)}, u32[]{:S(2)}, u32[]{:S(2)}) collective-permute-start(bf16[2,128,512]{2,1,0:T(8,128)(2,1)S(1)} %get-tuple-element.87), channel_id=1, source_target_pairs={{0,7},{1,6},{2,5},{3,4},{4,3},{5,2},{6,1},{7,0},{8,15},{9,14},{10,... | collective-permute-start | bytes 786440 | tf_op jit(solution)/shard_map/ppermute | solution.py:387
  123.4 21.7 %collective-permute-start.27 = (bf16[2,128,512]{2,1,0:T(8,128)(2,1)S(1)}, bf16[2,128,512]{2,1,0:T(8,128)(2,1)S(1)}, u32[]{:S(2)}, u32[]{:S(2)}) collective-permute-start(bf16[2,128,512]{2,1,0:T(8,128)(2,1)S(1)} %get-tuple-element.88), channel_id=1, source_target_pairs={{0,6},{1,7},{2,4},{3,5},{4,2},{5,3},{6,0},{7,1},{8,14},{9,15},{10,... | collective-permute-start | bytes 786440 | tf_op jit(solution)/shard_map/ppermute | solution.py:387
  124.6 13.2 %collective-permute-start.21 = (bf16[128,512]{1,0:T(8,128)(2,1)S(1)}, bf16[128,512]{1,0:T(8,128)(2,1)S(1)}, u32[]{:S(2)}, u32[]{:S(2)}) collective-permute-start(bf16[128,512]{1,0:T(8,128)(2,1)S(1)} %get-tuple-element.82), channel_id=1, source_target_pairs={{0,3},{1,2},{2,1},{3,0},{4,7},{5,6},{6,5},{7,4},{8,11},{9,10},{10,... | collective-permute-start | bytes 393224 | tf_op jit(solution)/shard_map/ppermute | solution.py:387
  124.6 16.6 %collective-permute-start.22 = (bf16[128,512]{1,0:T(8,128)(2,1)S(1)}, bf16[128,512]{1,0:T(8,128)(2,1)S(1)}, u32[]{:S(2)}, u32[]{:S(2)}) collective-permute-start(bf16[128,512]{1,0:T(8,128)(2,1)S(1)} %get-tuple-element.83), channel_id=1, source_target_pairs={{0,2},{1,3},{2,0},{3,1},{4,6},{5,7},{6,4},{7,5},{8,10},{9,11},{10,... | collective-permute-start | bytes 393224 | tf_op jit(solution)/shard_map/ppermute | solution.py:387
  125.5 17.6 %collective-permute-start.23 = (bf16[128,512]{1,0:T(8,128)(2,1)S(1)}, bf16[128,512]{1,0:T(8,128)(2,1)S(1)}, u32[]{:S(2)}, u32[]{:S(2)}) collective-permute-start(bf16[128,512]{1,0:T(8,128)(2,1)S(1)} %get-tuple-element.84), channel_id=1, source_target_pairs={{0,1},{1,0},{2,3},{3,2},{4,5},{5,4},{6,7},{7,6},{8,9},{9,8},{10,11... | collective-permute-start | bytes 393224 | tf_op jit(solution)/shard_map/ppermute | solution.py:387
  137.8 12.0 %collective-permute-start.28 = (bf16[2,128,512]{2,1,0:T(8,128)(2,1)S(1)}, bf16[2,128,512]{2,1,0:T(8,128)(2,1)S(1)}, u32[]{:S(2)}, u32[]{:S(2)}) collective-permute-start(bf16[2,128,512]{2,1,0:T(8,128)(2,1)S(1)} %get-tuple-element.89), channel_id=1, source_target_pairs={{0,3},{1,2},{2,1},{3,0},{4,7},{5,6},{6,5},{7,4},{8,11},{9,10},{10,... | collective-permute-start | bytes 786440 | tf_op jit(solution)/shard_map/ppermute | solution.py:387
  141.2 11.1 %collective-permute-start.29 = (bf16[2,128,512]{2,1,0:T(8,128)(2,1)S(1)}, bf16[2,128,512]{2,1,0:T(8,128)(2,1)S(1)}, u32[]{:S(2)}, u32[]{:S(2)}) collective-permute-start(bf16[2,128,512]{2,1,0:T(8,128)(2,1)S(1)} %get-tuple-element.90), channel_id=1, source_target_pairs={{0,2},{1,3},{2,0},{3,1},{4,6},{5,7},{6,4},{7,5},{8,10},{9,11},{10,... | collective-permute-start | bytes 786440 | tf_op jit(solution)/shard_map/ppermute | solution.py:387
  143.1 9.2 %collective-permute-start.30 = (bf16[2,128,512]{2,1,0:T(8,128)(2,1)S(1)}, bf16[2,128,512]{2,1,0:T(8,128)(2,1)S(1)}, u32[]{:S(2)}, u32[]{:S(2)}) collective-permute-start(bf16[2,128,512]{2,1,0:T(8,128)(2,1)S(1)} %get-tuple-element.91), channel_id=1, source_target_pairs={{0,1},{1,0},{2,3},{3,2},{4,5},{5,4},{6,7},{7,6},{8,9},{9,8},{10,11... | collective-permute-start | bytes 786440 | tf_op jit(solution)/shard_map/ppermute | solution.py:387
  143.1 14.4 %collective-permute-start.24 = (bf16[2,128,512]{2,1,0:T(8,128)(2,1)S(1)}, bf16[2,128,512]{2,1,0:T(8,128)(2,1)S(1)}, u32[]{:S(2)}, u32[]{:S(2)}) collective-permute-start(bf16[2,128,512]{2,1,0:T(8,128)(2,1)S(1)} %get-tuple-element.85), channel_id=1, source_target_pairs={{0,5},{1,4},{2,7},{3,6},{4,1},{5,0},{6,3},{7,2},{8,13},{9,12},{10,... | collective-permute-start | bytes 786440 | tf_op jit(solution)/shard_map/ppermute | solution.py:387
  145.1 16.2 %collective-permute-start.25 = (bf16[2,128,512]{2,1,0:T(8,128)(2,1)S(1)}, bf16[2,128,512]{2,1,0:T(8,128)(2,1)S(1)}, u32[]{:S(2)}, u32[]{:S(2)}) collective-permute-start(bf16[2,128,512]{2,1,0:T(8,128)(2,1)S(1)} %get-tuple-element.86), channel_id=1, source_target_pairs={{0,4},{1,5},{2,6},{3,7},{4,0},{5,1},{6,2},{7,3},{8,12},{9,13},{10,... | collective-permute-start | bytes 786440 | tf_op jit(solution)/shard_map/ppermute | solution.py:387
  (8 other events, 122.5 us)

commit v9 on v8

--- a/solution.py
+++ b/solution.py
@@ -374,6 +374,10 @@
     return [held[j] for j in range(count)]
 
 
+def send(part, d, count):
+    return lax.ppermute(part, "ctx", [(p, p ^ d) for p in range(count)])
+
+
 def exchange(parts):
     count = len(parts)
     order = partners(count)
@@ -383,10 +387,7 @@
         sent = jnp.take(jnp.take(jnp.stack(parts), where, axis=0), blocks, axis=0)
         came = lax.all_to_all(sent, "ctx", split_axis=0, concat_axis=0, tiled=True)
         return list(jnp.take(jnp.take(came, blocks, axis=0), np.array(order), axis=0))
-    return [parts[0]] + [
-        lax.ppermute(part, "ctx", [(p, p ^ d) for p in range(count)])
-        for d, part in zip(order[1:], parts[1:])
-    ]
+    return [parts[0]] + [send(part, d, count) for d, part in zip(order[1:], parts[1:])]
 
 
 def after(parts, other):
@@ -421,10 +422,20 @@
     cotangent, _ = lax.optimization_barrier((cotangent, head[0]))
     far = gather_start(cotangent)
     own, *rest = prepare_call([0] + masks[first:], *sources)
-    pair = exchange([own, *head, *rest])
-    gathered = gather_rest(cotangent, far, (pair[1:first], rest[:1]))
-    gathered = after(gathered, pair[-3:-1])
+    parts = [own, *head, *rest]
+    held = 4 <= n_ctx <= 8
+    near = slice(n_ctx // 2 + 1, n_ctx - 1)
+    if held:
+        pair = list(parts)
+        for k in (*range(1, near.start), n_ctx - 1):
+            pair[k] = send(parts[k], masks[k], n_ctx)
+    else:
+        pair = exchange(parts)
+    gathered = gather_rest(cotangent, far, (pair[1:first], pair[-1:], rest[:1]))
     upstream, *grad = project_call(me, out_weight, gathered, split(outer_gate))
+    if held:
+        waiting, _ = lax.optimization_barrier((parts[near], grad[0]))
+        pair[near] = [send(part, d, n_ctx) for d, part in zip(masks[near], waiting)]
     response = conv_call(
         functools.partial(response_kernel, n_ctx, inner), me, (after(pair, grad[0]),), tables, (), inner, 3
     )

time: 163 us -> 166 us (1.018)
  local copies, waits for them, and re-layouts: 3.2 us -> 11.7 us
  starting transfers between devices: 54.9 us -> 49.5 us
    unnamed x18 -> x44, local copies, waits for them, and re-layouts: 1.26 us -> 9.76 us
    ppermute x28, starting transfers between devices: 51.9 us -> 46.5 us  [send(): return lax.ppermute(part, 'ctx', [(p, p ^ d) for p in range(count)])]
  transfers between devices with their start and end apart: 31 -> 31, of which waited for: 11 -> 12; matrix products, arithmetic and copies ran while one was open for 1% -> 1% of each run, Pallas kernels for 26% -> 25%
where the time goes in v9:
time: 166 us
  waiting for transfers between devices  56.9 us (34%)
  starting transfers between devices  49.5 us (30%)
  Pallas kernels  46.8 us (28%)
  local copies, waits for them, and re-layouts  11.7 us (7%)
    ppermute x28, waiting for transfers between devices, send(): return lax.ppermute(part, 'ctx', [(p, p ^ d) for p in range(count)])  50.7 us
    ppermute x28, starting transfers between devices, send(): return lax.ppermute(part, 'ctx', [(p, p ^ d) for p in range(count)])  46.5 us
    pallas_call x2, Pallas kernels, conv_call(): pl.pallas_call(kernel, grid_spec=pltpu.PrefetchScalarGridSpec(num_scalar_...  24.1 us
    unnamed x44, local copies, waits for them, and re-layouts  9.76 us
    pallas_call x1, Pallas kernels, project_call(): pl.pallas_call(functools.partial(project_kernel, chunks, members), grid_s...  8.47 us
    pallas_call x2, Pallas kernels, prepare_call(): pl.pallas_call(functools.partial(prepare_kernel, masks, scale), in_specs=...  6.73 us
    ppermute x1, waiting for transfers between devices, gather_start(): lax.ppermute(block, 'group', [(g, g ^ count // 2) for g in range(count)])  6.27 us
    pallas_call x2, Pallas kernels, finish_call(): pl.pallas_call(functools.partial(finish_kernel, count), grid_spec=pltpu.P...  5.16 us
  transfers between devices with their start and end apart: 31, of which 12 were waited for; matrix products, arithmetic and copies ran while one was open for 1% of the time, Pallas kernels for 25%

profile of v9, /device:TPU:0, one launch (start us, length us, event | category | flops | bytes accessed | tf_op | source)
XLA Modules:
  0.0 165.8 jit_solution(13263749167494341126)
XLA Ops:
  0.6 2.9 %shard_map.156 = (bf16[2,128,512]{2,1,0:T(8,128)(2,1)}, bf16[2,128,512]{2,1,0:T(8,128)(2,1)}) custom-call(bf16[8,128,512]{2,1,0:T(8,128)(2,1)} %bitcast.15, bf16[8,128,512]{2,1,0:T(8,128)(2,1)} %bitcast.25, f32[8,128,512]{2,1,0:T(8,128)} %bitcast.36, f32[8,128]{1,0:T(8,128)} %bitcast.42), custom_call_target="tpu_custom_call" | custom-call | flops 1048576 | bytes 1572864 | tf_op jit(solution)/shard_map/pallas_call | solution.py:209
  3.5 3.0 %collective-permute-start.1 = (bf16[1024,512]{1,0:T(8,128)(2,1)S(1)}, bf16[1024,512]{1,0:T(8,128)(2,1)}, u32[]{:S(2)}, u32[]{:S(2)}) collective-permute-start(bf16[1024,512]{1,0:T(8,128)(2,1)S(1)} %copy-done.2), channel_id=1, source_target_pairs={{0,16},{8,24},{16,0},{24,8},{1,17},{9,25},{17,1},{25,9},{2,18},{10... | collective-permute-start | bytes 3145736 | tf_op jit(solution)/shard_map/ppermute | solution.py:358
  6.5 4.6 %collective-permute-start.2 = (bf16[2,128,512]{2,1,0:T(8,128)(2,1)}, bf16[2,128,512]{2,1,0:T(8,128)(2,1)S(1)}, u32[]{:S(2)}, u32[]{:S(2)}) collective-permute-start(bf16[2,128,512]{2,1,0:T(8,128)(2,1)} %get-tuple-element.52), channel_id=1, source_target_pairs={{0,7},{1,6},{2,5},{3,4},{4,3},{5,2},{6,1},{7,0},{8,15},{9,14},{10,... | collective-permute-start | bytes 786440 | tf_op jit(solution)/shard_map/ppermute | solution.py:378
  11.3 3.9 %shard_map.157 = (bf16[2,128,512]{2,1,0:T(8,128)(2,1)}, bf16[2,128,512]{2,1,0:T(8,128)(2,1)}, bf16[2,128,512]{2,1,0:T(8,128)(2,1)}, bf16[2,128,512]{2,1,0:T(8,12...) custom-call(bf16[8,128,512]{2,1,0:T(8,128)(2,1)} %bitcast.16, bf16[8,128,512]{2,1,0:T(8,128)(2,1)} %bitcast.26, ...), custom_call_target="tpu_custom_call" | custom-call | flops 3145728 | bytes 4718592 | tf_op jit(solution)/shard_map/pallas_call | solution.py:209
  15.8 7.2 %collective-permute-done.3.refs_2_ = bf16[2,128,512]{2,1,0:T(8,128)(2,1)S(1)} collective-permute-done((bf16[2,128,512]{2,1,0:T(8,128)(2,1)}, bf16[2,128,512]{2,1,0:T(8,128)(2,1)S(1)}, u32[]{:S(2)}, u32[]{:S(2)}) %collective-permute-start.3) | collective-permute-done | bytes 262176 | tf_op jit(solution)/shard_map/ppermute | solution.py:378
  23.5 6.3 %collective-permute-done.1.refs_6_ = bf16[1024,512]{1,0:T(8,128)(2,1)} collective-permute-done((bf16[1024,512]{1,0:T(8,128)(2,1)S(1)}, bf16[1024,512]{1,0:T(8,128)(2,1)}, u32[]{:S(2)}, u32[]{:S(2)}) %collective-permute-start.1) | collective-permute-done | bytes 1048608 | tf_op jit(solution)/shard_map/ppermute | solution.py:358
  29.8 5.2 %collective-permute-start.6 = (bf16[2,128,512]{2,1,0:T(8,128)(2,1)}, bf16[2,128,512]{2,1,0:T(8,128)(2,1)}, u32[]{:S(2)}, u32[]{:S(2)}) collective-permute-start(bf16[2,128,512]{2,1,0:T(8,128)(2,1)} %get-tuple-element.56), channel_id=1, source_target_pairs={{0,5},{1,4},{2,7},{3,6},{4,1},{5,0},{6,3},{7,2},{8,13},{9,12},{10,... | collective-permute-start | bytes 786440 | tf_op jit(solution)/shard_map/ppermute | solution.py:378
  36.5 8.5 %shard_map.158 = (bf16[8,128,512]{2,1,0:T(8,128)(2,1)S(1)}, bf16[128,512]{1,0:T(8,128)(2,1)S(1)}, bf16[128,512]{1,0:T(8,128)(2,1)S(1)}, bf16[128,512]{1,0:T(8,12...) custom-call(s32[2]{0:T(128)S(1)} %pad_add_fusion.me, ...), custom_call_target="tpu_custom_call" | custom-call | flops 4294967296 | bytes 8388608 | tf_op jit(solution)/shard_map/pallas_call | solution.py:333
  49.8 2.7 %collective-permute-start.8 = (bf16[2,128,512]{2,1,0:T(8,128)(2,1)}, bf16[2,128,512]{2,1,0:T(8,128)(2,1)S(1)}, u32[]{:S(2)}, u32[]{:S(2)}) collective-permute-start(bf16[2,128,512]{2,1,0:T(8,128)(2,1)} %get-tuple-element.65), channel_id=1, source_target_pairs={{0,3},{1,2},{2,1},{3,0},{4,7},{5,6},{6,5},{7,4},{8,11},{9,10},{10,... | collective-permute-start | bytes 786440 | tf_op jit(solution)/shard_map/ppermute | solution.py:378
  54.6 2.5 %collective-permute-start.10 = (bf16[128,512]{1,0:T(8,128)(2,1)}, bf16[128,512]{1,0:T(8,128)(2,1)S(1)}, u32[]{:S(2)}, u32[]{:S(2)}) collective-permute-start(bf16[128,512]{1,0:T(8,128)(2,1)} %copy-done.13), channel_id=1, source_target_pairs={{0,7},{1,6},{2,5},{3,4},{4,3},{5,2},{6,1},{7,0},{8,15},{9,14},{10,... | collective-permute-start | bytes 393224 | tf_op jit(solution)/shard_map/ppermute | solution.py:378
  57.1 2.3 %collective-permute-done.7.refs_4_ = bf16[2,128,512]{2,1,0:T(8,128)(2,1)} collective-permute-done((bf16[2,128,512]{2,1,0:T(8,128)(2,1)}, bf16[2,128,512]{2,1,0:T(8,128)(2,1)}, u32[]{:S(2)}, u32[]{:S(2)}) %collective-permute-start.7) | collective-permute-done | bytes 262176 | tf_op jit(solution)/shard_map/ppermute | solution.py:378
  59.4 2.4 %collective-permute-start.11 = (bf16[128,512]{1,0:T(8,128)(2,1)}, bf16[128,512]{1,0:T(8,128)(2,1)S(1)}, u32[]{:S(2)}, u32[]{:S(2)}) collective-permute-start(bf16[128,512]{1,0:T(8,128)(2,1)} %copy-done.12), channel_id=1, source_target_pairs={{0,6},{1,7},{2,4},{3,5},{4,2},{5,3},{6,0},{7,1},{8,14},{9,15},{10,... | collective-permute-start | bytes 393224 | tf_op jit(solution)/shard_map/ppermute | solution.py:378
  61.8 2.8 %collective-permute-done.8.refs_5_ = bf16[2,128,512]{2,1,0:T(8,128)(2,1)S(1)} collective-permute-done((bf16[2,128,512]{2,1,0:T(8,128)(2,1)}, bf16[2,128,512]{2,1,0:T(8,128)(2,1)S(1)}, u32[]{:S(2)}, u32[]{:S(2)}) %collective-permute-start.8) | collective-permute-done | bytes 262176 | tf_op jit(solution)/shard_map/ppermute | solution.py:378
  65.3 12.3 %collective-permute-done.9.refs_6_ = bf16[2,128,512]{2,1,0:T(8,128)(2,1)S(1)} collective-permute-done((bf16[2,128,512]{2,1,0:T(8,128)(2,1)}, bf16[2,128,512]{2,1,0:T(8,128)(2,1)S(1)}, u32[]{:S(2)}, u32[]{:S(2)}) %collective-permute-start.9) | collective-permute-done | bytes 262176 | tf_op jit(solution)/shard_map/ppermute | solution.py:378
  81.3 9.8 %shard_map.159 = (bf16[128,512]{1,0:T(8,128)(2,1)S(1)}, bf16[128,512]{1,0:T(8,128)(2,1)S(1)}, bf16[128,512]{1,0:T(8,128)(2,1)S(1)}, bf16[128,512]{1,0:T(8,128)(2...) custom-call(s32[2]{0:T(128)S(1)} %pad_add_fusion.me, ...), custom_call_target="tpu_custom_call" | custom-call | flops 3221225472 | bytes 4194304 | tf_op jit(solution)/shard_map/pallas_call | solution.py:154
  91.1 1.8 %collective-permute-start.15 = (bf16[128,512]{1,0:T(8,128)(2,1)S(1)}, bf16[128,512]{1,0:T(8,128)(2,1)S(1)}, u32[]{:S(2)}, u32[]{:S(2)}) collective-permute-start(bf16[128,512]{1,0:T(8,128)(2,1)S(1)} %copy-done.8), channel_id=1, source_target_pairs={{0,2},{1,3},{2,0},{3,1},{4,6},{5,7},{6,4},{7,5},{8,10},{9,11},{10,... | collective-permute-start | bytes 393224 | tf_op jit(solution)/shard_map/ppermute | solution.py:378
  92.9 1.7 %collective-permute-start.16 = (bf16[128,512]{1,0:T(8,128)(2,1)S(1)}, bf16[128,512]{1,0:T(8,128)(2,1)S(1)}, u32[]{:S(2)}, u32[]{:S(2)}) collective-permute-start(bf16[128,512]{1,0:T(8,128)(2,1)S(1)} %get-tuple-element.77), channel_id=1, source_target_pairs={{0,1},{1,0},{2,3},{3,2},{4,5},{5,4},{6,7},{7,6},{8,9},{9,8},{10,11... | collective-permute-start | bytes 393224 | tf_op jit(solution)/shard_map/ppermute | solution.py:378
  96.1 2.1 %collective-permute-start.18 = (bf16[128,512]{1,0:T(8,128)(2,1)S(1)}, bf16[128,512]{1,0:T(8,128)(2,1)S(1)}, u32[]{:S(2)}, u32[]{:S(2)}) collective-permute-start(bf16[128,512]{1,0:T(8,128)(2,1)S(1)} %get-tuple-element.81), channel_id=1, source_target_pairs={{0,6},{1,7},{2,4},{3,5},{4,2},{5,3},{6,0},{7,1},{8,14},{9,15},{10,... | collective-permute-start | bytes 393224 | tf_op jit(solution)/shard_map/ppermute | solution.py:378
  98.2 4.1 %collective-permute-start.20 = (bf16[128,512]{1,0:T(8,128)(2,1)S(1)}, bf16[128,512]{1,0:T(8,128)(2,1)S(1)}, u32[]{:S(2)}, u32[]{:S(2)}) collective-permute-start(bf16[128,512]{1,0:T(8,128)(2,1)S(1)} %get-tuple-element.83), channel_id=1, source_target_pairs={{0,4},{1,5},{2,6},{3,7},{4,0},{5,1},{6,2},{7,3},{8,12},{9,13},{10,... | collective-permute-start | bytes 393224 | tf_op jit(solution)/shard_map/ppermute | solution.py:378
  102.3 14.3 %shard_map.160 = (bf16[2,128,512]{2,1,0:T(8,128)(2,1)S(1)}, bf16[2,128,512]{2,1,0:T(8,128)(2,1)S(1)}, bf16[2,128,512]{2,1,0:T(8,128)(2,1)S(1)}, bf16[2,128,512]{...) custom-call(s32[2]{0:T(128)S(1)} %pad_add_fusion.me, ...), custom_call_target="tpu_custom_call" | custom-call | flops 5368709120 | bytes 4194304 | tf_op jit(solution)/shard_map/pallas_call | solution.py:154
  118.2 2.1 %collective-permute-start.27 = (bf16[2,128,512]{2,1,0:T(8,128)(2,1)S(1)}, bf16[2,128,512]{2,1,0:T(8,128)(2,1)S(1)}, u32[]{:S(2)}, u32[]{:S(2)}) collective-permute-start(bf16[2,128,512]{2,1,0:T(8,128)(2,1)S(1)} %get-tuple-element.90), channel_id=1, source_target_pairs={{0,6},{1,7},{2,4},{3,5},{4,2},{5,3},{6,0},{7,1},{8,14},{9,15},{10,... | collective-permute-start | bytes 786440 | tf_op jit(solution)/shard_map/ppermute | solution.py:378
  120.3 3.2 %collective-permute-start.22 = (bf16[128,512]{1,0:T(8,128)(2,1)S(1)}, bf16[128,512]{1,0:T(8,128)(2,1)S(1)}, u32[]{:S(2)}, u32[]{:S(2)}) collective-permute-start(bf16[128,512]{1,0:T(8,128)(2,1)S(1)} %get-tuple-element.85), channel_id=1, source_target_pairs={{0,2},{1,3},{2,0},{3,1},{4,6},{5,7},{6,4},{7,5},{8,10},{9,11},{10,... | collective-permute-start | bytes 393224 | tf_op jit(solution)/shard_map/ppermute | solution.py:378
  123.5 6.3 %collective-permute-done.20.refs_4_ = bf16[128,512]{1,0:T(8,128)(2,1)S(1)} collective-permute-done((bf16[128,512]{1,0:T(8,128)(2,1)S(1)}, bf16[128,512]{1,0:T(8,128)(2,1)S(1)}, u32[]{:S(2)}, u32[]{:S(2)}) %collective-permute-start.20) | collective-permute-done | bytes 131104 | tf_op jit(solution)/shard_map/ppermute | solution.py:378
  131.1 3.7 %collective-permute-done.21.refs_5_ = bf16[128,512]{1,0:T(8,128)(2,1)S(1)} collective-permute-done((bf16[128,512]{1,0:T(8,128)(2,1)S(1)}, bf16[128,512]{1,0:T(8,128)(2,1)S(1)}, u32[]{:S(2)}, u32[]{:S(2)}) %collective-permute-start.21) | collective-permute-done | bytes 131104 | tf_op jit(solution)/shard_map/ppermute | solution.py:378
  134.8 1.7 %collective-permute-start.28 = (bf16[2,128,512]{2,1,0:T(8,128)(2,1)S(1)}, bf16[2,128,512]{2,1,0:T(8,128)(2,1)S(1)}, u32[]{:S(2)}, u32[]{:S(2)}) collective-permute-start(bf16[2,128,512]{2,1,0:T(8,128)(2,1)S(1)} %get-tuple-element.91), channel_id=1, source_target_pairs={{0,3},{1,2},{2,1},{3,0},{4,7},{5,6},{6,5},{7,4},{8,11},{9,10},{10,... | collective-permute-start | bytes 786440 | tf_op jit(solution)/shard_map/ppermute | solution.py:378
  138.3 4.7 %collective-permute-start.24 = (bf16[2,128,512]{2,1,0:T(8,128)(2,1)S(1)}, bf16[2,128,512]{2,1,0:T(8,128)(2,1)S(1)}, u32[]{:S(2)}, u32[]{:S(2)}) collective-permute-start(bf16[2,128,512]{2,1,0:T(8,128)(2,1)S(1)} %get-tuple-element.87), channel_id=1, source_target_pairs={{0,5},{1,4},{2,7},{3,6},{4,1},{5,0},{6,3},{7,2},{8,13},{9,12},{10,... | collective-permute-start | bytes 786440 | tf_op jit(solution)/shard_map/ppermute | solution.py:378
  143.0 2.3 %shard_map.161 = bf16[8,128,512]{2,1,0:T(8,128)(2,1)} custom-call(s32[2]{0:T(128)S(1)} %pad_add_fusion.me, bf16[8,128,512]{2,1,0:T(8,128)(2,1)S(1)} %copy-done.5, bf16[128,512]{1,0:T(8,128)(2,1)S(1)} %get-tuple-element.79.refs_0_, bf16[128,512]{1,0:T(8,128)(2,1)S(1)} %collective-permute-done.17.refs_1_, ...), custom_call_target="tpu_custom_call" | custom-call | flops 3145728 | bytes 3145728 | tf_op jit(solution)/shard_map/pallas_call | solution.py:311
  145.3 5.1 %collective-permute-done.28.refs_15_ = bf16[2,128,512]{2,1,0:T(8,128)(2,1)S(1)} collective-permute-done((bf16[2,128,512]{2,1,0:T(8,128)(2,1)S(1)}, bf16[2,128,512]{2,1,0:T(8,128)(2,1)S(1)}, u32[]{:S(2)}, u32[]{:S(2)}) %collective-permute-start.28) | collective-permute-done | bytes 262176 | tf_op jit(solution)/shard_map/ppermute | solution.py:378
  150.4 4.8 %collective-permute-done.29.refs_16_ = bf16[2,128,512]{2,1,0:T(8,128)(2,1)S(1)} collective-permute-done((bf16[2,128,512]{2,1,0:T(8,128)(2,1)S(1)}, bf16[2,128,512]{2,1,0:T(8,128)(2,1)S(1)}, u32[]{:S(2)}, u32[]{:S(2)}) %collective-permute-start.29) | collective-permute-done | bytes 262176 | tf_op jit(solution)/shard_map/ppermute | solution.py:378
  155.2 3.5 %shard_map.162 = (bf16[8,128,512]{2,1,0:T(8,128)(2,1)}, bf16[8,128,512]{2,1,0:T(8,128)(2,1)}, f32[8,128,512]{2,1,0:T(8,128)}) custom-call(s32[2]{0:T(128)S(1)} %pad_add_fusion.me, bf16[8,128,512]{2,1,0:T(8,128)(2,1)S(1)} %bitcast.17, bf16[8,128,512]{2,1,0:T(8,128)(2,1)S(1)} %bitcast.18, bf16[8,128,512]{2,1,0:T(8,128)(2,1)S(1)} %bitcast.19, ...), custom_call_target="tpu_custom_call" | custom-call | flops 786432 | bytes 6291456 | tf_op jit(solution)/shard_map/pallas_call | solution.py:283
  158.7 2.7 %collective-permute-done.24.refs_4_ = bf16[2,128,512]{2,1,0:T(8,128)(2,1)S(1)} collective-permute-done((bf16[2,128,512]{2,1,0:T(8,128)(2,1)S(1)}, bf16[2,128,512]{2,1,0:T(8,128)(2,1)S(1)}, u32[]{:S(2)}, u32[]{:S(2)}) %collective-permute-start.24) | collective-permute-done | bytes 262176 | tf_op jit(solution)/shard_map/ppermute | solution.py:378
  161.4 2.7 %collective-permute-done.25.refs_5_ = bf16[2,128,512]{2,1,0:T(8,128)(2,1)S(1)} collective-permute-done((bf16[2,128,512]{2,1,0:T(8,128)(2,1)S(1)}, bf16[2,128,512]{2,1,0:T(8,128)(2,1)S(1)}, u32[]{:S(2)}, u32[]{:S(2)}) %collective-permute-start.25) | collective-permute-done | bytes 262176 | tf_op jit(solution)/shard_map/ppermute | solution.py:378
  (85 shorter events, 21.7 us)
Async XLA Ops:
  3.5 26.3 %collective-permute-start.1 = (bf16[1024,512]{1,0:T(8,128)(2,1)S(1)}, bf16[1024,512]{1,0:T(8,128)(2,1)}, u32[]{:S(2)}, u32[]{:S(2)}) collective-permute-start(bf16[1024,512]{1,0:T(8,128)(2,1)S(1)} %copy-done.2), channel_id=1, source_target_pairs={{0,16},{8,24},{16,0},{24,8},{1,17},{9,25},{17,1},{25,9},{2,18},{10... | collective-permute-start | bytes 3145736 | tf_op jit(solution)/shard_map/ppermute | solution.py:358
  6.5 16.5 %collective-permute-start.2 = (bf16[2,128,512]{2,1,0:T(8,128)(2,1)}, bf16[2,128,512]{2,1,0:T(8,128)(2,1)S(1)}, u32[]{:S(2)}, u32[]{:S(2)}) collective-permute-start(bf16[2,128,512]{2,1,0:T(8,128)(2,1)} %get-tuple-element.52), channel_id=1, source_target_pairs={{0,7},{1,6},{2,5},{3,4},{4,3},{5,2},{6,1},{7,0},{8,15},{9,14},{10,... | collective-permute-start | bytes 786440 | tf_op jit(solution)/shard_map/ppermute | solution.py:378
  11.1 11.9 %collective-permute-start.3 = (bf16[2,128,512]{2,1,0:T(8,128)(2,1)}, bf16[2,128,512]{2,1,0:T(8,128)(2,1)S(1)}, u32[]{:S(2)}, u32[]{:S(2)}) collective-permute-start(bf16[2,128,512]{2,1,0:T(8,128)(2,1)} %get-tuple-element.54), channel_id=1, source_target_pairs={{0,6},{1,7},{2,4},{3,5},{4,2},{5,3},{6,0},{7,1},{8,14},{9,15},{10,... | collective-permute-start | bytes 786440 | tf_op jit(solution)/shard_map/ppermute | solution.py:378
  15.2 8.3 %collective-permute-start.4 = (bf16[2,128,512]{2,1,0:T(8,128)(2,1)}, bf16[2,128,512]{2,1,0:T(8,128)(2,1)S(1)}, u32[]{:S(2)}, u32[]{:S(2)}) collective-permute-start(bf16[2,128,512]{2,1,0:T(8,128)(2,1)} %get-tuple-element.55), channel_id=1, source_target_pairs={{0,1},{1,0},{2,3},{3,2},{4,5},{5,4},{6,7},{7,6},{8,9},{9,8},{10,11... | collective-permute-start | bytes 786440 | tf_op jit(solution)/shard_map/ppermute | solution.py:378
  15.8 19.5 %collective-permute-start = (bf16[1024,512]{1,0:T(8,128)(2,1)S(1)}, bf16[1024,512]{1,0:T(8,128)(2,1)S(1)}, u32[]{:S(2)}, u32[]{:S(2)}) collective-permute-start(bf16[1024,512]{1,0:T(8,128)(2,1)S(1)} %copy-done.2), channel_id=1, source_target_pairs={{0,8},{8,0},{16,24},{24,16},{1,9},{9,1},{17,25},{25,17},{2,10},{10... | collective-permute-start | bytes 3145736 | tf_op jit(solution)/shard_map/ppermute | solution.py:372
  29.8 5.4 %collective-permute-start.5 = (bf16[1024,512]{1,0:T(8,128)(2,1)}, bf16[1024,512]{1,0:T(8,128)(2,1)}, u32[]{:S(2)}, u32[]{:S(2)}) collective-permute-start(bf16[1024,512]{1,0:T(8,128)(2,1)} %collective-permute-done.1.refs_6_), channel_id=1, source_target_pairs={{0,8},{8,0},{16,24},{24,16},{1,9},{9,1},{17,25},{25,17},{2,10},{10... | collective-permute-start | bytes 3145736 | tf_op jit(solution)/shard_map/ppermute | solution.py:372
  29.8 32.0 %collective-permute-start.6 = (bf16[2,128,512]{2,1,0:T(8,128)(2,1)}, bf16[2,128,512]{2,1,0:T(8,128)(2,1)}, u32[]{:S(2)}, u32[]{:S(2)}) collective-permute-start(bf16[2,128,512]{2,1,0:T(8,128)(2,1)} %get-tuple-element.56), channel_id=1, source_target_pairs={{0,5},{1,4},{2,7},{3,6},{4,1},{5,0},{6,3},{7,2},{8,13},{9,12},{10,... | collective-permute-start | bytes 786440 | tf_op jit(solution)/shard_map/ppermute | solution.py:378
  35.0 24.4 %collective-permute-start.7 = (bf16[2,128,512]{2,1,0:T(8,128)(2,1)}, bf16[2,128,512]{2,1,0:T(8,128)(2,1)}, u32[]{:S(2)}, u32[]{:S(2)}) collective-permute-start(bf16[2,128,512]{2,1,0:T(8,128)(2,1)} %get-tuple-element.62), channel_id=1, source_target_pairs={{0,4},{1,5},{2,6},{3,7},{4,0},{5,1},{6,2},{7,3},{8,12},{9,13},{10,... | collective-permute-start | bytes 786440 | tf_op jit(solution)/shard_map/ppermute | solution.py:378
  49.8 14.9 %collective-permute-start.8 = (bf16[2,128,512]{2,1,0:T(8,128)(2,1)}, bf16[2,128,512]{2,1,0:T(8,128)(2,1)S(1)}, u32[]{:S(2)}, u32[]{:S(2)}) collective-permute-start(bf16[2,128,512]{2,1,0:T(8,128)(2,1)} %get-tuple-element.65), channel_id=1, source_target_pairs={{0,3},{1,2},{2,1},{3,0},{4,7},{5,6},{6,5},{7,4},{8,11},{9,10},{10,... | collective-permute-start | bytes 786440 | tf_op jit(solution)/shard_map/ppermute | solution.py:378
  52.5 25.1 %collective-permute-start.9 = (bf16[2,128,512]{2,1,0:T(8,128)(2,1)}, bf16[2,128,512]{2,1,0:T(8,128)(2,1)S(1)}, u32[]{:S(2)}, u32[]{:S(2)}) collective-permute-start(bf16[2,128,512]{2,1,0:T(8,128)(2,1)} %get-tuple-element.66), channel_id=1, source_target_pairs={{0,2},{1,3},{2,0},{3,1},{4,6},{5,7},{6,4},{7,5},{8,10},{9,11},{10,... | collective-permute-start | bytes 786440 | tf_op jit(solution)/shard_map/ppermute | solution.py:378
  54.6 36.5 %collective-permute-start.10 = (bf16[128,512]{1,0:T(8,128)(2,1)}, bf16[128,512]{1,0:T(8,128)(2,1)S(1)}, u32[]{:S(2)}, u32[]{:S(2)}) collective-permute-start(bf16[128,512]{1,0:T(8,128)(2,1)} %copy-done.13), channel_id=1, source_target_pairs={{0,7},{1,6},{2,5},{3,4},{4,3},{5,2},{6,1},{7,0},{8,15},{9,14},{10,... | collective-permute-start | bytes 393224 | tf_op jit(solution)/shard_map/ppermute | solution.py:378
  59.4 33.5 %collective-permute-start.11 = (bf16[128,512]{1,0:T(8,128)(2,1)}, bf16[128,512]{1,0:T(8,128)(2,1)S(1)}, u32[]{:S(2)}, u32[]{:S(2)}) collective-permute-start(bf16[128,512]{1,0:T(8,128)(2,1)} %copy-done.12), channel_id=1, source_target_pairs={{0,6},{1,7},{2,4},{3,5},{4,2},{5,3},{6,0},{7,1},{8,14},{9,15},{10,... | collective-permute-start | bytes 393224 | tf_op jit(solution)/shard_map/ppermute | solution.py:378
  61.8 32.8 %collective-permute-start.12 = (bf16[128,512]{1,0:T(8,128)(2,1)}, bf16[128,512]{1,0:T(8,128)(2,1)S(1)}, u32[]{:S(2)}, u32[]{:S(2)}) collective-permute-start(bf16[128,512]{1,0:T(8,128)(2,1)} %copy-done.11), channel_id=1, source_target_pairs={{0,5},{1,4},{2,7},{3,6},{4,1},{5,0},{6,3},{7,2},{8,13},{9,12},{10,... | collective-permute-start | bytes 393224 | tf_op jit(solution)/shard_map/ppermute | solution.py:378
  64.7 31.4 %collective-permute-start.13 = (bf16[128,512]{1,0:T(8,128)(2,1)}, bf16[128,512]{1,0:T(8,128)(2,1)S(1)}, u32[]{:S(2)}, u32[]{:S(2)}) collective-permute-start(bf16[128,512]{1,0:T(8,128)(2,1)} %copy-done.10), channel_id=1, source_target_pairs={{0,4},{1,5},{2,6},{3,7},{4,0},{5,1},{6,2},{7,3},{8,12},{9,13},{10,... | collective-permute-start | bytes 393224 | tf_op jit(solution)/shard_map/ppermute | solution.py:378
  77.6 20.6 %collective-permute-start.14 = (bf16[128,512]{1,0:T(8,128)(2,1)}, bf16[128,512]{1,0:T(8,128)(2,1)S(1)}, u32[]{:S(2)}, u32[]{:S(2)}) collective-permute-start(bf16[128,512]{1,0:T(8,128)(2,1)} %copy-done.9), channel_id=1, source_target_pairs={{0,3},{1,2},{2,1},{3,0},{4,7},{5,6},{6,5},{7,4},{8,11},{9,10},{10,... | collective-permute-start | bytes 393224 | tf_op jit(solution)/shard_map/ppermute | solution.py:378
  91.1 7.1 %collective-permute-start.15 = (bf16[128,512]{1,0:T(8,128)(2,1)S(1)}, bf16[128,512]{1,0:T(8,128)(2,1)S(1)}, u32[]{:S(2)}, u32[]{:S(2)}) collective-permute-start(bf16[128,512]{1,0:T(8,128)(2,1)S(1)} %copy-done.8), channel_id=1, source_target_pairs={{0,2},{1,3},{2,0},{3,1},{4,6},{5,7},{6,4},{7,5},{8,10},{9,11},{10,... | collective-permute-start | bytes 393224 | tf_op jit(solution)/shard_map/ppermute | solution.py:378
  92.9 9.4 %collective-permute-start.16 = (bf16[128,512]{1,0:T(8,128)(2,1)S(1)}, bf16[128,512]{1,0:T(8,128)(2,1)S(1)}, u32[]{:S(2)}, u32[]{:S(2)}) collective-permute-start(bf16[128,512]{1,0:T(8,128)(2,1)S(1)} %get-tuple-element.77), channel_id=1, source_target_pairs={{0,1},{1,0},{2,3},{3,2},{4,5},{5,4},{6,7},{7,6},{8,9},{9,8},{10,11... | collective-permute-start | bytes 393224 | tf_op jit(solution)/shard_map/ppermute | solution.py:378
  94.6 23.5 %collective-permute-start.17 = (bf16[128,512]{1,0:T(8,128)(2,1)S(1)}, bf16[128,512]{1,0:T(8,128)(2,1)S(1)}, u32[]{:S(2)}, u32[]{:S(2)}) collective-permute-start(bf16[128,512]{1,0:T(8,128)(2,1)S(1)} %get-tuple-element.80), channel_id=1, source_target_pairs={{0,7},{1,6},{2,5},{3,4},{4,3},{5,2},{6,1},{7,0},{8,15},{9,14},{10,... | collective-permute-start | bytes 393224 | tf_op jit(solution)/shard_map/ppermute | solution.py:378
  96.1 24.2 %collective-permute-start.18 = (bf16[128,512]{1,0:T(8,128)(2,1)S(1)}, bf16[128,512]{1,0:T(8,128)(2,1)S(1)}, u32[]{:S(2)}, u32[]{:S(2)}) collective-permute-start(bf16[128,512]{1,0:T(8,128)(2,1)S(1)} %get-tuple-element.81), channel_id=1, source_target_pairs={{0,6},{1,7},{2,4},{3,5},{4,2},{5,3},{6,0},{7,1},{8,14},{9,15},{10,... | collective-permute-start | bytes 393224 | tf_op jit(solution)/shard_map/ppermute | solution.py:378
  98.2 22.1 %collective-permute-start.19 = (bf16[128,512]{1,0:T(8,128)(2,1)S(1)}, bf16[128,512]{1,0:T(8,128)(2,1)S(1)}, u32[]{:S(2)}, u32[]{:S(2)}) collective-permute-start(bf16[128,512]{1,0:T(8,128)(2,1)S(1)} %get-tuple-element.82), channel_id=1, source_target_pairs={{0,5},{1,4},{2,7},{3,6},{4,1},{5,0},{6,3},{7,2},{8,13},{9,12},{10,... | collective-permute-start | bytes 393224 | tf_op jit(solution)/shard_map/ppermute | solution.py:378
  98.2 44.8 %copy-start.5 = (bf16[8,128,512]{2,1,0:T(8,128)(2,1)S(1)}, bf16[8,128,512]{2,1,0:T(8,128)(2,1)}, u32[]{:S(2)}) copy-start(bf16[8,128,512]{2,1,0:T(8,128)(2,1)} %copy-done.4) | copy-start | bytes 3145732
  98.2 31.6 %collective-permute-start.20 = (bf16[128,512]{1,0:T(8,128)(2,1)S(1)}, bf16[128,512]{1,0:T(8,128)(2,1)S(1)}, u32[]{:S(2)}, u32[]{:S(2)}) collective-permute-start(bf16[128,512]{1,0:T(8,128)(2,1)S(1)} %get-tuple-element.83), channel_id=1, source_target_pairs={{0,4},{1,5},{2,6},{3,7},{4,0},{5,1},{6,2},{7,3},{8,12},{9,13},{10,... | collective-permute-start | bytes 393224 | tf_op jit(solution)/shard_map/ppermute | solution.py:378
  116.6 21.7 %collective-permute-start.26 = (bf16[2,128,512]{2,1,0:T(8,128)(2,1)S(1)}, bf16[2,128,512]{2,1,0:T(8,128)(2,1)S(1)}, u32[]{:S(2)}, u32[]{:S(2)}) collective-permute-start(bf16[2,128,512]{2,1,0:T(8,128)(2,1)S(1)} %get-tuple-element.89), channel_id=1, source_target_pairs={{0,7},{1,6},{2,5},{3,4},{4,3},{5,2},{6,1},{7,0},{8,15},{9,14},{10,... | collective-permute-start | bytes 786440 | tf_op jit(solution)/shard_map/ppermute | solution.py:378
  118.2 24.8 %collective-permute-start.27 = (bf16[2,128,512]{2,1,0:T(8,128)(2,1)S(1)}, bf16[2,128,512]{2,1,0:T(8,128)(2,1)S(1)}, u32[]{:S(2)}, u32[]{:S(2)}) collective-permute-start(bf16[2,128,512]{2,1,0:T(8,128)(2,1)S(1)} %get-tuple-element.90), channel_id=1, source_target_pairs={{0,6},{1,7},{2,4},{3,5},{4,2},{5,3},{6,0},{7,1},{8,14},{9,15},{10,... | collective-permute-start | bytes 786440 | tf_op jit(solution)/shard_map/ppermute | solution.py:378
  120.3 14.5 %collective-permute-start.21 = (bf16[128,512]{1,0:T(8,128)(2,1)S(1)}, bf16[128,512]{1,0:T(8,128)(2,1)S(1)}, u32[]{:S(2)}, u32[]{:S(2)}) collective-permute-start(bf16[128,512]{1,0:T(8,128)(2,1)S(1)} %get-tuple-element.84), channel_id=1, source_target_pairs={{0,3},{1,2},{2,1},{3,0},{4,7},{5,6},{6,5},{7,4},{8,11},{9,10},{10,... | collective-permute-start | bytes 393224 | tf_op jit(solution)/shard_map/ppermute | solution.py:378
  120.3 16.3 %collective-permute-start.22 = (bf16[128,512]{1,0:T(8,128)(2,1)S(1)}, bf16[128,512]{1,0:T(8,128)(2,1)S(1)}, u32[]{:S(2)}, u32[]{:S(2)}) collective-permute-start(bf16[128,512]{1,0:T(8,128)(2,1)S(1)} %get-tuple-element.85), channel_id=1, source_target_pairs={{0,2},{1,3},{2,0},{3,1},{4,6},{5,7},{6,4},{7,5},{8,10},{9,11},{10,... | collective-permute-start | bytes 393224 | tf_op jit(solution)/shard_map/ppermute | solution.py:378
  129.8 6.9 %collective-permute-start.23 = (bf16[128,512]{1,0:T(8,128)(2,1)S(1)}, bf16[128,512]{1,0:T(8,128)(2,1)S(1)}, u32[]{:S(2)}, u32[]{:S(2)}) collective-permute-start(bf16[128,512]{1,0:T(8,128)(2,1)S(1)} %get-tuple-element.86), channel_id=1, source_target_pairs={{0,1},{1,0},{2,3},{3,2},{4,5},{5,4},{6,7},{7,6},{8,9},{9,8},{10,11... | collective-permute-start | bytes 393224 | tf_op jit(solution)/shard_map/ppermute | solution.py:378
  134.8 15.5 %collective-permute-start.28 = (bf16[2,128,512]{2,1,0:T(8,128)(2,1)S(1)}, bf16[2,128,512]{2,1,0:T(8,128)(2,1)S(1)}, u32[]{:S(2)}, u32[]{:S(2)}) collective-permute-start(bf16[2,128,512]{2,1,0:T(8,128)(2,1)S(1)} %get-tuple-element.91), channel_id=1, source_target_pairs={{0,3},{1,2},{2,1},{3,0},{4,7},{5,6},{6,5},{7,4},{8,11},{9,10},{10,... | collective-permute-start | bytes 786440 | tf_op jit(solution)/shard_map/ppermute | solution.py:378
  136.6 18.6 %collective-permute-start.29 = (bf16[2,128,512]{2,1,0:T(8,128)(2,1)S(1)}, bf16[2,128,512]{2,1,0:T(8,128)(2,1)S(1)}, u32[]{:S(2)}, u32[]{:S(2)}) collective-permute-start(bf16[2,128,512]{2,1,0:T(8,128)(2,1)S(1)} %get-tuple-element.92), channel_id=1, source_target_pairs={{0,2},{1,3},{2,0},{3,1},{4,6},{5,7},{6,4},{7,5},{8,10},{9,11},{10,... | collective-permute-start | bytes 786440 | tf_op jit(solution)/shard_map/ppermute | solution.py:378
  136.7 18.5 %collective-permute-start.30 = (bf16[2,128,512]{2,1,0:T(8,128)(2,1)S(1)}, bf16[2,128,512]{2,1,0:T(8,128)(2,1)S(1)}, u32[]{:S(2)}, u32[]{:S(2)}) collective-permute-start(bf16[2,128,512]{2,1,0:T(8,128)(2,1)S(1)} %get-tuple-element.93), channel_id=1, source_target_pairs={{0,1},{1,0},{2,3},{3,2},{4,5},{5,4},{6,7},{7,6},{8,9},{9,8},{10,11... | collective-permute-start | bytes 786440 | tf_op jit(solution)/shard_map/ppermute | solution.py:378
  138.3 23.1 %collective-permute-start.24 = (bf16[2,128,512]{2,1,0:T(8,128)(2,1)S(1)}, bf16[2,128,512]{2,1,0:T(8,128)(2,1)S(1)}, u32[]{:S(2)}, u32[]{:S(2)}) collective-permute-start(bf16[2,128,512]{2,1,0:T(8,128)(2,1)S(1)} %get-tuple-element.87), channel_id=1, source_target_pairs={{0,5},{1,4},{2,7},{3,6},{4,1},{5,0},{6,3},{7,2},{8,13},{9,12},{10,... | collective-permute-start | bytes 786440 | tf_op jit(solution)/shard_map/ppermute | solution.py:378
  143.0 21.1 %collective-permute-start.25 = (bf16[2,128,512]{2,1,0:T(8,128)(2,1)S(1)}, bf16[2,128,512]{2,1,0:T(8,128)(2,1)S(1)}, u32[]{:S(2)}, u32[]{:S(2)}) collective-permute-start(bf16[2,128,512]{2,1,0:T(8,128)(2,1)S(1)} %get-tuple-element.88), channel_id=1, source_target_pairs={{0,4},{1,5},{2,6},{3,7},{4,0},{5,1},{6,2},{7,3},{8,12},{9,13},{10,... | collective-permute-start | bytes 786440 | tf_op jit(solution)/shard_map/ppermute | solution.py:378
  (21 other events, 228.6 us)

commit v10 on v8

--- a/solution.py
+++ b/solution.py
@@ -374,6 +374,10 @@
     return [held[j] for j in range(count)]
 
 
+def send(part, d, count):
+    return lax.ppermute(part, "ctx", [(p, p ^ d) for p in range(count)])
+
+
 def exchange(parts):
     count = len(parts)
     order = partners(count)
@@ -383,10 +387,7 @@
         sent = jnp.take(jnp.take(jnp.stack(parts), where, axis=0), blocks, axis=0)
         came = lax.all_to_all(sent, "ctx", split_axis=0, concat_axis=0, tiled=True)
         return list(jnp.take(jnp.take(came, blocks, axis=0), np.array(order), axis=0))
-    return [parts[0]] + [
-        lax.ppermute(part, "ctx", [(p, p ^ d) for p in range(count)])
-        for d, part in zip(order[1:], parts[1:])
-    ]
+    return [parts[0]] + [send(part, d, count) for d, part in zip(order[1:], parts[1:])]
 
 
 def after(parts, other):
@@ -422,8 +423,7 @@
     far = gather_start(cotangent)
     own, *rest = prepare_call([0] + masks[first:], *sources)
     pair = exchange([own, *head, *rest])
-    gathered = gather_rest(cotangent, far, (pair[1:first], rest[:1]))
-    gathered = after(gathered, pair[-3:-1])
+    gathered = gather_rest(cotangent, far, (pair[1:first], pair[-1:], rest[:1]))
     upstream, *grad = project_call(me, out_weight, gathered, split(outer_gate))
     response = conv_call(
         functools.partial(response_kernel, n_ctx, inner), me, (after(pair, grad[0]),), tables, (), inner, 3

time: 163 us -> 155 us (0.951)
  starting transfers between devices: 54.9 us -> 46.7 us
    ppermute x28, starting transfers between devices: 51.9 us -> 43.7 us  [send(): return lax.ppermute(part, 'ctx', [(p, p ^ d) for p in range(count)])]
  transfers between devices with their start and end apart: 31 -> 31, of which waited for: 11 -> 14; matrix products, arithmetic and copies ran while one was open for 1% -> 1% of each run, Pallas kernels for 26% -> 27%
where the time goes in v10:
time: 155 us
  waiting for transfers between devices  57.2 us (37%)
  Pallas kernels  46.7 us (30%)
  starting transfers between devices  46.7 us (30%)
  local copies, waits for them, and re-layouts  3.21 us (2%)
    ppermute x28, waiting for transfers between devices, send(): return lax.ppermute(part, 'ctx', [(p, p ^ d) for p in range(count)])  50.9 us
    ppermute x28, starting transfers between devices, send(): return lax.ppermute(part, 'ctx', [(p, p ^ d) for p in range(count)])  43.7 us
    pallas_call x2, Pallas kernels, conv_call(): pl.pallas_call(kernel, grid_spec=pltpu.PrefetchScalarGridSpec(num_scalar_...  24.1 us
    pallas_call x1, Pallas kernels, project_call(): pl.pallas_call(functools.partial(project_kernel, chunks, members), grid_s...  8.49 us
    pallas_call x2, Pallas kernels, prepare_call(): pl.pallas_call(functools.partial(prepare_kernel, masks, scale), in_specs=...  6.75 us
    ppermute x1, waiting for transfers between devices, gather_start(): lax.ppermute(block, 'group', [(g, g ^ count // 2) for g in range(count)])  6.26 us
    pallas_call x2, Pallas kernels, finish_call(): pl.pallas_call(functools.partial(finish_kernel, count), grid_spec=pltpu.P...  5.14 us
  transfers between devices with their start and end apart: 31, of which 14 were waited for; matrix products, arithmetic and copies ran while one was open for 1% of the time, Pallas kernels for 27%

profile of v10, /device:TPU:0, one launch (start us, length us, event | category | flops | bytes accessed | tf_op | source)
XLA Modules:
  0.0 154.6 jit_solution(3407053726147485792)
XLA Ops:
  0.6 2.9 %shard_map.156 = (bf16[2,128,512]{2,1,0:T(8,128)(2,1)}, bf16[2,128,512]{2,1,0:T(8,128)(2,1)}) custom-call(bf16[8,128,512]{2,1,0:T(8,128)(2,1)} %bitcast.15, bf16[8,128,512]{2,1,0:T(8,128)(2,1)} %bitcast.25, f32[8,128,512]{2,1,0:T(8,128)} %bitcast.36, f32[8,128]{1,0:T(8,128)} %bitcast.42), custom_call_target="tpu_custom_call" | custom-call | flops 1048576 | bytes 1572864 | tf_op jit(solution)/shard_map/pallas_call | solution.py:209
  3.5 3.0 %collective-permute-start.1 = (bf16[1024,512]{1,0:T(8,128)(2,1)S(1)}, bf16[1024,512]{1,0:T(8,128)(2,1)}, u32[]{:S(2)}, u32[]{:S(2)}) collective-permute-start(bf16[1024,512]{1,0:T(8,128)(2,1)S(1)} %copy-done.2), channel_id=1, source_target_pairs={{0,16},{8,24},{16,0},{24,8},{1,17},{9,25},{17,1},{25,9},{2,18},{10... | collective-permute-start | bytes 3145736 | tf_op jit(solution)/shard_map/ppermute | solution.py:358
  6.5 4.6 %collective-permute-start.2 = (bf16[2,128,512]{2,1,0:T(8,128)(2,1)}, bf16[2,128,512]{2,1,0:T(8,128)(2,1)S(1)}, u32[]{:S(2)}, u32[]{:S(2)}) collective-permute-start(bf16[2,128,512]{2,1,0:T(8,128)(2,1)} %get-tuple-element.50), channel_id=1, source_target_pairs={{0,7},{1,6},{2,5},{3,4},{4,3},{5,2},{6,1},{7,0},{8,15},{9,14},{10,... | collective-permute-start | bytes 786440 | tf_op jit(solution)/shard_map/ppermute | solution.py:378
  11.3 3.9 %shard_map.157 = (bf16[2,128,512]{2,1,0:T(8,128)(2,1)}, bf16[2,128,512]{2,1,0:T(8,128)(2,1)}, bf16[2,128,512]{2,1,0:T(8,128)(2,1)}, bf16[2,128,512]{2,1,0:T(8,12...) custom-call(bf16[8,128,512]{2,1,0:T(8,128)(2,1)} %bitcast.16, bf16[8,128,512]{2,1,0:T(8,128)(2,1)} %bitcast.26, ...), custom_call_target="tpu_custom_call" | custom-call | flops 3145728 | bytes 4718592 | tf_op jit(solution)/shard_map/pallas_call | solution.py:209
  15.8 7.2 %collective-permute-done.3.refs_2_ = bf16[2,128,512]{2,1,0:T(8,128)(2,1)S(1)} collective-permute-done((bf16[2,128,512]{2,1,0:T(8,128)(2,1)}, bf16[2,128,512]{2,1,0:T(8,128)(2,1)S(1)}, u32[]{:S(2)}, u32[]{:S(2)}) %collective-permute-start.3) | collective-permute-done | bytes 262176 | tf_op jit(solution)/shard_map/ppermute | solution.py:378
  23.5 6.3 %collective-permute-done.1.refs_6_ = bf16[1024,512]{1,0:T(8,128)(2,1)} collective-permute-done((bf16[1024,512]{1,0:T(8,128)(2,1)S(1)}, bf16[1024,512]{1,0:T(8,128)(2,1)}, u32[]{:S(2)}, u32[]{:S(2)}) %collective-permute-start.1) | collective-permute-done | bytes 1048608 | tf_op jit(solution)/shard_map/ppermute | solution.py:358
  29.8 5.2 %collective-permute-start.6 = (bf16[2,128,512]{2,1,0:T(8,128)(2,1)}, bf16[2,128,512]{2,1,0:T(8,128)(2,1)}, u32[]{:S(2)}, u32[]{:S(2)}) collective-permute-start(bf16[2,128,512]{2,1,0:T(8,128)(2,1)} %get-tuple-element.54), channel_id=1, source_target_pairs={{0,5},{1,4},{2,7},{3,6},{4,1},{5,0},{6,3},{7,2},{8,13},{9,12},{10,... | collective-permute-start | bytes 786440 | tf_op jit(solution)/shard_map/ppermute | solution.py:378
  35.2 2.7 %collective-permute-start.8 = (bf16[2,128,512]{2,1,0:T(8,128)(2,1)}, bf16[2,128,512]{2,1,0:T(8,128)(2,1)}, u32[]{:S(2)}, u32[]{:S(2)}) collective-permute-start(bf16[2,128,512]{2,1,0:T(8,128)(2,1)} %get-tuple-element.61), channel_id=1, source_target_pairs={{0,3},{1,2},{2,1},{3,0},{4,7},{5,6},{6,5},{7,4},{8,11},{9,10},{10,... | collective-permute-start | bytes 786440 | tf_op jit(solution)/shard_map/ppermute | solution.py:378
  41.4 8.5 %shard_map.158 = (bf16[8,128,512]{2,1,0:T(8,128)(2,1)S(1)}, bf16[128,512]{1,0:T(8,128)(2,1)S(1)}, bf16[128,512]{1,0:T(8,128)(2,1)S(1)}, bf16[128,512]{1,0:T(8,12...) custom-call(s32[2]{0:T(128)S(1)} %pad_add_fusion.me, ...), custom_call_target="tpu_custom_call" | custom-call | flops 4294967296 | bytes 8388608 | tf_op jit(solution)/shard_map/pallas_call | solution.py:333
  49.9 2.5 %collective-permute-start.10 = (bf16[128,512]{1,0:T(8,128)(2,1)S(1)}, bf16[128,512]{1,0:T(8,128)(2,1)S(1)}, u32[]{:S(2)}, u32[]{:S(2)}) collective-permute-start(bf16[128,512]{1,0:T(8,128)(2,1)S(1)} %get-tuple-element.65), channel_id=1, source_target_pairs={{0,7},{1,6},{2,5},{3,4},{4,3},{5,2},{6,1},{7,0},{8,15},{9,14},{10,... | collective-permute-start | bytes 393224 | tf_op jit(solution)/shard_map/ppermute | solution.py:378
  52.4 7.1 %collective-permute-done.7.refs_4_ = bf16[2,128,512]{2,1,0:T(8,128)(2,1)} collective-permute-done((bf16[2,128,512]{2,1,0:T(8,128)(2,1)}, bf16[2,128,512]{2,1,0:T(8,128)(2,1)}, u32[]{:S(2)}, u32[]{:S(2)}) %collective-permute-start.7) | collective-permute-done | bytes 262176 | tf_op jit(solution)/shard_map/ppermute | solution.py:378
  59.5 2.4 %collective-permute-start.11 = (bf16[128,512]{1,0:T(8,128)(2,1)S(1)}, bf16[128,512]{1,0:T(8,128)(2,1)S(1)}, u32[]{:S(2)}, u32[]{:S(2)}) collective-permute-start(bf16[128,512]{1,0:T(8,128)(2,1)S(1)} %get-tuple-element.66), channel_id=1, source_target_pairs={{0,6},{1,7},{2,4},{3,5},{4,2},{5,3},{6,0},{7,1},{8,14},{9,15},{10,... | collective-permute-start | bytes 393224 | tf_op jit(solution)/shard_map/ppermute | solution.py:378
  63.1 1.6 %collective-permute-start.13 = (bf16[128,512]{1,0:T(8,128)(2,1)S(1)}, bf16[128,512]{1,0:T(8,128)(2,1)S(1)}, u32[]{:S(2)}, u32[]{:S(2)}) collective-permute-start(bf16[128,512]{1,0:T(8,128)(2,1)S(1)} %get-tuple-element.68), channel_id=1, source_target_pairs={{0,4},{1,5},{2,6},{3,7},{4,0},{5,1},{6,2},{7,3},{8,12},{9,13},{10,... | collective-permute-start | bytes 393224 | tf_op jit(solution)/shard_map/ppermute | solution.py:378
  64.8 9.8 %shard_map.159 = (bf16[128,512]{1,0:T(8,128)(2,1)S(1)}, bf16[128,512]{1,0:T(8,128)(2,1)S(1)}, bf16[128,512]{1,0:T(8,128)(2,1)S(1)}, bf16[128,512]{1,0:T(8,128)(2...) custom-call(s32[2]{0:T(128)S(1)} %pad_add_fusion.me, ...), custom_call_target="tpu_custom_call" | custom-call | flops 3221225472 | bytes 4194304 | tf_op jit(solution)/shard_map/pallas_call | solution.py:154
  74.7 2.9 %collective-permute-start.15 = (bf16[128,512]{1,0:T(8,128)(2,1)S(1)}, bf16[128,512]{1,0:T(8,128)(2,1)S(1)}, u32[]{:S(2)}, u32[]{:S(2)}) collective-permute-start(bf16[128,512]{1,0:T(8,128)(2,1)S(1)} %get-tuple-element.72), channel_id=1, source_target_pairs={{0,2},{1,3},{2,0},{3,1},{4,6},{5,7},{6,4},{7,5},{8,10},{9,11},{10,... | collective-permute-start | bytes 393224 | tf_op jit(solution)/shard_map/ppermute | solution.py:378
  79.0 3.4 %collective-permute-start.17 = (bf16[128,512]{1,0:T(8,128)(2,1)S(1)}, bf16[128,512]{1,0:T(8,128)(2,1)S(1)}, u32[]{:S(2)}, u32[]{:S(2)}) collective-permute-start(bf16[128,512]{1,0:T(8,128)(2,1)S(1)} %get-tuple-element.76), channel_id=1, source_target_pairs={{0,7},{1,6},{2,5},{3,4},{4,3},{5,2},{6,1},{7,0},{8,15},{9,14},{10,... | collective-permute-start | bytes 393224 | tf_op jit(solution)/shard_map/ppermute | solution.py:378
  82.4 1.9 %collective-permute-start.18 = (bf16[128,512]{1,0:T(8,128)(2,1)S(1)}, bf16[128,512]{1,0:T(8,128)(2,1)S(1)}, u32[]{:S(2)}, u32[]{:S(2)}) collective-permute-start(bf16[128,512]{1,0:T(8,128)(2,1)S(1)} %get-tuple-element.77), channel_id=1, source_target_pairs={{0,6},{1,7},{2,4},{3,5},{4,2},{5,3},{6,0},{7,1},{8,14},{9,15},{10,... | collective-permute-start | bytes 393224 | tf_op jit(solution)/shard_map/ppermute | solution.py:378
  84.3 5.0 %collective-permute-done.15.refs_14_ = bf16[128,512]{1,0:T(8,128)(2,1)S(1)} collective-permute-done((bf16[128,512]{1,0:T(8,128)(2,1)S(1)}, bf16[128,512]{1,0:T(8,128)(2,1)S(1)}, u32[]{:S(2)}, u32[]{:S(2)}) %collective-permute-start.15) | collective-permute-done | bytes 131104 | tf_op jit(solution)/shard_map/ppermute | solution.py:378
  89.3 14.2 %shard_map.160 = (bf16[2,128,512]{2,1,0:T(8,128)(2,1)S(1)}, bf16[2,128,512]{2,1,0:T(8,128)(2,1)S(1)}, bf16[2,128,512]{2,1,0:T(8,128)(2,1)S(1)}, bf16[2,128,512]{...) custom-call(s32[2]{0:T(128)S(1)} %pad_add_fusion.me, ...), custom_call_target="tpu_custom_call" | custom-call | flops 5368709120 | bytes 4194304 | tf_op jit(solution)/shard_map/pallas_call | solution.py:154
  103.5 2.0 %collective-permute-start.26 = (bf16[2,128,512]{2,1,0:T(8,128)(2,1)S(1)}, bf16[2,128,512]{2,1,0:T(8,128)(2,1)S(1)}, u32[]{:S(2)}, u32[]{:S(2)}) collective-permute-start(bf16[2,128,512]{2,1,0:T(8,128)(2,1)S(1)} %get-tuple-element.85), channel_id=1, source_target_pairs={{0,7},{1,6},{2,5},{3,4},{4,3},{5,2},{6,1},{7,0},{8,15},{9,14},{10,... | collective-permute-start | bytes 786440 | tf_op jit(solution)/shard_map/ppermute | solution.py:378
  105.5 1.9 %collective-permute-start.27 = (bf16[2,128,512]{2,1,0:T(8,128)(2,1)S(1)}, bf16[2,128,512]{2,1,0:T(8,128)(2,1)S(1)}, u32[]{:S(2)}, u32[]{:S(2)}) collective-permute-start(bf16[2,128,512]{2,1,0:T(8,128)(2,1)S(1)} %get-tuple-element.86), channel_id=1, source_target_pairs={{0,6},{1,7},{2,4},{3,5},{4,2},{5,3},{6,0},{7,1},{8,14},{9,15},{10,... | collective-permute-start | bytes 786440 | tf_op jit(solution)/shard_map/ppermute | solution.py:378
  107.4 1.5 collective-permute-start.21
  110.9 12.1 %collective-permute-done.21.refs_5_ = bf16[128,512]{1,0:T(8,128)(2,1)S(1)} collective-permute-done((bf16[128,512]{1,0:T(8,128)(2,1)S(1)}, bf16[128,512]{1,0:T(8,128)(2,1)S(1)}, u32[]{:S(2)}, u32[]{:S(2)}) %collective-permute-start.21) | collective-permute-done | bytes 131104 | tf_op jit(solution)/shard_map/ppermute | solution.py:378
  126.6 2.4 %collective-permute-start.24 = (bf16[2,128,512]{2,1,0:T(8,128)(2,1)S(1)}, bf16[2,128,512]{2,1,0:T(8,128)(2,1)S(1)}, u32[]{:S(2)}, u32[]{:S(2)}) collective-permute-start(bf16[2,128,512]{2,1,0:T(8,128)(2,1)S(1)} %get-tuple-element.83), channel_id=1, source_target_pairs={{0,5},{1,4},{2,7},{3,6},{4,1},{5,0},{6,3},{7,2},{8,13},{9,12},{10,... | collective-permute-start | bytes 786440 | tf_op jit(solution)/shard_map/ppermute | solution.py:378
  129.0 2.5 %collective-permute-start.25 = (bf16[2,128,512]{2,1,0:T(8,128)(2,1)S(1)}, bf16[2,128,512]{2,1,0:T(8,128)(2,1)S(1)}, u32[]{:S(2)}, u32[]{:S(2)}) collective-permute-start(bf16[2,128,512]{2,1,0:T(8,128)(2,1)S(1)} %get-tuple-element.84), channel_id=1, source_target_pairs={{0,4},{1,5},{2,6},{3,7},{4,0},{5,1},{6,2},{7,3},{8,12},{9,13},{10,... | collective-permute-start | bytes 786440 | tf_op jit(solution)/shard_map/ppermute | solution.py:378
  131.5 2.3 %shard_map.161 = bf16[8,128,512]{2,1,0:T(8,128)(2,1)} custom-call(s32[2]{0:T(128)S(1)} %pad_add_fusion.me, bf16[8,128,512]{2,1,0:T(8,128)(2,1)S(1)} %get-tuple-element.56.upstream, bf16[128,512]{1,0:T(8,128)(2,1)S(1)} %get-tuple-element.75.refs_0_, bf16[128,512]{1,0:T(8,128)(2,1)S(1)} %collective-permute-done.17.refs_1_, ...), custom_call_target="tpu_custom_call" | custom-call | flops 3145728 | bytes 3145728 | tf_op jit(solution)/shard_map/pallas_call | solution.py:311
  133.8 5.7 %collective-permute-done.28.refs_15_ = bf16[2,128,512]{2,1,0:T(8,128)(2,1)S(1)} collective-permute-done((bf16[2,128,512]{2,1,0:T(8,128)(2,1)S(1)}, bf16[2,128,512]{2,1,0:T(8,128)(2,1)S(1)}, u32[]{:S(2)}, u32[]{:S(2)}) %collective-permute-start.28) | collective-permute-done | bytes 262176 | tf_op jit(solution)/shard_map/ppermute | solution.py:378
  139.5 3.5 %collective-permute-done.29.refs_16_ = bf16[2,128,512]{2,1,0:T(8,128)(2,1)S(1)} collective-permute-done((bf16[2,128,512]{2,1,0:T(8,128)(2,1)S(1)}, bf16[2,128,512]{2,1,0:T(8,128)(2,1)S(1)}, u32[]{:S(2)}, u32[]{:S(2)}) %collective-permute-start.29) | collective-permute-done | bytes 262176 | tf_op jit(solution)/shard_map/ppermute | solution.py:378
  143.3 3.5 %shard_map.162 = (bf16[8,128,512]{2,1,0:T(8,128)(2,1)}, bf16[8,128,512]{2,1,0:T(8,128)(2,1)}, f32[8,128,512]{2,1,0:T(8,128)}) custom-call(s32[2]{0:T(128)S(1)} %pad_add_fusion.me, bf16[8,128,512]{2,1,0:T(8,128)(2,1)S(1)} %bitcast.17, bf16[8,128,512]{2,1,0:T(8,128)(2,1)S(1)} %bitcast.18, bf16[8,128,512]{2,1,0:T(8,128)(2,1)S(1)} %bitcast.19, ...), custom_call_target="tpu_custom_call" | custom-call | flops 786432 | bytes 6291456 | tf_op jit(solution)/shard_map/pallas_call | solution.py:283
  146.8 2.1 %collective-permute-done.24.refs_4_ = bf16[2,128,512]{2,1,0:T(8,128)(2,1)S(1)} collective-permute-done((bf16[2,128,512]{2,1,0:T(8,128)(2,1)S(1)}, bf16[2,128,512]{2,1,0:T(8,128)(2,1)S(1)}, u32[]{:S(2)}, u32[]{:S(2)}) %collective-permute-start.24) | collective-permute-done | bytes 262176 | tf_op jit(solution)/shard_map/ppermute | solution.py:378
  148.9 4.1 %collective-permute-done.25.refs_5_ = bf16[2,128,512]{2,1,0:T(8,128)(2,1)S(1)} collective-permute-done((bf16[2,128,512]{2,1,0:T(8,128)(2,1)S(1)}, bf16[2,128,512]{2,1,0:T(8,128)(2,1)S(1)}, u32[]{:S(2)}, u32[]{:S(2)}) %collective-permute-start.25) | collective-permute-done | bytes 262176 | tf_op jit(solution)/shard_map/ppermute | solution.py:378
  153.0 1.6 %shard_map.163 = (bf16[8,128,512]{2,1,0:T(8,128)(2,1)}, bf16[8,128,512]{2,1,0:T(8,128)(2,1)}, f32[8,128,512]{2,1,0:T(8,128)}) custom-call(s32[2]{0:T(128)S(1)} %pad_add_fusion.me, bf16[8,128,512]{2,1,0:T(8,128)(2,1)S(1)} %bitcast.23, bf16[8,128,512]{2,1,0:T(8,128)(2,1)S(1)} %bitcast.24, ...), custom_call_target="tpu_custom_call", output_to_operand_aliasing={{0}: (7, {}), {1}: (8, {}), {2}: (9, {})} | custom-call | flops 262144 | bytes 2097152 | tf_op jit(solution)/shard_map/pallas_call | solution.py:283
  (59 shorter events, 13.6 us)
Async XLA Ops:
  3.5 26.3 %collective-permute-start.1 = (bf16[1024,512]{1,0:T(8,128)(2,1)S(1)}, bf16[1024,512]{1,0:T(8,128)(2,1)}, u32[]{:S(2)}, u32[]{:S(2)}) collective-permute-start(bf16[1024,512]{1,0:T(8,128)(2,1)S(1)} %copy-done.2), channel_id=1, source_target_pairs={{0,16},{8,24},{16,0},{24,8},{1,17},{9,25},{17,1},{25,9},{2,18},{10... | collective-permute-start | bytes 3145736 | tf_op jit(solution)/shard_map/ppermute | solution.py:358
  6.5 16.5 %collective-permute-start.2 = (bf16[2,128,512]{2,1,0:T(8,128)(2,1)}, bf16[2,128,512]{2,1,0:T(8,128)(2,1)S(1)}, u32[]{:S(2)}, u32[]{:S(2)}) collective-permute-start(bf16[2,128,512]{2,1,0:T(8,128)(2,1)} %get-tuple-element.50), channel_id=1, source_target_pairs={{0,7},{1,6},{2,5},{3,4},{4,3},{5,2},{6,1},{7,0},{8,15},{9,14},{10,... | collective-permute-start | bytes 786440 | tf_op jit(solution)/shard_map/ppermute | solution.py:378
  11.1 11.9 %collective-permute-start.3 = (bf16[2,128,512]{2,1,0:T(8,128)(2,1)}, bf16[2,128,512]{2,1,0:T(8,128)(2,1)S(1)}, u32[]{:S(2)}, u32[]{:S(2)}) collective-permute-start(bf16[2,128,512]{2,1,0:T(8,128)(2,1)} %get-tuple-element.52), channel_id=1, source_target_pairs={{0,6},{1,7},{2,4},{3,5},{4,2},{5,3},{6,0},{7,1},{8,14},{9,15},{10,... | collective-permute-start | bytes 786440 | tf_op jit(solution)/shard_map/ppermute | solution.py:378
  15.2 8.3 %collective-permute-start.4 = (bf16[2,128,512]{2,1,0:T(8,128)(2,1)}, bf16[2,128,512]{2,1,0:T(8,128)(2,1)S(1)}, u32[]{:S(2)}, u32[]{:S(2)}) collective-permute-start(bf16[2,128,512]{2,1,0:T(8,128)(2,1)} %get-tuple-element.53), channel_id=1, source_target_pairs={{0,1},{1,0},{2,3},{3,2},{4,5},{5,4},{6,7},{7,6},{8,9},{9,8},{10,11... | collective-permute-start | bytes 786440 | tf_op jit(solution)/shard_map/ppermute | solution.py:378
  15.8 24.1 %collective-permute-start = (bf16[1024,512]{1,0:T(8,128)(2,1)S(1)}, bf16[1024,512]{1,0:T(8,128)(2,1)S(1)}, u32[]{:S(2)}, u32[]{:S(2)}) collective-permute-start(bf16[1024,512]{1,0:T(8,128)(2,1)S(1)} %copy-done.2), channel_id=1, source_target_pairs={{0,8},{8,0},{16,24},{24,16},{1,9},{9,1},{17,25},{25,17},{2,10},{10... | collective-permute-start | bytes 3145736 | tf_op jit(solution)/shard_map/ppermute | solution.py:372
  29.8 10.3 %collective-permute-start.5 = (bf16[1024,512]{1,0:T(8,128)(2,1)}, bf16[1024,512]{1,0:T(8,128)(2,1)}, u32[]{:S(2)}, u32[]{:S(2)}) collective-permute-start(bf16[1024,512]{1,0:T(8,128)(2,1)} %collective-permute-done.1.refs_6_), channel_id=1, source_target_pairs={{0,8},{8,0},{16,24},{24,16},{1,9},{9,1},{17,25},{25,17},{2,10},{10... | collective-permute-start | bytes 3145736 | tf_op jit(solution)/shard_map/ppermute | solution.py:372
  29.8 34.9 %collective-permute-start.6 = (bf16[2,128,512]{2,1,0:T(8,128)(2,1)}, bf16[2,128,512]{2,1,0:T(8,128)(2,1)}, u32[]{:S(2)}, u32[]{:S(2)}) collective-permute-start(bf16[2,128,512]{2,1,0:T(8,128)(2,1)} %get-tuple-element.54), channel_id=1, source_target_pairs={{0,5},{1,4},{2,7},{3,6},{4,1},{5,0},{6,3},{7,2},{8,13},{9,12},{10,... | collective-permute-start | bytes 786440 | tf_op jit(solution)/shard_map/ppermute | solution.py:378
  35.0 24.4 %collective-permute-start.7 = (bf16[2,128,512]{2,1,0:T(8,128)(2,1)}, bf16[2,128,512]{2,1,0:T(8,128)(2,1)}, u32[]{:S(2)}, u32[]{:S(2)}) collective-permute-start(bf16[2,128,512]{2,1,0:T(8,128)(2,1)} %get-tuple-element.60), channel_id=1, source_target_pairs={{0,4},{1,5},{2,6},{3,7},{4,0},{5,1},{6,2},{7,3},{8,12},{9,13},{10,... | collective-permute-start | bytes 786440 | tf_op jit(solution)/shard_map/ppermute | solution.py:378
  35.2 26.7 %collective-permute-start.8 = (bf16[2,128,512]{2,1,0:T(8,128)(2,1)}, bf16[2,128,512]{2,1,0:T(8,128)(2,1)}, u32[]{:S(2)}, u32[]{:S(2)}) collective-permute-start(bf16[2,128,512]{2,1,0:T(8,128)(2,1)} %get-tuple-element.61), channel_id=1, source_target_pairs={{0,3},{1,2},{2,1},{3,0},{4,7},{5,6},{6,5},{7,4},{8,11},{9,10},{10,... | collective-permute-start | bytes 786440 | tf_op jit(solution)/shard_map/ppermute | solution.py:378
  39.9 23.2 %collective-permute-start.9 = (bf16[2,128,512]{2,1,0:T(8,128)(2,1)}, bf16[2,128,512]{2,1,0:T(8,128)(2,1)S(1)}, u32[]{:S(2)}, u32[]{:S(2)}) collective-permute-start(bf16[2,128,512]{2,1,0:T(8,128)(2,1)} %get-tuple-element.62), channel_id=1, source_target_pairs={{0,2},{1,3},{2,0},{3,1},{4,6},{5,7},{6,4},{7,5},{8,10},{9,11},{10,... | collective-permute-start | bytes 786440 | tf_op jit(solution)/shard_map/ppermute | solution.py:378
  49.9 24.8 %collective-permute-start.10 = (bf16[128,512]{1,0:T(8,128)(2,1)S(1)}, bf16[128,512]{1,0:T(8,128)(2,1)S(1)}, u32[]{:S(2)}, u32[]{:S(2)}) collective-permute-start(bf16[128,512]{1,0:T(8,128)(2,1)S(1)} %get-tuple-element.65), channel_id=1, source_target_pairs={{0,7},{1,6},{2,5},{3,4},{4,3},{5,2},{6,1},{7,0},{8,15},{9,14},{10,... | collective-permute-start | bytes 393224 | tf_op jit(solution)/shard_map/ppermute | solution.py:378
  59.5 18.2 %collective-permute-start.11 = (bf16[128,512]{1,0:T(8,128)(2,1)S(1)}, bf16[128,512]{1,0:T(8,128)(2,1)S(1)}, u32[]{:S(2)}, u32[]{:S(2)}) collective-permute-start(bf16[128,512]{1,0:T(8,128)(2,1)S(1)} %get-tuple-element.66), channel_id=1, source_target_pairs={{0,6},{1,7},{2,4},{3,5},{4,2},{5,3},{6,0},{7,1},{8,14},{9,15},{10,... | collective-permute-start | bytes 393224 | tf_op jit(solution)/shard_map/ppermute | solution.py:378
  61.8 17.2 %collective-permute-start.12 = (bf16[128,512]{1,0:T(8,128)(2,1)S(1)}, bf16[128,512]{1,0:T(8,128)(2,1)S(1)}, u32[]{:S(2)}, u32[]{:S(2)}) collective-permute-start(bf16[128,512]{1,0:T(8,128)(2,1)S(1)} %get-tuple-element.67), channel_id=1, source_target_pairs={{0,5},{1,4},{2,7},{3,6},{4,1},{5,0},{6,3},{7,2},{8,13},{9,12},{10,... | collective-permute-start | bytes 393224 | tf_op jit(solution)/shard_map/ppermute | solution.py:378
  63.1 19.3 %collective-permute-start.13 = (bf16[128,512]{1,0:T(8,128)(2,1)S(1)}, bf16[128,512]{1,0:T(8,128)(2,1)S(1)}, u32[]{:S(2)}, u32[]{:S(2)}) collective-permute-start(bf16[128,512]{1,0:T(8,128)(2,1)S(1)} %get-tuple-element.68), channel_id=1, source_target_pairs={{0,4},{1,5},{2,6},{3,7},{4,0},{5,1},{6,2},{7,3},{8,12},{9,13},{10,... | collective-permute-start | bytes 393224 | tf_op jit(solution)/shard_map/ppermute | solution.py:378
  64.7 19.6 %collective-permute-start.14 = (bf16[128,512]{1,0:T(8,128)(2,1)S(1)}, bf16[128,512]{1,0:T(8,128)(2,1)S(1)}, u32[]{:S(2)}, u32[]{:S(2)}) collective-permute-start(bf16[128,512]{1,0:T(8,128)(2,1)S(1)} %get-tuple-element.69), channel_id=1, source_target_pairs={{0,3},{1,2},{2,1},{3,0},{4,7},{5,6},{6,5},{7,4},{8,11},{9,10},{10,... | collective-permute-start | bytes 393224 | tf_op jit(solution)/shard_map/ppermute | solution.py:378
  74.7 14.6 %collective-permute-start.15 = (bf16[128,512]{1,0:T(8,128)(2,1)S(1)}, bf16[128,512]{1,0:T(8,128)(2,1)S(1)}, u32[]{:S(2)}, u32[]{:S(2)}) collective-permute-start(bf16[128,512]{1,0:T(8,128)(2,1)S(1)} %get-tuple-element.72), channel_id=1, source_target_pairs={{0,2},{1,3},{2,0},{3,1},{4,6},{5,7},{6,4},{7,5},{8,10},{9,11},{10,... | collective-permute-start | bytes 393224 | tf_op jit(solution)/shard_map/ppermute | solution.py:378
  77.6 11.6 %collective-permute-start.16 = (bf16[128,512]{1,0:T(8,128)(2,1)S(1)}, bf16[128,512]{1,0:T(8,128)(2,1)S(1)}, u32[]{:S(2)}, u32[]{:S(2)}) collective-permute-start(bf16[128,512]{1,0:T(8,128)(2,1)S(1)} %get-tuple-element.73), channel_id=1, source_target_pairs={{0,1},{1,0},{2,3},{3,2},{4,5},{5,4},{6,7},{7,6},{8,9},{9,8},{10,11... | collective-permute-start | bytes 393224 | tf_op jit(solution)/shard_map/ppermute | solution.py:378
  79.0 26.4 %collective-permute-start.17 = (bf16[128,512]{1,0:T(8,128)(2,1)S(1)}, bf16[128,512]{1,0:T(8,128)(2,1)S(1)}, u32[]{:S(2)}, u32[]{:S(2)}) collective-permute-start(bf16[128,512]{1,0:T(8,128)(2,1)S(1)} %get-tuple-element.76), channel_id=1, source_target_pairs={{0,7},{1,6},{2,5},{3,4},{4,3},{5,2},{6,1},{7,0},{8,15},{9,14},{10,... | collective-permute-start | bytes 393224 | tf_op jit(solution)/shard_map/ppermute | solution.py:378
  82.4 25.0 %collective-permute-start.18 = (bf16[128,512]{1,0:T(8,128)(2,1)S(1)}, bf16[128,512]{1,0:T(8,128)(2,1)S(1)}, u32[]{:S(2)}, u32[]{:S(2)}) collective-permute-start(bf16[128,512]{1,0:T(8,128)(2,1)S(1)} %get-tuple-element.77), channel_id=1, source_target_pairs={{0,6},{1,7},{2,4},{3,5},{4,2},{5,3},{6,0},{7,1},{8,14},{9,15},{10,... | collective-permute-start | bytes 393224 | tf_op jit(solution)/shard_map/ppermute | solution.py:378
  84.3 24.7 %collective-permute-start.19 = (bf16[128,512]{1,0:T(8,128)(2,1)S(1)}, bf16[128,512]{1,0:T(8,128)(2,1)S(1)}, u32[]{:S(2)}, u32[]{:S(2)}) collective-permute-start(bf16[128,512]{1,0:T(8,128)(2,1)S(1)} %get-tuple-element.78), channel_id=1, source_target_pairs={{0,5},{1,4},{2,7},{3,6},{4,1},{5,0},{6,3},{7,2},{8,13},{9,12},{10,... | collective-permute-start | bytes 393224 | tf_op jit(solution)/shard_map/ppermute | solution.py:378
  89.2 21.1 %collective-permute-start.20 = (bf16[128,512]{1,0:T(8,128)(2,1)S(1)}, bf16[128,512]{1,0:T(8,128)(2,1)S(1)}, u32[]{:S(2)}, u32[]{:S(2)}) collective-permute-start(bf16[128,512]{1,0:T(8,128)(2,1)S(1)} %get-tuple-element.79), channel_id=1, source_target_pairs={{0,4},{1,5},{2,6},{3,7},{4,0},{5,1},{6,2},{7,3},{8,12},{9,13},{10,... | collective-permute-start | bytes 393224 | tf_op jit(solution)/shard_map/ppermute | solution.py:378
  103.5 39.8 %copy-start = (bf16[1024,512]{1,0:T(8,128)(2,1)S(1)}, bf16[1024,512]{1,0:T(8,128)(2,1)}, u32[]{:S(2)}) copy-start(bf16[1024,512]{1,0:T(8,128)(2,1)} %param.14) | copy-start | bytes 3145732
  103.5 23.1 %collective-permute-start.26 = (bf16[2,128,512]{2,1,0:T(8,128)(2,1)S(1)}, bf16[2,128,512]{2,1,0:T(8,128)(2,1)S(1)}, u32[]{:S(2)}, u32[]{:S(2)}) collective-permute-start(bf16[2,128,512]{2,1,0:T(8,128)(2,1)S(1)} %get-tuple-element.85), channel_id=1, source_target_pairs={{0,7},{1,6},{2,5},{3,4},{4,3},{5,2},{6,1},{7,0},{8,15},{9,14},{10,... | collective-permute-start | bytes 786440 | tf_op jit(solution)/shard_map/ppermute | solution.py:378
  105.5 23.5 %collective-permute-start.27 = (bf16[2,128,512]{2,1,0:T(8,128)(2,1)S(1)}, bf16[2,128,512]{2,1,0:T(8,128)(2,1)S(1)}, u32[]{:S(2)}, u32[]{:S(2)}) collective-permute-start(bf16[2,128,512]{2,1,0:T(8,128)(2,1)S(1)} %get-tuple-element.86), channel_id=1, source_target_pairs={{0,6},{1,7},{2,4},{3,5},{4,2},{5,3},{6,0},{7,1},{8,14},{9,15},{10,... | collective-permute-start | bytes 786440 | tf_op jit(solution)/shard_map/ppermute | solution.py:378
  107.4 15.6 %collective-permute-start.21 = (bf16[128,512]{1,0:T(8,128)(2,1)S(1)}, bf16[128,512]{1,0:T(8,128)(2,1)S(1)}, u32[]{:S(2)}, u32[]{:S(2)}) collective-permute-start(bf16[128,512]{1,0:T(8,128)(2,1)S(1)} %get-tuple-element.80), channel_id=1, source_target_pairs={{0,3},{1,2},{2,1},{3,0},{4,7},{5,6},{6,5},{7,4},{8,11},{9,10},{10,... | collective-permute-start | bytes 393224 | tf_op jit(solution)/shard_map/ppermute | solution.py:378
  108.9 16.0 %collective-permute-start.22 = (bf16[128,512]{1,0:T(8,128)(2,1)S(1)}, bf16[128,512]{1,0:T(8,128)(2,1)S(1)}, u32[]{:S(2)}, u32[]{:S(2)}) collective-permute-start(bf16[128,512]{1,0:T(8,128)(2,1)S(1)} %get-tuple-element.81), channel_id=1, source_target_pairs={{0,2},{1,3},{2,0},{3,1},{4,6},{5,7},{6,4},{7,5},{8,10},{9,11},{10,... | collective-permute-start | bytes 393224 | tf_op jit(solution)/shard_map/ppermute | solution.py:378
  110.4 14.8 %collective-permute-start.23 = (bf16[128,512]{1,0:T(8,128)(2,1)S(1)}, bf16[128,512]{1,0:T(8,128)(2,1)S(1)}, u32[]{:S(2)}, u32[]{:S(2)}) collective-permute-start(bf16[128,512]{1,0:T(8,128)(2,1)S(1)} %get-tuple-element.82), channel_id=1, source_target_pairs={{0,1},{1,0},{2,3},{3,2},{4,5},{5,4},{6,7},{7,6},{8,9},{9,8},{10,11... | collective-permute-start | bytes 393224 | tf_op jit(solution)/shard_map/ppermute | solution.py:378
  123.1 16.4 %collective-permute-start.28 = (bf16[2,128,512]{2,1,0:T(8,128)(2,1)S(1)}, bf16[2,128,512]{2,1,0:T(8,128)(2,1)S(1)}, u32[]{:S(2)}, u32[]{:S(2)}) collective-permute-start(bf16[2,128,512]{2,1,0:T(8,128)(2,1)S(1)} %get-tuple-element.87), channel_id=1, source_target_pairs={{0,3},{1,2},{2,1},{3,0},{4,7},{5,6},{6,5},{7,4},{8,11},{9,10},{10,... | collective-permute-start | bytes 786440 | tf_op jit(solution)/shard_map/ppermute | solution.py:378
  124.9 18.1 %collective-permute-start.29 = (bf16[2,128,512]{2,1,0:T(8,128)(2,1)S(1)}, bf16[2,128,512]{2,1,0:T(8,128)(2,1)S(1)}, u32[]{:S(2)}, u32[]{:S(2)}) collective-permute-start(bf16[2,128,512]{2,1,0:T(8,128)(2,1)S(1)} %get-tuple-element.88), channel_id=1, source_target_pairs={{0,2},{1,3},{2,0},{3,1},{4,6},{5,7},{6,4},{7,5},{8,10},{9,11},{10,... | collective-permute-start | bytes 786440 | tf_op jit(solution)/shard_map/ppermute | solution.py:378
  125.1 18.2 %collective-permute-start.30 = (bf16[2,128,512]{2,1,0:T(8,128)(2,1)S(1)}, bf16[2,128,512]{2,1,0:T(8,128)(2,1)S(1)}, u32[]{:S(2)}, u32[]{:S(2)}) collective-permute-start(bf16[2,128,512]{2,1,0:T(8,128)(2,1)S(1)} %get-tuple-element.89), channel_id=1, source_target_pairs={{0,1},{1,0},{2,3},{3,2},{4,5},{5,4},{6,7},{7,6},{8,9},{9,8},{10,11... | collective-permute-start | bytes 786440 | tf_op jit(solution)/shard_map/ppermute | solution.py:378
  126.6 22.3 %collective-permute-start.24 = (bf16[2,128,512]{2,1,0:T(8,128)(2,1)S(1)}, bf16[2,128,512]{2,1,0:T(8,128)(2,1)S(1)}, u32[]{:S(2)}, u32[]{:S(2)}) collective-permute-start(bf16[2,128,512]{2,1,0:T(8,128)(2,1)S(1)} %get-tuple-element.83), channel_id=1, source_target_pairs={{0,5},{1,4},{2,7},{3,6},{4,1},{5,0},{6,3},{7,2},{8,13},{9,12},{10,... | collective-permute-start | bytes 786440 | tf_op jit(solution)/shard_map/ppermute | solution.py:378
  129.0 24.0 %collective-permute-start.25 = (bf16[2,128,512]{2,1,0:T(8,128)(2,1)S(1)}, bf16[2,128,512]{2,1,0:T(8,128)(2,1)S(1)}, u32[]{:S(2)}, u32[]{:S(2)}) collective-permute-start(bf16[2,128,512]{2,1,0:T(8,128)(2,1)S(1)} %get-tuple-element.84), channel_id=1, source_target_pairs={{0,4},{1,5},{2,6},{3,7},{4,0},{5,1},{6,2},{7,3},{8,12},{9,13},{10,... | collective-permute-start | bytes 786440 | tf_op jit(solution)/shard_map/ppermute | solution.py:378
  (8 other events, 161.4 us)

commit v11 on v10

--- a/solution.py
+++ b/solution.py
@@ -121,8 +121,14 @@
     scatter_slabs(rows, 1.0 / (SLABS * inner), outs, None, inner)
 
 
+def near_first(chunks):
+    return [0, 1, *range(chunks // 2 + 1, chunks), *range(2, chunks // 2 + 1)]
+
+
 def backward_kernel(chunks, inner, scale, me, *refs):
     pair, grad, refs = refs[:chunks], refs[chunks : 2 * chunks], refs[2 * chunks :]
+    grad = sorted(zip(near_first(chunks), grad), key=lambda item: item[0])
+    grad = [ref for _, ref in grad]
     (first, last, cos, sin, forward, backward), outs = refs[:6], refs[6:]
     tables = (first[...], cos[...], sin[...], forward[...], inner)
     back_tables = (last[...], cos[...], sin[...], backward[...], inner)
@@ -428,13 +434,12 @@
     response = conv_call(
         functools.partial(response_kernel, n_ctx, inner), me, (after(pair, grad[0]),), tables, (), inner, 3
     )
-    grad[-2:], _ = lax.optimization_barrier((grad[-2:], response[0]))
     grad_came = exchange(grad)
     resp_came = exchange(response)
     backs = conv_call(
         functools.partial(backward_kernel, n_ctx, inner, scale),
         me,
-        (pair, after(grad_came, response[0])),
+        (pair, after([grad_came[k] for k in near_first(n_ctx)], response[0])),
         tables,
         (2,),
         inner,

time: 155 us -> 153 us (0.987)
  waiting for transfers between devices: 57.2 us -> 49.6 us
  starting transfers between devices: 46.7 us -> 52.3 us
    ppermute x28, waiting for transfers between devices: 50.9 us -> 43.3 us  [send(): return lax.ppermute(part, 'ctx', [(p, p ^ d) for p in range(count)])]
    ppermute x28, starting transfers between devices: 43.7 us -> 49.3 us  [send(): return lax.ppermute(part, 'ctx', [(p, p ^ d) for p in range(count)])]
  transfers between devices with their start and end apart: 31 -> 31, of which waited for: 14 -> 9; matrix products, arithmetic and copies ran while one was open for 1% -> 1% of each run, Pallas kernels for 27% -> 28%
where the time goes in v11:
time: 153 us
  starting transfers between devices  52.3 us (34%)
  waiting for transfers between devices  49.6 us (32%)
  Pallas kernels  46.8 us (31%)
  local copies, waits for them, and re-layouts  3.21 us (2%)
    ppermute x28, starting transfers between devices, send(): return lax.ppermute(part, 'ctx', [(p, p ^ d) for p in range(count)])  49.3 us
    ppermute x28, waiting for transfers between devices, send(): return lax.ppermute(part, 'ctx', [(p, p ^ d) for p in range(count)])  43.3 us
    pallas_call x2, Pallas kernels, conv_call(): pl.pallas_call(kernel, grid_spec=pltpu.PrefetchScalarGridSpec(num_scalar_...  24.1 us
    pallas_call x1, Pallas kernels, project_call(): pl.pallas_call(functools.partial(project_kernel, chunks, members), grid_s...  8.49 us
    pallas_call x2, Pallas kernels, prepare_call(): pl.pallas_call(functools.partial(prepare_kernel, masks, scale), in_specs=...  6.75 us
    ppermute x1, waiting for transfers between devices, gather_start(): lax.ppermute(block, 'group', [(g, g ^ count // 2) for g in range(count)])  6.26 us
    pallas_call x2, Pallas kernels, finish_call(): pl.pallas_call(functools.partial(finish_kernel, count), grid_spec=pltpu.P...  5.16 us
  transfers between devices with their start and end apart: 31, of which 9 were waited for; matrix products, arithmetic and copies ran while one was open for 1% of the time, Pallas kernels for 28%

profile of v11, /device:TPU:0, one launch (start us, length us, event | category | flops | bytes accessed | tf_op | source)
XLA Modules:
  0.0 152.7 jit_solution(6243227712316594029)
XLA Ops:
  0.6 2.9 %shard_map.156 = (bf16[2,128,512]{2,1,0:T(8,128)(2,1)}, bf16[2,128,512]{2,1,0:T(8,128)(2,1)}) custom-call(bf16[8,128,512]{2,1,0:T(8,128)(2,1)} %bitcast.15, bf16[8,128,512]{2,1,0:T(8,128)(2,1)} %bitcast.25, f32[8,128,512]{2,1,0:T(8,128)} %bitcast.36, f32[8,128]{1,0:T(8,128)} %bitcast.42), custom_call_target="tpu_custom_call" | custom-call | flops 1048576 | bytes 1572864 | tf_op jit(solution)/shard_map/pallas_call | solution.py:215
  3.5 3.0 %collective-permute-start.1 = (bf16[1024,512]{1,0:T(8,128)(2,1)S(1)}, bf16[1024,512]{1,0:T(8,128)(2,1)}, u32[]{:S(2)}, u32[]{:S(2)}) collective-permute-start(bf16[1024,512]{1,0:T(8,128)(2,1)S(1)} %copy-done.2), channel_id=1, source_target_pairs={{0,16},{8,24},{16,0},{24,8},{1,17},{9,25},{17,1},{25,9},{2,18},{10... | collective-permute-start | bytes 3145736 | tf_op jit(solution)/shard_map/ppermute | solution.py:364
  6.5 4.6 %collective-permute-start.2 = (bf16[2,128,512]{2,1,0:T(8,128)(2,1)}, bf16[2,128,512]{2,1,0:T(8,128)(2,1)S(1)}, u32[]{:S(2)}, u32[]{:S(2)}) collective-permute-start(bf16[2,128,512]{2,1,0:T(8,128)(2,1)} %get-tuple-element.48), channel_id=1, source_target_pairs={{0,7},{1,6},{2,5},{3,4},{4,3},{5,2},{6,1},{7,0},{8,15},{9,14},{10,... | collective-permute-start | bytes 786440 | tf_op jit(solution)/shard_map/ppermute | solution.py:384
  11.3 3.9 %shard_map.157 = (bf16[2,128,512]{2,1,0:T(8,128)(2,1)}, bf16[2,128,512]{2,1,0:T(8,128)(2,1)}, bf16[2,128,512]{2,1,0:T(8,128)(2,1)}, bf16[2,128,512]{2,1,0:T(8,12...) custom-call(bf16[8,128,512]{2,1,0:T(8,128)(2,1)} %bitcast.16, bf16[8,128,512]{2,1,0:T(8,128)(2,1)} %bitcast.26, ...), custom_call_target="tpu_custom_call" | custom-call | flops 3145728 | bytes 4718592 | tf_op jit(solution)/shard_map/pallas_call | solution.py:215
  15.8 7.2 %collective-permute-done.3.refs_2_ = bf16[2,128,512]{2,1,0:T(8,128)(2,1)S(1)} collective-permute-done((bf16[2,128,512]{2,1,0:T(8,128)(2,1)}, bf16[2,128,512]{2,1,0:T(8,128)(2,1)S(1)}, u32[]{:S(2)}, u32[]{:S(2)}) %collective-permute-start.3) | collective-permute-done | bytes 262176 | tf_op jit(solution)/shard_map/ppermute | solution.py:384
  23.5 6.3 %collective-permute-done.1.refs_6_ = bf16[1024,512]{1,0:T(8,128)(2,1)} collective-permute-done((bf16[1024,512]{1,0:T(8,128)(2,1)S(1)}, bf16[1024,512]{1,0:T(8,128)(2,1)}, u32[]{:S(2)}, u32[]{:S(2)}) %collective-permute-start.1) | collective-permute-done | bytes 1048608 | tf_op jit(solution)/shard_map/ppermute | solution.py:364
  29.8 5.2 %collective-permute-start.6 = (bf16[2,128,512]{2,1,0:T(8,128)(2,1)}, bf16[2,128,512]{2,1,0:T(8,128)(2,1)}, u32[]{:S(2)}, u32[]{:S(2)}) collective-permute-start(bf16[2,128,512]{2,1,0:T(8,128)(2,1)} %get-tuple-element.52), channel_id=1, source_target_pairs={{0,5},{1,4},{2,7},{3,6},{4,1},{5,0},{6,3},{7,2},{8,13},{9,12},{10,... | collective-permute-start | bytes 786440 | tf_op jit(solution)/shard_map/ppermute | solution.py:384
  35.2 2.7 %collective-permute-start.8 = (bf16[2,128,512]{2,1,0:T(8,128)(2,1)}, bf16[2,128,512]{2,1,0:T(8,128)(2,1)}, u32[]{:S(2)}, u32[]{:S(2)}) collective-permute-start(bf16[2,128,512]{2,1,0:T(8,128)(2,1)} %get-tuple-element.59), channel_id=1, source_target_pairs={{0,3},{1,2},{2,1},{3,0},{4,7},{5,6},{6,5},{7,4},{8,11},{9,10},{10,... | collective-permute-start | bytes 786440 | tf_op jit(solution)/shard_map/ppermute | solution.py:384
  39.3 8.5 %shard_map.158 = (bf16[8,128,512]{2,1,0:T(8,128)(2,1)S(1)}, bf16[128,512]{1,0:T(8,128)(2,1)S(1)}, bf16[128,512]{1,0:T(8,128)(2,1)S(1)}, bf16[128,512]{1,0:T(8,12...) custom-call(s32[2]{0:T(128)S(1)} %pad_add_fusion.me, ...), custom_call_target="tpu_custom_call" | custom-call | flops 4294967296 | bytes 8388608 | tf_op jit(solution)/shard_map/pallas_call | solution.py:339
  47.8 2.5 %collective-permute-start.10 = (bf16[128,512]{1,0:T(8,128)(2,1)S(1)}, bf16[128,512]{1,0:T(8,128)(2,1)S(1)}, u32[]{:S(2)}, u32[]{:S(2)}) collective-permute-start(bf16[128,512]{1,0:T(8,128)(2,1)S(1)} %get-tuple-element.63), channel_id=1, source_target_pairs={{0,7},{1,6},{2,5},{3,4},{4,3},{5,2},{6,1},{7,0},{8,15},{9,14},{10,... | collective-permute-start | bytes 393224 | tf_op jit(solution)/shard_map/ppermute | solution.py:384
  50.4 9.1 %collective-permute-done.7.refs_4_ = bf16[2,128,512]{2,1,0:T(8,128)(2,1)} collective-permute-done((bf16[2,128,512]{2,1,0:T(8,128)(2,1)}, bf16[2,128,512]{2,1,0:T(8,128)(2,1)}, u32[]{:S(2)}, u32[]{:S(2)}) %collective-permute-start.7) | collective-permute-done | bytes 262176 | tf_op jit(solution)/shard_map/ppermute | solution.py:384
  61.4 2.0 %collective-permute-start.12 = (bf16[128,512]{1,0:T(8,128)(2,1)S(1)}, bf16[128,512]{1,0:T(8,128)(2,1)S(1)}, u32[]{:S(2)}, u32[]{:S(2)}) collective-permute-start(bf16[128,512]{1,0:T(8,128)(2,1)S(1)} %get-tuple-element.65), channel_id=1, source_target_pairs={{0,2},{1,3},{2,0},{3,1},{4,6},{5,7},{6,4},{7,5},{8,10},{9,11},{10,... | collective-permute-start | bytes 393224 | tf_op jit(solution)/shard_map/ppermute | solution.py:384
  65.0 2.4 %collective-permute-start.14 = (bf16[128,512]{1,0:T(8,128)(2,1)S(1)}, bf16[128,512]{1,0:T(8,128)(2,1)S(1)}, u32[]{:S(2)}, u32[]{:S(2)}) collective-permute-start(bf16[128,512]{1,0:T(8,128)(2,1)S(1)} %get-tuple-element.67), channel_id=1, source_target_pairs={{0,6},{1,7},{2,4},{3,5},{4,2},{5,3},{6,0},{7,1},{8,14},{9,15},{10,... | collective-permute-start | bytes 393224 | tf_op jit(solution)/shard_map/ppermute | solution.py:384
  68.5 1.7 %collective-permute-start.16 = (bf16[128,512]{1,0:T(8,128)(2,1)S(1)}, bf16[128,512]{1,0:T(8,128)(2,1)S(1)}, u32[]{:S(2)}, u32[]{:S(2)}) collective-permute-start(bf16[128,512]{1,0:T(8,128)(2,1)S(1)} %get-tuple-element.69), channel_id=1, source_target_pairs={{0,4},{1,5},{2,6},{3,7},{4,0},{5,1},{6,2},{7,3},{8,12},{9,13},{10,... | collective-permute-start | bytes 393224 | tf_op jit(solution)/shard_map/ppermute | solution.py:384
  70.3 9.8 %shard_map.159 = (bf16[128,512]{1,0:T(8,128)(2,1)S(1)}, bf16[128,512]{1,0:T(8,128)(2,1)S(1)}, bf16[128,512]{1,0:T(8,128)(2,1)S(1)}, bf16[128,512]{1,0:T(8,128)(2...) custom-call(s32[2]{0:T(128)S(1)} %pad_add_fusion.me, ...), custom_call_target="tpu_custom_call" | custom-call | flops 3221225472 | bytes 4194304 | tf_op jit(solution)/shard_map/pallas_call | solution.py:160
  80.1 2.5 %collective-permute-start.17 = (bf16[128,512]{1,0:T(8,128)(2,1)S(1)}, bf16[128,512]{1,0:T(8,128)(2,1)S(1)}, u32[]{:S(2)}, u32[]{:S(2)}) collective-permute-start(bf16[128,512]{1,0:T(8,128)(2,1)S(1)} %get-tuple-element.72), channel_id=1, source_target_pairs={{0,7},{1,6},{2,5},{3,4},{4,3},{5,2},{6,1},{7,0},{8,15},{9,14},{10,... | collective-permute-start | bytes 393224 | tf_op jit(solution)/shard_map/ppermute | solution.py:384
  82.6 2.4 %collective-permute-start.18 = (bf16[128,512]{1,0:T(8,128)(2,1)S(1)}, bf16[128,512]{1,0:T(8,128)(2,1)S(1)}, u32[]{:S(2)}, u32[]{:S(2)}) collective-permute-start(bf16[128,512]{1,0:T(8,128)(2,1)S(1)} %get-tuple-element.73), channel_id=1, source_target_pairs={{0,6},{1,7},{2,4},{3,5},{4,2},{5,3},{6,0},{7,1},{8,14},{9,15},{10,... | collective-permute-start | bytes 393224 | tf_op jit(solution)/shard_map/ppermute | solution.py:384
  85.0 2.9 %collective-permute-start.20 = (bf16[128,512]{1,0:T(8,128)(2,1)S(1)}, bf16[128,512]{1,0:T(8,128)(2,1)S(1)}, u32[]{:S(2)}, u32[]{:S(2)}) collective-permute-start(bf16[128,512]{1,0:T(8,128)(2,1)S(1)} %get-tuple-element.75), channel_id=1, source_target_pairs={{0,4},{1,5},{2,6},{3,7},{4,0},{5,1},{6,2},{7,3},{8,12},{9,13},{10,... | collective-permute-start | bytes 393224 | tf_op jit(solution)/shard_map/ppermute | solution.py:384
  87.8 7.8 %collective-permute-done.16.refs_15_ = bf16[128,512]{1,0:T(8,128)(2,1)S(1)} collective-permute-done((bf16[128,512]{1,0:T(8,128)(2,1)S(1)}, bf16[128,512]{1,0:T(8,128)(2,1)S(1)}, u32[]{:S(2)}, u32[]{:S(2)}) %collective-permute-start.16) | collective-permute-done | bytes 131104 | tf_op jit(solution)/shard_map/ppermute | solution.py:384
  95.7 14.3 %shard_map.160 = (bf16[2,128,512]{2,1,0:T(8,128)(2,1)S(1)}, bf16[2,128,512]{2,1,0:T(8,128)(2,1)S(1)}, bf16[2,128,512]{2,1,0:T(8,128)(2,1)S(1)}, bf16[2,128,512]{...) custom-call(s32[2]{0:T(128)S(1)} %pad_add_fusion.me, ...), custom_call_target="tpu_custom_call" | custom-call | flops 5368709120 | bytes 4194304 | tf_op jit(solution)/shard_map/pallas_call | solution.py:160
  110.0 2.1 %collective-permute-start.26 = (bf16[2,128,512]{2,1,0:T(8,128)(2,1)S(1)}, bf16[2,128,512]{2,1,0:T(8,128)(2,1)S(1)}, u32[]{:S(2)}, u32[]{:S(2)}) collective-permute-start(bf16[2,128,512]{2,1,0:T(8,128)(2,1)S(1)} %get-tuple-element.81), channel_id=1, source_target_pairs={{0,7},{1,6},{2,5},{3,4},{4,3},{5,2},{6,1},{7,0},{8,15},{9,14},{10,... | collective-permute-start | bytes 786440 | tf_op jit(solution)/shard_map/ppermute | solution.py:384
  113.5 3.3 %collective-permute-start.22 = (bf16[128,512]{1,0:T(8,128)(2,1)S(1)}, bf16[128,512]{1,0:T(8,128)(2,1)S(1)}, u32[]{:S(2)}, u32[]{:S(2)}) collective-permute-start(bf16[128,512]{1,0:T(8,128)(2,1)S(1)} %get-tuple-element.77), channel_id=1, source_target_pairs={{0,2},{1,3},{2,0},{3,1},{4,6},{5,7},{6,4},{7,5},{8,10},{9,11},{10,... | collective-permute-start | bytes 393224 | tf_op jit(solution)/shard_map/ppermute | solution.py:384
  117.0 10.2 %collective-permute-done.21.refs_5_ = bf16[128,512]{1,0:T(8,128)(2,1)S(1)} collective-permute-done((bf16[128,512]{1,0:T(8,128)(2,1)S(1)}, bf16[128,512]{1,0:T(8,128)(2,1)S(1)}, u32[]{:S(2)}, u32[]{:S(2)}) %collective-permute-start.21) | collective-permute-done | bytes 131104 | tf_op jit(solution)/shard_map/ppermute | solution.py:384
  127.2 3.4 %collective-permute-start.28 = (bf16[2,128,512]{2,1,0:T(8,128)(2,1)S(1)}, bf16[2,128,512]{2,1,0:T(8,128)(2,1)S(1)}, u32[]{:S(2)}, u32[]{:S(2)}) collective-permute-start(bf16[2,128,512]{2,1,0:T(8,128)(2,1)S(1)} %get-tuple-element.83), channel_id=1, source_target_pairs={{0,3},{1,2},{2,1},{3,0},{4,7},{5,6},{6,5},{7,4},{8,11},{9,10},{10,... | collective-permute-start | bytes 786440 | tf_op jit(solution)/shard_map/ppermute | solution.py:384
  130.6 1.9 %collective-permute-start.29 = (bf16[2,128,512]{2,1,0:T(8,128)(2,1)S(1)}, bf16[2,128,512]{2,1,0:T(8,128)(2,1)S(1)}, u32[]{:S(2)}, u32[]{:S(2)}) collective-permute-start(bf16[2,128,512]{2,1,0:T(8,128)(2,1)S(1)} %get-tuple-element.84), channel_id=1, source_target_pairs={{0,2},{1,3},{2,0},{3,1},{4,6},{5,7},{6,4},{7,5},{8,10},{9,11},{10,... | collective-permute-start | bytes 786440 | tf_op jit(solution)/shard_map/ppermute | solution.py:384
  132.5 1.9 %collective-permute-start.30 = (bf16[2,128,512]{2,1,0:T(8,128)(2,1)S(1)}, bf16[2,128,512]{2,1,0:T(8,128)(2,1)S(1)}, u32[]{:S(2)}, u32[]{:S(2)}) collective-permute-start(bf16[2,128,512]{2,1,0:T(8,128)(2,1)S(1)} %get-tuple-element.85), channel_id=1, source_target_pairs={{0,1},{1,0},{2,3},{3,2},{4,5},{5,4},{6,7},{7,6},{8,9},{9,8},{10,11... | collective-permute-start | bytes 786440 | tf_op jit(solution)/shard_map/ppermute | solution.py:384
  134.4 2.4 %collective-permute-start.25 = (bf16[2,128,512]{2,1,0:T(8,128)(2,1)S(1)}, bf16[2,128,512]{2,1,0:T(8,128)(2,1)S(1)}, u32[]{:S(2)}, u32[]{:S(2)}) collective-permute-start(bf16[2,128,512]{2,1,0:T(8,128)(2,1)S(1)} %get-tuple-element.80), channel_id=1, source_target_pairs={{0,4},{1,5},{2,6},{3,7},{4,0},{5,1},{6,2},{7,3},{8,12},{9,13},{10,... | collective-permute-start | bytes 786440 | tf_op jit(solution)/shard_map/ppermute | solution.py:384
  136.9 2.3 %shard_map.161 = bf16[8,128,512]{2,1,0:T(8,128)(2,1)} custom-call(s32[2]{0:T(128)S(1)} %pad_add_fusion.me, bf16[8,128,512]{2,1,0:T(8,128)(2,1)S(1)} %get-tuple-element.54.upstream, bf16[128,512]{1,0:T(8,128)(2,1)S(1)} %get-tuple-element.71.refs_0_, bf16[128,512]{1,0:T(8,128)(2,1)S(1)} %collective-permute-done.17.refs_1_, ...), custom_call_target="tpu_custom_call" | custom-call | flops 3145728 | bytes 3145728 | tf_op jit(solution)/shard_map/pallas_call | solution.py:317
  139.2 4.5 %collective-permute-done.29.refs_16_ = bf16[2,128,512]{2,1,0:T(8,128)(2,1)S(1)} collective-permute-done((bf16[2,128,512]{2,1,0:T(8,128)(2,1)S(1)}, bf16[2,128,512]{2,1,0:T(8,128)(2,1)S(1)}, u32[]{:S(2)}, u32[]{:S(2)}) %collective-permute-start.29) | collective-permute-done | bytes 262176 | tf_op jit(solution)/shard_map/ppermute | solution.py:384
  143.7 3.5 %shard_map.162 = (bf16[8,128,512]{2,1,0:T(8,128)(2,1)}, bf16[8,128,512]{2,1,0:T(8,128)(2,1)}, f32[8,128,512]{2,1,0:T(8,128)}) custom-call(s32[2]{0:T(128)S(1)} %pad_add_fusion.me, bf16[8,128,512]{2,1,0:T(8,128)(2,1)S(1)} %bitcast.17, bf16[8,128,512]{2,1,0:T(8,128)(2,1)S(1)} %bitcast.18, bf16[8,128,512]{2,1,0:T(8,128)(2,1)S(1)} %bitcast.19, ...), custom_call_target="tpu_custom_call" | custom-call | flops 786432 | bytes 6291456 | tf_op jit(solution)/shard_map/pallas_call | solution.py:289
  148.2 2.8 %collective-permute-done.25.refs_5_ = bf16[2,128,512]{2,1,0:T(8,128)(2,1)S(1)} collective-permute-done((bf16[2,128,512]{2,1,0:T(8,128)(2,1)S(1)}, bf16[2,128,512]{2,1,0:T(8,128)(2,1)S(1)}, u32[]{:S(2)}, u32[]{:S(2)}) %collective-permute-start.25) | collective-permute-done | bytes 262176 | tf_op jit(solution)/shard_map/ppermute | solution.py:384
  151.1 1.6 %shard_map.163 = (bf16[8,128,512]{2,1,0:T(8,128)(2,1)}, bf16[8,128,512]{2,1,0:T(8,128)(2,1)}, f32[8,128,512]{2,1,0:T(8,128)}) custom-call(s32[2]{0:T(128)S(1)} %pad_add_fusion.me, bf16[8,128,512]{2,1,0:T(8,128)(2,1)S(1)} %bitcast.23, bf16[8,128,512]{2,1,0:T(8,128)(2,1)S(1)} %bitcast.24, ...), custom_call_target="tpu_custom_call", output_to_operand_aliasing={{0}: (7, {}), {1}: (8, {}), {2}: (9, {})} | custom-call | flops 262144 | bytes 2097152 | tf_op jit(solution)/shard_map/pallas_call | solution.py:289
  (59 shorter events, 10.2 us)
Async XLA Ops:
  3.5 26.3 %collective-permute-start.1 = (bf16[1024,512]{1,0:T(8,128)(2,1)S(1)}, bf16[1024,512]{1,0:T(8,128)(2,1)}, u32[]{:S(2)}, u32[]{:S(2)}) collective-permute-start(bf16[1024,512]{1,0:T(8,128)(2,1)S(1)} %copy-done.2), channel_id=1, source_target_pairs={{0,16},{8,24},{16,0},{24,8},{1,17},{9,25},{17,1},{25,9},{2,18},{10... | collective-permute-start | bytes 3145736 | tf_op jit(solution)/shard_map/ppermute | solution.py:364
  6.5 16.5 %collective-permute-start.2 = (bf16[2,128,512]{2,1,0:T(8,128)(2,1)}, bf16[2,128,512]{2,1,0:T(8,128)(2,1)S(1)}, u32[]{:S(2)}, u32[]{:S(2)}) collective-permute-start(bf16[2,128,512]{2,1,0:T(8,128)(2,1)} %get-tuple-element.48), channel_id=1, source_target_pairs={{0,7},{1,6},{2,5},{3,4},{4,3},{5,2},{6,1},{7,0},{8,15},{9,14},{10,... | collective-permute-start | bytes 786440 | tf_op jit(solution)/shard_map/ppermute | solution.py:384
  11.1 11.9 %collective-permute-start.3 = (bf16[2,128,512]{2,1,0:T(8,128)(2,1)}, bf16[2,128,512]{2,1,0:T(8,128)(2,1)S(1)}, u32[]{:S(2)}, u32[]{:S(2)}) collective-permute-start(bf16[2,128,512]{2,1,0:T(8,128)(2,1)} %get-tuple-element.50), channel_id=1, source_target_pairs={{0,6},{1,7},{2,4},{3,5},{4,2},{5,3},{6,0},{7,1},{8,14},{9,15},{10,... | collective-permute-start | bytes 786440 | tf_op jit(solution)/shard_map/ppermute | solution.py:384
  15.2 8.3 %collective-permute-start.4 = (bf16[2,128,512]{2,1,0:T(8,128)(2,1)}, bf16[2,128,512]{2,1,0:T(8,128)(2,1)S(1)}, u32[]{:S(2)}, u32[]{:S(2)}) collective-permute-start(bf16[2,128,512]{2,1,0:T(8,128)(2,1)} %get-tuple-element.51), channel_id=1, source_target_pairs={{0,1},{1,0},{2,3},{3,2},{4,5},{5,4},{6,7},{7,6},{8,9},{9,8},{10,11... | collective-permute-start | bytes 786440 | tf_op jit(solution)/shard_map/ppermute | solution.py:384
  15.8 22.2 %collective-permute-start = (bf16[1024,512]{1,0:T(8,128)(2,1)S(1)}, bf16[1024,512]{1,0:T(8,128)(2,1)S(1)}, u32[]{:S(2)}, u32[]{:S(2)}) collective-permute-start(bf16[1024,512]{1,0:T(8,128)(2,1)S(1)} %copy-done.2), channel_id=1, source_target_pairs={{0,8},{8,0},{16,24},{24,16},{1,9},{9,1},{17,25},{25,17},{2,10},{10... | collective-permute-start | bytes 3145736 | tf_op jit(solution)/shard_map/ppermute | solution.py:378
  29.8 8.3 %collective-permute-start.5 = (bf16[1024,512]{1,0:T(8,128)(2,1)}, bf16[1024,512]{1,0:T(8,128)(2,1)}, u32[]{:S(2)}, u32[]{:S(2)}) collective-permute-start(bf16[1024,512]{1,0:T(8,128)(2,1)} %collective-permute-done.1.refs_6_), channel_id=1, source_target_pairs={{0,8},{8,0},{16,24},{24,16},{1,9},{9,1},{17,25},{25,17},{2,10},{10... | collective-permute-start | bytes 3145736 | tf_op jit(solution)/shard_map/ppermute | solution.py:378
  29.8 35.2 %collective-permute-start.6 = (bf16[2,128,512]{2,1,0:T(8,128)(2,1)}, bf16[2,128,512]{2,1,0:T(8,128)(2,1)}, u32[]{:S(2)}, u32[]{:S(2)}) collective-permute-start(bf16[2,128,512]{2,1,0:T(8,128)(2,1)} %get-tuple-element.52), channel_id=1, source_target_pairs={{0,5},{1,4},{2,7},{3,6},{4,1},{5,0},{6,3},{7,2},{8,13},{9,12},{10,... | collective-permute-start | bytes 786440 | tf_op jit(solution)/shard_map/ppermute | solution.py:384
  35.0 24.4 %collective-permute-start.7 = (bf16[2,128,512]{2,1,0:T(8,128)(2,1)}, bf16[2,128,512]{2,1,0:T(8,128)(2,1)}, u32[]{:S(2)}, u32[]{:S(2)}) collective-permute-start(bf16[2,128,512]{2,1,0:T(8,128)(2,1)} %get-tuple-element.58), channel_id=1, source_target_pairs={{0,4},{1,5},{2,6},{3,7},{4,0},{5,1},{6,2},{7,3},{8,12},{9,13},{10,... | collective-permute-start | bytes 786440 | tf_op jit(solution)/shard_map/ppermute | solution.py:384
  35.2 26.3 %collective-permute-start.8 = (bf16[2,128,512]{2,1,0:T(8,128)(2,1)}, bf16[2,128,512]{2,1,0:T(8,128)(2,1)}, u32[]{:S(2)}, u32[]{:S(2)}) collective-permute-start(bf16[2,128,512]{2,1,0:T(8,128)(2,1)} %get-tuple-element.59), channel_id=1, source_target_pairs={{0,3},{1,2},{2,1},{3,0},{4,7},{5,6},{6,5},{7,4},{8,11},{9,10},{10,... | collective-permute-start | bytes 786440 | tf_op jit(solution)/shard_map/ppermute | solution.py:384
  38.0 25.5 %collective-permute-start.9 = (bf16[2,128,512]{2,1,0:T(8,128)(2,1)}, bf16[2,128,512]{2,1,0:T(8,128)(2,1)S(1)}, u32[]{:S(2)}, u32[]{:S(2)}) collective-permute-start(bf16[2,128,512]{2,1,0:T(8,128)(2,1)} %get-tuple-element.60), channel_id=1, source_target_pairs={{0,2},{1,3},{2,0},{3,1},{4,6},{5,7},{6,4},{7,5},{8,10},{9,11},{10,... | collective-permute-start | bytes 786440 | tf_op jit(solution)/shard_map/ppermute | solution.py:384
  47.8 19.5 %collective-permute-start.10 = (bf16[128,512]{1,0:T(8,128)(2,1)S(1)}, bf16[128,512]{1,0:T(8,128)(2,1)S(1)}, u32[]{:S(2)}, u32[]{:S(2)}) collective-permute-start(bf16[128,512]{1,0:T(8,128)(2,1)S(1)} %get-tuple-element.63), channel_id=1, source_target_pairs={{0,7},{1,6},{2,5},{3,4},{4,3},{5,2},{6,1},{7,0},{8,15},{9,14},{10,... | collective-permute-start | bytes 393224 | tf_op jit(solution)/shard_map/ppermute | solution.py:384
  59.5 9.1 %collective-permute-start.11 = (bf16[128,512]{1,0:T(8,128)(2,1)S(1)}, bf16[128,512]{1,0:T(8,128)(2,1)S(1)}, u32[]{:S(2)}, u32[]{:S(2)}) collective-permute-start(bf16[128,512]{1,0:T(8,128)(2,1)S(1)} %get-tuple-element.64), channel_id=1, source_target_pairs={{0,3},{1,2},{2,1},{3,0},{4,7},{5,6},{6,5},{7,4},{8,11},{9,10},{10,... | collective-permute-start | bytes 393224 | tf_op jit(solution)/shard_map/ppermute | solution.py:384
  61.4 18.7 %collective-permute-start.12 = (bf16[128,512]{1,0:T(8,128)(2,1)S(1)}, bf16[128,512]{1,0:T(8,128)(2,1)S(1)}, u32[]{:S(2)}, u32[]{:S(2)}) collective-permute-start(bf16[128,512]{1,0:T(8,128)(2,1)S(1)} %get-tuple-element.65), channel_id=1, source_target_pairs={{0,2},{1,3},{2,0},{3,1},{4,6},{5,7},{6,4},{7,5},{8,10},{9,11},{10,... | collective-permute-start | bytes 393224 | tf_op jit(solution)/shard_map/ppermute | solution.py:384
  63.4 19.1 %collective-permute-start.13 = (bf16[128,512]{1,0:T(8,128)(2,1)S(1)}, bf16[128,512]{1,0:T(8,128)(2,1)S(1)}, u32[]{:S(2)}, u32[]{:S(2)}) collective-permute-start(bf16[128,512]{1,0:T(8,128)(2,1)S(1)} %get-tuple-element.66), channel_id=1, source_target_pairs={{0,1},{1,0},{2,3},{3,2},{4,5},{5,4},{6,7},{7,6},{8,9},{9,8},{10,11... | collective-permute-start | bytes 393224 | tf_op jit(solution)/shard_map/ppermute | solution.py:384
  65.0 20.0 %collective-permute-start.14 = (bf16[128,512]{1,0:T(8,128)(2,1)S(1)}, bf16[128,512]{1,0:T(8,128)(2,1)S(1)}, u32[]{:S(2)}, u32[]{:S(2)}) collective-permute-start(bf16[128,512]{1,0:T(8,128)(2,1)S(1)} %get-tuple-element.67), channel_id=1, source_target_pairs={{0,6},{1,7},{2,4},{3,5},{4,2},{5,3},{6,0},{7,1},{8,14},{9,15},{10,... | collective-permute-start | bytes 393224 | tf_op jit(solution)/shard_map/ppermute | solution.py:384
  67.4 17.6 %collective-permute-start.15 = (bf16[128,512]{1,0:T(8,128)(2,1)S(1)}, bf16[128,512]{1,0:T(8,128)(2,1)S(1)}, u32[]{:S(2)}, u32[]{:S(2)}) collective-permute-start(bf16[128,512]{1,0:T(8,128)(2,1)S(1)} %get-tuple-element.68), channel_id=1, source_target_pairs={{0,5},{1,4},{2,7},{3,6},{4,1},{5,0},{6,3},{7,2},{8,13},{9,12},{10,... | collective-permute-start | bytes 393224 | tf_op jit(solution)/shard_map/ppermute | solution.py:384
  68.5 27.2 %collective-permute-start.16 = (bf16[128,512]{1,0:T(8,128)(2,1)S(1)}, bf16[128,512]{1,0:T(8,128)(2,1)S(1)}, u32[]{:S(2)}, u32[]{:S(2)}) collective-permute-start(bf16[128,512]{1,0:T(8,128)(2,1)S(1)} %get-tuple-element.69), channel_id=1, source_target_pairs={{0,4},{1,5},{2,6},{3,7},{4,0},{5,1},{6,2},{7,3},{8,12},{9,13},{10,... | collective-permute-start | bytes 393224 | tf_op jit(solution)/shard_map/ppermute | solution.py:384
  80.1 32.0 %collective-permute-start.17 = (bf16[128,512]{1,0:T(8,128)(2,1)S(1)}, bf16[128,512]{1,0:T(8,128)(2,1)S(1)}, u32[]{:S(2)}, u32[]{:S(2)}) collective-permute-start(bf16[128,512]{1,0:T(8,128)(2,1)S(1)} %get-tuple-element.72), channel_id=1, source_target_pairs={{0,7},{1,6},{2,5},{3,4},{4,3},{5,2},{6,1},{7,0},{8,15},{9,14},{10,... | collective-permute-start | bytes 393224 | tf_op jit(solution)/shard_map/ppermute | solution.py:384
  82.6 30.9 %collective-permute-start.18 = (bf16[128,512]{1,0:T(8,128)(2,1)S(1)}, bf16[128,512]{1,0:T(8,128)(2,1)S(1)}, u32[]{:S(2)}, u32[]{:S(2)}) collective-permute-start(bf16[128,512]{1,0:T(8,128)(2,1)S(1)} %get-tuple-element.73), channel_id=1, source_target_pairs={{0,6},{1,7},{2,4},{3,5},{4,2},{5,3},{6,0},{7,1},{8,14},{9,15},{10,... | collective-permute-start | bytes 393224 | tf_op jit(solution)/shard_map/ppermute | solution.py:384
  85.0 28.5 %collective-permute-start.19 = (bf16[128,512]{1,0:T(8,128)(2,1)S(1)}, bf16[128,512]{1,0:T(8,128)(2,1)S(1)}, u32[]{:S(2)}, u32[]{:S(2)}) collective-permute-start(bf16[128,512]{1,0:T(8,128)(2,1)S(1)} %get-tuple-element.74), channel_id=1, source_target_pairs={{0,5},{1,4},{2,7},{3,6},{4,1},{5,0},{6,3},{7,2},{8,13},{9,12},{10,... | collective-permute-start | bytes 393224 | tf_op jit(solution)/shard_map/ppermute | solution.py:384
  85.0 31.8 %collective-permute-start.20 = (bf16[128,512]{1,0:T(8,128)(2,1)S(1)}, bf16[128,512]{1,0:T(8,128)(2,1)S(1)}, u32[]{:S(2)}, u32[]{:S(2)}) collective-permute-start(bf16[128,512]{1,0:T(8,128)(2,1)S(1)} %get-tuple-element.75), channel_id=1, source_target_pairs={{0,4},{1,5},{2,6},{3,7},{4,0},{5,1},{6,2},{7,3},{8,12},{9,13},{10,... | collective-permute-start | bytes 393224 | tf_op jit(solution)/shard_map/ppermute | solution.py:384
  109.9 33.8 %copy-start = (bf16[1024,512]{1,0:T(8,128)(2,1)S(1)}, bf16[1024,512]{1,0:T(8,128)(2,1)}, u32[]{:S(2)}) copy-start(bf16[1024,512]{1,0:T(8,128)(2,1)} %param.14) | copy-start | bytes 3145732
  110.0 24.5 %collective-permute-start.26 = (bf16[2,128,512]{2,1,0:T(8,128)(2,1)S(1)}, bf16[2,128,512]{2,1,0:T(8,128)(2,1)S(1)}, u32[]{:S(2)}, u32[]{:S(2)}) collective-permute-start(bf16[2,128,512]{2,1,0:T(8,128)(2,1)S(1)} %get-tuple-element.81), channel_id=1, source_target_pairs={{0,7},{1,6},{2,5},{3,4},{4,3},{5,2},{6,1},{7,0},{8,15},{9,14},{10,... | collective-permute-start | bytes 786440 | tf_op jit(solution)/shard_map/ppermute | solution.py:384
  112.1 22.4 %collective-permute-start.27 = (bf16[2,128,512]{2,1,0:T(8,128)(2,1)S(1)}, bf16[2,128,512]{2,1,0:T(8,128)(2,1)S(1)}, u32[]{:S(2)}, u32[]{:S(2)}) collective-permute-start(bf16[2,128,512]{2,1,0:T(8,128)(2,1)S(1)} %get-tuple-element.82), channel_id=1, source_target_pairs={{0,6},{1,7},{2,4},{3,5},{4,2},{5,3},{6,0},{7,1},{8,14},{9,15},{10,... | collective-permute-start | bytes 786440 | tf_op jit(solution)/shard_map/ppermute | solution.py:384
  113.5 13.7 %collective-permute-start.21 = (bf16[128,512]{1,0:T(8,128)(2,1)S(1)}, bf16[128,512]{1,0:T(8,128)(2,1)S(1)}, u32[]{:S(2)}, u32[]{:S(2)}) collective-permute-start(bf16[128,512]{1,0:T(8,128)(2,1)S(1)} %get-tuple-element.76), channel_id=1, source_target_pairs={{0,3},{1,2},{2,1},{3,0},{4,7},{5,6},{6,5},{7,4},{8,11},{9,10},{10,... | collective-permute-start | bytes 393224 | tf_op jit(solution)/shard_map/ppermute | solution.py:384
  113.5 17.1 %collective-permute-start.22 = (bf16[128,512]{1,0:T(8,128)(2,1)S(1)}, bf16[128,512]{1,0:T(8,128)(2,1)S(1)}, u32[]{:S(2)}, u32[]{:S(2)}) collective-permute-start(bf16[128,512]{1,0:T(8,128)(2,1)S(1)} %get-tuple-element.77), channel_id=1, source_target_pairs={{0,2},{1,3},{2,0},{3,1},{4,6},{5,7},{6,4},{7,5},{8,10},{9,11},{10,... | collective-permute-start | bytes 393224 | tf_op jit(solution)/shard_map/ppermute | solution.py:384
  116.8 15.7 %collective-permute-start.23 = (bf16[128,512]{1,0:T(8,128)(2,1)S(1)}, bf16[128,512]{1,0:T(8,128)(2,1)S(1)}, u32[]{:S(2)}, u32[]{:S(2)}) collective-permute-start(bf16[128,512]{1,0:T(8,128)(2,1)S(1)} %get-tuple-element.78), channel_id=1, source_target_pairs={{0,1},{1,0},{2,3},{3,2},{4,5},{5,4},{6,7},{7,6},{8,9},{9,8},{10,11... | collective-permute-start | bytes 393224 | tf_op jit(solution)/shard_map/ppermute | solution.py:384
  127.2 12.0 %collective-permute-start.28 = (bf16[2,128,512]{2,1,0:T(8,128)(2,1)S(1)}, bf16[2,128,512]{2,1,0:T(8,128)(2,1)S(1)}, u32[]{:S(2)}, u32[]{:S(2)}) collective-permute-start(bf16[2,128,512]{2,1,0:T(8,128)(2,1)S(1)} %get-tuple-element.83), channel_id=1, source_target_pairs={{0,3},{1,2},{2,1},{3,0},{4,7},{5,6},{6,5},{7,4},{8,11},{9,10},{10,... | collective-permute-start | bytes 786440 | tf_op jit(solution)/shard_map/ppermute | solution.py:384
  130.6 13.1 %collective-permute-start.29 = (bf16[2,128,512]{2,1,0:T(8,128)(2,1)S(1)}, bf16[2,128,512]{2,1,0:T(8,128)(2,1)S(1)}, u32[]{:S(2)}, u32[]{:S(2)}) collective-permute-start(bf16[2,128,512]{2,1,0:T(8,128)(2,1)S(1)} %get-tuple-element.84), channel_id=1, source_target_pairs={{0,2},{1,3},{2,0},{3,1},{4,6},{5,7},{6,4},{7,5},{8,10},{9,11},{10,... | collective-permute-start | bytes 786440 | tf_op jit(solution)/shard_map/ppermute | solution.py:384
  132.5 11.2 %collective-permute-start.30 = (bf16[2,128,512]{2,1,0:T(8,128)(2,1)S(1)}, bf16[2,128,512]{2,1,0:T(8,128)(2,1)S(1)}, u32[]{:S(2)}, u32[]{:S(2)}) collective-permute-start(bf16[2,128,512]{2,1,0:T(8,128)(2,1)S(1)} %get-tuple-element.85), channel_id=1, source_target_pairs={{0,1},{1,0},{2,3},{3,2},{4,5},{5,4},{6,7},{7,6},{8,9},{9,8},{10,11... | collective-permute-start | bytes 786440 | tf_op jit(solution)/shard_map/ppermute | solution.py:384
  134.4 13.8 %collective-permute-start.24 = (bf16[2,128,512]{2,1,0:T(8,128)(2,1)S(1)}, bf16[2,128,512]{2,1,0:T(8,128)(2,1)S(1)}, u32[]{:S(2)}, u32[]{:S(2)}) collective-permute-start(bf16[2,128,512]{2,1,0:T(8,128)(2,1)S(1)} %get-tuple-element.79), channel_id=1, source_target_pairs={{0,5},{1,4},{2,7},{3,6},{4,1},{5,0},{6,3},{7,2},{8,13},{9,12},{10,... | collective-permute-start | bytes 786440 | tf_op jit(solution)/shard_map/ppermute | solution.py:384
  134.4 16.6 %collective-permute-start.25 = (bf16[2,128,512]{2,1,0:T(8,128)(2,1)S(1)}, bf16[2,128,512]{2,1,0:T(8,128)(2,1)S(1)}, u32[]{:S(2)}, u32[]{:S(2)}) collective-permute-start(bf16[2,128,512]{2,1,0:T(8,128)(2,1)S(1)} %get-tuple-element.80), channel_id=1, source_target_pairs={{0,4},{1,5},{2,6},{3,7},{4,0},{5,1},{6,2},{7,3},{8,12},{9,13},{10,... | collective-permute-start | bytes 786440 | tf_op jit(solution)/shard_map/ppermute | solution.py:384
  (8 other events, 192.5 us)

commit v12 on v10

--- a/solution.py
+++ b/solution.py
@@ -111,8 +111,22 @@
     return (left[0] * right[0] + left[1] * right[1], left[1] * right[0] - left[0] * right[1])
 
 
+def pair_order(chunks):
+    half = chunks // 2
+    return [*range(half), *range(half + 1, chunks - 1), half, chunks - 1]
+
+
+def grad_order(chunks):
+    half = chunks // 2
+    return [0, 1, *range(half + 1, chunks), *range(2, half + 1)]
+
+
+def in_place(refs, order):
+    return [refs[order.index(k)] for k in range(len(refs))]
+
+
 def response_kernel(chunks, inner, me, *refs):
-    pair, refs = refs[:chunks], refs[chunks:]
+    pair, refs = in_place(refs[:chunks], pair_order(chunks)), refs[chunks:]
     (first, last, cos, sin, forward, backward), outs = refs[:6], refs[6:]
     tables = (first[...], cos[...], sin[...], forward[...], inner)
     prod = forward_dft(gather_slabs([ref[0] for ref in pair], inner), *tables)
@@ -123,6 +137,7 @@
 
 def backward_kernel(chunks, inner, scale, me, *refs):
     pair, grad, refs = refs[:chunks], refs[chunks : 2 * chunks], refs[2 * chunks :]
+    pair, grad = in_place(pair, pair_order(chunks)), in_place(grad, grad_order(chunks))
     (first, last, cos, sin, forward, backward), outs = refs[:6], refs[6:]
     tables = (first[...], cos[...], sin[...], forward[...], inner)
     back_tables = (last[...], cos[...], sin[...], backward[...], inner)
@@ -423,18 +438,18 @@
     far = gather_start(cotangent)
     own, *rest = prepare_call([0] + masks[first:], *sources)
     pair = exchange([own, *head, *rest])
-    gathered = gather_rest(cotangent, far, (pair[1:first], pair[-1:], rest[:1]))
+    gathered = gather_rest(cotangent, far, (pair[1:first], pair[-1:], rest[:1], tables[:2]))
+    pair_sent = [pair[k] for k in pair_order(n_ctx)]
     upstream, *grad = project_call(me, out_weight, gathered, split(outer_gate))
     response = conv_call(
-        functools.partial(response_kernel, n_ctx, inner), me, (after(pair, grad[0]),), tables, (), inner, 3
-    )
-    grad[-2:], _ = lax.optimization_barrier((grad[-2:], response[0]))
+        functools.partial(response_kernel, n_ctx, inner), me, (after(pair_sent, grad[0]),), tables, (), inner, 3
+    )
     grad_came = exchange(grad)
     resp_came = exchange(response)
     backs = conv_call(
         functools.partial(backward_kernel, n_ctx, inner, scale),
         me,
-        (pair, after(grad_came, response[0])),
+        (pair_sent, after([grad_came[k] for k in grad_order(n_ctx)], response[0])),
         tables,
         (2,),
         inner,

time: 155 us -> 152 us (0.981)
  waiting for transfers between devices: 57.2 us -> 50.7 us
  starting transfers between devices: 46.7 us -> 50 us
    ppermute x28, waiting for transfers between devices: 50.9 us -> 44.6 us  [send(): return lax.ppermute(part, 'ctx', [(p, p ^ d) for p in range(count)])]
    ppermute x28, starting transfers between devices: 43.7 us -> 47 us  [send(): return lax.ppermute(part, 'ctx', [(p, p ^ d) for p in range(count)])]
  transfers between devices with their start and end apart: 31 -> 31, of which waited for: 14 -> 12; matrix products, arithmetic and copies ran while one was open for 1% -> 1% of each run, Pallas kernels for 27% -> 28%
where the time goes in v12:
time: 152 us
  waiting for transfers between devices  50.7 us (33%)
  starting transfers between devices  50 us (33%)
  Pallas kernels  46.8 us (31%)
  local copies, waits for them, and re-layouts  3.2 us (2%)
    ppermute x28, starting transfers between devices, send(): return lax.ppermute(part, 'ctx', [(p, p ^ d) for p in range(count)])  47 us
    ppermute x28, waiting for transfers between devices, send(): return lax.ppermute(part, 'ctx', [(p, p ^ d) for p in range(count)])  44.6 us
    pallas_call x2, Pallas kernels, conv_call(): pl.pallas_call(kernel, grid_spec=pltpu.PrefetchScalarGridSpec(num_scalar_...  24.1 us
    pallas_call x1, Pallas kernels, project_call(): pl.pallas_call(functools.partial(project_kernel, chunks, members), grid_s...  8.49 us
    pallas_call x2, Pallas kernels, prepare_call(): pl.pallas_call(functools.partial(prepare_kernel, masks, scale), in_specs=...  6.75 us
    ppermute x1, waiting for transfers between devices, gather_start(): lax.ppermute(block, 'group', [(g, g ^ count // 2) for g in range(count)])  6.16 us
    pallas_call x2, Pallas kernels, finish_call(): pl.pallas_call(functools.partial(finish_kernel, count), grid_spec=pltpu.P...  5.16 us
  transfers between devices with their start and end apart: 31, of which 12 were waited for; matrix products, arithmetic and copies ran while one was open for 1% of the time, Pallas kernels for 28%

profile of v12, /device:TPU:0, one launch (start us, length us, event | category | flops | bytes accessed | tf_op | source)
XLA Modules:
  0.0 151.7 jit_solution(6995795658801734302)
XLA Ops:
  0.6 2.9 %shard_map.156 = (bf16[2,128,512]{2,1,0:T(8,128)(2,1)}, bf16[2,128,512]{2,1,0:T(8,128)(2,1)}) custom-call(bf16[8,128,512]{2,1,0:T(8,128)(2,1)} %bitcast.15, bf16[8,128,512]{2,1,0:T(8,128)(2,1)} %bitcast.25, f32[8,128,512]{2,1,0:T(8,128)} %bitcast.36, f32[8,128]{1,0:T(8,128)} %bitcast.42), custom_call_target="tpu_custom_call" | custom-call | flops 1048576 | bytes 1572864 | tf_op jit(solution)/shard_map/pallas_call | solution.py:224
  3.5 3.0 %collective-permute-start.1 = (bf16[1024,512]{1,0:T(8,128)(2,1)S(1)}, bf16[1024,512]{1,0:T(8,128)(2,1)}, u32[]{:S(2)}, u32[]{:S(2)}) collective-permute-start(bf16[1024,512]{1,0:T(8,128)(2,1)S(1)} %copy-done.2), channel_id=1, source_target_pairs={{0,16},{8,24},{16,0},{24,8},{1,17},{9,25},{17,1},{25,9},{2,18},{10... | collective-permute-start | bytes 3145736 | tf_op jit(solution)/shard_map/ppermute | solution.py:373
  6.5 4.6 %collective-permute-start.2 = (bf16[2,128,512]{2,1,0:T(8,128)(2,1)}, bf16[2,128,512]{2,1,0:T(8,128)(2,1)S(1)}, u32[]{:S(2)}, u32[]{:S(2)}) collective-permute-start(bf16[2,128,512]{2,1,0:T(8,128)(2,1)} %get-tuple-element.48), channel_id=1, source_target_pairs={{0,7},{1,6},{2,5},{3,4},{4,3},{5,2},{6,1},{7,0},{8,15},{9,14},{10,... | collective-permute-start | bytes 786440 | tf_op jit(solution)/shard_map/ppermute | solution.py:393
  11.3 3.9 %shard_map.157 = (bf16[2,128,512]{2,1,0:T(8,128)(2,1)}, bf16[2,128,512]{2,1,0:T(8,128)(2,1)}, bf16[2,128,512]{2,1,0:T(8,128)(2,1)}, bf16[2,128,512]{2,1,0:T(8,12...) custom-call(bf16[8,128,512]{2,1,0:T(8,128)(2,1)} %bitcast.16, bf16[8,128,512]{2,1,0:T(8,128)(2,1)} %bitcast.26, ...), custom_call_target="tpu_custom_call" | custom-call | flops 3145728 | bytes 4718592 | tf_op jit(solution)/shard_map/pallas_call | solution.py:224
  17.7 5.3 %collective-permute-done.3.refs_2_ = bf16[2,128,512]{2,1,0:T(8,128)(2,1)S(1)} collective-permute-done((bf16[2,128,512]{2,1,0:T(8,128)(2,1)}, bf16[2,128,512]{2,1,0:T(8,128)(2,1)S(1)}, u32[]{:S(2)}, u32[]{:S(2)}) %collective-permute-start.3) | collective-permute-done | bytes 262176 | tf_op jit(solution)/shard_map/ppermute | solution.py:393
  23.6 6.2 %collective-permute-done.1.refs_6_ = bf16[1024,512]{1,0:T(8,128)(2,1)} collective-permute-done((bf16[1024,512]{1,0:T(8,128)(2,1)S(1)}, bf16[1024,512]{1,0:T(8,128)(2,1)}, u32[]{:S(2)}, u32[]{:S(2)}) %collective-permute-start.1) | collective-permute-done | bytes 1048608 | tf_op jit(solution)/shard_map/ppermute | solution.py:373
  29.8 5.2 %collective-permute-start.6 = (bf16[2,128,512]{2,1,0:T(8,128)(2,1)}, bf16[2,128,512]{2,1,0:T(8,128)(2,1)}, u32[]{:S(2)}, u32[]{:S(2)}) collective-permute-start(bf16[2,128,512]{2,1,0:T(8,128)(2,1)} %get-tuple-element.52), channel_id=1, source_target_pairs={{0,5},{1,4},{2,7},{3,6},{4,1},{5,0},{6,3},{7,2},{8,13},{9,12},{10,... | collective-permute-start | bytes 786440 | tf_op jit(solution)/shard_map/ppermute | solution.py:393
  35.1 2.9 %collective-permute-start.8 = (bf16[2,128,512]{2,1,0:T(8,128)(2,1)}, bf16[2,128,512]{2,1,0:T(8,128)(2,1)}, u32[]{:S(2)}, u32[]{:S(2)}) collective-permute-start(bf16[2,128,512]{2,1,0:T(8,128)(2,1)} %get-tuple-element.59), channel_id=1, source_target_pairs={{0,2},{1,3},{2,0},{3,1},{4,6},{5,7},{6,4},{7,5},{8,10},{9,11},{10,... | collective-permute-start | bytes 786440 | tf_op jit(solution)/shard_map/ppermute | solution.py:393
  39.4 8.5 %shard_map.158 = (bf16[8,128,512]{2,1,0:T(8,128)(2,1)S(1)}, bf16[128,512]{1,0:T(8,128)(2,1)S(1)}, bf16[128,512]{1,0:T(8,128)(2,1)S(1)}, bf16[128,512]{1,0:T(8,12...) custom-call(s32[2]{0:T(128)S(1)} %pad_add_fusion.me, ...), custom_call_target="tpu_custom_call" | custom-call | flops 4294967296 | bytes 8388608 | tf_op jit(solution)/shard_map/pallas_call | solution.py:348
  47.9 2.5 %collective-permute-start.10 = (bf16[128,512]{1,0:T(8,128)(2,1)S(1)}, bf16[128,512]{1,0:T(8,128)(2,1)S(1)}, u32[]{:S(2)}, u32[]{:S(2)}) collective-permute-start(bf16[128,512]{1,0:T(8,128)(2,1)S(1)} %get-tuple-element.63), channel_id=1, source_target_pairs={{0,7},{1,6},{2,5},{3,4},{4,3},{5,2},{6,1},{7,0},{8,15},{9,14},{10,... | collective-permute-start | bytes 393224 | tf_op jit(solution)/shard_map/ppermute | solution.py:393
  50.4 4.1 %collective-permute-done.7.refs_4_ = bf16[2,128,512]{2,1,0:T(8,128)(2,1)} collective-permute-done((bf16[2,128,512]{2,1,0:T(8,128)(2,1)}, bf16[2,128,512]{2,1,0:T(8,128)(2,1)}, u32[]{:S(2)}, u32[]{:S(2)}) %collective-permute-start.7) | collective-permute-done | bytes 262176 | tf_op jit(solution)/shard_map/ppermute | solution.py:393
  54.5 7.0 %collective-permute-done.8.refs_5_ = bf16[2,128,512]{2,1,0:T(8,128)(2,1)} collective-permute-done((bf16[2,128,512]{2,1,0:T(8,128)(2,1)}, bf16[2,128,512]{2,1,0:T(8,128)(2,1)}, u32[]{:S(2)}, u32[]{:S(2)}) %collective-permute-start.8) | collective-permute-done | bytes 262176 | tf_op jit(solution)/shard_map/ppermute | solution.py:393
  62.7 2.6 %collective-permute-done.10.refs_9_ = bf16[128,512]{1,0:T(8,128)(2,1)S(1)} collective-permute-done((bf16[128,512]{1,0:T(8,128)(2,1)S(1)}, bf16[128,512]{1,0:T(8,128)(2,1)S(1)}, u32[]{:S(2)}, u32[]{:S(2)}) %collective-permute-start.10) | collective-permute-done | bytes 131104 | tf_op jit(solution)/shard_map/ppermute | solution.py:393
  65.3 2.9 %collective-permute-start.15 = (bf16[128,512]{1,0:T(8,128)(2,1)S(1)}, bf16[128,512]{1,0:T(8,128)(2,1)S(1)}, u32[]{:S(2)}, u32[]{:S(2)}) collective-permute-start(bf16[128,512]{1,0:T(8,128)(2,1)S(1)} %get-tuple-element.68), channel_id=1, source_target_pairs={{0,5},{1,4},{2,7},{3,6},{4,1},{5,0},{6,3},{7,2},{8,13},{9,12},{10,... | collective-permute-start | bytes 393224 | tf_op jit(solution)/shard_map/ppermute | solution.py:393
  68.9 9.8 %shard_map.159 = (bf16[128,512]{1,0:T(8,128)(2,1)S(1)}, bf16[128,512]{1,0:T(8,128)(2,1)S(1)}, bf16[128,512]{1,0:T(8,128)(2,1)S(1)}, bf16[128,512]{1,0:T(8,128)(2...) custom-call(s32[2]{0:T(128)S(1)} %pad_add_fusion.me, ...), custom_call_target="tpu_custom_call" | custom-call | flops 3221225472 | bytes 4194304 | tf_op jit(solution)/shard_map/pallas_call | solution.py:169
  78.7 1.9 %collective-permute-start.17 = (bf16[128,512]{1,0:T(8,128)(2,1)S(1)}, bf16[128,512]{1,0:T(8,128)(2,1)S(1)}, u32[]{:S(2)}, u32[]{:S(2)}) collective-permute-start(bf16[128,512]{1,0:T(8,128)(2,1)S(1)} %get-tuple-element.72), channel_id=1, source_target_pairs={{0,7},{1,6},{2,5},{3,4},{4,3},{5,2},{6,1},{7,0},{8,15},{9,14},{10,... | collective-permute-start | bytes 393224 | tf_op jit(solution)/shard_map/ppermute | solution.py:393
  80.7 2.7 %collective-permute-start.18 = (bf16[128,512]{1,0:T(8,128)(2,1)S(1)}, bf16[128,512]{1,0:T(8,128)(2,1)S(1)}, u32[]{:S(2)}, u32[]{:S(2)}) collective-permute-start(bf16[128,512]{1,0:T(8,128)(2,1)S(1)} %get-tuple-element.73), channel_id=1, source_target_pairs={{0,6},{1,7},{2,4},{3,5},{4,2},{5,3},{6,0},{7,1},{8,14},{9,15},{10,... | collective-permute-start | bytes 393224 | tf_op jit(solution)/shard_map/ppermute | solution.py:393
  84.0 2.4 %collective-permute-start.20 = (bf16[128,512]{1,0:T(8,128)(2,1)S(1)}, bf16[128,512]{1,0:T(8,128)(2,1)S(1)}, u32[]{:S(2)}, u32[]{:S(2)}) collective-permute-start(bf16[128,512]{1,0:T(8,128)(2,1)S(1)} %get-tuple-element.75), channel_id=1, source_target_pairs={{0,4},{1,5},{2,6},{3,7},{4,0},{5,1},{6,2},{7,3},{8,12},{9,13},{10,... | collective-permute-start | bytes 393224 | tf_op jit(solution)/shard_map/ppermute | solution.py:393
  86.5 8.3 %collective-permute-done.16.refs_15_ = bf16[128,512]{1,0:T(8,128)(2,1)S(1)} collective-permute-done((bf16[128,512]{1,0:T(8,128)(2,1)S(1)}, bf16[128,512]{1,0:T(8,128)(2,1)S(1)}, u32[]{:S(2)}, u32[]{:S(2)}) %collective-permute-start.16) | collective-permute-done | bytes 131104 | tf_op jit(solution)/shard_map/ppermute | solution.py:393
  94.8 14.3 %shard_map.160 = (bf16[2,128,512]{2,1,0:T(8,128)(2,1)S(1)}, bf16[2,128,512]{2,1,0:T(8,128)(2,1)S(1)}, bf16[2,128,512]{2,1,0:T(8,128)(2,1)S(1)}, bf16[2,128,512]{...) custom-call(s32[2]{0:T(128)S(1)} %pad_add_fusion.me, ...), custom_call_target="tpu_custom_call" | custom-call | flops 5368709120 | bytes 4194304 | tf_op jit(solution)/shard_map/pallas_call | solution.py:169
  109.2 4.8 %collective-permute-start.27 = (bf16[2,128,512]{2,1,0:T(8,128)(2,1)S(1)}, bf16[2,128,512]{2,1,0:T(8,128)(2,1)S(1)}, u32[]{:S(2)}, u32[]{:S(2)}) collective-permute-start(bf16[2,128,512]{2,1,0:T(8,128)(2,1)S(1)} %get-tuple-element.82), channel_id=1, source_target_pairs={{0,6},{1,7},{2,4},{3,5},{4,2},{5,3},{6,0},{7,1},{8,14},{9,15},{10,... | collective-permute-start | bytes 786440 | tf_op jit(solution)/shard_map/ppermute | solution.py:393
  114.0 1.9 %collective-permute-start.22 = (bf16[128,512]{1,0:T(8,128)(2,1)S(1)}, bf16[128,512]{1,0:T(8,128)(2,1)S(1)}, u32[]{:S(2)}, u32[]{:S(2)}) collective-permute-start(bf16[128,512]{1,0:T(8,128)(2,1)S(1)} %get-tuple-element.77), channel_id=1, source_target_pairs={{0,2},{1,3},{2,0},{3,1},{4,6},{5,7},{6,4},{7,5},{8,10},{9,11},{10,... | collective-permute-start | bytes 393224 | tf_op jit(solution)/shard_map/ppermute | solution.py:393
  117.5 6.8 %collective-permute-done.21.refs_5_ = bf16[128,512]{1,0:T(8,128)(2,1)S(1)} collective-permute-done((bf16[128,512]{1,0:T(8,128)(2,1)S(1)}, bf16[128,512]{1,0:T(8,128)(2,1)S(1)}, u32[]{:S(2)}, u32[]{:S(2)}) %collective-permute-start.21) | collective-permute-done | bytes 131104 | tf_op jit(solution)/shard_map/ppermute | solution.py:393
  124.3 2.5 %collective-permute-start.28 = (bf16[2,128,512]{2,1,0:T(8,128)(2,1)S(1)}, bf16[2,128,512]{2,1,0:T(8,128)(2,1)S(1)}, u32[]{:S(2)}, u32[]{:S(2)}) collective-permute-start(bf16[2,128,512]{2,1,0:T(8,128)(2,1)S(1)} %get-tuple-element.83), channel_id=1, source_target_pairs={{0,3},{1,2},{2,1},{3,0},{4,7},{5,6},{6,5},{7,4},{8,11},{9,10},{10,... | collective-permute-start | bytes 786440 | tf_op jit(solution)/shard_map/ppermute | solution.py:393
  128.8 3.3 %collective-permute-start.30 = (bf16[2,128,512]{2,1,0:T(8,128)(2,1)S(1)}, bf16[2,128,512]{2,1,0:T(8,128)(2,1)S(1)}, u32[]{:S(2)}, u32[]{:S(2)}) collective-permute-start(bf16[2,128,512]{2,1,0:T(8,128)(2,1)S(1)} %get-tuple-element.85), channel_id=1, source_target_pairs={{0,1},{1,0},{2,3},{3,2},{4,5},{5,4},{6,7},{7,6},{8,9},{9,8},{10,11... | collective-permute-start | bytes 786440 | tf_op jit(solution)/shard_map/ppermute | solution.py:393
  132.1 2.7 %collective-permute-start.24 = (bf16[2,128,512]{2,1,0:T(8,128)(2,1)S(1)}, bf16[2,128,512]{2,1,0:T(8,128)(2,1)S(1)}, u32[]{:S(2)}, u32[]{:S(2)}) collective-permute-start(bf16[2,128,512]{2,1,0:T(8,128)(2,1)S(1)} %get-tuple-element.79), channel_id=1, source_target_pairs={{0,5},{1,4},{2,7},{3,6},{4,1},{5,0},{6,3},{7,2},{8,13},{9,12},{10,... | collective-permute-start | bytes 786440 | tf_op jit(solution)/shard_map/ppermute | solution.py:393
  135.7 2.3 %shard_map.161 = bf16[8,128,512]{2,1,0:T(8,128)(2,1)} custom-call(s32[2]{0:T(128)S(1)} %pad_add_fusion.me, bf16[8,128,512]{2,1,0:T(8,128)(2,1)S(1)} %get-tuple-element.54.upstream, bf16[128,512]{1,0:T(8,128)(2,1)S(1)} %get-tuple-element.71.refs_0_, bf16[128,512]{1,0:T(8,128)(2,1)S(1)} %collective-permute-done.17.refs_1_, ...), custom_call_target="tpu_custom_call" | custom-call | flops 3145728 | bytes 3145728 | tf_op jit(solution)/shard_map/pallas_call | solution.py:326
  138.0 4.4 %collective-permute-done.29.refs_16_ = bf16[2,128,512]{2,1,0:T(8,128)(2,1)S(1)} collective-permute-done((bf16[2,128,512]{2,1,0:T(8,128)(2,1)S(1)}, bf16[2,128,512]{2,1,0:T(8,128)(2,1)S(1)}, u32[]{:S(2)}, u32[]{:S(2)}) %collective-permute-start.29) | collective-permute-done | bytes 262176 | tf_op jit(solution)/shard_map/ppermute | solution.py:393
  142.4 3.5 %shard_map.162 = (bf16[8,128,512]{2,1,0:T(8,128)(2,1)}, bf16[8,128,512]{2,1,0:T(8,128)(2,1)}, f32[8,128,512]{2,1,0:T(8,128)}) custom-call(s32[2]{0:T(128)S(1)} %pad_add_fusion.me, bf16[8,128,512]{2,1,0:T(8,128)(2,1)S(1)} %bitcast.17, bf16[8,128,512]{2,1,0:T(8,128)(2,1)S(1)} %bitcast.18, bf16[8,128,512]{2,1,0:T(8,128)(2,1)S(1)} %bitcast.19, ...), custom_call_target="tpu_custom_call" | custom-call | flops 786432 | bytes 6291456 | tf_op jit(solution)/shard_map/pallas_call | solution.py:298
  145.9 2.2 %collective-permute-done.24.refs_4_ = bf16[2,128,512]{2,1,0:T(8,128)(2,1)S(1)} collective-permute-done((bf16[2,128,512]{2,1,0:T(8,128)(2,1)S(1)}, bf16[2,128,512]{2,1,0:T(8,128)(2,1)S(1)}, u32[]{:S(2)}, u32[]{:S(2)}) %collective-permute-start.24) | collective-permute-done | bytes 262176 | tf_op jit(solution)/shard_map/ppermute | solution.py:393
  148.1 2.0 %collective-permute-done.25.refs_5_ = bf16[2,128,512]{2,1,0:T(8,128)(2,1)S(1)} collective-permute-done((bf16[2,128,512]{2,1,0:T(8,128)(2,1)S(1)}, bf16[2,128,512]{2,1,0:T(8,128)(2,1)S(1)}, u32[]{:S(2)}, u32[]{:S(2)}) %collective-permute-start.25) | collective-permute-done | bytes 262176 | tf_op jit(solution)/shard_map/ppermute | solution.py:393
  150.0 1.6 %shard_map.163 = (bf16[8,128,512]{2,1,0:T(8,128)(2,1)}, bf16[8,128,512]{2,1,0:T(8,128)(2,1)}, f32[8,128,512]{2,1,0:T(8,128)}) custom-call(s32[2]{0:T(128)S(1)} %pad_add_fusion.me, bf16[8,128,512]{2,1,0:T(8,128)(2,1)S(1)} %bitcast.23, bf16[8,128,512]{2,1,0:T(8,128)(2,1)S(1)} %bitcast.24, ...), custom_call_target="tpu_custom_call", output_to_operand_aliasing={{0}: (7, {}), {1}: (8, {}), {2}: (9, {})} | custom-call | flops 262144 | bytes 2097152 | tf_op jit(solution)/shard_map/pallas_call | solution.py:298
  (59 shorter events, 11.9 us)
Async XLA Ops:
  3.5 26.3 %collective-permute-start.1 = (bf16[1024,512]{1,0:T(8,128)(2,1)S(1)}, bf16[1024,512]{1,0:T(8,128)(2,1)}, u32[]{:S(2)}, u32[]{:S(2)}) collective-permute-start(bf16[1024,512]{1,0:T(8,128)(2,1)S(1)} %copy-done.2), channel_id=1, source_target_pairs={{0,16},{8,24},{16,0},{24,8},{1,17},{9,25},{17,1},{25,9},{2,18},{10... | collective-permute-start | bytes 3145736 | tf_op jit(solution)/shard_map/ppermute | solution.py:373
  6.5 16.5 %collective-permute-start.2 = (bf16[2,128,512]{2,1,0:T(8,128)(2,1)}, bf16[2,128,512]{2,1,0:T(8,128)(2,1)S(1)}, u32[]{:S(2)}, u32[]{:S(2)}) collective-permute-start(bf16[2,128,512]{2,1,0:T(8,128)(2,1)} %get-tuple-element.48), channel_id=1, source_target_pairs={{0,7},{1,6},{2,5},{3,4},{4,3},{5,2},{6,1},{7,0},{8,15},{9,14},{10,... | collective-permute-start | bytes 786440 | tf_op jit(solution)/shard_map/ppermute | solution.py:393
  11.1 11.9 %collective-permute-start.3 = (bf16[2,128,512]{2,1,0:T(8,128)(2,1)}, bf16[2,128,512]{2,1,0:T(8,128)(2,1)S(1)}, u32[]{:S(2)}, u32[]{:S(2)}) collective-permute-start(bf16[2,128,512]{2,1,0:T(8,128)(2,1)} %get-tuple-element.50), channel_id=1, source_target_pairs={{0,6},{1,7},{2,4},{3,5},{4,2},{5,3},{6,0},{7,1},{8,14},{9,15},{10,... | collective-permute-start | bytes 786440 | tf_op jit(solution)/shard_map/ppermute | solution.py:393
  15.2 8.4 %collective-permute-start.4 = (bf16[2,128,512]{2,1,0:T(8,128)(2,1)}, bf16[2,128,512]{2,1,0:T(8,128)(2,1)}, u32[]{:S(2)}, u32[]{:S(2)}) collective-permute-start(bf16[2,128,512]{2,1,0:T(8,128)(2,1)} %get-tuple-element.51), channel_id=1, source_target_pairs={{0,1},{1,0},{2,3},{3,2},{4,5},{5,4},{6,7},{7,6},{8,9},{9,8},{10,11... | collective-permute-start | bytes 786440 | tf_op jit(solution)/shard_map/ppermute | solution.py:393
  15.8 22.3 %collective-permute-start = (bf16[1024,512]{1,0:T(8,128)(2,1)S(1)}, bf16[1024,512]{1,0:T(8,128)(2,1)S(1)}, u32[]{:S(2)}, u32[]{:S(2)}) collective-permute-start(bf16[1024,512]{1,0:T(8,128)(2,1)S(1)} %copy-done.2), channel_id=1, source_target_pairs={{0,8},{8,0},{16,24},{24,16},{1,9},{9,1},{17,25},{25,17},{2,10},{10... | collective-permute-start | bytes 3145736 | tf_op jit(solution)/shard_map/ppermute | solution.py:387
  29.8 8.3 %collective-permute-start.5 = (bf16[1024,512]{1,0:T(8,128)(2,1)}, bf16[1024,512]{1,0:T(8,128)(2,1)}, u32[]{:S(2)}, u32[]{:S(2)}) collective-permute-start(bf16[1024,512]{1,0:T(8,128)(2,1)} %collective-permute-done.1.refs_6_), channel_id=1, source_target_pairs={{0,8},{8,0},{16,24},{24,16},{1,9},{9,1},{17,25},{25,17},{2,10},{10... | collective-permute-start | bytes 3145736 | tf_op jit(solution)/shard_map/ppermute | solution.py:387
  29.8 31.7 %collective-permute-start.6 = (bf16[2,128,512]{2,1,0:T(8,128)(2,1)}, bf16[2,128,512]{2,1,0:T(8,128)(2,1)}, u32[]{:S(2)}, u32[]{:S(2)}) collective-permute-start(bf16[2,128,512]{2,1,0:T(8,128)(2,1)} %get-tuple-element.52), channel_id=1, source_target_pairs={{0,5},{1,4},{2,7},{3,6},{4,1},{5,0},{6,3},{7,2},{8,13},{9,12},{10,... | collective-permute-start | bytes 786440 | tf_op jit(solution)/shard_map/ppermute | solution.py:393
  35.0 19.5 %collective-permute-start.7 = (bf16[2,128,512]{2,1,0:T(8,128)(2,1)}, bf16[2,128,512]{2,1,0:T(8,128)(2,1)}, u32[]{:S(2)}, u32[]{:S(2)}) collective-permute-start(bf16[2,128,512]{2,1,0:T(8,128)(2,1)} %get-tuple-element.58), channel_id=1, source_target_pairs={{0,3},{1,2},{2,1},{3,0},{4,7},{5,6},{6,5},{7,4},{8,11},{9,10},{10,... | collective-permute-start | bytes 786440 | tf_op jit(solution)/shard_map/ppermute | solution.py:393
  35.1 26.3 %collective-permute-start.8 = (bf16[2,128,512]{2,1,0:T(8,128)(2,1)}, bf16[2,128,512]{2,1,0:T(8,128)(2,1)}, u32[]{:S(2)}, u32[]{:S(2)}) collective-permute-start(bf16[2,128,512]{2,1,0:T(8,128)(2,1)} %get-tuple-element.59), channel_id=1, source_target_pairs={{0,2},{1,3},{2,0},{3,1},{4,6},{5,7},{6,4},{7,5},{8,10},{9,11},{10,... | collective-permute-start | bytes 786440 | tf_op jit(solution)/shard_map/ppermute | solution.py:393
  38.1 23.4 %collective-permute-start.9 = (bf16[2,128,512]{2,1,0:T(8,128)(2,1)}, bf16[2,128,512]{2,1,0:T(8,128)(2,1)S(1)}, u32[]{:S(2)}, u32[]{:S(2)}) collective-permute-start(bf16[2,128,512]{2,1,0:T(8,128)(2,1)} %get-tuple-element.60), channel_id=1, source_target_pairs={{0,4},{1,5},{2,6},{3,7},{4,0},{5,1},{6,2},{7,3},{8,12},{9,13},{10,... | collective-permute-start | bytes 786440 | tf_op jit(solution)/shard_map/ppermute | solution.py:393
  47.9 17.5 %collective-permute-start.10 = (bf16[128,512]{1,0:T(8,128)(2,1)S(1)}, bf16[128,512]{1,0:T(8,128)(2,1)S(1)}, u32[]{:S(2)}, u32[]{:S(2)}) collective-permute-start(bf16[128,512]{1,0:T(8,128)(2,1)S(1)} %get-tuple-element.63), channel_id=1, source_target_pairs={{0,7},{1,6},{2,5},{3,4},{4,3},{5,2},{6,1},{7,0},{8,15},{9,14},{10,... | collective-permute-start | bytes 393224 | tf_op jit(solution)/shard_map/ppermute | solution.py:393
  54.5 13.8 %collective-permute-start.11 = (bf16[128,512]{1,0:T(8,128)(2,1)S(1)}, bf16[128,512]{1,0:T(8,128)(2,1)S(1)}, u32[]{:S(2)}, u32[]{:S(2)}) collective-permute-start(bf16[128,512]{1,0:T(8,128)(2,1)S(1)} %get-tuple-element.64), channel_id=1, source_target_pairs={{0,3},{1,2},{2,1},{3,0},{4,7},{5,6},{6,5},{7,4},{8,11},{9,10},{10,... | collective-permute-start | bytes 393224 | tf_op jit(solution)/shard_map/ppermute | solution.py:393
  61.5 17.3 %collective-permute-start.12 = (bf16[128,512]{1,0:T(8,128)(2,1)S(1)}, bf16[128,512]{1,0:T(8,128)(2,1)S(1)}, u32[]{:S(2)}, u32[]{:S(2)}) collective-permute-start(bf16[128,512]{1,0:T(8,128)(2,1)S(1)} %get-tuple-element.65), channel_id=1, source_target_pairs={{0,2},{1,3},{2,0},{3,1},{4,6},{5,7},{6,4},{7,5},{8,10},{9,11},{10,... | collective-permute-start | bytes 393224 | tf_op jit(solution)/shard_map/ppermute | solution.py:393
  61.5 19.2 %collective-permute-start.13 = (bf16[128,512]{1,0:T(8,128)(2,1)S(1)}, bf16[128,512]{1,0:T(8,128)(2,1)S(1)}, u32[]{:S(2)}, u32[]{:S(2)}) collective-permute-start(bf16[128,512]{1,0:T(8,128)(2,1)S(1)} %get-tuple-element.66), channel_id=1, source_target_pairs={{0,1},{1,0},{2,3},{3,2},{4,5},{5,4},{6,7},{7,6},{8,9},{9,8},{10,11... | collective-permute-start | bytes 393224 | tf_op jit(solution)/shard_map/ppermute | solution.py:393
  61.5 21.9 %collective-permute-start.14 = (bf16[128,512]{1,0:T(8,128)(2,1)S(1)}, bf16[128,512]{1,0:T(8,128)(2,1)S(1)}, u32[]{:S(2)}, u32[]{:S(2)}) collective-permute-start(bf16[128,512]{1,0:T(8,128)(2,1)S(1)} %get-tuple-element.67), channel_id=1, source_target_pairs={{0,6},{1,7},{2,4},{3,5},{4,2},{5,3},{6,0},{7,1},{8,14},{9,15},{10,... | collective-permute-start | bytes 393224 | tf_op jit(solution)/shard_map/ppermute | solution.py:393
  65.3 18.7 %collective-permute-start.15 = (bf16[128,512]{1,0:T(8,128)(2,1)S(1)}, bf16[128,512]{1,0:T(8,128)(2,1)S(1)}, u32[]{:S(2)}, u32[]{:S(2)}) collective-permute-start(bf16[128,512]{1,0:T(8,128)(2,1)S(1)} %get-tuple-element.68), channel_id=1, source_target_pairs={{0,5},{1,4},{2,7},{3,6},{4,1},{5,0},{6,3},{7,2},{8,13},{9,12},{10,... | collective-permute-start | bytes 393224 | tf_op jit(solution)/shard_map/ppermute | solution.py:393
  68.2 26.6 %collective-permute-start.16 = (bf16[128,512]{1,0:T(8,128)(2,1)S(1)}, bf16[128,512]{1,0:T(8,128)(2,1)S(1)}, u32[]{:S(2)}, u32[]{:S(2)}) collective-permute-start(bf16[128,512]{1,0:T(8,128)(2,1)S(1)} %get-tuple-element.69), channel_id=1, source_target_pairs={{0,4},{1,5},{2,6},{3,7},{4,0},{5,1},{6,2},{7,3},{8,12},{9,13},{10,... | collective-permute-start | bytes 393224 | tf_op jit(solution)/shard_map/ppermute | solution.py:393
  78.7 30.4 %collective-permute-start.17 = (bf16[128,512]{1,0:T(8,128)(2,1)S(1)}, bf16[128,512]{1,0:T(8,128)(2,1)S(1)}, u32[]{:S(2)}, u32[]{:S(2)}) collective-permute-start(bf16[128,512]{1,0:T(8,128)(2,1)S(1)} %get-tuple-element.72), channel_id=1, source_target_pairs={{0,7},{1,6},{2,5},{3,4},{4,3},{5,2},{6,1},{7,0},{8,15},{9,14},{10,... | collective-permute-start | bytes 393224 | tf_op jit(solution)/shard_map/ppermute | solution.py:393
  80.7 33.3 %collective-permute-start.18 = (bf16[128,512]{1,0:T(8,128)(2,1)S(1)}, bf16[128,512]{1,0:T(8,128)(2,1)S(1)}, u32[]{:S(2)}, u32[]{:S(2)}) collective-permute-start(bf16[128,512]{1,0:T(8,128)(2,1)S(1)} %get-tuple-element.73), channel_id=1, source_target_pairs={{0,6},{1,7},{2,4},{3,5},{4,2},{5,3},{6,0},{7,1},{8,14},{9,15},{10,... | collective-permute-start | bytes 393224 | tf_op jit(solution)/shard_map/ppermute | solution.py:393
  83.4 30.6 %collective-permute-start.19 = (bf16[128,512]{1,0:T(8,128)(2,1)S(1)}, bf16[128,512]{1,0:T(8,128)(2,1)S(1)}, u32[]{:S(2)}, u32[]{:S(2)}) collective-permute-start(bf16[128,512]{1,0:T(8,128)(2,1)S(1)} %get-tuple-element.74), channel_id=1, source_target_pairs={{0,5},{1,4},{2,7},{3,6},{4,1},{5,0},{6,3},{7,2},{8,13},{9,12},{10,... | collective-permute-start | bytes 393224 | tf_op jit(solution)/shard_map/ppermute | solution.py:393
  84.0 31.9 %collective-permute-start.20 = (bf16[128,512]{1,0:T(8,128)(2,1)S(1)}, bf16[128,512]{1,0:T(8,128)(2,1)S(1)}, u32[]{:S(2)}, u32[]{:S(2)}) collective-permute-start(bf16[128,512]{1,0:T(8,128)(2,1)S(1)} %get-tuple-element.75), channel_id=1, source_target_pairs={{0,4},{1,5},{2,6},{3,7},{4,0},{5,1},{6,2},{7,3},{8,12},{9,13},{10,... | collective-permute-start | bytes 393224 | tf_op jit(solution)/shard_map/ppermute | solution.py:393
  109.1 33.3 %copy-start = (bf16[1024,512]{1,0:T(8,128)(2,1)S(1)}, bf16[1024,512]{1,0:T(8,128)(2,1)}, u32[]{:S(2)}) copy-start(bf16[1024,512]{1,0:T(8,128)(2,1)} %param.14) | copy-start | bytes 3145732
  109.1 23.0 %collective-permute-start.26 = (bf16[2,128,512]{2,1,0:T(8,128)(2,1)S(1)}, bf16[2,128,512]{2,1,0:T(8,128)(2,1)S(1)}, u32[]{:S(2)}, u32[]{:S(2)}) collective-permute-start(bf16[2,128,512]{2,1,0:T(8,128)(2,1)S(1)} %get-tuple-element.81), channel_id=1, source_target_pairs={{0,7},{1,6},{2,5},{3,4},{4,3},{5,2},{6,1},{7,0},{8,15},{9,14},{10,... | collective-permute-start | bytes 786440 | tf_op jit(solution)/shard_map/ppermute | solution.py:393
  109.2 25.6 %collective-permute-start.27 = (bf16[2,128,512]{2,1,0:T(8,128)(2,1)S(1)}, bf16[2,128,512]{2,1,0:T(8,128)(2,1)S(1)}, u32[]{:S(2)}, u32[]{:S(2)}) collective-permute-start(bf16[2,128,512]{2,1,0:T(8,128)(2,1)S(1)} %get-tuple-element.82), channel_id=1, source_target_pairs={{0,6},{1,7},{2,4},{3,5},{4,2},{5,3},{6,0},{7,1},{8,14},{9,15},{10,... | collective-permute-start | bytes 786440 | tf_op jit(solution)/shard_map/ppermute | solution.py:393
  114.0 10.3 %collective-permute-start.21 = (bf16[128,512]{1,0:T(8,128)(2,1)S(1)}, bf16[128,512]{1,0:T(8,128)(2,1)S(1)}, u32[]{:S(2)}, u32[]{:S(2)}) collective-permute-start(bf16[128,512]{1,0:T(8,128)(2,1)S(1)} %get-tuple-element.76), channel_id=1, source_target_pairs={{0,3},{1,2},{2,1},{3,0},{4,7},{5,6},{6,5},{7,4},{8,11},{9,10},{10,... | collective-permute-start | bytes 393224 | tf_op jit(solution)/shard_map/ppermute | solution.py:393
  114.0 14.1 %collective-permute-start.22 = (bf16[128,512]{1,0:T(8,128)(2,1)S(1)}, bf16[128,512]{1,0:T(8,128)(2,1)S(1)}, u32[]{:S(2)}, u32[]{:S(2)}) collective-permute-start(bf16[128,512]{1,0:T(8,128)(2,1)S(1)} %get-tuple-element.77), channel_id=1, source_target_pairs={{0,2},{1,3},{2,0},{3,1},{4,6},{5,7},{6,4},{7,5},{8,10},{9,11},{10,... | collective-permute-start | bytes 393224 | tf_op jit(solution)/shard_map/ppermute | solution.py:393
  115.9 12.8 %collective-permute-start.23 = (bf16[128,512]{1,0:T(8,128)(2,1)S(1)}, bf16[128,512]{1,0:T(8,128)(2,1)S(1)}, u32[]{:S(2)}, u32[]{:S(2)}) collective-permute-start(bf16[128,512]{1,0:T(8,128)(2,1)S(1)} %get-tuple-element.78), channel_id=1, source_target_pairs={{0,1},{1,0},{2,3},{3,2},{4,5},{5,4},{6,7},{7,6},{8,9},{9,8},{10,11... | collective-permute-start | bytes 393224 | tf_op jit(solution)/shard_map/ppermute | solution.py:393
  124.3 13.7 %collective-permute-start.28 = (bf16[2,128,512]{2,1,0:T(8,128)(2,1)S(1)}, bf16[2,128,512]{2,1,0:T(8,128)(2,1)S(1)}, u32[]{:S(2)}, u32[]{:S(2)}) collective-permute-start(bf16[2,128,512]{2,1,0:T(8,128)(2,1)S(1)} %get-tuple-element.83), channel_id=1, source_target_pairs={{0,3},{1,2},{2,1},{3,0},{4,7},{5,6},{6,5},{7,4},{8,11},{9,10},{10,... | collective-permute-start | bytes 786440 | tf_op jit(solution)/shard_map/ppermute | solution.py:393
  128.1 14.3 %collective-permute-start.29 = (bf16[2,128,512]{2,1,0:T(8,128)(2,1)S(1)}, bf16[2,128,512]{2,1,0:T(8,128)(2,1)S(1)}, u32[]{:S(2)}, u32[]{:S(2)}) collective-permute-start(bf16[2,128,512]{2,1,0:T(8,128)(2,1)S(1)} %get-tuple-element.84), channel_id=1, source_target_pairs={{0,2},{1,3},{2,0},{3,1},{4,6},{5,7},{6,4},{7,5},{8,10},{9,11},{10,... | collective-permute-start | bytes 786440 | tf_op jit(solution)/shard_map/ppermute | solution.py:393
  128.8 13.6 %collective-permute-start.30 = (bf16[2,128,512]{2,1,0:T(8,128)(2,1)S(1)}, bf16[2,128,512]{2,1,0:T(8,128)(2,1)S(1)}, u32[]{:S(2)}, u32[]{:S(2)}) collective-permute-start(bf16[2,128,512]{2,1,0:T(8,128)(2,1)S(1)} %get-tuple-element.85), channel_id=1, source_target_pairs={{0,1},{1,0},{2,3},{3,2},{4,5},{5,4},{6,7},{7,6},{8,9},{9,8},{10,11... | collective-permute-start | bytes 786440 | tf_op jit(solution)/shard_map/ppermute | solution.py:393
  132.1 16.0 %collective-permute-start.24 = (bf16[2,128,512]{2,1,0:T(8,128)(2,1)S(1)}, bf16[2,128,512]{2,1,0:T(8,128)(2,1)S(1)}, u32[]{:S(2)}, u32[]{:S(2)}) collective-permute-start(bf16[2,128,512]{2,1,0:T(8,128)(2,1)S(1)} %get-tuple-element.79), channel_id=1, source_target_pairs={{0,5},{1,4},{2,7},{3,6},{4,1},{5,0},{6,3},{7,2},{8,13},{9,12},{10,... | collective-permute-start | bytes 786440 | tf_op jit(solution)/shard_map/ppermute | solution.py:393
  134.8 15.2 %collective-permute-start.25 = (bf16[2,128,512]{2,1,0:T(8,128)(2,1)S(1)}, bf16[2,128,512]{2,1,0:T(8,128)(2,1)S(1)}, u32[]{:S(2)}, u32[]{:S(2)}) collective-permute-start(bf16[2,128,512]{2,1,0:T(8,128)(2,1)S(1)} %get-tuple-element.80), channel_id=1, source_target_pairs={{0,4},{1,5},{2,6},{3,7},{4,0},{5,1},{6,2},{7,3},{8,12},{9,13},{10,... | collective-permute-start | bytes 786440 | tf_op jit(solution)/shard_map/ppermute | solution.py:393
  (8 other events, 185.1 us)

commit v13 on v12

--- a/solution.py
+++ b/solution.py
@@ -445,7 +445,8 @@
         functools.partial(response_kernel, n_ctx, inner), me, (after(pair_sent, grad[0]),), tables, (), inner, 3
     )
     grad_came = exchange(grad)
-    resp_came = exchange(response)
+    waiting, _ = lax.optimization_barrier((list(response[2:]), grad_came[1:]))
+    resp_came = exchange([*response[:2], *waiting])
     backs = conv_call(
         functools.partial(backward_kernel, n_ctx, inner, scale),
         me,

time: 152 us -> 153 us (level)
  starting transfers between devices: 50 us -> 54.8 us
  waiting for transfers between devices: 50.7 us -> 46.6 us
    ppermute x28, starting transfers between devices: 47 us -> 51.8 us  [send(): return lax.ppermute(part, 'ctx', [(p, p ^ d) for p in range(count)])]
    ppermute x28, waiting for transfers between devices: 44.6 us -> 40.5 us  [send(): return lax.ppermute(part, 'ctx', [(p, p ^ d) for p in range(count)])]
  transfers between devices with their start and end apart: 31 -> 31, of which waited for: 12 -> 13; matrix products, arithmetic and copies ran while one was open for 1% -> 1% of each run, Pallas kernels for 28% -> 28%
where the time goes in v13:
time: 153 us; the launch traced here: 152 us
  starting transfers between devices  54.8 us (36%)
  Pallas kernels  46.8 us (31%)
  waiting for transfers between devices  46.6 us (30%)
  local copies, waits for them, and re-layouts  3.2 us (2%)
    ppermute x28, starting transfers between devices, send(): return lax.ppermute(part, 'ctx', [(p, p ^ d) for p in range(count)])  51.8 us
    ppermute x28, waiting for transfers between devices, send(): return lax.ppermute(part, 'ctx', [(p, p ^ d) for p in range(count)])  40.5 us
    pallas_call x2, Pallas kernels, conv_call(): pl.pallas_call(kernel, grid_spec=pltpu.PrefetchScalarGridSpec(num_scalar_...  24.1 us
    pallas_call x1, Pallas kernels, project_call(): pl.pallas_call(functools.partial(project_kernel, chunks, members), grid_s...  8.49 us
    pallas_call x2, Pallas kernels, prepare_call(): pl.pallas_call(functools.partial(prepare_kernel, masks, scale), in_specs=...  6.75 us
    ppermute x1, waiting for transfers between devices, gather_start(): lax.ppermute(block, 'group', [(g, g ^ count // 2) for g in range(count)])  6.16 us
    pallas_call x2, Pallas kernels, finish_call(): pl.pallas_call(functools.partial(finish_kernel, count), grid_spec=pltpu.P...  5.16 us
  transfers between devices with their start and end apart: 31, of which 13 were waited for; matrix products, arithmetic and copies ran while one was open for 1% of the time, Pallas kernels for 28%

profile of v13, /device:TPU:0, one launch (start us, length us, event | category | flops | bytes accessed | tf_op | source)
XLA Modules:
  0.0 152.4 jit_solution(4448473886248222180)
XLA Ops:
  0.6 2.9 %shard_map.156 = (bf16[2,128,512]{2,1,0:T(8,128)(2,1)}, bf16[2,128,512]{2,1,0:T(8,128)(2,1)}) custom-call(bf16[8,128,512]{2,1,0:T(8,128)(2,1)} %bitcast.15, bf16[8,128,512]{2,1,0:T(8,128)(2,1)} %bitcast.25, f32[8,128,512]{2,1,0:T(8,128)} %bitcast.36, f32[8,128]{1,0:T(8,128)} %bitcast.42), custom_call_target="tpu_custom_call" | custom-call | flops 1048576 | bytes 1572864 | tf_op jit(solution)/shard_map/pallas_call | solution.py:224
  3.5 3.0 %collective-permute-start.1 = (bf16[1024,512]{1,0:T(8,128)(2,1)S(1)}, bf16[1024,512]{1,0:T(8,128)(2,1)}, u32[]{:S(2)}, u32[]{:S(2)}) collective-permute-start(bf16[1024,512]{1,0:T(8,128)(2,1)S(1)} %copy-done.2), channel_id=1, source_target_pairs={{0,16},{8,24},{16,0},{24,8},{1,17},{9,25},{17,1},{25,9},{2,18},{10... | collective-permute-start | bytes 3145736 | tf_op jit(solution)/shard_map/ppermute | solution.py:373
  6.5 4.6 %collective-permute-start.2 = (bf16[2,128,512]{2,1,0:T(8,128)(2,1)}, bf16[2,128,512]{2,1,0:T(8,128)(2,1)S(1)}, u32[]{:S(2)}, u32[]{:S(2)}) collective-permute-start(bf16[2,128,512]{2,1,0:T(8,128)(2,1)} %get-tuple-element.54), channel_id=1, source_target_pairs={{0,7},{1,6},{2,5},{3,4},{4,3},{5,2},{6,1},{7,0},{8,15},{9,14},{10,... | collective-permute-start | bytes 786440 | tf_op jit(solution)/shard_map/ppermute | solution.py:393
  11.3 3.9 %shard_map.157 = (bf16[2,128,512]{2,1,0:T(8,128)(2,1)}, bf16[2,128,512]{2,1,0:T(8,128)(2,1)}, bf16[2,128,512]{2,1,0:T(8,128)(2,1)}, bf16[2,128,512]{2,1,0:T(8,12...) custom-call(bf16[8,128,512]{2,1,0:T(8,128)(2,1)} %bitcast.16, bf16[8,128,512]{2,1,0:T(8,128)(2,1)} %bitcast.26, ...), custom_call_target="tpu_custom_call" | custom-call | flops 3145728 | bytes 4718592 | tf_op jit(solution)/shard_map/pallas_call | solution.py:224
  17.7 5.3 %collective-permute-done.3.refs_2_ = bf16[2,128,512]{2,1,0:T(8,128)(2,1)S(1)} collective-permute-done((bf16[2,128,512]{2,1,0:T(8,128)(2,1)}, bf16[2,128,512]{2,1,0:T(8,128)(2,1)S(1)}, u32[]{:S(2)}, u32[]{:S(2)}) %collective-permute-start.3) | collective-permute-done | bytes 262176 | tf_op jit(solution)/shard_map/ppermute | solution.py:393
  23.6 6.2 %collective-permute-done.1.refs_6_ = bf16[1024,512]{1,0:T(8,128)(2,1)} collective-permute-done((bf16[1024,512]{1,0:T(8,128)(2,1)S(1)}, bf16[1024,512]{1,0:T(8,128)(2,1)}, u32[]{:S(2)}, u32[]{:S(2)}) %collective-permute-start.1) | collective-permute-done | bytes 1048608 | tf_op jit(solution)/shard_map/ppermute | solution.py:373
  29.8 5.2 %collective-permute-start.6 = (bf16[2,128,512]{2,1,0:T(8,128)(2,1)}, bf16[2,128,512]{2,1,0:T(8,128)(2,1)}, u32[]{:S(2)}, u32[]{:S(2)}) collective-permute-start(bf16[2,128,512]{2,1,0:T(8,128)(2,1)} %get-tuple-element.58), channel_id=1, source_target_pairs={{0,5},{1,4},{2,7},{3,6},{4,1},{5,0},{6,3},{7,2},{8,13},{9,12},{10,... | collective-permute-start | bytes 786440 | tf_op jit(solution)/shard_map/ppermute | solution.py:393
  35.1 2.9 %collective-permute-start.8 = (bf16[2,128,512]{2,1,0:T(8,128)(2,1)}, bf16[2,128,512]{2,1,0:T(8,128)(2,1)}, u32[]{:S(2)}, u32[]{:S(2)}) collective-permute-start(bf16[2,128,512]{2,1,0:T(8,128)(2,1)} %get-tuple-element.65), channel_id=1, source_target_pairs={{0,2},{1,3},{2,0},{3,1},{4,6},{5,7},{6,4},{7,5},{8,10},{9,11},{10,... | collective-permute-start | bytes 786440 | tf_op jit(solution)/shard_map/ppermute | solution.py:393
  39.4 8.5 %shard_map.158 = (bf16[8,128,512]{2,1,0:T(8,128)(2,1)S(1)}, bf16[128,512]{1,0:T(8,128)(2,1)S(1)}, bf16[128,512]{1,0:T(8,128)(2,1)S(1)}, bf16[128,512]{1,0:T(8,12...) custom-call(s32[2]{0:T(128)S(1)} %pad_add_fusion.me, ...), custom_call_target="tpu_custom_call" | custom-call | flops 4294967296 | bytes 8388608 | tf_op jit(solution)/shard_map/pallas_call | solution.py:348
  47.9 2.5 %collective-permute-start.10 = (bf16[128,512]{1,0:T(8,128)(2,1)S(1)}, bf16[128,512]{1,0:T(8,128)(2,1)S(1)}, u32[]{:S(2)}, u32[]{:S(2)}) collective-permute-start(bf16[128,512]{1,0:T(8,128)(2,1)S(1)} %get-tuple-element.69), channel_id=1, source_target_pairs={{0,7},{1,6},{2,5},{3,4},{4,3},{5,2},{6,1},{7,0},{8,15},{9,14},{10,... | collective-permute-start | bytes 393224 | tf_op jit(solution)/shard_map/ppermute | solution.py:393
  50.4 4.1 %collective-permute-done.7.refs_4_ = bf16[2,128,512]{2,1,0:T(8,128)(2,1)} collective-permute-done((bf16[2,128,512]{2,1,0:T(8,128)(2,1)}, bf16[2,128,512]{2,1,0:T(8,128)(2,1)}, u32[]{:S(2)}, u32[]{:S(2)}) %collective-permute-start.7) | collective-permute-done | bytes 262176 | tf_op jit(solution)/shard_map/ppermute | solution.py:393
  54.5 7.0 %collective-permute-done.8.refs_5_ = bf16[2,128,512]{2,1,0:T(8,128)(2,1)} collective-permute-done((bf16[2,128,512]{2,1,0:T(8,128)(2,1)}, bf16[2,128,512]{2,1,0:T(8,128)(2,1)}, u32[]{:S(2)}, u32[]{:S(2)}) %collective-permute-start.8) | collective-permute-done | bytes 262176 | tf_op jit(solution)/shard_map/ppermute | solution.py:393
  62.7 2.6 %collective-permute-done.10.refs_9_ = bf16[128,512]{1,0:T(8,128)(2,1)S(1)} collective-permute-done((bf16[128,512]{1,0:T(8,128)(2,1)S(1)}, bf16[128,512]{1,0:T(8,128)(2,1)S(1)}, u32[]{:S(2)}, u32[]{:S(2)}) %collective-permute-start.10) | collective-permute-done | bytes 131104 | tf_op jit(solution)/shard_map/ppermute | solution.py:393
  65.3 2.9 %collective-permute-start.15 = (bf16[128,512]{1,0:T(8,128)(2,1)S(1)}, bf16[128,512]{1,0:T(8,128)(2,1)S(1)}, u32[]{:S(2)}, u32[]{:S(2)}) collective-permute-start(bf16[128,512]{1,0:T(8,128)(2,1)S(1)} %get-tuple-element.74), channel_id=1, source_target_pairs={{0,5},{1,4},{2,7},{3,6},{4,1},{5,0},{6,3},{7,2},{8,13},{9,12},{10,... | collective-permute-start | bytes 393224 | tf_op jit(solution)/shard_map/ppermute | solution.py:393
  68.9 9.8 %shard_map.159 = (bf16[128,512]{1,0:T(8,128)(2,1)S(1)}, bf16[128,512]{1,0:T(8,128)(2,1)S(1)}, bf16[128,512]{1,0:T(8,128)(2,1)S(1)}, bf16[128,512]{1,0:T(8,128)(2...) custom-call(s32[2]{0:T(128)S(1)} %pad_add_fusion.me, ...), custom_call_target="tpu_custom_call" | custom-call | flops 3221225472 | bytes 4194304 | tf_op jit(solution)/shard_map/pallas_call | solution.py:169
  78.7 1.9 %collective-permute-start.17 = (bf16[128,512]{1,0:T(8,128)(2,1)S(1)}, bf16[128,512]{1,0:T(8,128)(2,1)S(1)}, u32[]{:S(2)}, u32[]{:S(2)}) collective-permute-start(bf16[128,512]{1,0:T(8,128)(2,1)S(1)} %get-tuple-element.78), channel_id=1, source_target_pairs={{0,7},{1,6},{2,5},{3,4},{4,3},{5,2},{6,1},{7,0},{8,15},{9,14},{10,... | collective-permute-start | bytes 393224 | tf_op jit(solution)/shard_map/ppermute | solution.py:393
  81.8 3.2 %collective-permute-done.16.refs_15_ = bf16[128,512]{1,0:T(8,128)(2,1)S(1)} collective-permute-done((bf16[128,512]{1,0:T(8,128)(2,1)S(1)}, bf16[128,512]{1,0:T(8,128)(2,1)S(1)}, u32[]{:S(2)}, u32[]{:S(2)}) %collective-permute-start.16) | collective-permute-done | bytes 131104 | tf_op jit(solution)/shard_map/ppermute | solution.py:393
  85.0 7.1 %collective-permute-start.18 = (bf16[128,512]{1,0:T(8,128)(2,1)S(1)}, bf16[128,512]{1,0:T(8,128)(2,1)S(1)}, u32[]{:S(2)}, u32[]{:S(2)}) collective-permute-start(bf16[128,512]{1,0:T(8,128)(2,1)S(1)} %get-tuple-element.85), channel_id=1, source_target_pairs={{0,6},{1,7},{2,4},{3,5},{4,2},{5,3},{6,0},{7,1},{8,14},{9,15},{10,... | collective-permute-start | bytes 393224 | tf_op jit(solution)/shard_map/ppermute | solution.py:393
  92.1 2.4 %collective-permute-start.20 = (bf16[128,512]{1,0:T(8,128)(2,1)S(1)}, bf16[128,512]{1,0:T(8,128)(2,1)S(1)}, u32[]{:S(2)}, u32[]{:S(2)}) collective-permute-start(bf16[128,512]{1,0:T(8,128)(2,1)S(1)} %get-tuple-element.87), channel_id=1, source_target_pairs={{0,4},{1,5},{2,6},{3,7},{4,0},{5,1},{6,2},{7,3},{8,12},{9,13},{10,... | collective-permute-start | bytes 393224 | tf_op jit(solution)/shard_map/ppermute | solution.py:393
  94.5 14.3 %shard_map.160 = (bf16[2,128,512]{2,1,0:T(8,128)(2,1)S(1)}, bf16[2,128,512]{2,1,0:T(8,128)(2,1)S(1)}, bf16[2,128,512]{2,1,0:T(8,128)(2,1)S(1)}, bf16[2,128,512]{...) custom-call(s32[2]{0:T(128)S(1)} %pad_add_fusion.me, ...), custom_call_target="tpu_custom_call" | custom-call | flops 5368709120 | bytes 4194304 | tf_op jit(solution)/shard_map/pallas_call | solution.py:169
  110.3 3.8 %collective-permute-start.27 = (bf16[2,128,512]{2,1,0:T(8,128)(2,1)S(1)}, bf16[2,128,512]{2,1,0:T(8,128)(2,1)S(1)}, u32[]{:S(2)}, u32[]{:S(2)}) collective-permute-start(bf16[2,128,512]{2,1,0:T(8,128)(2,1)S(1)} %get-tuple-element.94), channel_id=1, source_target_pairs={{0,6},{1,7},{2,4},{3,5},{4,2},{5,3},{6,0},{7,1},{8,14},{9,15},{10,... | collective-permute-start | bytes 786440 | tf_op jit(solution)/shard_map/ppermute | solution.py:393
  115.7 1.9 %collective-permute-start.23 = (bf16[128,512]{1,0:T(8,128)(2,1)S(1)}, bf16[128,512]{1,0:T(8,128)(2,1)S(1)}, u32[]{:S(2)}, u32[]{:S(2)}) collective-permute-start(bf16[128,512]{1,0:T(8,128)(2,1)S(1)} %get-tuple-element.90), channel_id=1, source_target_pairs={{0,1},{1,0},{2,3},{3,2},{4,5},{5,4},{6,7},{7,6},{8,9},{9,8},{10,11... | collective-permute-start | bytes 393224 | tf_op jit(solution)/shard_map/ppermute | solution.py:393
  117.6 6.8 %collective-permute-done.21.refs_5_ = bf16[128,512]{1,0:T(8,128)(2,1)S(1)} collective-permute-done((bf16[128,512]{1,0:T(8,128)(2,1)S(1)}, bf16[128,512]{1,0:T(8,128)(2,1)S(1)}, u32[]{:S(2)}, u32[]{:S(2)}) %collective-permute-start.21) | collective-permute-done | bytes 131104 | tf_op jit(solution)/shard_map/ppermute | solution.py:393
  124.4 2.6 %collective-permute-start.28 = (bf16[2,128,512]{2,1,0:T(8,128)(2,1)S(1)}, bf16[2,128,512]{2,1,0:T(8,128)(2,1)S(1)}, u32[]{:S(2)}, u32[]{:S(2)}) collective-permute-start(bf16[2,128,512]{2,1,0:T(8,128)(2,1)S(1)} %get-tuple-element.95), channel_id=1, source_target_pairs={{0,3},{1,2},{2,1},{3,0},{4,7},{5,6},{6,5},{7,4},{8,11},{9,10},{10,... | collective-permute-start | bytes 786440 | tf_op jit(solution)/shard_map/ppermute | solution.py:393
  128.6 2.3 %collective-permute-start.29 = (bf16[2,128,512]{2,1,0:T(8,128)(2,1)S(1)}, bf16[2,128,512]{2,1,0:T(8,128)(2,1)S(1)}, u32[]{:S(2)}, u32[]{:S(2)}) collective-permute-start(bf16[2,128,512]{2,1,0:T(8,128)(2,1)S(1)} %get-tuple-element.96), channel_id=1, source_target_pairs={{0,2},{1,3},{2,0},{3,1},{4,6},{5,7},{6,4},{7,5},{8,10},{9,11},{10,... | collective-permute-start | bytes 786440 | tf_op jit(solution)/shard_map/ppermute | solution.py:393
  131.0 3.4 %collective-permute-start.30 = (bf16[2,128,512]{2,1,0:T(8,128)(2,1)S(1)}, bf16[2,128,512]{2,1,0:T(8,128)(2,1)S(1)}, u32[]{:S(2)}, u32[]{:S(2)}) collective-permute-start(bf16[2,128,512]{2,1,0:T(8,128)(2,1)S(1)} %get-tuple-element.97), channel_id=1, source_target_pairs={{0,1},{1,0},{2,3},{3,2},{4,5},{5,4},{6,7},{7,6},{8,9},{9,8},{10,11... | collective-permute-start | bytes 786440 | tf_op jit(solution)/shard_map/ppermute | solution.py:393
  134.7 2.1 %collective-permute-start.25 = (bf16[2,128,512]{2,1,0:T(8,128)(2,1)S(1)}, bf16[2,128,512]{2,1,0:T(8,128)(2,1)S(1)}, u32[]{:S(2)}, u32[]{:S(2)}) collective-permute-start(bf16[2,128,512]{2,1,0:T(8,128)(2,1)S(1)} %get-tuple-element.92), channel_id=1, source_target_pairs={{0,4},{1,5},{2,6},{3,7},{4,0},{5,1},{6,2},{7,3},{8,12},{9,13},{10,... | collective-permute-start | bytes 786440 | tf_op jit(solution)/shard_map/ppermute | solution.py:393
  136.8 2.3 %shard_map.161 = bf16[8,128,512]{2,1,0:T(8,128)(2,1)} custom-call(s32[2]{0:T(128)S(1)} %pad_add_fusion.me, bf16[8,128,512]{2,1,0:T(8,128)(2,1)S(1)} %get-tuple-element.60.upstream, bf16[128,512]{1,0:T(8,128)(2,1)S(1)} %get-tuple-element.77.refs_0_, bf16[128,512]{1,0:T(8,128)(2,1)S(1)} %collective-permute-done.17.refs_1_, ...), custom_call_target="tpu_custom_call" | custom-call | flops 3145728 | bytes 3145728 | tf_op jit(solution)/shard_map/pallas_call | solution.py:326
  139.1 4.4 %collective-permute-done.29.refs_16_ = bf16[2,128,512]{2,1,0:T(8,128)(2,1)S(1)} collective-permute-done((bf16[2,128,512]{2,1,0:T(8,128)(2,1)S(1)}, bf16[2,128,512]{2,1,0:T(8,128)(2,1)S(1)}, u32[]{:S(2)}, u32[]{:S(2)}) %collective-permute-start.29) | collective-permute-done | bytes 262176 | tf_op jit(solution)/shard_map/ppermute | solution.py:393
  143.5 3.5 %shard_map.162 = (bf16[8,128,512]{2,1,0:T(8,128)(2,1)}, bf16[8,128,512]{2,1,0:T(8,128)(2,1)}, f32[8,128,512]{2,1,0:T(8,128)}) custom-call(s32[2]{0:T(128)S(1)} %pad_add_fusion.me, bf16[8,128,512]{2,1,0:T(8,128)(2,1)S(1)} %bitcast.17, bf16[8,128,512]{2,1,0:T(8,128)(2,1)S(1)} %bitcast.18, bf16[8,128,512]{2,1,0:T(8,128)(2,1)S(1)} %bitcast.19, ...), custom_call_target="tpu_custom_call" | custom-call | flops 786432 | bytes 6291456 | tf_op jit(solution)/shard_map/pallas_call | solution.py:298
  147.0 1.7 %collective-permute-done.24.refs_4_ = bf16[2,128,512]{2,1,0:T(8,128)(2,1)S(1)} collective-permute-done((bf16[2,128,512]{2,1,0:T(8,128)(2,1)S(1)}, bf16[2,128,512]{2,1,0:T(8,128)(2,1)S(1)}, u32[]{:S(2)}, u32[]{:S(2)}) %collective-permute-start.24) | collective-permute-done | bytes 262176 | tf_op jit(solution)/shard_map/ppermute | solution.py:393
  148.7 2.0 %collective-permute-done.25.refs_5_ = bf16[2,128,512]{2,1,0:T(8,128)(2,1)S(1)} collective-permute-done((bf16[2,128,512]{2,1,0:T(8,128)(2,1)S(1)}, bf16[2,128,512]{2,1,0:T(8,128)(2,1)S(1)}, u32[]{:S(2)}, u32[]{:S(2)}) %collective-permute-start.25) | collective-permute-done | bytes 262176 | tf_op jit(solution)/shard_map/ppermute | solution.py:393
  (59 shorter events, 14.5 us)
Async XLA Ops:
  3.5 26.3 %collective-permute-start.1 = (bf16[1024,512]{1,0:T(8,128)(2,1)S(1)}, bf16[1024,512]{1,0:T(8,128)(2,1)}, u32[]{:S(2)}, u32[]{:S(2)}) collective-permute-start(bf16[1024,512]{1,0:T(8,128)(2,1)S(1)} %copy-done.2), channel_id=1, source_target_pairs={{0,16},{8,24},{16,0},{24,8},{1,17},{9,25},{17,1},{25,9},{2,18},{10... | collective-permute-start | bytes 3145736 | tf_op jit(solution)/shard_map/ppermute | solution.py:373
  6.5 16.5 %collective-permute-start.2 = (bf16[2,128,512]{2,1,0:T(8,128)(2,1)}, bf16[2,128,512]{2,1,0:T(8,128)(2,1)S(1)}, u32[]{:S(2)}, u32[]{:S(2)}) collective-permute-start(bf16[2,128,512]{2,1,0:T(8,128)(2,1)} %get-tuple-element.54), channel_id=1, source_target_pairs={{0,7},{1,6},{2,5},{3,4},{4,3},{5,2},{6,1},{7,0},{8,15},{9,14},{10,... | collective-permute-start | bytes 786440 | tf_op jit(solution)/shard_map/ppermute | solution.py:393
  11.1 11.9 %collective-permute-start.3 = (bf16[2,128,512]{2,1,0:T(8,128)(2,1)}, bf16[2,128,512]{2,1,0:T(8,128)(2,1)S(1)}, u32[]{:S(2)}, u32[]{:S(2)}) collective-permute-start(bf16[2,128,512]{2,1,0:T(8,128)(2,1)} %get-tuple-element.56), channel_id=1, source_target_pairs={{0,6},{1,7},{2,4},{3,5},{4,2},{5,3},{6,0},{7,1},{8,14},{9,15},{10,... | collective-permute-start | bytes 786440 | tf_op jit(solution)/shard_map/ppermute | solution.py:393
  15.2 8.4 %collective-permute-start.4 = (bf16[2,128,512]{2,1,0:T(8,128)(2,1)}, bf16[2,128,512]{2,1,0:T(8,128)(2,1)}, u32[]{:S(2)}, u32[]{:S(2)}) collective-permute-start(bf16[2,128,512]{2,1,0:T(8,128)(2,1)} %get-tuple-element.57), channel_id=1, source_target_pairs={{0,1},{1,0},{2,3},{3,2},{4,5},{5,4},{6,7},{7,6},{8,9},{9,8},{10,11... | collective-permute-start | bytes 786440 | tf_op jit(solution)/shard_map/ppermute | solution.py:393
  15.8 22.3 %collective-permute-start = (bf16[1024,512]{1,0:T(8,128)(2,1)S(1)}, bf16[1024,512]{1,0:T(8,128)(2,1)S(1)}, u32[]{:S(2)}, u32[]{:S(2)}) collective-permute-start(bf16[1024,512]{1,0:T(8,128)(2,1)S(1)} %copy-done.2), channel_id=1, source_target_pairs={{0,8},{8,0},{16,24},{24,16},{1,9},{9,1},{17,25},{25,17},{2,10},{10... | collective-permute-start | bytes 3145736 | tf_op jit(solution)/shard_map/ppermute | solution.py:387
  29.8 8.3 %collective-permute-start.5 = (bf16[1024,512]{1,0:T(8,128)(2,1)}, bf16[1024,512]{1,0:T(8,128)(2,1)}, u32[]{:S(2)}, u32[]{:S(2)}) collective-permute-start(bf16[1024,512]{1,0:T(8,128)(2,1)} %collective-permute-done.1.refs_6_), channel_id=1, source_target_pairs={{0,8},{8,0},{16,24},{24,16},{1,9},{9,1},{17,25},{25,17},{2,10},{10... | collective-permute-start | bytes 3145736 | tf_op jit(solution)/shard_map/ppermute | solution.py:387
  29.8 31.7 %collective-permute-start.6 = (bf16[2,128,512]{2,1,0:T(8,128)(2,1)}, bf16[2,128,512]{2,1,0:T(8,128)(2,1)}, u32[]{:S(2)}, u32[]{:S(2)}) collective-permute-start(bf16[2,128,512]{2,1,0:T(8,128)(2,1)} %get-tuple-element.58), channel_id=1, source_target_pairs={{0,5},{1,4},{2,7},{3,6},{4,1},{5,0},{6,3},{7,2},{8,13},{9,12},{10,... | collective-permute-start | bytes 786440 | tf_op jit(solution)/shard_map/ppermute | solution.py:393
  35.0 19.5 %collective-permute-start.7 = (bf16[2,128,512]{2,1,0:T(8,128)(2,1)}, bf16[2,128,512]{2,1,0:T(8,128)(2,1)}, u32[]{:S(2)}, u32[]{:S(2)}) collective-permute-start(bf16[2,128,512]{2,1,0:T(8,128)(2,1)} %get-tuple-element.64), channel_id=1, source_target_pairs={{0,3},{1,2},{2,1},{3,0},{4,7},{5,6},{6,5},{7,4},{8,11},{9,10},{10,... | collective-permute-start | bytes 786440 | tf_op jit(solution)/shard_map/ppermute | solution.py:393
  35.1 26.3 %collective-permute-start.8 = (bf16[2,128,512]{2,1,0:T(8,128)(2,1)}, bf16[2,128,512]{2,1,0:T(8,128)(2,1)}, u32[]{:S(2)}, u32[]{:S(2)}) collective-permute-start(bf16[2,128,512]{2,1,0:T(8,128)(2,1)} %get-tuple-element.65), channel_id=1, source_target_pairs={{0,2},{1,3},{2,0},{3,1},{4,6},{5,7},{6,4},{7,5},{8,10},{9,11},{10,... | collective-permute-start | bytes 786440 | tf_op jit(solution)/shard_map/ppermute | solution.py:393
  38.1 23.4 %collective-permute-start.9 = (bf16[2,128,512]{2,1,0:T(8,128)(2,1)}, bf16[2,128,512]{2,1,0:T(8,128)(2,1)S(1)}, u32[]{:S(2)}, u32[]{:S(2)}) collective-permute-start(bf16[2,128,512]{2,1,0:T(8,128)(2,1)} %get-tuple-element.66), channel_id=1, source_target_pairs={{0,4},{1,5},{2,6},{3,7},{4,0},{5,1},{6,2},{7,3},{8,12},{9,13},{10,... | collective-permute-start | bytes 786440 | tf_op jit(solution)/shard_map/ppermute | solution.py:393
  47.9 17.5 %collective-permute-start.10 = (bf16[128,512]{1,0:T(8,128)(2,1)S(1)}, bf16[128,512]{1,0:T(8,128)(2,1)S(1)}, u32[]{:S(2)}, u32[]{:S(2)}) collective-permute-start(bf16[128,512]{1,0:T(8,128)(2,1)S(1)} %get-tuple-element.69), channel_id=1, source_target_pairs={{0,7},{1,6},{2,5},{3,4},{4,3},{5,2},{6,1},{7,0},{8,15},{9,14},{10,... | collective-permute-start | bytes 393224 | tf_op jit(solution)/shard_map/ppermute | solution.py:393
  54.5 13.8 %collective-permute-start.11 = (bf16[128,512]{1,0:T(8,128)(2,1)S(1)}, bf16[128,512]{1,0:T(8,128)(2,1)S(1)}, u32[]{:S(2)}, u32[]{:S(2)}) collective-permute-start(bf16[128,512]{1,0:T(8,128)(2,1)S(1)} %get-tuple-element.70), channel_id=1, source_target_pairs={{0,3},{1,2},{2,1},{3,0},{4,7},{5,6},{6,5},{7,4},{8,11},{9,10},{10,... | collective-permute-start | bytes 393224 | tf_op jit(solution)/shard_map/ppermute | solution.py:393
  61.5 17.3 %collective-permute-start.12 = (bf16[128,512]{1,0:T(8,128)(2,1)S(1)}, bf16[128,512]{1,0:T(8,128)(2,1)S(1)}, u32[]{:S(2)}, u32[]{:S(2)}) collective-permute-start(bf16[128,512]{1,0:T(8,128)(2,1)S(1)} %get-tuple-element.71), channel_id=1, source_target_pairs={{0,2},{1,3},{2,0},{3,1},{4,6},{5,7},{6,4},{7,5},{8,10},{9,11},{10,... | collective-permute-start | bytes 393224 | tf_op jit(solution)/shard_map/ppermute | solution.py:393
  61.5 19.2 %collective-permute-start.13 = (bf16[128,512]{1,0:T(8,128)(2,1)S(1)}, bf16[128,512]{1,0:T(8,128)(2,1)S(1)}, u32[]{:S(2)}, u32[]{:S(2)}) collective-permute-start(bf16[128,512]{1,0:T(8,128)(2,1)S(1)} %get-tuple-element.72), channel_id=1, source_target_pairs={{0,1},{1,0},{2,3},{3,2},{4,5},{5,4},{6,7},{7,6},{8,9},{9,8},{10,11... | collective-permute-start | bytes 393224 | tf_op jit(solution)/shard_map/ppermute | solution.py:393
  61.5 19.2 %collective-permute-start.14 = (bf16[128,512]{1,0:T(8,128)(2,1)S(1)}, bf16[128,512]{1,0:T(8,128)(2,1)S(1)}, u32[]{:S(2)}, u32[]{:S(2)}) collective-permute-start(bf16[128,512]{1,0:T(8,128)(2,1)S(1)} %get-tuple-element.73), channel_id=1, source_target_pairs={{0,6},{1,7},{2,4},{3,5},{4,2},{5,3},{6,0},{7,1},{8,14},{9,15},{10,... | collective-permute-start | bytes 393224 | tf_op jit(solution)/shard_map/ppermute | solution.py:393
  65.3 16.4 %collective-permute-start.15 = (bf16[128,512]{1,0:T(8,128)(2,1)S(1)}, bf16[128,512]{1,0:T(8,128)(2,1)S(1)}, u32[]{:S(2)}, u32[]{:S(2)}) collective-permute-start(bf16[128,512]{1,0:T(8,128)(2,1)S(1)} %get-tuple-element.74), channel_id=1, source_target_pairs={{0,5},{1,4},{2,7},{3,6},{4,1},{5,0},{6,3},{7,2},{8,13},{9,12},{10,... | collective-permute-start | bytes 393224 | tf_op jit(solution)/shard_map/ppermute | solution.py:393
  68.2 16.8 %collective-permute-start.16 = (bf16[128,512]{1,0:T(8,128)(2,1)S(1)}, bf16[128,512]{1,0:T(8,128)(2,1)S(1)}, u32[]{:S(2)}, u32[]{:S(2)}) collective-permute-start(bf16[128,512]{1,0:T(8,128)(2,1)S(1)} %get-tuple-element.75), channel_id=1, source_target_pairs={{0,4},{1,5},{2,6},{3,7},{4,0},{5,1},{6,2},{7,3},{8,12},{9,13},{10,... | collective-permute-start | bytes 393224 | tf_op jit(solution)/shard_map/ppermute | solution.py:393
  78.7 31.6 %collective-permute-start.17 = (bf16[128,512]{1,0:T(8,128)(2,1)S(1)}, bf16[128,512]{1,0:T(8,128)(2,1)S(1)}, u32[]{:S(2)}, u32[]{:S(2)}) collective-permute-start(bf16[128,512]{1,0:T(8,128)(2,1)S(1)} %get-tuple-element.78), channel_id=1, source_target_pairs={{0,7},{1,6},{2,5},{3,4},{4,3},{5,2},{6,1},{7,0},{8,15},{9,14},{10,... | collective-permute-start | bytes 393224 | tf_op jit(solution)/shard_map/ppermute | solution.py:393
  85.0 29.1 %collective-permute-start.18 = (bf16[128,512]{1,0:T(8,128)(2,1)S(1)}, bf16[128,512]{1,0:T(8,128)(2,1)S(1)}, u32[]{:S(2)}, u32[]{:S(2)}) collective-permute-start(bf16[128,512]{1,0:T(8,128)(2,1)S(1)} %get-tuple-element.85), channel_id=1, source_target_pairs={{0,6},{1,7},{2,4},{3,5},{4,2},{5,3},{6,0},{7,1},{8,14},{9,15},{10,... | collective-permute-start | bytes 393224 | tf_op jit(solution)/shard_map/ppermute | solution.py:393
  92.1 22.0 %collective-permute-start.19 = (bf16[128,512]{1,0:T(8,128)(2,1)S(1)}, bf16[128,512]{1,0:T(8,128)(2,1)S(1)}, u32[]{:S(2)}, u32[]{:S(2)}) collective-permute-start(bf16[128,512]{1,0:T(8,128)(2,1)S(1)} %get-tuple-element.86), channel_id=1, source_target_pairs={{0,5},{1,4},{2,7},{3,6},{4,1},{5,0},{6,3},{7,2},{8,13},{9,12},{10,... | collective-permute-start | bytes 393224 | tf_op jit(solution)/shard_map/ppermute | solution.py:393
  92.1 23.6 %collective-permute-start.20 = (bf16[128,512]{1,0:T(8,128)(2,1)S(1)}, bf16[128,512]{1,0:T(8,128)(2,1)S(1)}, u32[]{:S(2)}, u32[]{:S(2)}) collective-permute-start(bf16[128,512]{1,0:T(8,128)(2,1)S(1)} %get-tuple-element.87), channel_id=1, source_target_pairs={{0,4},{1,5},{2,6},{3,7},{4,0},{5,1},{6,2},{7,3},{8,12},{9,13},{10,... | collective-permute-start | bytes 393224 | tf_op jit(solution)/shard_map/ppermute | solution.py:393
  108.8 34.7 %copy-start = (bf16[1024,512]{1,0:T(8,128)(2,1)S(1)}, bf16[1024,512]{1,0:T(8,128)(2,1)}, u32[]{:S(2)}) copy-start(bf16[1024,512]{1,0:T(8,128)(2,1)} %param.14) | copy-start | bytes 3145732
  108.8 25.5 %collective-permute-start.26 = (bf16[2,128,512]{2,1,0:T(8,128)(2,1)S(1)}, bf16[2,128,512]{2,1,0:T(8,128)(2,1)S(1)}, u32[]{:S(2)}, u32[]{:S(2)}) collective-permute-start(bf16[2,128,512]{2,1,0:T(8,128)(2,1)S(1)} %get-tuple-element.93), channel_id=1, source_target_pairs={{0,7},{1,6},{2,5},{3,4},{4,3},{5,2},{6,1},{7,0},{8,15},{9,14},{10,... | collective-permute-start | bytes 786440 | tf_op jit(solution)/shard_map/ppermute | solution.py:393
  110.3 24.4 %collective-permute-start.27 = (bf16[2,128,512]{2,1,0:T(8,128)(2,1)S(1)}, bf16[2,128,512]{2,1,0:T(8,128)(2,1)S(1)}, u32[]{:S(2)}, u32[]{:S(2)}) collective-permute-start(bf16[2,128,512]{2,1,0:T(8,128)(2,1)S(1)} %get-tuple-element.94), channel_id=1, source_target_pairs={{0,6},{1,7},{2,4},{3,5},{4,2},{5,3},{6,0},{7,1},{8,14},{9,15},{10,... | collective-permute-start | bytes 786440 | tf_op jit(solution)/shard_map/ppermute | solution.py:393
  114.1 10.3 %collective-permute-start.21 = (bf16[128,512]{1,0:T(8,128)(2,1)S(1)}, bf16[128,512]{1,0:T(8,128)(2,1)S(1)}, u32[]{:S(2)}, u32[]{:S(2)}) collective-permute-start(bf16[128,512]{1,0:T(8,128)(2,1)S(1)} %get-tuple-element.88), channel_id=1, source_target_pairs={{0,3},{1,2},{2,1},{3,0},{4,7},{5,6},{6,5},{7,4},{8,11},{9,10},{10,... | collective-permute-start | bytes 393224 | tf_op jit(solution)/shard_map/ppermute | solution.py:393
  114.1 14.5 %collective-permute-start.22 = (bf16[128,512]{1,0:T(8,128)(2,1)S(1)}, bf16[128,512]{1,0:T(8,128)(2,1)S(1)}, u32[]{:S(2)}, u32[]{:S(2)}) collective-permute-start(bf16[128,512]{1,0:T(8,128)(2,1)S(1)} %get-tuple-element.89), channel_id=1, source_target_pairs={{0,2},{1,3},{2,0},{3,1},{4,6},{5,7},{6,4},{7,5},{8,10},{9,11},{10,... | collective-permute-start | bytes 393224 | tf_op jit(solution)/shard_map/ppermute | solution.py:393
  115.7 15.3 %collective-permute-start.23 = (bf16[128,512]{1,0:T(8,128)(2,1)S(1)}, bf16[128,512]{1,0:T(8,128)(2,1)S(1)}, u32[]{:S(2)}, u32[]{:S(2)}) collective-permute-start(bf16[128,512]{1,0:T(8,128)(2,1)S(1)} %get-tuple-element.90), channel_id=1, source_target_pairs={{0,1},{1,0},{2,3},{3,2},{4,5},{5,4},{6,7},{7,6},{8,9},{9,8},{10,11... | collective-permute-start | bytes 393224 | tf_op jit(solution)/shard_map/ppermute | solution.py:393
  124.4 14.7 %collective-permute-start.28 = (bf16[2,128,512]{2,1,0:T(8,128)(2,1)S(1)}, bf16[2,128,512]{2,1,0:T(8,128)(2,1)S(1)}, u32[]{:S(2)}, u32[]{:S(2)}) collective-permute-start(bf16[2,128,512]{2,1,0:T(8,128)(2,1)S(1)} %get-tuple-element.95), channel_id=1, source_target_pairs={{0,3},{1,2},{2,1},{3,0},{4,7},{5,6},{6,5},{7,4},{8,11},{9,10},{10,... | collective-permute-start | bytes 786440 | tf_op jit(solution)/shard_map/ppermute | solution.py:393
  128.6 14.9 %collective-permute-start.29 = (bf16[2,128,512]{2,1,0:T(8,128)(2,1)S(1)}, bf16[2,128,512]{2,1,0:T(8,128)(2,1)S(1)}, u32[]{:S(2)}, u32[]{:S(2)}) collective-permute-start(bf16[2,128,512]{2,1,0:T(8,128)(2,1)S(1)} %get-tuple-element.96), channel_id=1, source_target_pairs={{0,2},{1,3},{2,0},{3,1},{4,6},{5,7},{6,4},{7,5},{8,10},{9,11},{10,... | collective-permute-start | bytes 786440 | tf_op jit(solution)/shard_map/ppermute | solution.py:393
  131.0 12.5 %collective-permute-start.30 = (bf16[2,128,512]{2,1,0:T(8,128)(2,1)S(1)}, bf16[2,128,512]{2,1,0:T(8,128)(2,1)S(1)}, u32[]{:S(2)}, u32[]{:S(2)}) collective-permute-start(bf16[2,128,512]{2,1,0:T(8,128)(2,1)S(1)} %get-tuple-element.97), channel_id=1, source_target_pairs={{0,1},{1,0},{2,3},{3,2},{4,5},{5,4},{6,7},{7,6},{8,9},{9,8},{10,11... | collective-permute-start | bytes 786440 | tf_op jit(solution)/shard_map/ppermute | solution.py:393
  134.3 14.4 %collective-permute-start.24 = (bf16[2,128,512]{2,1,0:T(8,128)(2,1)S(1)}, bf16[2,128,512]{2,1,0:T(8,128)(2,1)S(1)}, u32[]{:S(2)}, u32[]{:S(2)}) collective-permute-start(bf16[2,128,512]{2,1,0:T(8,128)(2,1)S(1)} %get-tuple-element.91), channel_id=1, source_target_pairs={{0,5},{1,4},{2,7},{3,6},{4,1},{5,0},{6,3},{7,2},{8,13},{9,12},{10,... | collective-permute-start | bytes 786440 | tf_op jit(solution)/shard_map/ppermute | solution.py:393
  134.7 16.0 %collective-permute-start.25 = (bf16[2,128,512]{2,1,0:T(8,128)(2,1)S(1)}, bf16[2,128,512]{2,1,0:T(8,128)(2,1)S(1)}, u32[]{:S(2)}, u32[]{:S(2)}) collective-permute-start(bf16[2,128,512]{2,1,0:T(8,128)(2,1)S(1)} %get-tuple-element.92), channel_id=1, source_target_pairs={{0,4},{1,5},{2,6},{3,7},{4,0},{5,1},{6,2},{7,3},{8,12},{9,13},{10,... | collective-permute-start | bytes 786440 | tf_op jit(solution)/shard_map/ppermute | solution.py:393
  (8 other events, 186.5 us)

commit v14 on v12

--- a/solution.py
+++ b/solution.py
@@ -86,7 +86,7 @@
     return jnp.dot(last, jnp.concatenate(turned, axis=1), preferred_element_type=F32)
 
 
-def scatter_slabs(rows, scale, outs, lead, inner):
+def scatter_slabs(rows, scale, outs, lead, at_rows, inner):
     local = outs[0].shape[-1]
     per = local // inner
     scaled = rows * scale
@@ -98,9 +98,9 @@
             ).astype(BF16)
             lanes = slice(part * inner, (part + 1) * inner)
             if lead is None:
-                out[:, lanes] = tile
+                out[at_rows, lanes] = tile
             else:
-                out[lead, :, lanes] = tile
+                out[lead, at_rows, lanes] = tile
 
 
 def times_plain(left, right):
@@ -129,10 +129,14 @@
     pair, refs = in_place(refs[:chunks], pair_order(chunks)), refs[chunks:]
     (first, last, cos, sin, forward, backward), outs = refs[:6], refs[6:]
     tables = (first[...], cos[...], sin[...], forward[...], inner)
-    prod = forward_dft(gather_slabs([ref[0] for ref in pair], inner), *tables)
-    taps = forward_dft(gather_slabs([ref[1] for ref in pair], inner), *tables)
-    rows = inverse_dft(times_plain(prod, taps), last[...], cos[...], sin[...], backward[...], inner)
-    scatter_slabs(rows, 1.0 / (SLABS * inner), outs, None, inner)
+    for at in range(0, outs[0].shape[-2], STEP):
+        rows = slice(at, at + STEP)
+        prod = forward_dft(gather_slabs([ref[0, rows] for ref in pair], inner), *tables)
+        taps = forward_dft(gather_slabs([ref[1, rows] for ref in pair], inner), *tables)
+        result = inverse_dft(
+            times_plain(prod, taps), last[...], cos[...], sin[...], backward[...], inner
+        )
+        scatter_slabs(result, 1.0 / (SLABS * inner), outs, None, rows, inner)
 
 
 def backward_kernel(chunks, inner, scale, me, *refs):
@@ -141,13 +145,15 @@
     (first, last, cos, sin, forward, backward), outs = refs[:6], refs[6:]
     tables = (first[...], cos[...], sin[...], forward[...], inner)
     back_tables = (last[...], cos[...], sin[...], backward[...], inner)
-    grad_spec = forward_dft(gather_slabs([ref[...] for ref in grad], inner), *tables)
-    taps = forward_dft(gather_slabs([ref[1] for ref in pair], inner), *tables)
-    rows = inverse_dft(times_conj(grad_spec, taps), *back_tables)
-    scatter_slabs(rows, 1.0 / (SLABS * inner), outs, 0, inner)
-    prod = forward_dft(gather_slabs([ref[0] for ref in pair], inner), *tables)
-    rows = inverse_dft(times_conj(grad_spec, prod), *back_tables)
-    scatter_slabs(rows, scale / (SLABS * inner), outs, 1, inner)
+    for at in range(0, outs[0].shape[-2], STEP):
+        rows = slice(at, at + STEP)
+        grad_spec = forward_dft(gather_slabs([ref[rows] for ref in grad], inner), *tables)
+        taps = forward_dft(gather_slabs([ref[1, rows] for ref in pair], inner), *tables)
+        result = inverse_dft(times_conj(grad_spec, taps), *back_tables)
+        scatter_slabs(result, 1.0 / (SLABS * inner), outs, 0, rows, inner)
+        prod = forward_dft(gather_slabs([ref[0, rows] for ref in pair], inner), *tables)
+        result = inverse_dft(times_conj(grad_spec, prod), *back_tables)
+        scatter_slabs(result, scale / (SLABS * inner), outs, 1, rows, inner)
 
 
 def conv_call(kernel, me, operands, tables, lead, inner, transforms):
@@ -156,7 +162,7 @@
     def rows_of(shape):
         middle = shape[:-2]
         return pl.BlockSpec(
-            middle + (STEP, local), lambda i, me: (0,) * len(middle) + (i, 0)
+            middle + (2 * STEP, local), lambda i, me: (0,) * len(middle) + (i, 0)
         )
 
     def whole(table):
@@ -170,7 +176,7 @@
         kernel,
         grid_spec=pltpu.PrefetchScalarGridSpec(
             num_scalar_prefetch=1,
-            grid=(channels // STEP,),
+            grid=(channels // (2 * STEP),),
             in_specs=[rows_of(chunk.shape) for chunk in flat] + [whole(t) for t in tables],
             out_specs=[rows_of(out_shape)] * chunks,
         ),

time: 152 us -> 155 us (1.020)
  waiting for transfers between devices: 50.7 us -> 59.3 us
  Pallas kernels: 46.8 us -> 43.9 us
  starting transfers between devices: 50 us -> 47.2 us
    ppermute x28, waiting for transfers between devices: 44.6 us -> 53.1 us  [send(): return lax.ppermute(part, 'ctx', [(p, p ^ d) for p in range(count)])]
    pallas_call x2, Pallas kernels: 24.1 us -> 21.2 us  [conv_call(): pl.pallas_call(kernel, grid_spec=pltpu.PrefetchScalarGridSpec(num_scalar_...]
    ppermute x28, starting transfers between devices: 47 us -> 44.2 us  [send(): return lax.ppermute(part, 'ctx', [(p, p ^ d) for p in range(count)])]
  transfers between devices with their start and end apart: 31 -> 31, of which waited for: 12 -> 12; matrix products, arithmetic and copies ran while one was open for 1% -> 1% of each run, Pallas kernels for 28% -> 26%
where the time goes in v14:
time: 155 us; the launch traced here: 154 us
  waiting for transfers between devices  59.3 us (38%)
  starting transfers between devices  47.2 us (30%)
  Pallas kernels  43.9 us (28%)
  local copies, waits for them, and re-layouts  3.2 us (2%)
    ppermute x28, waiting for transfers between devices, send(): return lax.ppermute(part, 'ctx', [(p, p ^ d) for p in range(count)])  53.1 us
    ppermute x28, starting transfers between devices, send(): return lax.ppermute(part, 'ctx', [(p, p ^ d) for p in range(count)])  44.2 us
    pallas_call x2, Pallas kernels, conv_call(): pl.pallas_call(kernel, grid_spec=pltpu.PrefetchScalarGridSpec(num_scalar_...  21.2 us
    pallas_call x1, Pallas kernels, project_call(): pl.pallas_call(functools.partial(project_kernel, chunks, members), grid_s...  8.49 us
    pallas_call x2, Pallas kernels, prepare_call(): pl.pallas_call(functools.partial(prepare_kernel, masks, scale), in_specs=...  6.75 us
    ppermute x1, waiting for transfers between devices, gather_start(): lax.ppermute(block, 'group', [(g, g ^ count // 2) for g in range(count)])  6.16 us
    pallas_call x2, Pallas kernels, finish_call(): pl.pallas_call(functools.partial(finish_kernel, count), grid_spec=pltpu.P...  5.16 us
  transfers between devices with their start and end apart: 31, of which 12 were waited for; matrix products, arithmetic and copies ran while one was open for 1% of the time, Pallas kernels for 26%

profile of v14, /device:TPU:0, one launch (start us, length us, event | category | flops | bytes accessed | tf_op | source)
XLA Modules:
  0.0 154.5 jit_solution(10740953540243304254)
XLA Ops:
  0.6 2.9 %shard_map.156 = (bf16[2,128,512]{2,1,0:T(8,128)(2,1)}, bf16[2,128,512]{2,1,0:T(8,128)(2,1)}) custom-call(bf16[8,128,512]{2,1,0:T(8,128)(2,1)} %bitcast.15, bf16[8,128,512]{2,1,0:T(8,128)(2,1)} %bitcast.25, f32[8,128,512]{2,1,0:T(8,128)} %bitcast.36, f32[8,128]{1,0:T(8,128)} %bitcast.42), custom_call_target="tpu_custom_call" | custom-call | flops 1048576 | bytes 1572864 | tf_op jit(solution)/shard_map/pallas_call | solution.py:230
  3.5 3.0 %collective-permute-start.1 = (bf16[1024,512]{1,0:T(8,128)(2,1)S(1)}, bf16[1024,512]{1,0:T(8,128)(2,1)}, u32[]{:S(2)}, u32[]{:S(2)}) collective-permute-start(bf16[1024,512]{1,0:T(8,128)(2,1)S(1)} %copy-done.2), channel_id=1, source_target_pairs={{0,16},{8,24},{16,0},{24,8},{1,17},{9,25},{17,1},{25,9},{2,18},{10... | collective-permute-start | bytes 3145736 | tf_op jit(solution)/shard_map/ppermute | solution.py:379
  6.5 4.6 %collective-permute-start.2 = (bf16[2,128,512]{2,1,0:T(8,128)(2,1)}, bf16[2,128,512]{2,1,0:T(8,128)(2,1)S(1)}, u32[]{:S(2)}, u32[]{:S(2)}) collective-permute-start(bf16[2,128,512]{2,1,0:T(8,128)(2,1)} %get-tuple-element.48), channel_id=1, source_target_pairs={{0,7},{1,6},{2,5},{3,4},{4,3},{5,2},{6,1},{7,0},{8,15},{9,14},{10,... | collective-permute-start | bytes 786440 | tf_op jit(solution)/shard_map/ppermute | solution.py:399
  11.3 3.9 %shard_map.157 = (bf16[2,128,512]{2,1,0:T(8,128)(2,1)}, bf16[2,128,512]{2,1,0:T(8,128)(2,1)}, bf16[2,128,512]{2,1,0:T(8,128)(2,1)}, bf16[2,128,512]{2,1,0:T(8,12...) custom-call(bf16[8,128,512]{2,1,0:T(8,128)(2,1)} %bitcast.16, bf16[8,128,512]{2,1,0:T(8,128)(2,1)} %bitcast.26, ...), custom_call_target="tpu_custom_call" | custom-call | flops 3145728 | bytes 4718592 | tf_op jit(solution)/shard_map/pallas_call | solution.py:230
  17.7 5.3 %collective-permute-done.3.refs_2_ = bf16[2,128,512]{2,1,0:T(8,128)(2,1)S(1)} collective-permute-done((bf16[2,128,512]{2,1,0:T(8,128)(2,1)}, bf16[2,128,512]{2,1,0:T(8,128)(2,1)S(1)}, u32[]{:S(2)}, u32[]{:S(2)}) %collective-permute-start.3) | collective-permute-done | bytes 262176 | tf_op jit(solution)/shard_map/ppermute | solution.py:399
  23.6 6.2 %collective-permute-done.1.refs_6_ = bf16[1024,512]{1,0:T(8,128)(2,1)} collective-permute-done((bf16[1024,512]{1,0:T(8,128)(2,1)S(1)}, bf16[1024,512]{1,0:T(8,128)(2,1)}, u32[]{:S(2)}, u32[]{:S(2)}) %collective-permute-start.1) | collective-permute-done | bytes 1048608 | tf_op jit(solution)/shard_map/ppermute | solution.py:379
  29.8 5.2 %collective-permute-start.6 = (bf16[2,128,512]{2,1,0:T(8,128)(2,1)}, bf16[2,128,512]{2,1,0:T(8,128)(2,1)}, u32[]{:S(2)}, u32[]{:S(2)}) collective-permute-start(bf16[2,128,512]{2,1,0:T(8,128)(2,1)} %get-tuple-element.52), channel_id=1, source_target_pairs={{0,5},{1,4},{2,7},{3,6},{4,1},{5,0},{6,3},{7,2},{8,13},{9,12},{10,... | collective-permute-start | bytes 786440 | tf_op jit(solution)/shard_map/ppermute | solution.py:399
  35.1 2.9 %collective-permute-start.8 = (bf16[2,128,512]{2,1,0:T(8,128)(2,1)}, bf16[2,128,512]{2,1,0:T(8,128)(2,1)}, u32[]{:S(2)}, u32[]{:S(2)}) collective-permute-start(bf16[2,128,512]{2,1,0:T(8,128)(2,1)} %get-tuple-element.59), channel_id=1, source_target_pairs={{0,2},{1,3},{2,0},{3,1},{4,6},{5,7},{6,4},{7,5},{8,10},{9,11},{10,... | collective-permute-start | bytes 786440 | tf_op jit(solution)/shard_map/ppermute | solution.py:399
  39.4 8.5 %shard_map.158 = (bf16[8,128,512]{2,1,0:T(8,128)(2,1)S(1)}, bf16[128,512]{1,0:T(8,128)(2,1)S(1)}, bf16[128,512]{1,0:T(8,128)(2,1)S(1)}, bf16[128,512]{1,0:T(8,12...) custom-call(s32[2]{0:T(128)S(1)} %pad_add_fusion.me, ...), custom_call_target="tpu_custom_call" | custom-call | flops 4294967296 | bytes 8388608 | tf_op jit(solution)/shard_map/pallas_call | solution.py:354
  47.9 2.5 %collective-permute-start.10 = (bf16[128,512]{1,0:T(8,128)(2,1)S(1)}, bf16[128,512]{1,0:T(8,128)(2,1)S(1)}, u32[]{:S(2)}, u32[]{:S(2)}) collective-permute-start(bf16[128,512]{1,0:T(8,128)(2,1)S(1)} %get-tuple-element.63), channel_id=1, source_target_pairs={{0,7},{1,6},{2,5},{3,4},{4,3},{5,2},{6,1},{7,0},{8,15},{9,14},{10,... | collective-permute-start | bytes 393224 | tf_op jit(solution)/shard_map/ppermute | solution.py:399
  50.4 4.1 %collective-permute-done.7.refs_4_ = bf16[2,128,512]{2,1,0:T(8,128)(2,1)} collective-permute-done((bf16[2,128,512]{2,1,0:T(8,128)(2,1)}, bf16[2,128,512]{2,1,0:T(8,128)(2,1)}, u32[]{:S(2)}, u32[]{:S(2)}) %collective-permute-start.7) | collective-permute-done | bytes 262176 | tf_op jit(solution)/shard_map/ppermute | solution.py:399
  54.5 7.0 %collective-permute-done.8.refs_5_ = bf16[2,128,512]{2,1,0:T(8,128)(2,1)} collective-permute-done((bf16[2,128,512]{2,1,0:T(8,128)(2,1)}, bf16[2,128,512]{2,1,0:T(8,128)(2,1)}, u32[]{:S(2)}, u32[]{:S(2)}) %collective-permute-start.8) | collective-permute-done | bytes 262176 | tf_op jit(solution)/shard_map/ppermute | solution.py:399
  62.7 2.6 %collective-permute-done.10.refs_9_ = bf16[128,512]{1,0:T(8,128)(2,1)S(1)} collective-permute-done((bf16[128,512]{1,0:T(8,128)(2,1)S(1)}, bf16[128,512]{1,0:T(8,128)(2,1)S(1)}, u32[]{:S(2)}, u32[]{:S(2)}) %collective-permute-start.10) | collective-permute-done | bytes 131104 | tf_op jit(solution)/shard_map/ppermute | solution.py:399
  65.3 2.9 %collective-permute-start.15 = (bf16[128,512]{1,0:T(8,128)(2,1)S(1)}, bf16[128,512]{1,0:T(8,128)(2,1)S(1)}, u32[]{:S(2)}, u32[]{:S(2)}) collective-permute-start(bf16[128,512]{1,0:T(8,128)(2,1)S(1)} %get-tuple-element.68), channel_id=1, source_target_pairs={{0,5},{1,4},{2,7},{3,6},{4,1},{5,0},{6,3},{7,2},{8,13},{9,12},{10,... | collective-permute-start | bytes 393224 | tf_op jit(solution)/shard_map/ppermute | solution.py:399
  68.9 8.4 %shard_map.159 = (bf16[128,512]{1,0:T(8,128)(2,1)S(1)}, bf16[128,512]{1,0:T(8,128)(2,1)S(1)}, bf16[128,512]{1,0:T(8,128)(2,1)S(1)}, bf16[128,512]{1,0:T(8,128)(2...) custom-call(s32[2]{0:T(128)S(1)} %pad_add_fusion.me, ...), custom_call_target="tpu_custom_call" | custom-call | flops 3221225472 | bytes 4194304 | tf_op jit(solution)/shard_map/pallas_call | solution.py:175
  77.3 1.9 %collective-permute-start.17 = (bf16[128,512]{1,0:T(8,128)(2,1)S(1)}, bf16[128,512]{1,0:T(8,128)(2,1)S(1)}, u32[]{:S(2)}, u32[]{:S(2)}) collective-permute-start(bf16[128,512]{1,0:T(8,128)(2,1)S(1)} %get-tuple-element.72), channel_id=1, source_target_pairs={{0,7},{1,6},{2,5},{3,4},{4,3},{5,2},{6,1},{7,0},{8,15},{9,14},{10,... | collective-permute-start | bytes 393224 | tf_op jit(solution)/shard_map/ppermute | solution.py:399
  79.2 2.7 %collective-permute-start.18 = (bf16[128,512]{1,0:T(8,128)(2,1)S(1)}, bf16[128,512]{1,0:T(8,128)(2,1)S(1)}, u32[]{:S(2)}, u32[]{:S(2)}) collective-permute-start(bf16[128,512]{1,0:T(8,128)(2,1)S(1)} %get-tuple-element.73), channel_id=1, source_target_pairs={{0,6},{1,7},{2,4},{3,5},{4,2},{5,3},{6,0},{7,1},{8,14},{9,15},{10,... | collective-permute-start | bytes 393224 | tf_op jit(solution)/shard_map/ppermute | solution.py:399
  82.6 10.4 %collective-permute-done.15.refs_14_ = bf16[128,512]{1,0:T(8,128)(2,1)S(1)} collective-permute-done((bf16[128,512]{1,0:T(8,128)(2,1)S(1)}, bf16[128,512]{1,0:T(8,128)(2,1)S(1)}, u32[]{:S(2)}, u32[]{:S(2)}) %collective-permute-start.15) | collective-permute-done | bytes 131104 | tf_op jit(solution)/shard_map/ppermute | solution.py:399
  93.0 1.8 %collective-permute-done.16.refs_15_ = bf16[128,512]{1,0:T(8,128)(2,1)S(1)} collective-permute-done((bf16[128,512]{1,0:T(8,128)(2,1)S(1)}, bf16[128,512]{1,0:T(8,128)(2,1)S(1)}, u32[]{:S(2)}, u32[]{:S(2)}) %collective-permute-start.16) | collective-permute-done | bytes 131104 | tf_op jit(solution)/shard_map/ppermute | solution.py:399
  94.8 12.9 %shard_map.160 = (bf16[2,128,512]{2,1,0:T(8,128)(2,1)S(1)}, bf16[2,128,512]{2,1,0:T(8,128)(2,1)S(1)}, bf16[2,128,512]{2,1,0:T(8,128)(2,1)S(1)}, bf16[2,128,512]{...) custom-call(s32[2]{0:T(128)S(1)} %pad_add_fusion.me, ...), custom_call_target="tpu_custom_call" | custom-call | flops 5368709120 | bytes 4194304 | tf_op jit(solution)/shard_map/pallas_call | solution.py:175
  107.7 2.5 %collective-permute-start.26 = (bf16[2,128,512]{2,1,0:T(8,128)(2,1)S(1)}, bf16[2,128,512]{2,1,0:T(8,128)(2,1)S(1)}, u32[]{:S(2)}, u32[]{:S(2)}) collective-permute-start(bf16[2,128,512]{2,1,0:T(8,128)(2,1)S(1)} %get-tuple-element.81), channel_id=1, source_target_pairs={{0,7},{1,6},{2,5},{3,4},{4,3},{5,2},{6,1},{7,0},{8,15},{9,14},{10,... | collective-permute-start | bytes 786440 | tf_op jit(solution)/shard_map/ppermute | solution.py:399
  110.2 2.3 %collective-permute-start.27 = (bf16[2,128,512]{2,1,0:T(8,128)(2,1)S(1)}, bf16[2,128,512]{2,1,0:T(8,128)(2,1)S(1)}, u32[]{:S(2)}, u32[]{:S(2)}) collective-permute-start(bf16[2,128,512]{2,1,0:T(8,128)(2,1)S(1)} %get-tuple-element.82), channel_id=1, source_target_pairs={{0,6},{1,7},{2,4},{3,5},{4,2},{5,3},{6,0},{7,1},{8,14},{9,15},{10,... | collective-permute-start | bytes 786440 | tf_op jit(solution)/shard_map/ppermute | solution.py:399
  112.6 1.9 %collective-permute-start.22 = (bf16[128,512]{1,0:T(8,128)(2,1)S(1)}, bf16[128,512]{1,0:T(8,128)(2,1)S(1)}, u32[]{:S(2)}, u32[]{:S(2)}) collective-permute-start(bf16[128,512]{1,0:T(8,128)(2,1)S(1)} %get-tuple-element.77), channel_id=1, source_target_pairs={{0,2},{1,3},{2,0},{3,1},{4,6},{5,7},{6,4},{7,5},{8,10},{9,11},{10,... | collective-permute-start | bytes 393224 | tf_op jit(solution)/shard_map/ppermute | solution.py:399
  116.1 9.0 %collective-permute-done.21.refs_5_ = bf16[128,512]{1,0:T(8,128)(2,1)S(1)} collective-permute-done((bf16[128,512]{1,0:T(8,128)(2,1)S(1)}, bf16[128,512]{1,0:T(8,128)(2,1)S(1)}, u32[]{:S(2)}, u32[]{:S(2)}) %collective-permute-start.21) | collective-permute-done | bytes 131104 | tf_op jit(solution)/shard_map/ppermute | solution.py:399
  125.0 3.4 %collective-permute-start.28 = (bf16[2,128,512]{2,1,0:T(8,128)(2,1)S(1)}, bf16[2,128,512]{2,1,0:T(8,128)(2,1)S(1)}, u32[]{:S(2)}, u32[]{:S(2)}) collective-permute-start(bf16[2,128,512]{2,1,0:T(8,128)(2,1)S(1)} %get-tuple-element.83), channel_id=1, source_target_pairs={{0,3},{1,2},{2,1},{3,0},{4,7},{5,6},{6,5},{7,4},{8,11},{9,10},{10,... | collective-permute-start | bytes 786440 | tf_op jit(solution)/shard_map/ppermute | solution.py:399
  128.5 1.9 %collective-permute-start.29 = (bf16[2,128,512]{2,1,0:T(8,128)(2,1)S(1)}, bf16[2,128,512]{2,1,0:T(8,128)(2,1)S(1)}, u32[]{:S(2)}, u32[]{:S(2)}) collective-permute-start(bf16[2,128,512]{2,1,0:T(8,128)(2,1)S(1)} %get-tuple-element.84), channel_id=1, source_target_pairs={{0,2},{1,3},{2,0},{3,1},{4,6},{5,7},{6,4},{7,5},{8,10},{9,11},{10,... | collective-permute-start | bytes 786440 | tf_op jit(solution)/shard_map/ppermute | solution.py:399
  131.8 2.9 %collective-permute-start.25 = (bf16[2,128,512]{2,1,0:T(8,128)(2,1)S(1)}, bf16[2,128,512]{2,1,0:T(8,128)(2,1)S(1)}, u32[]{:S(2)}, u32[]{:S(2)}) collective-permute-start(bf16[2,128,512]{2,1,0:T(8,128)(2,1)S(1)} %get-tuple-element.80), channel_id=1, source_target_pairs={{0,4},{1,5},{2,6},{3,7},{4,0},{5,1},{6,2},{7,3},{8,12},{9,13},{10,... | collective-permute-start | bytes 786440 | tf_op jit(solution)/shard_map/ppermute | solution.py:399
  134.7 2.3 %shard_map.161 = bf16[8,128,512]{2,1,0:T(8,128)(2,1)} custom-call(s32[2]{0:T(128)S(1)} %pad_add_fusion.me, bf16[8,128,512]{2,1,0:T(8,128)(2,1)S(1)} %get-tuple-element.54.upstream, bf16[128,512]{1,0:T(8,128)(2,1)S(1)} %get-tuple-element.71.refs_0_, bf16[128,512]{1,0:T(8,128)(2,1)S(1)} %collective-permute-done.17.refs_1_, ...), custom_call_target="tpu_custom_call" | custom-call | flops 3145728 | bytes 3145728 | tf_op jit(solution)/shard_map/pallas_call | solution.py:332
  137.0 3.0 %collective-permute-done.28.refs_15_ = bf16[2,128,512]{2,1,0:T(8,128)(2,1)S(1)} collective-permute-done((bf16[2,128,512]{2,1,0:T(8,128)(2,1)S(1)}, bf16[2,128,512]{2,1,0:T(8,128)(2,1)S(1)}, u32[]{:S(2)}, u32[]{:S(2)}) %collective-permute-start.28) | collective-permute-done | bytes 262176 | tf_op jit(solution)/shard_map/ppermute | solution.py:399
  140.0 6.6 %collective-permute-done.29.refs_16_ = bf16[2,128,512]{2,1,0:T(8,128)(2,1)S(1)} collective-permute-done((bf16[2,128,512]{2,1,0:T(8,128)(2,1)S(1)}, bf16[2,128,512]{2,1,0:T(8,128)(2,1)S(1)}, u32[]{:S(2)}, u32[]{:S(2)}) %collective-permute-start.29) | collective-permute-done | bytes 262176 | tf_op jit(solution)/shard_map/ppermute | solution.py:399
  146.6 3.5 %shard_map.162 = (bf16[8,128,512]{2,1,0:T(8,128)(2,1)}, bf16[8,128,512]{2,1,0:T(8,128)(2,1)}, f32[8,128,512]{2,1,0:T(8,128)}) custom-call(s32[2]{0:T(128)S(1)} %pad_add_fusion.me, bf16[8,128,512]{2,1,0:T(8,128)(2,1)S(1)} %bitcast.17, bf16[8,128,512]{2,1,0:T(8,128)(2,1)S(1)} %bitcast.18, bf16[8,128,512]{2,1,0:T(8,128)(2,1)S(1)} %bitcast.19, ...), custom_call_target="tpu_custom_call" | custom-call | flops 786432 | bytes 6291456 | tf_op jit(solution)/shard_map/pallas_call | solution.py:304
  150.1 2.7 %collective-permute-done.25.refs_5_ = bf16[2,128,512]{2,1,0:T(8,128)(2,1)S(1)} collective-permute-done((bf16[2,128,512]{2,1,0:T(8,128)(2,1)S(1)}, bf16[2,128,512]{2,1,0:T(8,128)(2,1)S(1)}, u32[]{:S(2)}, u32[]{:S(2)}) %collective-permute-start.25) | collective-permute-done | bytes 262176 | tf_op jit(solution)/shard_map/ppermute | solution.py:399
  (59 shorter events, 12.1 us)
Async XLA Ops:
  3.5 26.3 %collective-permute-start.1 = (bf16[1024,512]{1,0:T(8,128)(2,1)S(1)}, bf16[1024,512]{1,0:T(8,128)(2,1)}, u32[]{:S(2)}, u32[]{:S(2)}) collective-permute-start(bf16[1024,512]{1,0:T(8,128)(2,1)S(1)} %copy-done.2), channel_id=1, source_target_pairs={{0,16},{8,24},{16,0},{24,8},{1,17},{9,25},{17,1},{25,9},{2,18},{10... | collective-permute-start | bytes 3145736 | tf_op jit(solution)/shard_map/ppermute | solution.py:379
  6.5 16.5 %collective-permute-start.2 = (bf16[2,128,512]{2,1,0:T(8,128)(2,1)}, bf16[2,128,512]{2,1,0:T(8,128)(2,1)S(1)}, u32[]{:S(2)}, u32[]{:S(2)}) collective-permute-start(bf16[2,128,512]{2,1,0:T(8,128)(2,1)} %get-tuple-element.48), channel_id=1, source_target_pairs={{0,7},{1,6},{2,5},{3,4},{4,3},{5,2},{6,1},{7,0},{8,15},{9,14},{10,... | collective-permute-start | bytes 786440 | tf_op jit(solution)/shard_map/ppermute | solution.py:399
  11.1 11.9 %collective-permute-start.3 = (bf16[2,128,512]{2,1,0:T(8,128)(2,1)}, bf16[2,128,512]{2,1,0:T(8,128)(2,1)S(1)}, u32[]{:S(2)}, u32[]{:S(2)}) collective-permute-start(bf16[2,128,512]{2,1,0:T(8,128)(2,1)} %get-tuple-element.50), channel_id=1, source_target_pairs={{0,6},{1,7},{2,4},{3,5},{4,2},{5,3},{6,0},{7,1},{8,14},{9,15},{10,... | collective-permute-start | bytes 786440 | tf_op jit(solution)/shard_map/ppermute | solution.py:399
  15.2 8.4 %collective-permute-start.4 = (bf16[2,128,512]{2,1,0:T(8,128)(2,1)}, bf16[2,128,512]{2,1,0:T(8,128)(2,1)}, u32[]{:S(2)}, u32[]{:S(2)}) collective-permute-start(bf16[2,128,512]{2,1,0:T(8,128)(2,1)} %get-tuple-element.51), channel_id=1, source_target_pairs={{0,1},{1,0},{2,3},{3,2},{4,5},{5,4},{6,7},{7,6},{8,9},{9,8},{10,11... | collective-permute-start | bytes 786440 | tf_op jit(solution)/shard_map/ppermute | solution.py:399
  15.8 22.3 %collective-permute-start = (bf16[1024,512]{1,0:T(8,128)(2,1)S(1)}, bf16[1024,512]{1,0:T(8,128)(2,1)S(1)}, u32[]{:S(2)}, u32[]{:S(2)}) collective-permute-start(bf16[1024,512]{1,0:T(8,128)(2,1)S(1)} %copy-done.2), channel_id=1, source_target_pairs={{0,8},{8,0},{16,24},{24,16},{1,9},{9,1},{17,25},{25,17},{2,10},{10... | collective-permute-start | bytes 3145736 | tf_op jit(solution)/shard_map/ppermute | solution.py:393
  29.8 8.3 %collective-permute-start.5 = (bf16[1024,512]{1,0:T(8,128)(2,1)}, bf16[1024,512]{1,0:T(8,128)(2,1)}, u32[]{:S(2)}, u32[]{:S(2)}) collective-permute-start(bf16[1024,512]{1,0:T(8,128)(2,1)} %collective-permute-done.1.refs_6_), channel_id=1, source_target_pairs={{0,8},{8,0},{16,24},{24,16},{1,9},{9,1},{17,25},{25,17},{2,10},{10... | collective-permute-start | bytes 3145736 | tf_op jit(solution)/shard_map/ppermute | solution.py:393
  29.8 31.7 %collective-permute-start.6 = (bf16[2,128,512]{2,1,0:T(8,128)(2,1)}, bf16[2,128,512]{2,1,0:T(8,128)(2,1)}, u32[]{:S(2)}, u32[]{:S(2)}) collective-permute-start(bf16[2,128,512]{2,1,0:T(8,128)(2,1)} %get-tuple-element.52), channel_id=1, source_target_pairs={{0,5},{1,4},{2,7},{3,6},{4,1},{5,0},{6,3},{7,2},{8,13},{9,12},{10,... | collective-permute-start | bytes 786440 | tf_op jit(solution)/shard_map/ppermute | solution.py:399
  35.0 19.5 %collective-permute-start.7 = (bf16[2,128,512]{2,1,0:T(8,128)(2,1)}, bf16[2,128,512]{2,1,0:T(8,128)(2,1)}, u32[]{:S(2)}, u32[]{:S(2)}) collective-permute-start(bf16[2,128,512]{2,1,0:T(8,128)(2,1)} %get-tuple-element.58), channel_id=1, source_target_pairs={{0,3},{1,2},{2,1},{3,0},{4,7},{5,6},{6,5},{7,4},{8,11},{9,10},{10,... | collective-permute-start | bytes 786440 | tf_op jit(solution)/shard_map/ppermute | solution.py:399
  35.1 26.3 %collective-permute-start.8 = (bf16[2,128,512]{2,1,0:T(8,128)(2,1)}, bf16[2,128,512]{2,1,0:T(8,128)(2,1)}, u32[]{:S(2)}, u32[]{:S(2)}) collective-permute-start(bf16[2,128,512]{2,1,0:T(8,128)(2,1)} %get-tuple-element.59), channel_id=1, source_target_pairs={{0,2},{1,3},{2,0},{3,1},{4,6},{5,7},{6,4},{7,5},{8,10},{9,11},{10,... | collective-permute-start | bytes 786440 | tf_op jit(solution)/shard_map/ppermute | solution.py:399
  38.1 23.4 %collective-permute-start.9 = (bf16[2,128,512]{2,1,0:T(8,128)(2,1)}, bf16[2,128,512]{2,1,0:T(8,128)(2,1)S(1)}, u32[]{:S(2)}, u32[]{:S(2)}) collective-permute-start(bf16[2,128,512]{2,1,0:T(8,128)(2,1)} %get-tuple-element.60), channel_id=1, source_target_pairs={{0,4},{1,5},{2,6},{3,7},{4,0},{5,1},{6,2},{7,3},{8,12},{9,13},{10,... | collective-permute-start | bytes 786440 | tf_op jit(solution)/shard_map/ppermute | solution.py:399
  47.9 17.5 %collective-permute-start.10 = (bf16[128,512]{1,0:T(8,128)(2,1)S(1)}, bf16[128,512]{1,0:T(8,128)(2,1)S(1)}, u32[]{:S(2)}, u32[]{:S(2)}) collective-permute-start(bf16[128,512]{1,0:T(8,128)(2,1)S(1)} %get-tuple-element.63), channel_id=1, source_target_pairs={{0,7},{1,6},{2,5},{3,4},{4,3},{5,2},{6,1},{7,0},{8,15},{9,14},{10,... | collective-permute-start | bytes 393224 | tf_op jit(solution)/shard_map/ppermute | solution.py:399
  54.5 13.8 %collective-permute-start.11 = (bf16[128,512]{1,0:T(8,128)(2,1)S(1)}, bf16[128,512]{1,0:T(8,128)(2,1)S(1)}, u32[]{:S(2)}, u32[]{:S(2)}) collective-permute-start(bf16[128,512]{1,0:T(8,128)(2,1)S(1)} %get-tuple-element.64), channel_id=1, source_target_pairs={{0,3},{1,2},{2,1},{3,0},{4,7},{5,6},{6,5},{7,4},{8,11},{9,10},{10,... | collective-permute-start | bytes 393224 | tf_op jit(solution)/shard_map/ppermute | solution.py:399
  61.5 15.8 %collective-permute-start.12 = (bf16[128,512]{1,0:T(8,128)(2,1)S(1)}, bf16[128,512]{1,0:T(8,128)(2,1)S(1)}, u32[]{:S(2)}, u32[]{:S(2)}) collective-permute-start(bf16[128,512]{1,0:T(8,128)(2,1)S(1)} %get-tuple-element.65), channel_id=1, source_target_pairs={{0,2},{1,3},{2,0},{3,1},{4,6},{5,7},{6,4},{7,5},{8,10},{9,11},{10,... | collective-permute-start | bytes 393224 | tf_op jit(solution)/shard_map/ppermute | solution.py:399
  61.5 17.8 %collective-permute-start.13 = (bf16[128,512]{1,0:T(8,128)(2,1)S(1)}, bf16[128,512]{1,0:T(8,128)(2,1)S(1)}, u32[]{:S(2)}, u32[]{:S(2)}) collective-permute-start(bf16[128,512]{1,0:T(8,128)(2,1)S(1)} %get-tuple-element.66), channel_id=1, source_target_pairs={{0,1},{1,0},{2,3},{3,2},{4,5},{5,4},{6,7},{7,6},{8,9},{9,8},{10,11... | collective-permute-start | bytes 393224 | tf_op jit(solution)/shard_map/ppermute | solution.py:399
  61.5 20.4 %collective-permute-start.14 = (bf16[128,512]{1,0:T(8,128)(2,1)S(1)}, bf16[128,512]{1,0:T(8,128)(2,1)S(1)}, u32[]{:S(2)}, u32[]{:S(2)}) collective-permute-start(bf16[128,512]{1,0:T(8,128)(2,1)S(1)} %get-tuple-element.67), channel_id=1, source_target_pairs={{0,6},{1,7},{2,4},{3,5},{4,2},{5,3},{6,0},{7,1},{8,14},{9,15},{10,... | collective-permute-start | bytes 393224 | tf_op jit(solution)/shard_map/ppermute | solution.py:399
  65.3 27.6 %collective-permute-start.15 = (bf16[128,512]{1,0:T(8,128)(2,1)S(1)}, bf16[128,512]{1,0:T(8,128)(2,1)S(1)}, u32[]{:S(2)}, u32[]{:S(2)}) collective-permute-start(bf16[128,512]{1,0:T(8,128)(2,1)S(1)} %get-tuple-element.68), channel_id=1, source_target_pairs={{0,5},{1,4},{2,7},{3,6},{4,1},{5,0},{6,3},{7,2},{8,13},{9,12},{10,... | collective-permute-start | bytes 393224 | tf_op jit(solution)/shard_map/ppermute | solution.py:399
  68.2 26.6 %collective-permute-start.16 = (bf16[128,512]{1,0:T(8,128)(2,1)S(1)}, bf16[128,512]{1,0:T(8,128)(2,1)S(1)}, u32[]{:S(2)}, u32[]{:S(2)}) collective-permute-start(bf16[128,512]{1,0:T(8,128)(2,1)S(1)} %get-tuple-element.69), channel_id=1, source_target_pairs={{0,4},{1,5},{2,6},{3,7},{4,0},{5,1},{6,2},{7,3},{8,12},{9,13},{10,... | collective-permute-start | bytes 393224 | tf_op jit(solution)/shard_map/ppermute | solution.py:399
  77.3 33.0 %collective-permute-start.17 = (bf16[128,512]{1,0:T(8,128)(2,1)S(1)}, bf16[128,512]{1,0:T(8,128)(2,1)S(1)}, u32[]{:S(2)}, u32[]{:S(2)}) collective-permute-start(bf16[128,512]{1,0:T(8,128)(2,1)S(1)} %get-tuple-element.72), channel_id=1, source_target_pairs={{0,7},{1,6},{2,5},{3,4},{4,3},{5,2},{6,1},{7,0},{8,15},{9,14},{10,... | collective-permute-start | bytes 393224 | tf_op jit(solution)/shard_map/ppermute | solution.py:399
  79.2 33.3 %collective-permute-start.18 = (bf16[128,512]{1,0:T(8,128)(2,1)S(1)}, bf16[128,512]{1,0:T(8,128)(2,1)S(1)}, u32[]{:S(2)}, u32[]{:S(2)}) collective-permute-start(bf16[128,512]{1,0:T(8,128)(2,1)S(1)} %get-tuple-element.73), channel_id=1, source_target_pairs={{0,6},{1,7},{2,4},{3,5},{4,2},{5,3},{6,0},{7,1},{8,14},{9,15},{10,... | collective-permute-start | bytes 393224 | tf_op jit(solution)/shard_map/ppermute | solution.py:399
  81.9 30.7 %collective-permute-start.19 = (bf16[128,512]{1,0:T(8,128)(2,1)S(1)}, bf16[128,512]{1,0:T(8,128)(2,1)S(1)}, u32[]{:S(2)}, u32[]{:S(2)}) collective-permute-start(bf16[128,512]{1,0:T(8,128)(2,1)S(1)} %get-tuple-element.74), channel_id=1, source_target_pairs={{0,5},{1,4},{2,7},{3,6},{4,1},{5,0},{6,3},{7,2},{8,13},{9,12},{10,... | collective-permute-start | bytes 393224 | tf_op jit(solution)/shard_map/ppermute | solution.py:399
  93.0 21.5 %collective-permute-start.20 = (bf16[128,512]{1,0:T(8,128)(2,1)S(1)}, bf16[128,512]{1,0:T(8,128)(2,1)S(1)}, u32[]{:S(2)}, u32[]{:S(2)}) collective-permute-start(bf16[128,512]{1,0:T(8,128)(2,1)S(1)} %get-tuple-element.75), channel_id=1, source_target_pairs={{0,4},{1,5},{2,6},{3,7},{4,0},{5,1},{6,2},{7,3},{8,12},{9,13},{10,... | collective-permute-start | bytes 393224 | tf_op jit(solution)/shard_map/ppermute | solution.py:399
  107.7 38.9 %copy-start = (bf16[1024,512]{1,0:T(8,128)(2,1)S(1)}, bf16[1024,512]{1,0:T(8,128)(2,1)}, u32[]{:S(2)}) copy-start(bf16[1024,512]{1,0:T(8,128)(2,1)} %param.14) | copy-start | bytes 3145732
  107.7 22.6 %collective-permute-start.26 = (bf16[2,128,512]{2,1,0:T(8,128)(2,1)S(1)}, bf16[2,128,512]{2,1,0:T(8,128)(2,1)S(1)}, u32[]{:S(2)}, u32[]{:S(2)}) collective-permute-start(bf16[2,128,512]{2,1,0:T(8,128)(2,1)S(1)} %get-tuple-element.81), channel_id=1, source_target_pairs={{0,7},{1,6},{2,5},{3,4},{4,3},{5,2},{6,1},{7,0},{8,15},{9,14},{10,... | collective-permute-start | bytes 786440 | tf_op jit(solution)/shard_map/ppermute | solution.py:399
  110.2 21.6 %collective-permute-start.27 = (bf16[2,128,512]{2,1,0:T(8,128)(2,1)S(1)}, bf16[2,128,512]{2,1,0:T(8,128)(2,1)S(1)}, u32[]{:S(2)}, u32[]{:S(2)}) collective-permute-start(bf16[2,128,512]{2,1,0:T(8,128)(2,1)S(1)} %get-tuple-element.82), channel_id=1, source_target_pairs={{0,6},{1,7},{2,4},{3,5},{4,2},{5,3},{6,0},{7,1},{8,14},{9,15},{10,... | collective-permute-start | bytes 786440 | tf_op jit(solution)/shard_map/ppermute | solution.py:399
  112.6 12.5 %collective-permute-start.21 = (bf16[128,512]{1,0:T(8,128)(2,1)S(1)}, bf16[128,512]{1,0:T(8,128)(2,1)S(1)}, u32[]{:S(2)}, u32[]{:S(2)}) collective-permute-start(bf16[128,512]{1,0:T(8,128)(2,1)S(1)} %get-tuple-element.76), channel_id=1, source_target_pairs={{0,3},{1,2},{2,1},{3,0},{4,7},{5,6},{6,5},{7,4},{8,11},{9,10},{10,... | collective-permute-start | bytes 393224 | tf_op jit(solution)/shard_map/ppermute | solution.py:399
  112.6 15.9 %collective-permute-start.22 = (bf16[128,512]{1,0:T(8,128)(2,1)S(1)}, bf16[128,512]{1,0:T(8,128)(2,1)S(1)}, u32[]{:S(2)}, u32[]{:S(2)}) collective-permute-start(bf16[128,512]{1,0:T(8,128)(2,1)S(1)} %get-tuple-element.77), channel_id=1, source_target_pairs={{0,2},{1,3},{2,0},{3,1},{4,6},{5,7},{6,4},{7,5},{8,10},{9,11},{10,... | collective-permute-start | bytes 393224 | tf_op jit(solution)/shard_map/ppermute | solution.py:399
  114.5 15.8 %collective-permute-start.23 = (bf16[128,512]{1,0:T(8,128)(2,1)S(1)}, bf16[128,512]{1,0:T(8,128)(2,1)S(1)}, u32[]{:S(2)}, u32[]{:S(2)}) collective-permute-start(bf16[128,512]{1,0:T(8,128)(2,1)S(1)} %get-tuple-element.78), channel_id=1, source_target_pairs={{0,1},{1,0},{2,3},{3,2},{4,5},{5,4},{6,7},{7,6},{8,9},{9,8},{10,11... | collective-permute-start | bytes 393224 | tf_op jit(solution)/shard_map/ppermute | solution.py:399
  125.0 15.0 %collective-permute-start.28 = (bf16[2,128,512]{2,1,0:T(8,128)(2,1)S(1)}, bf16[2,128,512]{2,1,0:T(8,128)(2,1)S(1)}, u32[]{:S(2)}, u32[]{:S(2)}) collective-permute-start(bf16[2,128,512]{2,1,0:T(8,128)(2,1)S(1)} %get-tuple-element.83), channel_id=1, source_target_pairs={{0,3},{1,2},{2,1},{3,0},{4,7},{5,6},{6,5},{7,4},{8,11},{9,10},{10,... | collective-permute-start | bytes 786440 | tf_op jit(solution)/shard_map/ppermute | solution.py:399
  128.5 18.1 %collective-permute-start.29 = (bf16[2,128,512]{2,1,0:T(8,128)(2,1)S(1)}, bf16[2,128,512]{2,1,0:T(8,128)(2,1)S(1)}, u32[]{:S(2)}, u32[]{:S(2)}) collective-permute-start(bf16[2,128,512]{2,1,0:T(8,128)(2,1)S(1)} %get-tuple-element.84), channel_id=1, source_target_pairs={{0,2},{1,3},{2,0},{3,1},{4,6},{5,7},{6,4},{7,5},{8,10},{9,11},{10,... | collective-permute-start | bytes 786440 | tf_op jit(solution)/shard_map/ppermute | solution.py:399
  130.3 16.3 %collective-permute-start.30 = (bf16[2,128,512]{2,1,0:T(8,128)(2,1)S(1)}, bf16[2,128,512]{2,1,0:T(8,128)(2,1)S(1)}, u32[]{:S(2)}, u32[]{:S(2)}) collective-permute-start(bf16[2,128,512]{2,1,0:T(8,128)(2,1)S(1)} %get-tuple-element.85), channel_id=1, source_target_pairs={{0,1},{1,0},{2,3},{3,2},{4,5},{5,4},{6,7},{7,6},{8,9},{9,8},{10,11... | collective-permute-start | bytes 786440 | tf_op jit(solution)/shard_map/ppermute | solution.py:399
  130.3 19.8 %collective-permute-start.24 = (bf16[2,128,512]{2,1,0:T(8,128)(2,1)S(1)}, bf16[2,128,512]{2,1,0:T(8,128)(2,1)S(1)}, u32[]{:S(2)}, u32[]{:S(2)}) collective-permute-start(bf16[2,128,512]{2,1,0:T(8,128)(2,1)S(1)} %get-tuple-element.79), channel_id=1, source_target_pairs={{0,5},{1,4},{2,7},{3,6},{4,1},{5,0},{6,3},{7,2},{8,13},{9,12},{10,... | collective-permute-start | bytes 786440 | tf_op jit(solution)/shard_map/ppermute | solution.py:399
  131.8 21.0 %collective-permute-start.25 = (bf16[2,128,512]{2,1,0:T(8,128)(2,1)S(1)}, bf16[2,128,512]{2,1,0:T(8,128)(2,1)S(1)}, u32[]{:S(2)}, u32[]{:S(2)}) collective-permute-start(bf16[2,128,512]{2,1,0:T(8,128)(2,1)S(1)} %get-tuple-element.80), channel_id=1, source_target_pairs={{0,4},{1,5},{2,6},{3,7},{4,0},{5,1},{6,2},{7,3},{8,12},{9,13},{10,... | collective-permute-start | bytes 786440 | tf_op jit(solution)/shard_map/ppermute | solution.py:399
  (8 other events, 190.7 us)

commit v15 on v14

--- a/solution.py
+++ b/solution.py
@@ -451,7 +451,8 @@
         functools.partial(response_kernel, n_ctx, inner), me, (after(pair_sent, grad[0]),), tables, (), inner, 3
     )
     grad_came = exchange(grad)
-    resp_came = exchange(response)
+    waiting, _ = lax.optimization_barrier((list(response[2:]), grad_came[1:]))
+    resp_came = exchange([*response[:2], *waiting])
     backs = conv_call(
         functools.partial(backward_kernel, n_ctx, inner, scale),
         me,

time: 155 us -> 152 us (0.981)
  waiting for transfers between devices: 59.3 us -> 56.1 us
    ppermute x28, waiting for transfers between devices: 53.1 us -> 50 us  [send(): return lax.ppermute(part, 'ctx', [(p, p ^ d) for p in range(count)])]
where the time goes in v15:
time: 152 us
  waiting for transfers between devices  56.1 us (37%)
  starting transfers between devices  47.6 us (31%)
  Pallas kernels  43.9 us (29%)
  local copies, waits for them, and re-layouts  3.2 us (2%)
    ppermute x28, waiting for transfers between devices, send(): return lax.ppermute(part, 'ctx', [(p, p ^ d) for p in range(count)])  50 us
    ppermute x28, starting transfers between devices, send(): return lax.ppermute(part, 'ctx', [(p, p ^ d) for p in range(count)])  44.5 us
    pallas_call x2, Pallas kernels, conv_call(): pl.pallas_call(kernel, grid_spec=pltpu.PrefetchScalarGridSpec(num_scalar_...  21.2 us
    pallas_call x1, Pallas kernels, project_call(): pl.pallas_call(functools.partial(project_kernel, chunks, members), grid_s...  8.49 us
    pallas_call x2, Pallas kernels, prepare_call(): pl.pallas_call(functools.partial(prepare_kernel, masks, scale), in_specs=...  6.75 us
    ppermute x1, waiting for transfers between devices, gather_start(): lax.ppermute(block, 'group', [(g, g ^ count // 2) for g in range(count)])  6.16 us
    pallas_call x2, Pallas kernels, finish_call(): pl.pallas_call(functools.partial(finish_kernel, count), grid_spec=pltpu.P...  5.16 us
  transfers between devices with their start and end apart: 31, of which 12 were waited for; matrix products, arithmetic and copies ran while one was open for 1% of the time, Pallas kernels for 26%

profile of v15, /device:TPU:0, one launch (start us, length us, event | category | flops | bytes accessed | tf_op | source)
XLA Modules:
  0.0 151.7 jit_solution(15834142742840171963)
XLA Ops:
  0.6 2.9 %shard_map.156 = (bf16[2,128,512]{2,1,0:T(8,128)(2,1)}, bf16[2,128,512]{2,1,0:T(8,128)(2,1)}) custom-call(bf16[8,128,512]{2,1,0:T(8,128)(2,1)} %bitcast.15, bf16[8,128,512]{2,1,0:T(8,128)(2,1)} %bitcast.25, f32[8,128,512]{2,1,0:T(8,128)} %bitcast.36, f32[8,128]{1,0:T(8,128)} %bitcast.42), custom_call_target="tpu_custom_call" | custom-call | flops 1048576 | bytes 1572864 | tf_op jit(solution)/shard_map/pallas_call | solution.py:230
  3.5 3.0 %collective-permute-start.1 = (bf16[1024,512]{1,0:T(8,128)(2,1)S(1)}, bf16[1024,512]{1,0:T(8,128)(2,1)}, u32[]{:S(2)}, u32[]{:S(2)}) collective-permute-start(bf16[1024,512]{1,0:T(8,128)(2,1)S(1)} %copy-done.2), channel_id=1, source_target_pairs={{0,16},{8,24},{16,0},{24,8},{1,17},{9,25},{17,1},{25,9},{2,18},{10... | collective-permute-start | bytes 3145736 | tf_op jit(solution)/shard_map/ppermute | solution.py:379
  6.5 4.6 %collective-permute-start.2 = (bf16[2,128,512]{2,1,0:T(8,128)(2,1)}, bf16[2,128,512]{2,1,0:T(8,128)(2,1)S(1)}, u32[]{:S(2)}, u32[]{:S(2)}) collective-permute-start(bf16[2,128,512]{2,1,0:T(8,128)(2,1)} %get-tuple-element.54), channel_id=1, source_target_pairs={{0,7},{1,6},{2,5},{3,4},{4,3},{5,2},{6,1},{7,0},{8,15},{9,14},{10,... | collective-permute-start | bytes 786440 | tf_op jit(solution)/shard_map/ppermute | solution.py:399
  11.3 3.9 %shard_map.157 = (bf16[2,128,512]{2,1,0:T(8,128)(2,1)}, bf16[2,128,512]{2,1,0:T(8,128)(2,1)}, bf16[2,128,512]{2,1,0:T(8,128)(2,1)}, bf16[2,128,512]{2,1,0:T(8,12...) custom-call(bf16[8,128,512]{2,1,0:T(8,128)(2,1)} %bitcast.16, bf16[8,128,512]{2,1,0:T(8,128)(2,1)} %bitcast.26, ...), custom_call_target="tpu_custom_call" | custom-call | flops 3145728 | bytes 4718592 | tf_op jit(solution)/shard_map/pallas_call | solution.py:230
  17.7 5.3 %collective-permute-done.3.refs_2_ = bf16[2,128,512]{2,1,0:T(8,128)(2,1)S(1)} collective-permute-done((bf16[2,128,512]{2,1,0:T(8,128)(2,1)}, bf16[2,128,512]{2,1,0:T(8,128)(2,1)S(1)}, u32[]{:S(2)}, u32[]{:S(2)}) %collective-permute-start.3) | collective-permute-done | bytes 262176 | tf_op jit(solution)/shard_map/ppermute | solution.py:399
  23.6 6.2 %collective-permute-done.1.refs_6_ = bf16[1024,512]{1,0:T(8,128)(2,1)} collective-permute-done((bf16[1024,512]{1,0:T(8,128)(2,1)S(1)}, bf16[1024,512]{1,0:T(8,128)(2,1)}, u32[]{:S(2)}, u32[]{:S(2)}) %collective-permute-start.1) | collective-permute-done | bytes 1048608 | tf_op jit(solution)/shard_map/ppermute | solution.py:379
  29.8 5.2 %collective-permute-start.6 = (bf16[2,128,512]{2,1,0:T(8,128)(2,1)}, bf16[2,128,512]{2,1,0:T(8,128)(2,1)}, u32[]{:S(2)}, u32[]{:S(2)}) collective-permute-start(bf16[2,128,512]{2,1,0:T(8,128)(2,1)} %get-tuple-element.58), channel_id=1, source_target_pairs={{0,5},{1,4},{2,7},{3,6},{4,1},{5,0},{6,3},{7,2},{8,13},{9,12},{10,... | collective-permute-start | bytes 786440 | tf_op jit(solution)/shard_map/ppermute | solution.py:399
  35.1 2.9 %collective-permute-start.8 = (bf16[2,128,512]{2,1,0:T(8,128)(2,1)}, bf16[2,128,512]{2,1,0:T(8,128)(2,1)}, u32[]{:S(2)}, u32[]{:S(2)}) collective-permute-start(bf16[2,128,512]{2,1,0:T(8,128)(2,1)} %get-tuple-element.65), channel_id=1, source_target_pairs={{0,2},{1,3},{2,0},{3,1},{4,6},{5,7},{6,4},{7,5},{8,10},{9,11},{10,... | collective-permute-start | bytes 786440 | tf_op jit(solution)/shard_map/ppermute | solution.py:399
  39.4 8.5 %shard_map.158 = (bf16[8,128,512]{2,1,0:T(8,128)(2,1)S(1)}, bf16[128,512]{1,0:T(8,128)(2,1)S(1)}, bf16[128,512]{1,0:T(8,128)(2,1)S(1)}, bf16[128,512]{1,0:T(8,12...) custom-call(s32[2]{0:T(128)S(1)} %pad_add_fusion.me, ...), custom_call_target="tpu_custom_call" | custom-call | flops 4294967296 | bytes 8388608 | tf_op jit(solution)/shard_map/pallas_call | solution.py:354
  47.9 2.5 %collective-permute-start.10 = (bf16[128,512]{1,0:T(8,128)(2,1)S(1)}, bf16[128,512]{1,0:T(8,128)(2,1)S(1)}, u32[]{:S(2)}, u32[]{:S(2)}) collective-permute-start(bf16[128,512]{1,0:T(8,128)(2,1)S(1)} %get-tuple-element.69), channel_id=1, source_target_pairs={{0,7},{1,6},{2,5},{3,4},{4,3},{5,2},{6,1},{7,0},{8,15},{9,14},{10,... | collective-permute-start | bytes 393224 | tf_op jit(solution)/shard_map/ppermute | solution.py:399
  50.4 4.1 %collective-permute-done.7.refs_4_ = bf16[2,128,512]{2,1,0:T(8,128)(2,1)} collective-permute-done((bf16[2,128,512]{2,1,0:T(8,128)(2,1)}, bf16[2,128,512]{2,1,0:T(8,128)(2,1)}, u32[]{:S(2)}, u32[]{:S(2)}) %collective-permute-start.7) | collective-permute-done | bytes 262176 | tf_op jit(solution)/shard_map/ppermute | solution.py:399
  54.5 7.0 %collective-permute-done.8.refs_5_ = bf16[2,128,512]{2,1,0:T(8,128)(2,1)} collective-permute-done((bf16[2,128,512]{2,1,0:T(8,128)(2,1)}, bf16[2,128,512]{2,1,0:T(8,128)(2,1)}, u32[]{:S(2)}, u32[]{:S(2)}) %collective-permute-start.8) | collective-permute-done | bytes 262176 | tf_op jit(solution)/shard_map/ppermute | solution.py:399
  62.7 2.6 %collective-permute-done.10.refs_9_ = bf16[128,512]{1,0:T(8,128)(2,1)S(1)} collective-permute-done((bf16[128,512]{1,0:T(8,128)(2,1)S(1)}, bf16[128,512]{1,0:T(8,128)(2,1)S(1)}, u32[]{:S(2)}, u32[]{:S(2)}) %collective-permute-start.10) | collective-permute-done | bytes 131104 | tf_op jit(solution)/shard_map/ppermute | solution.py:399
  65.3 2.9 %collective-permute-start.15 = (bf16[128,512]{1,0:T(8,128)(2,1)S(1)}, bf16[128,512]{1,0:T(8,128)(2,1)S(1)}, u32[]{:S(2)}, u32[]{:S(2)}) collective-permute-start(bf16[128,512]{1,0:T(8,128)(2,1)S(1)} %get-tuple-element.74), channel_id=1, source_target_pairs={{0,5},{1,4},{2,7},{3,6},{4,1},{5,0},{6,3},{7,2},{8,13},{9,12},{10,... | collective-permute-start | bytes 393224 | tf_op jit(solution)/shard_map/ppermute | solution.py:399
  68.9 8.4 %shard_map.159 = (bf16[128,512]{1,0:T(8,128)(2,1)S(1)}, bf16[128,512]{1,0:T(8,128)(2,1)S(1)}, bf16[128,512]{1,0:T(8,128)(2,1)S(1)}, bf16[128,512]{1,0:T(8,128)(2...) custom-call(s32[2]{0:T(128)S(1)} %pad_add_fusion.me, ...), custom_call_target="tpu_custom_call" | custom-call | flops 3221225472 | bytes 4194304 | tf_op jit(solution)/shard_map/pallas_call | solution.py:175
  77.3 1.9 %collective-permute-start.17 = (bf16[128,512]{1,0:T(8,128)(2,1)S(1)}, bf16[128,512]{1,0:T(8,128)(2,1)S(1)}, u32[]{:S(2)}, u32[]{:S(2)}) collective-permute-start(bf16[128,512]{1,0:T(8,128)(2,1)S(1)} %get-tuple-element.78), channel_id=1, source_target_pairs={{0,7},{1,6},{2,5},{3,4},{4,3},{5,2},{6,1},{7,0},{8,15},{9,14},{10,... | collective-permute-start | bytes 393224 | tf_op jit(solution)/shard_map/ppermute | solution.py:399
  79.2 3.9 %collective-permute-done.15.refs_14_ = bf16[128,512]{1,0:T(8,128)(2,1)S(1)} collective-permute-done((bf16[128,512]{1,0:T(8,128)(2,1)S(1)}, bf16[128,512]{1,0:T(8,128)(2,1)S(1)}, u32[]{:S(2)}, u32[]{:S(2)}) %collective-permute-start.15) | collective-permute-done | bytes 131104 | tf_op jit(solution)/shard_map/ppermute | solution.py:399
  83.2 6.0 %collective-permute-done.16.refs_15_ = bf16[128,512]{1,0:T(8,128)(2,1)S(1)} collective-permute-done((bf16[128,512]{1,0:T(8,128)(2,1)S(1)}, bf16[128,512]{1,0:T(8,128)(2,1)S(1)}, u32[]{:S(2)}, u32[]{:S(2)}) %collective-permute-start.16) | collective-permute-done | bytes 131104 | tf_op jit(solution)/shard_map/ppermute | solution.py:399
  89.2 5.4 %collective-permute-start.20 = (bf16[128,512]{1,0:T(8,128)(2,1)S(1)}, bf16[128,512]{1,0:T(8,128)(2,1)S(1)}, u32[]{:S(2)}, u32[]{:S(2)}) collective-permute-start(bf16[128,512]{1,0:T(8,128)(2,1)S(1)} %get-tuple-element.87), channel_id=1, source_target_pairs={{0,4},{1,5},{2,6},{3,7},{4,0},{5,1},{6,2},{7,3},{8,12},{9,13},{10,... | collective-permute-start | bytes 393224 | tf_op jit(solution)/shard_map/ppermute | solution.py:399
  94.6 12.8 %shard_map.160 = (bf16[2,128,512]{2,1,0:T(8,128)(2,1)S(1)}, bf16[2,128,512]{2,1,0:T(8,128)(2,1)S(1)}, bf16[2,128,512]{2,1,0:T(8,128)(2,1)S(1)}, bf16[2,128,512]{...) custom-call(s32[2]{0:T(128)S(1)} %pad_add_fusion.me, ...), custom_call_target="tpu_custom_call" | custom-call | flops 5368709120 | bytes 4194304 | tf_op jit(solution)/shard_map/pallas_call | solution.py:175
  107.5 2.3 %collective-permute-start.26 = (bf16[2,128,512]{2,1,0:T(8,128)(2,1)S(1)}, bf16[2,128,512]{2,1,0:T(8,128)(2,1)S(1)}, u32[]{:S(2)}, u32[]{:S(2)}) collective-permute-start(bf16[2,128,512]{2,1,0:T(8,128)(2,1)S(1)} %get-tuple-element.93), channel_id=1, source_target_pairs={{0,7},{1,6},{2,5},{3,4},{4,3},{5,2},{6,1},{7,0},{8,15},{9,14},{10,... | collective-permute-start | bytes 786440 | tf_op jit(solution)/shard_map/ppermute | solution.py:399
  109.9 4.4 %collective-permute-start.22 = (bf16[128,512]{1,0:T(8,128)(2,1)S(1)}, bf16[128,512]{1,0:T(8,128)(2,1)S(1)}, u32[]{:S(2)}, u32[]{:S(2)}) collective-permute-start(bf16[128,512]{1,0:T(8,128)(2,1)S(1)} %get-tuple-element.89), channel_id=1, source_target_pairs={{0,2},{1,3},{2,0},{3,1},{4,6},{5,7},{6,4},{7,5},{8,10},{9,11},{10,... | collective-permute-start | bytes 393224 | tf_op jit(solution)/shard_map/ppermute | solution.py:399
  114.3 8.1 %collective-permute-done.21.refs_5_ = bf16[128,512]{1,0:T(8,128)(2,1)S(1)} collective-permute-done((bf16[128,512]{1,0:T(8,128)(2,1)S(1)}, bf16[128,512]{1,0:T(8,128)(2,1)S(1)}, u32[]{:S(2)}, u32[]{:S(2)}) %collective-permute-start.21) | collective-permute-done | bytes 131104 | tf_op jit(solution)/shard_map/ppermute | solution.py:399
  122.4 2.9 %collective-permute-start.28 = (bf16[2,128,512]{2,1,0:T(8,128)(2,1)S(1)}, bf16[2,128,512]{2,1,0:T(8,128)(2,1)S(1)}, u32[]{:S(2)}, u32[]{:S(2)}) collective-permute-start(bf16[2,128,512]{2,1,0:T(8,128)(2,1)S(1)} %get-tuple-element.95), channel_id=1, source_target_pairs={{0,3},{1,2},{2,1},{3,0},{4,7},{5,6},{6,5},{7,4},{8,11},{9,10},{10,... | collective-permute-start | bytes 786440 | tf_op jit(solution)/shard_map/ppermute | solution.py:399
  126.7 1.7 %collective-permute-start.30 = (bf16[2,128,512]{2,1,0:T(8,128)(2,1)S(1)}, bf16[2,128,512]{2,1,0:T(8,128)(2,1)S(1)}, u32[]{:S(2)}, u32[]{:S(2)}) collective-permute-start(bf16[2,128,512]{2,1,0:T(8,128)(2,1)S(1)} %get-tuple-element.97), channel_id=1, source_target_pairs={{0,1},{1,0},{2,3},{3,2},{4,5},{5,4},{6,7},{7,6},{8,9},{9,8},{10,11... | collective-permute-start | bytes 786440 | tf_op jit(solution)/shard_map/ppermute | solution.py:399
  128.5 3.5 %collective-permute-start.25 = (bf16[2,128,512]{2,1,0:T(8,128)(2,1)S(1)}, bf16[2,128,512]{2,1,0:T(8,128)(2,1)S(1)}, u32[]{:S(2)}, u32[]{:S(2)}) collective-permute-start(bf16[2,128,512]{2,1,0:T(8,128)(2,1)S(1)} %get-tuple-element.92), channel_id=1, source_target_pairs={{0,4},{1,5},{2,6},{3,7},{4,0},{5,1},{6,2},{7,3},{8,12},{9,13},{10,... | collective-permute-start | bytes 786440 | tf_op jit(solution)/shard_map/ppermute | solution.py:399
  132.0 2.3 %shard_map.161 = bf16[8,128,512]{2,1,0:T(8,128)(2,1)} custom-call(s32[2]{0:T(128)S(1)} %pad_add_fusion.me, bf16[8,128,512]{2,1,0:T(8,128)(2,1)S(1)} %get-tuple-element.60.upstream, bf16[128,512]{1,0:T(8,128)(2,1)S(1)} %get-tuple-element.77.refs_0_, bf16[128,512]{1,0:T(8,128)(2,1)S(1)} %collective-permute-done.17.refs_1_, ...), custom_call_target="tpu_custom_call" | custom-call | flops 3145728 | bytes 3145728 | tf_op jit(solution)/shard_map/pallas_call | solution.py:332
  134.3 4.8 %collective-permute-done.29.refs_16_ = bf16[2,128,512]{2,1,0:T(8,128)(2,1)S(1)} collective-permute-done((bf16[2,128,512]{2,1,0:T(8,128)(2,1)S(1)}, bf16[2,128,512]{2,1,0:T(8,128)(2,1)S(1)}, u32[]{:S(2)}, u32[]{:S(2)}) %collective-permute-start.29) | collective-permute-done | bytes 262176 | tf_op jit(solution)/shard_map/ppermute | solution.py:399
  139.1 3.5 %shard_map.162 = (bf16[8,128,512]{2,1,0:T(8,128)(2,1)}, bf16[8,128,512]{2,1,0:T(8,128)(2,1)}, f32[8,128,512]{2,1,0:T(8,128)}) custom-call(s32[2]{0:T(128)S(1)} %pad_add_fusion.me, bf16[8,128,512]{2,1,0:T(8,128)(2,1)S(1)} %bitcast.17, bf16[8,128,512]{2,1,0:T(8,128)(2,1)S(1)} %bitcast.18, bf16[8,128,512]{2,1,0:T(8,128)(2,1)S(1)} %bitcast.19, ...), custom_call_target="tpu_custom_call" | custom-call | flops 786432 | bytes 6291456 | tf_op jit(solution)/shard_map/pallas_call | solution.py:304
  142.7 4.6 %collective-permute-done.24.refs_4_ = bf16[2,128,512]{2,1,0:T(8,128)(2,1)S(1)} collective-permute-done((bf16[2,128,512]{2,1,0:T(8,128)(2,1)S(1)}, bf16[2,128,512]{2,1,0:T(8,128)(2,1)S(1)}, u32[]{:S(2)}, u32[]{:S(2)}) %collective-permute-start.24) | collective-permute-done | bytes 262176 | tf_op jit(solution)/shard_map/ppermute | solution.py:399
  147.2 2.8 %collective-permute-done.25.refs_5_ = bf16[2,128,512]{2,1,0:T(8,128)(2,1)S(1)} collective-permute-done((bf16[2,128,512]{2,1,0:T(8,128)(2,1)S(1)}, bf16[2,128,512]{2,1,0:T(8,128)(2,1)S(1)}, u32[]{:S(2)}, u32[]{:S(2)}) %collective-permute-start.25) | collective-permute-done | bytes 262176 | tf_op jit(solution)/shard_map/ppermute | solution.py:399
  150.1 1.6 %shard_map.163 = (bf16[8,128,512]{2,1,0:T(8,128)(2,1)}, bf16[8,128,512]{2,1,0:T(8,128)(2,1)}, f32[8,128,512]{2,1,0:T(8,128)}) custom-call(s32[2]{0:T(128)S(1)} %pad_add_fusion.me, bf16[8,128,512]{2,1,0:T(8,128)(2,1)S(1)} %bitcast.23, bf16[8,128,512]{2,1,0:T(8,128)(2,1)S(1)} %bitcast.24, ...), custom_call_target="tpu_custom_call", output_to_operand_aliasing={{0}: (7, {}), {1}: (8, {}), {2}: (9, {})} | custom-call | flops 262144 | bytes 2097152 | tf_op jit(solution)/shard_map/pallas_call | solution.py:304
  (59 shorter events, 8.3 us)
Async XLA Ops:
  3.5 26.3 %collective-permute-start.1 = (bf16[1024,512]{1,0:T(8,128)(2,1)S(1)}, bf16[1024,512]{1,0:T(8,128)(2,1)}, u32[]{:S(2)}, u32[]{:S(2)}) collective-permute-start(bf16[1024,512]{1,0:T(8,128)(2,1)S(1)} %copy-done.2), channel_id=1, source_target_pairs={{0,16},{8,24},{16,0},{24,8},{1,17},{9,25},{17,1},{25,9},{2,18},{10... | collective-permute-start | bytes 3145736 | tf_op jit(solution)/shard_map/ppermute | solution.py:379
  6.5 16.5 %collective-permute-start.2 = (bf16[2,128,512]{2,1,0:T(8,128)(2,1)}, bf16[2,128,512]{2,1,0:T(8,128)(2,1)S(1)}, u32[]{:S(2)}, u32[]{:S(2)}) collective-permute-start(bf16[2,128,512]{2,1,0:T(8,128)(2,1)} %get-tuple-element.54), channel_id=1, source_target_pairs={{0,7},{1,6},{2,5},{3,4},{4,3},{5,2},{6,1},{7,0},{8,15},{9,14},{10,... | collective-permute-start | bytes 786440 | tf_op jit(solution)/shard_map/ppermute | solution.py:399
  11.1 11.9 %collective-permute-start.3 = (bf16[2,128,512]{2,1,0:T(8,128)(2,1)}, bf16[2,128,512]{2,1,0:T(8,128)(2,1)S(1)}, u32[]{:S(2)}, u32[]{:S(2)}) collective-permute-start(bf16[2,128,512]{2,1,0:T(8,128)(2,1)} %get-tuple-element.56), channel_id=1, source_target_pairs={{0,6},{1,7},{2,4},{3,5},{4,2},{5,3},{6,0},{7,1},{8,14},{9,15},{10,... | collective-permute-start | bytes 786440 | tf_op jit(solution)/shard_map/ppermute | solution.py:399
  15.2 8.4 %collective-permute-start.4 = (bf16[2,128,512]{2,1,0:T(8,128)(2,1)}, bf16[2,128,512]{2,1,0:T(8,128)(2,1)}, u32[]{:S(2)}, u32[]{:S(2)}) collective-permute-start(bf16[2,128,512]{2,1,0:T(8,128)(2,1)} %get-tuple-element.57), channel_id=1, source_target_pairs={{0,1},{1,0},{2,3},{3,2},{4,5},{5,4},{6,7},{7,6},{8,9},{9,8},{10,11... | collective-permute-start | bytes 786440 | tf_op jit(solution)/shard_map/ppermute | solution.py:399
  15.8 22.3 %collective-permute-start = (bf16[1024,512]{1,0:T(8,128)(2,1)S(1)}, bf16[1024,512]{1,0:T(8,128)(2,1)S(1)}, u32[]{:S(2)}, u32[]{:S(2)}) collective-permute-start(bf16[1024,512]{1,0:T(8,128)(2,1)S(1)} %copy-done.2), channel_id=1, source_target_pairs={{0,8},{8,0},{16,24},{24,16},{1,9},{9,1},{17,25},{25,17},{2,10},{10... | collective-permute-start | bytes 3145736 | tf_op jit(solution)/shard_map/ppermute | solution.py:393
  29.8 8.3 %collective-permute-start.5 = (bf16[1024,512]{1,0:T(8,128)(2,1)}, bf16[1024,512]{1,0:T(8,128)(2,1)}, u32[]{:S(2)}, u32[]{:S(2)}) collective-permute-start(bf16[1024,512]{1,0:T(8,128)(2,1)} %collective-permute-done.1.refs_6_), channel_id=1, source_target_pairs={{0,8},{8,0},{16,24},{24,16},{1,9},{9,1},{17,25},{25,17},{2,10},{10... | collective-permute-start | bytes 3145736 | tf_op jit(solution)/shard_map/ppermute | solution.py:393
  29.8 31.7 %collective-permute-start.6 = (bf16[2,128,512]{2,1,0:T(8,128)(2,1)}, bf16[2,128,512]{2,1,0:T(8,128)(2,1)}, u32[]{:S(2)}, u32[]{:S(2)}) collective-permute-start(bf16[2,128,512]{2,1,0:T(8,128)(2,1)} %get-tuple-element.58), channel_id=1, source_target_pairs={{0,5},{1,4},{2,7},{3,6},{4,1},{5,0},{6,3},{7,2},{8,13},{9,12},{10,... | collective-permute-start | bytes 786440 | tf_op jit(solution)/shard_map/ppermute | solution.py:399
  35.0 19.5 %collective-permute-start.7 = (bf16[2,128,512]{2,1,0:T(8,128)(2,1)}, bf16[2,128,512]{2,1,0:T(8,128)(2,1)}, u32[]{:S(2)}, u32[]{:S(2)}) collective-permute-start(bf16[2,128,512]{2,1,0:T(8,128)(2,1)} %get-tuple-element.64), channel_id=1, source_target_pairs={{0,3},{1,2},{2,1},{3,0},{4,7},{5,6},{6,5},{7,4},{8,11},{9,10},{10,... | collective-permute-start | bytes 786440 | tf_op jit(solution)/shard_map/ppermute | solution.py:399
  35.1 26.3 %collective-permute-start.8 = (bf16[2,128,512]{2,1,0:T(8,128)(2,1)}, bf16[2,128,512]{2,1,0:T(8,128)(2,1)}, u32[]{:S(2)}, u32[]{:S(2)}) collective-permute-start(bf16[2,128,512]{2,1,0:T(8,128)(2,1)} %get-tuple-element.65), channel_id=1, source_target_pairs={{0,2},{1,3},{2,0},{3,1},{4,6},{5,7},{6,4},{7,5},{8,10},{9,11},{10,... | collective-permute-start | bytes 786440 | tf_op jit(solution)/shard_map/ppermute | solution.py:399
  38.1 23.4 %collective-permute-start.9 = (bf16[2,128,512]{2,1,0:T(8,128)(2,1)}, bf16[2,128,512]{2,1,0:T(8,128)(2,1)S(1)}, u32[]{:S(2)}, u32[]{:S(2)}) collective-permute-start(bf16[2,128,512]{2,1,0:T(8,128)(2,1)} %get-tuple-element.66), channel_id=1, source_target_pairs={{0,4},{1,5},{2,6},{3,7},{4,0},{5,1},{6,2},{7,3},{8,12},{9,13},{10,... | collective-permute-start | bytes 786440 | tf_op jit(solution)/shard_map/ppermute | solution.py:399
  47.9 17.5 %collective-permute-start.10 = (bf16[128,512]{1,0:T(8,128)(2,1)S(1)}, bf16[128,512]{1,0:T(8,128)(2,1)S(1)}, u32[]{:S(2)}, u32[]{:S(2)}) collective-permute-start(bf16[128,512]{1,0:T(8,128)(2,1)S(1)} %get-tuple-element.69), channel_id=1, source_target_pairs={{0,7},{1,6},{2,5},{3,4},{4,3},{5,2},{6,1},{7,0},{8,15},{9,14},{10,... | collective-permute-start | bytes 393224 | tf_op jit(solution)/shard_map/ppermute | solution.py:399
  54.5 13.8 %collective-permute-start.11 = (bf16[128,512]{1,0:T(8,128)(2,1)S(1)}, bf16[128,512]{1,0:T(8,128)(2,1)S(1)}, u32[]{:S(2)}, u32[]{:S(2)}) collective-permute-start(bf16[128,512]{1,0:T(8,128)(2,1)S(1)} %get-tuple-element.70), channel_id=1, source_target_pairs={{0,3},{1,2},{2,1},{3,0},{4,7},{5,6},{6,5},{7,4},{8,11},{9,10},{10,... | collective-permute-start | bytes 393224 | tf_op jit(solution)/shard_map/ppermute | solution.py:399
  61.5 15.8 %collective-permute-start.12 = (bf16[128,512]{1,0:T(8,128)(2,1)S(1)}, bf16[128,512]{1,0:T(8,128)(2,1)S(1)}, u32[]{:S(2)}, u32[]{:S(2)}) collective-permute-start(bf16[128,512]{1,0:T(8,128)(2,1)S(1)} %get-tuple-element.71), channel_id=1, source_target_pairs={{0,2},{1,3},{2,0},{3,1},{4,6},{5,7},{6,4},{7,5},{8,10},{9,11},{10,... | collective-permute-start | bytes 393224 | tf_op jit(solution)/shard_map/ppermute | solution.py:399
  61.5 17.8 %collective-permute-start.13 = (bf16[128,512]{1,0:T(8,128)(2,1)S(1)}, bf16[128,512]{1,0:T(8,128)(2,1)S(1)}, u32[]{:S(2)}, u32[]{:S(2)}) collective-permute-start(bf16[128,512]{1,0:T(8,128)(2,1)S(1)} %get-tuple-element.72), channel_id=1, source_target_pairs={{0,1},{1,0},{2,3},{3,2},{4,5},{5,4},{6,7},{7,6},{8,9},{9,8},{10,11... | collective-permute-start | bytes 393224 | tf_op jit(solution)/shard_map/ppermute | solution.py:399
  61.5 17.7 %collective-permute-start.14 = (bf16[128,512]{1,0:T(8,128)(2,1)S(1)}, bf16[128,512]{1,0:T(8,128)(2,1)S(1)}, u32[]{:S(2)}, u32[]{:S(2)}) collective-permute-start(bf16[128,512]{1,0:T(8,128)(2,1)S(1)} %get-tuple-element.73), channel_id=1, source_target_pairs={{0,6},{1,7},{2,4},{3,5},{4,2},{5,3},{6,0},{7,1},{8,14},{9,15},{10,... | collective-permute-start | bytes 393224 | tf_op jit(solution)/shard_map/ppermute | solution.py:399
  65.3 17.8 %collective-permute-start.15 = (bf16[128,512]{1,0:T(8,128)(2,1)S(1)}, bf16[128,512]{1,0:T(8,128)(2,1)S(1)}, u32[]{:S(2)}, u32[]{:S(2)}) collective-permute-start(bf16[128,512]{1,0:T(8,128)(2,1)S(1)} %get-tuple-element.74), channel_id=1, source_target_pairs={{0,5},{1,4},{2,7},{3,6},{4,1},{5,0},{6,3},{7,2},{8,13},{9,12},{10,... | collective-permute-start | bytes 393224 | tf_op jit(solution)/shard_map/ppermute | solution.py:399
  68.2 21.0 %collective-permute-start.16 = (bf16[128,512]{1,0:T(8,128)(2,1)S(1)}, bf16[128,512]{1,0:T(8,128)(2,1)S(1)}, u32[]{:S(2)}, u32[]{:S(2)}) collective-permute-start(bf16[128,512]{1,0:T(8,128)(2,1)S(1)} %get-tuple-element.75), channel_id=1, source_target_pairs={{0,4},{1,5},{2,6},{3,7},{4,0},{5,1},{6,2},{7,3},{8,12},{9,13},{10,... | collective-permute-start | bytes 393224 | tf_op jit(solution)/shard_map/ppermute | solution.py:399
  77.3 32.5 %collective-permute-start.17 = (bf16[128,512]{1,0:T(8,128)(2,1)S(1)}, bf16[128,512]{1,0:T(8,128)(2,1)S(1)}, u32[]{:S(2)}, u32[]{:S(2)}) collective-permute-start(bf16[128,512]{1,0:T(8,128)(2,1)S(1)} %get-tuple-element.78), channel_id=1, source_target_pairs={{0,7},{1,6},{2,5},{3,4},{4,3},{5,2},{6,1},{7,0},{8,15},{9,14},{10,... | collective-permute-start | bytes 393224 | tf_op jit(solution)/shard_map/ppermute | solution.py:399
  89.2 20.6 %collective-permute-start.18 = (bf16[128,512]{1,0:T(8,128)(2,1)S(1)}, bf16[128,512]{1,0:T(8,128)(2,1)S(1)}, u32[]{:S(2)}, u32[]{:S(2)}) collective-permute-start(bf16[128,512]{1,0:T(8,128)(2,1)S(1)} %get-tuple-element.85), channel_id=1, source_target_pairs={{0,6},{1,7},{2,4},{3,5},{4,2},{5,3},{6,0},{7,1},{8,14},{9,15},{10,... | collective-permute-start | bytes 393224 | tf_op jit(solution)/shard_map/ppermute | solution.py:399
  89.2 20.7 %collective-permute-start.19 = (bf16[128,512]{1,0:T(8,128)(2,1)S(1)}, bf16[128,512]{1,0:T(8,128)(2,1)S(1)}, u32[]{:S(2)}, u32[]{:S(2)}) collective-permute-start(bf16[128,512]{1,0:T(8,128)(2,1)S(1)} %get-tuple-element.86), channel_id=1, source_target_pairs={{0,5},{1,4},{2,7},{3,6},{4,1},{5,0},{6,3},{7,2},{8,13},{9,12},{10,... | collective-permute-start | bytes 393224 | tf_op jit(solution)/shard_map/ppermute | solution.py:399
  89.2 25.1 %collective-permute-start.20 = (bf16[128,512]{1,0:T(8,128)(2,1)S(1)}, bf16[128,512]{1,0:T(8,128)(2,1)S(1)}, u32[]{:S(2)}, u32[]{:S(2)}) collective-permute-start(bf16[128,512]{1,0:T(8,128)(2,1)S(1)} %get-tuple-element.87), channel_id=1, source_target_pairs={{0,4},{1,5},{2,6},{3,7},{4,0},{5,1},{6,2},{7,3},{8,12},{9,13},{10,... | collective-permute-start | bytes 393224 | tf_op jit(solution)/shard_map/ppermute | solution.py:399
  107.5 31.7 %copy-start = (bf16[1024,512]{1,0:T(8,128)(2,1)S(1)}, bf16[1024,512]{1,0:T(8,128)(2,1)}, u32[]{:S(2)}) copy-start(bf16[1024,512]{1,0:T(8,128)(2,1)} %param.14) | copy-start | bytes 3145732
  107.5 21.0 %collective-permute-start.26 = (bf16[2,128,512]{2,1,0:T(8,128)(2,1)S(1)}, bf16[2,128,512]{2,1,0:T(8,128)(2,1)S(1)}, u32[]{:S(2)}, u32[]{:S(2)}) collective-permute-start(bf16[2,128,512]{2,1,0:T(8,128)(2,1)S(1)} %get-tuple-element.93), channel_id=1, source_target_pairs={{0,7},{1,6},{2,5},{3,4},{4,3},{5,2},{6,1},{7,0},{8,15},{9,14},{10,... | collective-permute-start | bytes 786440 | tf_op jit(solution)/shard_map/ppermute | solution.py:399
  109.8 18.7 %collective-permute-start.27 = (bf16[2,128,512]{2,1,0:T(8,128)(2,1)S(1)}, bf16[2,128,512]{2,1,0:T(8,128)(2,1)S(1)}, u32[]{:S(2)}, u32[]{:S(2)}) collective-permute-start(bf16[2,128,512]{2,1,0:T(8,128)(2,1)S(1)} %get-tuple-element.94), channel_id=1, source_target_pairs={{0,6},{1,7},{2,4},{3,5},{4,2},{5,3},{6,0},{7,1},{8,14},{9,15},{10,... | collective-permute-start | bytes 786440 | tf_op jit(solution)/shard_map/ppermute | solution.py:399
  109.8 12.6 %collective-permute-start.21 = (bf16[128,512]{1,0:T(8,128)(2,1)S(1)}, bf16[128,512]{1,0:T(8,128)(2,1)S(1)}, u32[]{:S(2)}, u32[]{:S(2)}) collective-permute-start(bf16[128,512]{1,0:T(8,128)(2,1)S(1)} %get-tuple-element.88), channel_id=1, source_target_pairs={{0,3},{1,2},{2,1},{3,0},{4,7},{5,6},{6,5},{7,4},{8,11},{9,10},{10,... | collective-permute-start | bytes 393224 | tf_op jit(solution)/shard_map/ppermute | solution.py:399
  109.9 15.5 %collective-permute-start.22 = (bf16[128,512]{1,0:T(8,128)(2,1)S(1)}, bf16[128,512]{1,0:T(8,128)(2,1)S(1)}, u32[]{:S(2)}, u32[]{:S(2)}) collective-permute-start(bf16[128,512]{1,0:T(8,128)(2,1)S(1)} %get-tuple-element.89), channel_id=1, source_target_pairs={{0,2},{1,3},{2,0},{3,1},{4,6},{5,7},{6,4},{7,5},{8,10},{9,11},{10,... | collective-permute-start | bytes 393224 | tf_op jit(solution)/shard_map/ppermute | solution.py:399
  114.3 12.4 %collective-permute-start.23 = (bf16[128,512]{1,0:T(8,128)(2,1)S(1)}, bf16[128,512]{1,0:T(8,128)(2,1)S(1)}, u32[]{:S(2)}, u32[]{:S(2)}) collective-permute-start(bf16[128,512]{1,0:T(8,128)(2,1)S(1)} %get-tuple-element.90), channel_id=1, source_target_pairs={{0,1},{1,0},{2,3},{3,2},{4,5},{5,4},{6,7},{7,6},{8,9},{9,8},{10,11... | collective-permute-start | bytes 393224 | tf_op jit(solution)/shard_map/ppermute | solution.py:399
  122.4 11.9 %collective-permute-start.28 = (bf16[2,128,512]{2,1,0:T(8,128)(2,1)S(1)}, bf16[2,128,512]{2,1,0:T(8,128)(2,1)S(1)}, u32[]{:S(2)}, u32[]{:S(2)}) collective-permute-start(bf16[2,128,512]{2,1,0:T(8,128)(2,1)S(1)} %get-tuple-element.95), channel_id=1, source_target_pairs={{0,3},{1,2},{2,1},{3,0},{4,7},{5,6},{6,5},{7,4},{8,11},{9,10},{10,... | collective-permute-start | bytes 786440 | tf_op jit(solution)/shard_map/ppermute | solution.py:399
  125.3 13.8 %collective-permute-start.29 = (bf16[2,128,512]{2,1,0:T(8,128)(2,1)S(1)}, bf16[2,128,512]{2,1,0:T(8,128)(2,1)S(1)}, u32[]{:S(2)}, u32[]{:S(2)}) collective-permute-start(bf16[2,128,512]{2,1,0:T(8,128)(2,1)S(1)} %get-tuple-element.96), channel_id=1, source_target_pairs={{0,2},{1,3},{2,0},{3,1},{4,6},{5,7},{6,4},{7,5},{8,10},{9,11},{10,... | collective-permute-start | bytes 786440 | tf_op jit(solution)/shard_map/ppermute | solution.py:399
  126.7 12.4 %collective-permute-start.30 = (bf16[2,128,512]{2,1,0:T(8,128)(2,1)S(1)}, bf16[2,128,512]{2,1,0:T(8,128)(2,1)S(1)}, u32[]{:S(2)}, u32[]{:S(2)}) collective-permute-start(bf16[2,128,512]{2,1,0:T(8,128)(2,1)S(1)} %get-tuple-element.97), channel_id=1, source_target_pairs={{0,1},{1,0},{2,3},{3,2},{4,5},{5,4},{6,7},{7,6},{8,9},{9,8},{10,11... | collective-permute-start | bytes 786440 | tf_op jit(solution)/shard_map/ppermute | solution.py:399
  128.4 18.8 %collective-permute-start.24 = (bf16[2,128,512]{2,1,0:T(8,128)(2,1)S(1)}, bf16[2,128,512]{2,1,0:T(8,128)(2,1)S(1)}, u32[]{:S(2)}, u32[]{:S(2)}) collective-permute-start(bf16[2,128,512]{2,1,0:T(8,128)(2,1)S(1)} %get-tuple-element.91), channel_id=1, source_target_pairs={{0,5},{1,4},{2,7},{3,6},{4,1},{5,0},{6,3},{7,2},{8,13},{9,12},{10,... | collective-permute-start | bytes 786440 | tf_op jit(solution)/shard_map/ppermute | solution.py:399
  128.5 21.6 %collective-permute-start.25 = (bf16[2,128,512]{2,1,0:T(8,128)(2,1)S(1)}, bf16[2,128,512]{2,1,0:T(8,128)(2,1)S(1)}, u32[]{:S(2)}, u32[]{:S(2)}) collective-permute-start(bf16[2,128,512]{2,1,0:T(8,128)(2,1)S(1)} %get-tuple-element.92), channel_id=1, source_target_pairs={{0,4},{1,5},{2,6},{3,7},{4,0},{5,1},{6,2},{7,3},{8,12},{9,13},{10,... | collective-permute-start | bytes 786440 | tf_op jit(solution)/shard_map/ppermute | solution.py:399
  (8 other events, 183.5 us)

commit v16 on v14

--- a/solution.py
+++ b/solution.py
@@ -451,7 +451,8 @@
         functools.partial(response_kernel, n_ctx, inner), me, (after(pair_sent, grad[0]),), tables, (), inner, 3
     )
     grad_came = exchange(grad)
-    resp_came = exchange(response)
+    waiting, _ = lax.optimization_barrier((list(response[3:]), grad_came[1:]))
+    resp_came = exchange([*response[:3], *waiting])
     backs = conv_call(
         functools.partial(backward_kernel, n_ctx, inner, scale),
         me,

time: 155 us -> 155 us (level)
  transfers between devices with their start and end apart: 31 -> 31, of which waited for: 12 -> 11; matrix products, arithmetic and copies ran while one was open for 1% -> 1% of each run, Pallas kernels for 26% -> 26%
where the time goes in v16:
time: 155 us; the launch traced here: 154 us
  waiting for transfers between devices  58.4 us (38%)
  starting transfers between devices  47.7 us (31%)
  Pallas kernels  43.9 us (28%)
  local copies, waits for them, and re-layouts  3.2 us (2%)
    ppermute x28, waiting for transfers between devices, send(): return lax.ppermute(part, 'ctx', [(p, p ^ d) for p in range(count)])  52.2 us
    ppermute x28, starting transfers between devices, send(): return lax.ppermute(part, 'ctx', [(p, p ^ d) for p in range(count)])  44.7 us
    pallas_call x2, Pallas kernels, conv_call(): pl.pallas_call(kernel, grid_spec=pltpu.PrefetchScalarGridSpec(num_scalar_...  21.2 us
    pallas_call x1, Pallas kernels, project_call(): pl.pallas_call(functools.partial(project_kernel, chunks, members), grid_s...  8.49 us
    pallas_call x2, Pallas kernels, prepare_call(): pl.pallas_call(functools.partial(prepare_kernel, masks, scale), in_specs=...  6.75 us
    ppermute x1, waiting for transfers between devices, gather_start(): lax.ppermute(block, 'group', [(g, g ^ count // 2) for g in range(count)])  6.16 us
    pallas_call x2, Pallas kernels, finish_call(): pl.pallas_call(functools.partial(finish_kernel, count), grid_spec=pltpu.P...  5.16 us
  transfers between devices with their start and end apart: 31, of which 11 were waited for; matrix products, arithmetic and copies ran while one was open for 1% of the time, Pallas kernels for 26%

profile of v16, /device:TPU:0, one launch (start us, length us, event | category | flops | bytes accessed | tf_op | source)
XLA Modules:
  0.0 154.2 jit_solution(8890205146708859382)
XLA Ops:
  0.6 2.9 %shard_map.156 = (bf16[2,128,512]{2,1,0:T(8,128)(2,1)}, bf16[2,128,512]{2,1,0:T(8,128)(2,1)}) custom-call(bf16[8,128,512]{2,1,0:T(8,128)(2,1)} %bitcast.15, bf16[8,128,512]{2,1,0:T(8,128)(2,1)} %bitcast.25, f32[8,128,512]{2,1,0:T(8,128)} %bitcast.36, f32[8,128]{1,0:T(8,128)} %bitcast.42), custom_call_target="tpu_custom_call" | custom-call | flops 1048576 | bytes 1572864 | tf_op jit(solution)/shard_map/pallas_call | solution.py:230
  3.5 3.0 %collective-permute-start.1 = (bf16[1024,512]{1,0:T(8,128)(2,1)S(1)}, bf16[1024,512]{1,0:T(8,128)(2,1)}, u32[]{:S(2)}, u32[]{:S(2)}) collective-permute-start(bf16[1024,512]{1,0:T(8,128)(2,1)S(1)} %copy-done.2), channel_id=1, source_target_pairs={{0,16},{8,24},{16,0},{24,8},{1,17},{9,25},{17,1},{25,9},{2,18},{10... | collective-permute-start | bytes 3145736 | tf_op jit(solution)/shard_map/ppermute | solution.py:379
  6.5 4.6 %collective-permute-start.2 = (bf16[2,128,512]{2,1,0:T(8,128)(2,1)}, bf16[2,128,512]{2,1,0:T(8,128)(2,1)S(1)}, u32[]{:S(2)}, u32[]{:S(2)}) collective-permute-start(bf16[2,128,512]{2,1,0:T(8,128)(2,1)} %get-tuple-element.53), channel_id=1, source_target_pairs={{0,7},{1,6},{2,5},{3,4},{4,3},{5,2},{6,1},{7,0},{8,15},{9,14},{10,... | collective-permute-start | bytes 786440 | tf_op jit(solution)/shard_map/ppermute | solution.py:399
  11.3 3.9 %shard_map.157 = (bf16[2,128,512]{2,1,0:T(8,128)(2,1)}, bf16[2,128,512]{2,1,0:T(8,128)(2,1)}, bf16[2,128,512]{2,1,0:T(8,128)(2,1)}, bf16[2,128,512]{2,1,0:T(8,12...) custom-call(bf16[8,128,512]{2,1,0:T(8,128)(2,1)} %bitcast.16, bf16[8,128,512]{2,1,0:T(8,128)(2,1)} %bitcast.26, ...), custom_call_target="tpu_custom_call" | custom-call | flops 3145728 | bytes 4718592 | tf_op jit(solution)/shard_map/pallas_call | solution.py:230
  17.7 5.3 %collective-permute-done.3.refs_2_ = bf16[2,128,512]{2,1,0:T(8,128)(2,1)S(1)} collective-permute-done((bf16[2,128,512]{2,1,0:T(8,128)(2,1)}, bf16[2,128,512]{2,1,0:T(8,128)(2,1)S(1)}, u32[]{:S(2)}, u32[]{:S(2)}) %collective-permute-start.3) | collective-permute-done | bytes 262176 | tf_op jit(solution)/shard_map/ppermute | solution.py:399
  23.6 6.2 %collective-permute-done.1.refs_6_ = bf16[1024,512]{1,0:T(8,128)(2,1)} collective-permute-done((bf16[1024,512]{1,0:T(8,128)(2,1)S(1)}, bf16[1024,512]{1,0:T(8,128)(2,1)}, u32[]{:S(2)}, u32[]{:S(2)}) %collective-permute-start.1) | collective-permute-done | bytes 1048608 | tf_op jit(solution)/shard_map/ppermute | solution.py:379
  29.8 5.2 %collective-permute-start.6 = (bf16[2,128,512]{2,1,0:T(8,128)(2,1)}, bf16[2,128,512]{2,1,0:T(8,128)(2,1)}, u32[]{:S(2)}, u32[]{:S(2)}) collective-permute-start(bf16[2,128,512]{2,1,0:T(8,128)(2,1)} %get-tuple-element.57), channel_id=1, source_target_pairs={{0,5},{1,4},{2,7},{3,6},{4,1},{5,0},{6,3},{7,2},{8,13},{9,12},{10,... | collective-permute-start | bytes 786440 | tf_op jit(solution)/shard_map/ppermute | solution.py:399
  35.1 2.9 %collective-permute-start.8 = (bf16[2,128,512]{2,1,0:T(8,128)(2,1)}, bf16[2,128,512]{2,1,0:T(8,128)(2,1)}, u32[]{:S(2)}, u32[]{:S(2)}) collective-permute-start(bf16[2,128,512]{2,1,0:T(8,128)(2,1)} %get-tuple-element.64), channel_id=1, source_target_pairs={{0,2},{1,3},{2,0},{3,1},{4,6},{5,7},{6,4},{7,5},{8,10},{9,11},{10,... | collective-permute-start | bytes 786440 | tf_op jit(solution)/shard_map/ppermute | solution.py:399
  39.4 8.5 %shard_map.158 = (bf16[8,128,512]{2,1,0:T(8,128)(2,1)S(1)}, bf16[128,512]{1,0:T(8,128)(2,1)S(1)}, bf16[128,512]{1,0:T(8,128)(2,1)S(1)}, bf16[128,512]{1,0:T(8,12...) custom-call(s32[2]{0:T(128)S(1)} %pad_add_fusion.me, ...), custom_call_target="tpu_custom_call" | custom-call | flops 4294967296 | bytes 8388608 | tf_op jit(solution)/shard_map/pallas_call | solution.py:354
  47.9 2.5 %collective-permute-start.10 = (bf16[128,512]{1,0:T(8,128)(2,1)S(1)}, bf16[128,512]{1,0:T(8,128)(2,1)S(1)}, u32[]{:S(2)}, u32[]{:S(2)}) collective-permute-start(bf16[128,512]{1,0:T(8,128)(2,1)S(1)} %get-tuple-element.68), channel_id=1, source_target_pairs={{0,7},{1,6},{2,5},{3,4},{4,3},{5,2},{6,1},{7,0},{8,15},{9,14},{10,... | collective-permute-start | bytes 393224 | tf_op jit(solution)/shard_map/ppermute | solution.py:399
  50.4 4.1 %collective-permute-done.7.refs_4_ = bf16[2,128,512]{2,1,0:T(8,128)(2,1)} collective-permute-done((bf16[2,128,512]{2,1,0:T(8,128)(2,1)}, bf16[2,128,512]{2,1,0:T(8,128)(2,1)}, u32[]{:S(2)}, u32[]{:S(2)}) %collective-permute-start.7) | collective-permute-done | bytes 262176 | tf_op jit(solution)/shard_map/ppermute | solution.py:399
  54.5 7.0 %collective-permute-done.8.refs_5_ = bf16[2,128,512]{2,1,0:T(8,128)(2,1)} collective-permute-done((bf16[2,128,512]{2,1,0:T(8,128)(2,1)}, bf16[2,128,512]{2,1,0:T(8,128)(2,1)}, u32[]{:S(2)}, u32[]{:S(2)}) %collective-permute-start.8) | collective-permute-done | bytes 262176 | tf_op jit(solution)/shard_map/ppermute | solution.py:399
  62.7 2.6 %collective-permute-done.10.refs_9_ = bf16[128,512]{1,0:T(8,128)(2,1)S(1)} collective-permute-done((bf16[128,512]{1,0:T(8,128)(2,1)S(1)}, bf16[128,512]{1,0:T(8,128)(2,1)S(1)}, u32[]{:S(2)}, u32[]{:S(2)}) %collective-permute-start.10) | collective-permute-done | bytes 131104 | tf_op jit(solution)/shard_map/ppermute | solution.py:399
  65.3 2.9 %collective-permute-start.15 = (bf16[128,512]{1,0:T(8,128)(2,1)S(1)}, bf16[128,512]{1,0:T(8,128)(2,1)S(1)}, u32[]{:S(2)}, u32[]{:S(2)}) collective-permute-start(bf16[128,512]{1,0:T(8,128)(2,1)S(1)} %get-tuple-element.73), channel_id=1, source_target_pairs={{0,5},{1,4},{2,7},{3,6},{4,1},{5,0},{6,3},{7,2},{8,13},{9,12},{10,... | collective-permute-start | bytes 393224 | tf_op jit(solution)/shard_map/ppermute | solution.py:399
  68.9 8.4 %shard_map.159 = (bf16[128,512]{1,0:T(8,128)(2,1)S(1)}, bf16[128,512]{1,0:T(8,128)(2,1)S(1)}, bf16[128,512]{1,0:T(8,128)(2,1)S(1)}, bf16[128,512]{1,0:T(8,128)(2...) custom-call(s32[2]{0:T(128)S(1)} %pad_add_fusion.me, ...), custom_call_target="tpu_custom_call" | custom-call | flops 3221225472 | bytes 4194304 | tf_op jit(solution)/shard_map/pallas_call | solution.py:175
  77.3 1.9 %collective-permute-start.17 = (bf16[128,512]{1,0:T(8,128)(2,1)S(1)}, bf16[128,512]{1,0:T(8,128)(2,1)S(1)}, u32[]{:S(2)}, u32[]{:S(2)}) collective-permute-start(bf16[128,512]{1,0:T(8,128)(2,1)S(1)} %get-tuple-element.77), channel_id=1, source_target_pairs={{0,7},{1,6},{2,5},{3,4},{4,3},{5,2},{6,1},{7,0},{8,15},{9,14},{10,... | collective-permute-start | bytes 393224 | tf_op jit(solution)/shard_map/ppermute | solution.py:399
  79.2 2.7 %collective-permute-start.18 = (bf16[128,512]{1,0:T(8,128)(2,1)S(1)}, bf16[128,512]{1,0:T(8,128)(2,1)S(1)}, u32[]{:S(2)}, u32[]{:S(2)}) collective-permute-start(bf16[128,512]{1,0:T(8,128)(2,1)S(1)} %get-tuple-element.78), channel_id=1, source_target_pairs={{0,6},{1,7},{2,4},{3,5},{4,2},{5,3},{6,0},{7,1},{8,14},{9,15},{10,... | collective-permute-start | bytes 393224 | tf_op jit(solution)/shard_map/ppermute | solution.py:399
  81.9 8.3 %collective-permute-done.15.refs_14_ = bf16[128,512]{1,0:T(8,128)(2,1)S(1)} collective-permute-done((bf16[128,512]{1,0:T(8,128)(2,1)S(1)}, bf16[128,512]{1,0:T(8,128)(2,1)S(1)}, u32[]{:S(2)}, u32[]{:S(2)}) %collective-permute-start.15) | collective-permute-done | bytes 131104 | tf_op jit(solution)/shard_map/ppermute | solution.py:399
  90.2 1.8 %collective-permute-done.16.refs_15_ = bf16[128,512]{1,0:T(8,128)(2,1)S(1)} collective-permute-done((bf16[128,512]{1,0:T(8,128)(2,1)S(1)}, bf16[128,512]{1,0:T(8,128)(2,1)S(1)}, u32[]{:S(2)}, u32[]{:S(2)}) %collective-permute-start.16) | collective-permute-done | bytes 131104 | tf_op jit(solution)/shard_map/ppermute | solution.py:399
  92.5 3.4 %collective-permute-start.20 = (bf16[128,512]{1,0:T(8,128)(2,1)S(1)}, bf16[128,512]{1,0:T(8,128)(2,1)S(1)}, u32[]{:S(2)}, u32[]{:S(2)}) collective-permute-start(bf16[128,512]{1,0:T(8,128)(2,1)S(1)} %get-tuple-element.85), channel_id=1, source_target_pairs={{0,4},{1,5},{2,6},{3,7},{4,0},{5,1},{6,2},{7,3},{8,12},{9,13},{10,... | collective-permute-start | bytes 393224 | tf_op jit(solution)/shard_map/ppermute | solution.py:399
  95.9 12.8 %shard_map.160 = (bf16[2,128,512]{2,1,0:T(8,128)(2,1)S(1)}, bf16[2,128,512]{2,1,0:T(8,128)(2,1)S(1)}, bf16[2,128,512]{2,1,0:T(8,128)(2,1)S(1)}, bf16[2,128,512]{...) custom-call(s32[2]{0:T(128)S(1)} %pad_add_fusion.me, ...), custom_call_target="tpu_custom_call" | custom-call | flops 5368709120 | bytes 4194304 | tf_op jit(solution)/shard_map/pallas_call | solution.py:175
  108.9 3.7 %collective-permute-start.27 = (bf16[2,128,512]{2,1,0:T(8,128)(2,1)S(1)}, bf16[2,128,512]{2,1,0:T(8,128)(2,1)S(1)}, u32[]{:S(2)}, u32[]{:S(2)}) collective-permute-start(bf16[2,128,512]{2,1,0:T(8,128)(2,1)S(1)} %get-tuple-element.92), channel_id=1, source_target_pairs={{0,6},{1,7},{2,4},{3,5},{4,2},{5,3},{6,0},{7,1},{8,14},{9,15},{10,... | collective-permute-start | bytes 786440 | tf_op jit(solution)/shard_map/ppermute | solution.py:399
  112.6 3.0 %collective-permute-start.22 = (bf16[128,512]{1,0:T(8,128)(2,1)S(1)}, bf16[128,512]{1,0:T(8,128)(2,1)S(1)}, u32[]{:S(2)}, u32[]{:S(2)}) collective-permute-start(bf16[128,512]{1,0:T(8,128)(2,1)S(1)} %get-tuple-element.87), channel_id=1, source_target_pairs={{0,2},{1,3},{2,0},{3,1},{4,6},{5,7},{6,4},{7,5},{8,10},{9,11},{10,... | collective-permute-start | bytes 393224 | tf_op jit(solution)/shard_map/ppermute | solution.py:399
  116.1 9.5 %collective-permute-done.21.refs_5_ = bf16[128,512]{1,0:T(8,128)(2,1)S(1)} collective-permute-done((bf16[128,512]{1,0:T(8,128)(2,1)S(1)}, bf16[128,512]{1,0:T(8,128)(2,1)S(1)}, u32[]{:S(2)}, u32[]{:S(2)}) %collective-permute-start.21) | collective-permute-done | bytes 131104 | tf_op jit(solution)/shard_map/ppermute | solution.py:399
  125.6 2.3 %collective-permute-start.28 = (bf16[2,128,512]{2,1,0:T(8,128)(2,1)S(1)}, bf16[2,128,512]{2,1,0:T(8,128)(2,1)S(1)}, u32[]{:S(2)}, u32[]{:S(2)}) collective-permute-start(bf16[2,128,512]{2,1,0:T(8,128)(2,1)S(1)} %get-tuple-element.93), channel_id=1, source_target_pairs={{0,3},{1,2},{2,1},{3,0},{4,7},{5,6},{6,5},{7,4},{8,11},{9,10},{10,... | collective-permute-start | bytes 786440 | tf_op jit(solution)/shard_map/ppermute | solution.py:399
  129.3 2.7 %collective-permute-start.24 = (bf16[2,128,512]{2,1,0:T(8,128)(2,1)S(1)}, bf16[2,128,512]{2,1,0:T(8,128)(2,1)S(1)}, u32[]{:S(2)}, u32[]{:S(2)}) collective-permute-start(bf16[2,128,512]{2,1,0:T(8,128)(2,1)S(1)} %get-tuple-element.89), channel_id=1, source_target_pairs={{0,5},{1,4},{2,7},{3,6},{4,1},{5,0},{6,3},{7,2},{8,13},{9,12},{10,... | collective-permute-start | bytes 786440 | tf_op jit(solution)/shard_map/ppermute | solution.py:399
  131.9 1.7 %collective-permute-start.25 = (bf16[2,128,512]{2,1,0:T(8,128)(2,1)S(1)}, bf16[2,128,512]{2,1,0:T(8,128)(2,1)S(1)}, u32[]{:S(2)}, u32[]{:S(2)}) collective-permute-start(bf16[2,128,512]{2,1,0:T(8,128)(2,1)S(1)} %get-tuple-element.90), channel_id=1, source_target_pairs={{0,4},{1,5},{2,6},{3,7},{4,0},{5,1},{6,2},{7,3},{8,12},{9,13},{10,... | collective-permute-start | bytes 786440 | tf_op jit(solution)/shard_map/ppermute | solution.py:399
  133.7 2.3 %shard_map.161 = bf16[8,128,512]{2,1,0:T(8,128)(2,1)} custom-call(s32[2]{0:T(128)S(1)} %pad_add_fusion.me, bf16[8,128,512]{2,1,0:T(8,128)(2,1)S(1)} %get-tuple-element.59.upstream, bf16[128,512]{1,0:T(8,128)(2,1)S(1)} %get-tuple-element.76.refs_0_, bf16[128,512]{1,0:T(8,128)(2,1)S(1)} %collective-permute-done.17.refs_1_, ...), custom_call_target="tpu_custom_call" | custom-call | flops 3145728 | bytes 3145728 | tf_op jit(solution)/shard_map/pallas_call | solution.py:332
  136.0 8.9 %collective-permute-done.28.refs_15_ = bf16[2,128,512]{2,1,0:T(8,128)(2,1)S(1)} collective-permute-done((bf16[2,128,512]{2,1,0:T(8,128)(2,1)S(1)}, bf16[2,128,512]{2,1,0:T(8,128)(2,1)S(1)}, u32[]{:S(2)}, u32[]{:S(2)}) %collective-permute-start.28) | collective-permute-done | bytes 262176 | tf_op jit(solution)/shard_map/ppermute | solution.py:399
  144.9 3.5 %shard_map.162 = (bf16[8,128,512]{2,1,0:T(8,128)(2,1)}, bf16[8,128,512]{2,1,0:T(8,128)(2,1)}, f32[8,128,512]{2,1,0:T(8,128)}) custom-call(s32[2]{0:T(128)S(1)} %pad_add_fusion.me, bf16[8,128,512]{2,1,0:T(8,128)(2,1)S(1)} %bitcast.17, bf16[8,128,512]{2,1,0:T(8,128)(2,1)S(1)} %bitcast.18, bf16[8,128,512]{2,1,0:T(8,128)(2,1)S(1)} %bitcast.19, ...), custom_call_target="tpu_custom_call" | custom-call | flops 786432 | bytes 6291456 | tf_op jit(solution)/shard_map/pallas_call | solution.py:304
  148.4 4.1 %collective-permute-done.25.refs_5_ = bf16[2,128,512]{2,1,0:T(8,128)(2,1)S(1)} collective-permute-done((bf16[2,128,512]{2,1,0:T(8,128)(2,1)S(1)}, bf16[2,128,512]{2,1,0:T(8,128)(2,1)S(1)}, u32[]{:S(2)}, u32[]{:S(2)}) %collective-permute-start.25) | collective-permute-done | bytes 262176 | tf_op jit(solution)/shard_map/ppermute | solution.py:399
  152.5 1.6 %shard_map.163 = (bf16[8,128,512]{2,1,0:T(8,128)(2,1)}, bf16[8,128,512]{2,1,0:T(8,128)(2,1)}, f32[8,128,512]{2,1,0:T(8,128)}) custom-call(s32[2]{0:T(128)S(1)} %pad_add_fusion.me, bf16[8,128,512]{2,1,0:T(8,128)(2,1)S(1)} %bitcast.23, bf16[8,128,512]{2,1,0:T(8,128)(2,1)S(1)} %bitcast.24, ...), custom_call_target="tpu_custom_call", output_to_operand_aliasing={{0}: (7, {}), {1}: (8, {}), {2}: (9, {})} | custom-call | flops 262144 | bytes 2097152 | tf_op jit(solution)/shard_map/pallas_call | solution.py:304
  (59 shorter events, 9.3 us)
Async XLA Ops:
  3.5 26.3 %collective-permute-start.1 = (bf16[1024,512]{1,0:T(8,128)(2,1)S(1)}, bf16[1024,512]{1,0:T(8,128)(2,1)}, u32[]{:S(2)}, u32[]{:S(2)}) collective-permute-start(bf16[1024,512]{1,0:T(8,128)(2,1)S(1)} %copy-done.2), channel_id=1, source_target_pairs={{0,16},{8,24},{16,0},{24,8},{1,17},{9,25},{17,1},{25,9},{2,18},{10... | collective-permute-start | bytes 3145736 | tf_op jit(solution)/shard_map/ppermute | solution.py:379
  6.5 16.5 %collective-permute-start.2 = (bf16[2,128,512]{2,1,0:T(8,128)(2,1)}, bf16[2,128,512]{2,1,0:T(8,128)(2,1)S(1)}, u32[]{:S(2)}, u32[]{:S(2)}) collective-permute-start(bf16[2,128,512]{2,1,0:T(8,128)(2,1)} %get-tuple-element.53), channel_id=1, source_target_pairs={{0,7},{1,6},{2,5},{3,4},{4,3},{5,2},{6,1},{7,0},{8,15},{9,14},{10,... | collective-permute-start | bytes 786440 | tf_op jit(solution)/shard_map/ppermute | solution.py:399
  11.1 11.9 %collective-permute-start.3 = (bf16[2,128,512]{2,1,0:T(8,128)(2,1)}, bf16[2,128,512]{2,1,0:T(8,128)(2,1)S(1)}, u32[]{:S(2)}, u32[]{:S(2)}) collective-permute-start(bf16[2,128,512]{2,1,0:T(8,128)(2,1)} %get-tuple-element.55), channel_id=1, source_target_pairs={{0,6},{1,7},{2,4},{3,5},{4,2},{5,3},{6,0},{7,1},{8,14},{9,15},{10,... | collective-permute-start | bytes 786440 | tf_op jit(solution)/shard_map/ppermute | solution.py:399
  15.2 8.4 %collective-permute-start.4 = (bf16[2,128,512]{2,1,0:T(8,128)(2,1)}, bf16[2,128,512]{2,1,0:T(8,128)(2,1)}, u32[]{:S(2)}, u32[]{:S(2)}) collective-permute-start(bf16[2,128,512]{2,1,0:T(8,128)(2,1)} %get-tuple-element.56), channel_id=1, source_target_pairs={{0,1},{1,0},{2,3},{3,2},{4,5},{5,4},{6,7},{7,6},{8,9},{9,8},{10,11... | collective-permute-start | bytes 786440 | tf_op jit(solution)/shard_map/ppermute | solution.py:399
  15.8 22.3 %collective-permute-start = (bf16[1024,512]{1,0:T(8,128)(2,1)S(1)}, bf16[1024,512]{1,0:T(8,128)(2,1)S(1)}, u32[]{:S(2)}, u32[]{:S(2)}) collective-permute-start(bf16[1024,512]{1,0:T(8,128)(2,1)S(1)} %copy-done.2), channel_id=1, source_target_pairs={{0,8},{8,0},{16,24},{24,16},{1,9},{9,1},{17,25},{25,17},{2,10},{10... | collective-permute-start | bytes 3145736 | tf_op jit(solution)/shard_map/ppermute | solution.py:393
  29.8 8.3 %collective-permute-start.5 = (bf16[1024,512]{1,0:T(8,128)(2,1)}, bf16[1024,512]{1,0:T(8,128)(2,1)}, u32[]{:S(2)}, u32[]{:S(2)}) collective-permute-start(bf16[1024,512]{1,0:T(8,128)(2,1)} %collective-permute-done.1.refs_6_), channel_id=1, source_target_pairs={{0,8},{8,0},{16,24},{24,16},{1,9},{9,1},{17,25},{25,17},{2,10},{10... | collective-permute-start | bytes 3145736 | tf_op jit(solution)/shard_map/ppermute | solution.py:393
  29.8 31.7 %collective-permute-start.6 = (bf16[2,128,512]{2,1,0:T(8,128)(2,1)}, bf16[2,128,512]{2,1,0:T(8,128)(2,1)}, u32[]{:S(2)}, u32[]{:S(2)}) collective-permute-start(bf16[2,128,512]{2,1,0:T(8,128)(2,1)} %get-tuple-element.57), channel_id=1, source_target_pairs={{0,5},{1,4},{2,7},{3,6},{4,1},{5,0},{6,3},{7,2},{8,13},{9,12},{10,... | collective-permute-start | bytes 786440 | tf_op jit(solution)/shard_map/ppermute | solution.py:399
  35.0 19.5 %collective-permute-start.7 = (bf16[2,128,512]{2,1,0:T(8,128)(2,1)}, bf16[2,128,512]{2,1,0:T(8,128)(2,1)}, u32[]{:S(2)}, u32[]{:S(2)}) collective-permute-start(bf16[2,128,512]{2,1,0:T(8,128)(2,1)} %get-tuple-element.63), channel_id=1, source_target_pairs={{0,3},{1,2},{2,1},{3,0},{4,7},{5,6},{6,5},{7,4},{8,11},{9,10},{10,... | collective-permute-start | bytes 786440 | tf_op jit(solution)/shard_map/ppermute | solution.py:399
  35.1 26.3 %collective-permute-start.8 = (bf16[2,128,512]{2,1,0:T(8,128)(2,1)}, bf16[2,128,512]{2,1,0:T(8,128)(2,1)}, u32[]{:S(2)}, u32[]{:S(2)}) collective-permute-start(bf16[2,128,512]{2,1,0:T(8,128)(2,1)} %get-tuple-element.64), channel_id=1, source_target_pairs={{0,2},{1,3},{2,0},{3,1},{4,6},{5,7},{6,4},{7,5},{8,10},{9,11},{10,... | collective-permute-start | bytes 786440 | tf_op jit(solution)/shard_map/ppermute | solution.py:399
  38.1 23.4 %collective-permute-start.9 = (bf16[2,128,512]{2,1,0:T(8,128)(2,1)}, bf16[2,128,512]{2,1,0:T(8,128)(2,1)S(1)}, u32[]{:S(2)}, u32[]{:S(2)}) collective-permute-start(bf16[2,128,512]{2,1,0:T(8,128)(2,1)} %get-tuple-element.65), channel_id=1, source_target_pairs={{0,4},{1,5},{2,6},{3,7},{4,0},{5,1},{6,2},{7,3},{8,12},{9,13},{10,... | collective-permute-start | bytes 786440 | tf_op jit(solution)/shard_map/ppermute | solution.py:399
  47.9 17.5 %collective-permute-start.10 = (bf16[128,512]{1,0:T(8,128)(2,1)S(1)}, bf16[128,512]{1,0:T(8,128)(2,1)S(1)}, u32[]{:S(2)}, u32[]{:S(2)}) collective-permute-start(bf16[128,512]{1,0:T(8,128)(2,1)S(1)} %get-tuple-element.68), channel_id=1, source_target_pairs={{0,7},{1,6},{2,5},{3,4},{4,3},{5,2},{6,1},{7,0},{8,15},{9,14},{10,... | collective-permute-start | bytes 393224 | tf_op jit(solution)/shard_map/ppermute | solution.py:399
  54.5 13.8 %collective-permute-start.11 = (bf16[128,512]{1,0:T(8,128)(2,1)S(1)}, bf16[128,512]{1,0:T(8,128)(2,1)S(1)}, u32[]{:S(2)}, u32[]{:S(2)}) collective-permute-start(bf16[128,512]{1,0:T(8,128)(2,1)S(1)} %get-tuple-element.69), channel_id=1, source_target_pairs={{0,3},{1,2},{2,1},{3,0},{4,7},{5,6},{6,5},{7,4},{8,11},{9,10},{10,... | collective-permute-start | bytes 393224 | tf_op jit(solution)/shard_map/ppermute | solution.py:399
  61.5 15.8 %collective-permute-start.12 = (bf16[128,512]{1,0:T(8,128)(2,1)S(1)}, bf16[128,512]{1,0:T(8,128)(2,1)S(1)}, u32[]{:S(2)}, u32[]{:S(2)}) collective-permute-start(bf16[128,512]{1,0:T(8,128)(2,1)S(1)} %get-tuple-element.70), channel_id=1, source_target_pairs={{0,2},{1,3},{2,0},{3,1},{4,6},{5,7},{6,4},{7,5},{8,10},{9,11},{10,... | collective-permute-start | bytes 393224 | tf_op jit(solution)/shard_map/ppermute | solution.py:399
  61.5 17.8 %collective-permute-start.13 = (bf16[128,512]{1,0:T(8,128)(2,1)S(1)}, bf16[128,512]{1,0:T(8,128)(2,1)S(1)}, u32[]{:S(2)}, u32[]{:S(2)}) collective-permute-start(bf16[128,512]{1,0:T(8,128)(2,1)S(1)} %get-tuple-element.71), channel_id=1, source_target_pairs={{0,1},{1,0},{2,3},{3,2},{4,5},{5,4},{6,7},{7,6},{8,9},{9,8},{10,11... | collective-permute-start | bytes 393224 | tf_op jit(solution)/shard_map/ppermute | solution.py:399
  61.5 20.4 %collective-permute-start.14 = (bf16[128,512]{1,0:T(8,128)(2,1)S(1)}, bf16[128,512]{1,0:T(8,128)(2,1)S(1)}, u32[]{:S(2)}, u32[]{:S(2)}) collective-permute-start(bf16[128,512]{1,0:T(8,128)(2,1)S(1)} %get-tuple-element.72), channel_id=1, source_target_pairs={{0,6},{1,7},{2,4},{3,5},{4,2},{5,3},{6,0},{7,1},{8,14},{9,15},{10,... | collective-permute-start | bytes 393224 | tf_op jit(solution)/shard_map/ppermute | solution.py:399
  65.3 24.8 %collective-permute-start.15 = (bf16[128,512]{1,0:T(8,128)(2,1)S(1)}, bf16[128,512]{1,0:T(8,128)(2,1)S(1)}, u32[]{:S(2)}, u32[]{:S(2)}) collective-permute-start(bf16[128,512]{1,0:T(8,128)(2,1)S(1)} %get-tuple-element.73), channel_id=1, source_target_pairs={{0,5},{1,4},{2,7},{3,6},{4,1},{5,0},{6,3},{7,2},{8,13},{9,12},{10,... | collective-permute-start | bytes 393224 | tf_op jit(solution)/shard_map/ppermute | solution.py:399
  68.2 23.8 %collective-permute-start.16 = (bf16[128,512]{1,0:T(8,128)(2,1)S(1)}, bf16[128,512]{1,0:T(8,128)(2,1)S(1)}, u32[]{:S(2)}, u32[]{:S(2)}) collective-permute-start(bf16[128,512]{1,0:T(8,128)(2,1)S(1)} %get-tuple-element.74), channel_id=1, source_target_pairs={{0,4},{1,5},{2,6},{3,7},{4,0},{5,1},{6,2},{7,3},{8,12},{9,13},{10,... | collective-permute-start | bytes 393224 | tf_op jit(solution)/shard_map/ppermute | solution.py:399
  77.3 31.6 %collective-permute-start.17 = (bf16[128,512]{1,0:T(8,128)(2,1)S(1)}, bf16[128,512]{1,0:T(8,128)(2,1)S(1)}, u32[]{:S(2)}, u32[]{:S(2)}) collective-permute-start(bf16[128,512]{1,0:T(8,128)(2,1)S(1)} %get-tuple-element.77), channel_id=1, source_target_pairs={{0,7},{1,6},{2,5},{3,4},{4,3},{5,2},{6,1},{7,0},{8,15},{9,14},{10,... | collective-permute-start | bytes 393224 | tf_op jit(solution)/shard_map/ppermute | solution.py:399
  79.2 33.4 %collective-permute-start.18 = (bf16[128,512]{1,0:T(8,128)(2,1)S(1)}, bf16[128,512]{1,0:T(8,128)(2,1)S(1)}, u32[]{:S(2)}, u32[]{:S(2)}) collective-permute-start(bf16[128,512]{1,0:T(8,128)(2,1)S(1)} %get-tuple-element.78), channel_id=1, source_target_pairs={{0,6},{1,7},{2,4},{3,5},{4,2},{5,3},{6,0},{7,1},{8,14},{9,15},{10,... | collective-permute-start | bytes 393224 | tf_op jit(solution)/shard_map/ppermute | solution.py:399
  92.0 20.6 %collective-permute-start.19 = (bf16[128,512]{1,0:T(8,128)(2,1)S(1)}, bf16[128,512]{1,0:T(8,128)(2,1)S(1)}, u32[]{:S(2)}, u32[]{:S(2)}) collective-permute-start(bf16[128,512]{1,0:T(8,128)(2,1)S(1)} %get-tuple-element.84), channel_id=1, source_target_pairs={{0,5},{1,4},{2,7},{3,6},{4,1},{5,0},{6,3},{7,2},{8,13},{9,12},{10,... | collective-permute-start | bytes 393224 | tf_op jit(solution)/shard_map/ppermute | solution.py:399
  92.5 23.1 %collective-permute-start.20 = (bf16[128,512]{1,0:T(8,128)(2,1)S(1)}, bf16[128,512]{1,0:T(8,128)(2,1)S(1)}, u32[]{:S(2)}, u32[]{:S(2)}) collective-permute-start(bf16[128,512]{1,0:T(8,128)(2,1)S(1)} %get-tuple-element.85), channel_id=1, source_target_pairs={{0,4},{1,5},{2,6},{3,7},{4,0},{5,1},{6,2},{7,3},{8,12},{9,13},{10,... | collective-permute-start | bytes 393224 | tf_op jit(solution)/shard_map/ppermute | solution.py:399
  108.8 36.1 %copy-start = (bf16[1024,512]{1,0:T(8,128)(2,1)S(1)}, bf16[1024,512]{1,0:T(8,128)(2,1)}, u32[]{:S(2)}) copy-start(bf16[1024,512]{1,0:T(8,128)(2,1)} %param.14) | copy-start | bytes 3145732
  108.8 20.5 %collective-permute-start.26 = (bf16[2,128,512]{2,1,0:T(8,128)(2,1)S(1)}, bf16[2,128,512]{2,1,0:T(8,128)(2,1)S(1)}, u32[]{:S(2)}, u32[]{:S(2)}) collective-permute-start(bf16[2,128,512]{2,1,0:T(8,128)(2,1)S(1)} %get-tuple-element.91), channel_id=1, source_target_pairs={{0,7},{1,6},{2,5},{3,4},{4,3},{5,2},{6,1},{7,0},{8,15},{9,14},{10,... | collective-permute-start | bytes 786440 | tf_op jit(solution)/shard_map/ppermute | solution.py:399
  108.9 23.1 %collective-permute-start.27 = (bf16[2,128,512]{2,1,0:T(8,128)(2,1)S(1)}, bf16[2,128,512]{2,1,0:T(8,128)(2,1)S(1)}, u32[]{:S(2)}, u32[]{:S(2)}) collective-permute-start(bf16[2,128,512]{2,1,0:T(8,128)(2,1)S(1)} %get-tuple-element.92), channel_id=1, source_target_pairs={{0,6},{1,7},{2,4},{3,5},{4,2},{5,3},{6,0},{7,1},{8,14},{9,15},{10,... | collective-permute-start | bytes 786440 | tf_op jit(solution)/shard_map/ppermute | solution.py:399
  112.6 13.0 %collective-permute-start.21 = (bf16[128,512]{1,0:T(8,128)(2,1)S(1)}, bf16[128,512]{1,0:T(8,128)(2,1)S(1)}, u32[]{:S(2)}, u32[]{:S(2)}) collective-permute-start(bf16[128,512]{1,0:T(8,128)(2,1)S(1)} %get-tuple-element.86), channel_id=1, source_target_pairs={{0,3},{1,2},{2,1},{3,0},{4,7},{5,6},{6,5},{7,4},{8,11},{9,10},{10,... | collective-permute-start | bytes 393224 | tf_op jit(solution)/shard_map/ppermute | solution.py:399
  112.6 15.2 %collective-permute-start.22 = (bf16[128,512]{1,0:T(8,128)(2,1)S(1)}, bf16[128,512]{1,0:T(8,128)(2,1)S(1)}, u32[]{:S(2)}, u32[]{:S(2)}) collective-permute-start(bf16[128,512]{1,0:T(8,128)(2,1)S(1)} %get-tuple-element.87), channel_id=1, source_target_pairs={{0,2},{1,3},{2,0},{3,1},{4,6},{5,7},{6,4},{7,5},{8,10},{9,11},{10,... | collective-permute-start | bytes 393224 | tf_op jit(solution)/shard_map/ppermute | solution.py:399
  115.6 13.6 %collective-permute-start.23 = (bf16[128,512]{1,0:T(8,128)(2,1)S(1)}, bf16[128,512]{1,0:T(8,128)(2,1)S(1)}, u32[]{:S(2)}, u32[]{:S(2)}) collective-permute-start(bf16[128,512]{1,0:T(8,128)(2,1)S(1)} %get-tuple-element.88), channel_id=1, source_target_pairs={{0,1},{1,0},{2,3},{3,2},{4,5},{5,4},{6,7},{7,6},{8,9},{9,8},{10,11... | collective-permute-start | bytes 393224 | tf_op jit(solution)/shard_map/ppermute | solution.py:399
  125.6 19.3 %collective-permute-start.28 = (bf16[2,128,512]{2,1,0:T(8,128)(2,1)S(1)}, bf16[2,128,512]{2,1,0:T(8,128)(2,1)S(1)}, u32[]{:S(2)}, u32[]{:S(2)}) collective-permute-start(bf16[2,128,512]{2,1,0:T(8,128)(2,1)S(1)} %get-tuple-element.93), channel_id=1, source_target_pairs={{0,3},{1,2},{2,1},{3,0},{4,7},{5,6},{6,5},{7,4},{8,11},{9,10},{10,... | collective-permute-start | bytes 786440 | tf_op jit(solution)/shard_map/ppermute | solution.py:399
  127.9 17.0 %collective-permute-start.29 = (bf16[2,128,512]{2,1,0:T(8,128)(2,1)S(1)}, bf16[2,128,512]{2,1,0:T(8,128)(2,1)S(1)}, u32[]{:S(2)}, u32[]{:S(2)}) collective-permute-start(bf16[2,128,512]{2,1,0:T(8,128)(2,1)S(1)} %get-tuple-element.94), channel_id=1, source_target_pairs={{0,2},{1,3},{2,0},{3,1},{4,6},{5,7},{6,4},{7,5},{8,10},{9,11},{10,... | collective-permute-start | bytes 786440 | tf_op jit(solution)/shard_map/ppermute | solution.py:399
  129.3 15.6 %collective-permute-start.30 = (bf16[2,128,512]{2,1,0:T(8,128)(2,1)S(1)}, bf16[2,128,512]{2,1,0:T(8,128)(2,1)S(1)}, u32[]{:S(2)}, u32[]{:S(2)}) collective-permute-start(bf16[2,128,512]{2,1,0:T(8,128)(2,1)S(1)} %get-tuple-element.95), channel_id=1, source_target_pairs={{0,1},{1,0},{2,3},{3,2},{4,5},{5,4},{6,7},{7,6},{8,9},{9,8},{10,11... | collective-permute-start | bytes 786440 | tf_op jit(solution)/shard_map/ppermute | solution.py:399
  129.3 19.1 %collective-permute-start.24 = (bf16[2,128,512]{2,1,0:T(8,128)(2,1)S(1)}, bf16[2,128,512]{2,1,0:T(8,128)(2,1)S(1)}, u32[]{:S(2)}, u32[]{:S(2)}) collective-permute-start(bf16[2,128,512]{2,1,0:T(8,128)(2,1)S(1)} %get-tuple-element.89), channel_id=1, source_target_pairs={{0,5},{1,4},{2,7},{3,6},{4,1},{5,0},{6,3},{7,2},{8,13},{9,12},{10,... | collective-permute-start | bytes 786440 | tf_op jit(solution)/shard_map/ppermute | solution.py:399
  131.9 20.6 %collective-permute-start.25 = (bf16[2,128,512]{2,1,0:T(8,128)(2,1)S(1)}, bf16[2,128,512]{2,1,0:T(8,128)(2,1)S(1)}, u32[]{:S(2)}, u32[]{:S(2)}) collective-permute-start(bf16[2,128,512]{2,1,0:T(8,128)(2,1)S(1)} %get-tuple-element.90), channel_id=1, source_target_pairs={{0,4},{1,5},{2,6},{3,7},{4,0},{5,1},{6,2},{7,3},{8,12},{9,13},{10,... | collective-permute-start | bytes 786440 | tf_op jit(solution)/shard_map/ppermute | solution.py:399
  (8 other events, 187.9 us)
